TPU v7x, 256 devices: a whole 4x4x8 slice. The times are simulated.
256 devices in a mesh: blk: 64 (over y_lo, x, z), grid: 4 (over y_hi, core).
Axes of the slice: x: 4, y: 4 (y_hi: 2, y_lo: 2; y = y_hi * 2 + y_lo), z: 8, core: 2. Of those that a mesh axis runs over, the one named last changes fastest.
Arguments:
- patches: bfloat16 [4, 8192, 1024], P('grid', 'blk'), may hold values from -6 to 6
- stem_weight: bfloat16 [2, 1024, 768], replicated, may hold values from -0.125 to 0.125
- norm_gain: bfloat16 [768], replicated, may hold values from 0.25 to 1.75
- w_qkv: bfloat16 [768, 1280], replicated, may hold values from -0.21875 to 0.21875
- w_out: bfloat16 [768, 768], replicated, may hold values from -0.21875 to 0.21875
- per_head_scale: float32 [12], replicated, may hold values from 0.05 to 1, as said below
- positions: int32 [8192], replicated, may hold values from 0 to 8191, each once
- d_out: bfloat16 [4, 8192, 768], P('grid', 'blk'), may hold values from -48 to 48
Outputs:
- d_stem_weight: float32 [2, 1024, 768], P(None, None, ('blk', 'grid'))
- d_norm_gain: float32 [768], P(('blk', 'grid'))
- d_w_qkv: float32 [768, 1280], P(('blk', 'grid'))
- d_w_out: float32 [768, 768], P(None, ('blk', 'grid'))
Inputs may be any that keep to these rules, and one draw needn't show every extreme that they name: A permutation of the 8192 positions of a band. `per_head_scale`: positive.
All inputs are finite; a program needn't handle non-finite values.
Results may differ from a plain program's by a relative error of at most 0.015.
The roundings to bfloat16 on the way count: a program that leaves them out, or rounds other values in their place, can miss the bound.
Values may be sent and summed in bfloat16 or wider, within the bound.
No kernel may reach another device: no remote copies, remote signals or barrier semaphores. Data moves between devices by JAX's collectives and lax.ppermute only.
A program may use at most 128 MiB of HBM per device.

v0:
```python
import jax
import jax.numpy as jnp
from jax import lax
from jax.sharding import PartitionSpec as P

QUERY_HEADS = 12
KEY_VALUE_HEADS = 4
HEAD_SIZE = 64
TC = 16


def shifted(x, axis, by):
    peers = lax.axis_size(axis)
    pairs = [(i, i + by) for i in range(peers) if 0 <= i + by < peers]
    return lax.ppermute(x, axis, pairs)


def passed_along(x, axis, by):
    peers = lax.axis_size(axis)
    return lax.ppermute(x, axis, [(i, (i + by) % peers) for i in range(peers)])


def row_norm(values):
    return values * lax.rsqrt(jnp.mean(values * values, axis=-1, keepdims=True) + 1e-05)


def head_norm(values):
    return values * lax.rsqrt(jnp.mean(values * values, axis=-1, keepdims=True) + 1e-06)


def shards(patches, stem_weight, norm_gain, w_qkv, w_out, per_head_scale, positions, d_out):
    tiles = patches[0]
    grad_out = d_out[0]
    token_rows = tiles.shape[0]
    group_factor = QUERY_HEADS // KEY_VALUE_HEADS
    query_span_width = QUERY_HEADS * HEAD_SIZE
    key_span_width = KEY_VALUE_HEADS * HEAD_SIZE
    arrived = shifted(tiles[:TC], "grid", -1)
    below = jnp.concatenate([tiles[TC:], arrived], axis=0)
    stem = jnp.dot(tiles, stem_weight[0], preferred_element_type=jnp.float32)
    stem = stem + jnp.dot(below, stem_weight[1], preferred_element_type=jnp.float32)
    token_f = lax.optimization_barrier(stem.astype(jnp.bfloat16)).astype(jnp.float32)
    gain_f = norm_gain.astype(jnp.float32)
    normed = row_norm(token_f)
    hidden = (normed * gain_f).astype(jnp.bfloat16)
    query_key_value = jnp.dot(hidden, w_qkv, preferred_element_type=jnp.float32)
    query = query_key_value[:, :query_span_width].reshape(token_rows, QUERY_HEADS, HEAD_SIZE)
    key = query_key_value[:, query_span_width : query_span_width + key_span_width].reshape(
        token_rows, KEY_VALUE_HEADS, HEAD_SIZE
    )
    query_normalized = head_norm(query).astype(jnp.bfloat16)
    key_n = head_norm(key).astype(jnp.bfloat16).reshape(token_rows, key_span_width)
    value = query_key_value[:, query_span_width + key_span_width :].astype(jnp.bfloat16)
    attention_gradient = jnp.dot(grad_out, w_out.T, preferred_element_type=jnp.float32).astype(
        jnp.bfloat16
    )
    kv_own = jnp.concatenate([key_n, value], axis=1)
    blk_count = lax.axis_size("blk")
    own_index = lax.axis_index("blk")
    blocks = [kv_own]
    moving = kv_own
    for offset in range(1, 4):
        moving = passed_along(moving, "blk", 1)
        blocks.append(moving)
    causal_window = jnp.concatenate(blocks, axis=0)
    key_pos = jnp.concatenate(
        [
            lax.dynamic_slice_in_dim(
                positions, (own_index - offset) % blk_count * token_rows, token_rows
            )
            for offset in range(4)
        ]
    )
    query_pos = lax.dynamic_slice_in_dim(positions, own_index * token_rows, token_rows)
    visible = (key_pos[None, :] <= query_pos[:, None])[None]
    every_key = causal_window.shape[0]
    query_cube = query_normalized.reshape(token_rows, KEY_VALUE_HEADS, group_factor, HEAD_SIZE)
    gradient_cube = attention_gradient.reshape(token_rows, KEY_VALUE_HEADS, group_factor, HEAD_SIZE)
    key_cube = causal_window[:, :key_span_width].reshape(every_key, KEY_VALUE_HEADS, HEAD_SIZE)
    value_cube = causal_window[:, key_span_width:].reshape(every_key, KEY_VALUE_HEADS, HEAD_SIZE)
    score_scales = per_head_scale.reshape(KEY_VALUE_HEADS, group_factor)
    prob_list = []
    low_list = []
    attn_list = []
    for query_head_group in range(KEY_VALUE_HEADS):
        scale_col = score_scales[query_head_group][:, None, None]
        attention_scores = (
            jnp.einsum(
                "trd,sd->rts",
                query_cube[:, query_head_group],
                key_cube[:, query_head_group],
                preferred_element_type=jnp.float32,
            )
            * scale_col
        )
        attention_scores = jnp.where(visible, attention_scores, -1e30)
        top = jnp.max(attention_scores, axis=-1, keepdims=True)
        weights = jnp.where(visible, jnp.exp(attention_scores - top), 0.0)
        probs = weights / jnp.sum(weights, axis=-1, keepdims=True)
        probability_narrow = probs.astype(jnp.bfloat16)
        prob_list.append(probs)
        low_list.append(probability_narrow)
        attn_list.append(
            jnp.einsum(
                "rts,sd->trd",
                probability_narrow,
                value_cube[:, query_head_group],
                preferred_element_type=jnp.float32,
            )
        )
    attention_output = (
        jnp.stack(attn_list, axis=1).reshape(token_rows, query_span_width).astype(jnp.bfloat16)
    )
    out_term = jnp.dot(attention_output.T, grad_out, preferred_element_type=jnp.float32)
    d_w_out = lax.psum_scatter(out_term, ("blk", "grid"), scatter_dimension=1, tiled=True)
    dquery_list = []
    dkey_list = []
    dvalue_list = []
    for query_head_group in range(KEY_VALUE_HEADS):
        scale_col = score_scales[query_head_group][:, None, None]
        grad_group = gradient_cube[:, query_head_group]
        softmax_delta = jnp.sum(
            grad_group.astype(jnp.float32) * attn_list[query_head_group], axis=-1
        )
        probability_gradient = jnp.einsum(
            "trd,sd->rts",
            grad_group,
            value_cube[:, query_head_group],
            preferred_element_type=jnp.float32,
        )
        score_gradient = (
            scale_col
            * prob_list[query_head_group]
            * (probability_gradient - softmax_delta.T[:, :, None])
        ).astype(jnp.bfloat16)
        dquery_list.append(
            jnp.einsum(
                "rts,sd->trd",
                score_gradient,
                key_cube[:, query_head_group],
                preferred_element_type=jnp.float32,
            )
        )
        dkey_list.append(
            jnp.einsum(
                "rts,trd->sd",
                score_gradient,
                query_cube[:, query_head_group],
                preferred_element_type=jnp.float32,
            )
        )
        dvalue_list.append(
            jnp.einsum(
                "rts,trd->sd",
                low_list[query_head_group],
                grad_group,
                preferred_element_type=jnp.float32,
            )
        )
    query_gradient = jnp.stack(dquery_list, axis=1).reshape(token_rows, QUERY_HEADS, HEAD_SIZE)
    dkey_all = jnp.stack(dkey_list, axis=1).reshape(every_key, key_span_width)
    dvalue_all = jnp.stack(dvalue_list, axis=1).reshape(every_key, key_span_width)
    partial_terms = jnp.concatenate([dkey_all, dvalue_all], axis=1)
    pieces = [partial_terms[offset * token_rows : (offset + 1) * token_rows] for offset in range(4)]
    carried_state = pieces[3]
    for offset in (2, 1, 0):
        carried_state = passed_along(carried_state, "blk", -1) + pieces[offset]
    pull_query = jax.vjp(head_norm, query)[1]
    gather_key = jax.vjp(head_norm, key)[1]
    dq_full = pull_query(query_gradient)[0].reshape(token_rows, query_span_width)
    key_gradient_whole = gather_key(
        carried_state[:, :key_span_width].reshape(token_rows, KEY_VALUE_HEADS, HEAD_SIZE)
    )[0].reshape(token_rows, key_span_width)
    d_qkv = jnp.concatenate(
        [dq_full, key_gradient_whole, carried_state[:, key_span_width:]], axis=1
    ).astype(jnp.bfloat16)
    qkv_term = jnp.dot(hidden.T, d_qkv, preferred_element_type=jnp.float32)
    d_hidden = jnp.dot(d_qkv, w_qkv.T, preferred_element_type=jnp.float32)
    gain_term = jnp.sum(d_hidden * normed, axis=0)
    pull_tokens = jax.vjp(row_norm, token_f)[1]
    d_tokens = (grad_out.astype(jnp.float32) + pull_tokens(d_hidden * gain_f)[0]).astype(
        jnp.bfloat16
    )
    stem_term = jnp.stack(
        [
            jnp.dot(tiles.T, d_tokens, preferred_element_type=jnp.float32),
            jnp.dot(below.T, d_tokens, preferred_element_type=jnp.float32),
        ]
    )
    d_stem_weight, d_norm_gain, d_w_qkv = (
        lax.psum_scatter(stem_term, ("blk", "grid"), scatter_dimension=2, tiled=True),
        lax.psum_scatter(gain_term, ("blk", "grid"), scatter_dimension=0, tiled=True),
        lax.psum_scatter(qkv_term, ("blk", "grid"), scatter_dimension=0, tiled=True),
    )
    return (d_stem_weight, d_norm_gain, d_w_qkv, d_w_out)


def solution(mesh):
    placed = (P("grid", "blk", None), P(), P(), P(), P(), P(), P(), P("grid", "blk", None))
    return jax.shard_map(
        shards,
        mesh=mesh,
        in_specs=placed,
        out_specs=(
            P(None, None, ("blk", "grid")),
            P(("blk", "grid")),
            P(("blk", "grid"), None),
            P(None, ("blk", "grid")),
        ),
        check_vma=False,
    )
```

profile of v0, /device:TPU:1, one launch (start us, length us, event | category | flops | bytes accessed | tf_op | source)
XLA Modules:
  0.0 440.1 jit_solution(5615072598088670736)
XLA Ops:
  7.2 0.9 slice_bitcast_fusion.73
  8.2 5.1 %collective-permute-start = (bf16[16,1024]{1,0:T(8,128)(2,1)S(1)}, bf16[16,1024]{1,0:T(8,128)(2,1)S(1)}, u32[]{:S(2)}, u32[]{:S(2)}) collective-permute-start(bf16[16,1024]{1,0:T(8,128)(2,1)S(1)} %slice_bitcast_fusion.73), channel_id=1, source_target_pairs={{1,0},{2,1},{3,2},{5,4},{6,5},{7,6},{9,8},{10,9},{11,10},{13,12},{... | collective-permute-start | bytes 98312 | tf_op jit(solution)/shard_map/ppermute | solution.py:15
  13.4 1.0 slice_bitcast_fusion
  14.4 2.7 fusion.6
  17.0 2.1 convolution_convert_fusion
  20.9 1.9 fusion.45
  27.3 9.0 %collective-permute-done.1 = bf16[128,512]{1,0:T(8,128)(2,1)} collective-permute-done((bf16[128,512]{1,0:T(8,128)(2,1)}, bf16[128,512]{1,0:T(8,128)(2,1)}, u32[]{:S(2)}, u32[]{:S(2)}) %collective-permute-start.1) | collective-permute-done | bytes 131104 | tf_op jit(solution)/shard_map/ppermute | solution.py:20
  37.0 0.9 copy.97
  37.9 7.7 %collective-permute-done.2 = bf16[128,512]{1,0:T(8,128)(2,1)} collective-permute-done((bf16[128,512]{1,0:T(8,128)(2,1)}, bf16[128,512]{1,0:T(8,128)(2,1)}, u32[]{:S(2)}, u32[]{:S(2)}) %collective-permute-start.2) | collective-permute-done | bytes 131104 | tf_op jit(solution)/shard_map/ppermute | solution.py:20
  45.6 1.4 multiply_convert_fusion
  47.0 6.8 %collective-permute-done.3 = bf16[128,512]{1,0:T(8,128)(2,1)S(1)} collective-permute-done((bf16[128,512]{1,0:T(8,128)(2,1)}, bf16[128,512]{1,0:T(8,128)(2,1)S(1)}, u32[]{:S(2)}, u32[]{:S(2)}) %collective-permute-start.3) | collective-permute-done | bytes 131104 | tf_op jit(solution)/shard_map/ppermute | solution.py:20
  53.9 1.0 pad_maximum_fusion.1
  55.2 2.3 fusion.100
  57.5 1.3 fusion.59
  59.0 1.0 convolution_bitcast_fusion.8
  60.1 2.3 fusion.98
  62.4 1.2 fusion.61
  65.3 2.3 fusion.99
  67.6 1.2 fusion.60
  70.5 2.3 fusion.97
  72.8 1.2 fusion.58
  74.3 1.9 multiply_reduce_fusion.4
  76.2 1.4 fusion.41
  80.5 0.9 convolution_bitcast_fusion.13
  85.8 1.1 pad_maximum_fusion.4
  87.0 0.9 copy.96
  87.9 1.1 pad_maximum_fusion.2
  90.7 1.9 copy.98
  92.6 1.0 pad_maximum_fusion.8
  93.6 1.8 collective-permute-done.4
  95.4 1.0 fusion.66
  96.4 5.0 %collective-permute-start.5 = (f32[128,512]{1,0:T(8,128)S(1)}, f32[128,512]{1,0:T(8,128)S(1)}, u32[]{:S(2)}, u32[]{:S(2)}) collective-permute-start(f32[128,512]{1,0:T(8,128)S(1)} %fusion.66), channel_id=1, source_target_pairs={{0,252},{4,0},{8,4},{12,8},{16,12},{20,16},{24,20},{28,24},{32,28}... | collective-permute-start | bytes 786440 | tf_op jit(solution)/shard_map/ppermute | solution.py:20
  101.4 1.9 fusion.70
  103.4 1.4 collective-permute-done.5
  104.8 6.2 %collective-permute-start.6 = (f32[128,512]{1,0:T(8,128)S(1)}, f32[128,512]{1,0:T(8,128)S(1)}, u32[]{:S(2)}, u32[]{:S(2)}) collective-permute-start(f32[128,512]{1,0:T(8,128)S(1)} %fusion.63), channel_id=1, source_target_pairs={{0,252},{4,0},{8,4},{12,8},{16,12},{20,16},{24,20},{28,24},{32,28}... | collective-permute-start | bytes 786440 | tf_op jit(solution)/shard_map/ppermute | solution.py:20
  111.8 2.5 collective-permute-done.6
  115.0 1.0 slice.324
  116.0 0.9 slice_multiply_fusion
  117.2 1.0 fusion.75
  118.2 1.8 fusion.51
  120.1 2.6 fusion.73
  124.3 3.2 pad_maximum_fusion
  127.5 10.3 %copy.113 = f32[2,1024,768]{1,0,2:T(2,128)} copy(f32[2,1024,768]{1,2,0:T(8,128)} %pad_maximum_fusion) | data formatting | bytes 12582912 | tf_op jit(solution)/shard_map/stack | solution.py:184
  137.8 81.7 %all-reduce.1 = f32[768]{0:T(1024)S(1)} all-reduce(f32[768]{0:T(1024)S(1)} %get-tuple-element.12), channel_id=3, replica_groups=mesh['blk'=64,'grid'=4] {'blk','grid'}, use_global_device_ids=true, to_apply=%region_20.21.clone | all-reduce | flops 768 | bytes 6144
  220.2 208.8 %all-reduce.7.cloned.1.call-done = (f32[2,1024,768]{1,0,2:T(2,128)}, f32[768,1280]{1,0:T(8,128)}, f32[768,768]{0,1:T(8,128)}) async-done(((f32[2,1024,768]{1,0,2:T(2,128)}, f32[768,1280]{1,0:T(8,128)}, f32[768,768]{0,1:T(8,128)}), (f32[2,1024,768]{1,0,2:T(2,128)}, f32[768,1280]{1,0:T(8,128)}, f32[768,768]{0,1:T(8,128)})) %all-reduce.7.cloned.1.call-update) | async-done | bytes 12582928
  429.0 1.3 constant_dynamic-slice_fusion.2
  430.3 1.4 constant_dynamic-slice_fusion
  431.7 1.5 constant_dynamic-slice_fusion.1
  (152 shorter events, 23.9 us)
Async XLA Ops:
  7.2 16.3 %copy-start = (bf16[768,1280]{1,0:T(8,128)(2,1)S(1)}, bf16[768,1280]{1,0:T(8,128)(2,1)}, u32[]{:S(2)}) copy-start(bf16[768,1280]{1,0:T(8,128)(2,1)} %param.11) | copy-start | bytes 5898244
  7.2 9.9 %copy-start.9 = (bf16[768,768]{1,0:T(8,128)(2,1)S(1)}, bf16[768,768]{1,0:T(8,128)(2,1)}, u32[]{:S(2)}) copy-start(bf16[768,768]{1,0:T(8,128)(2,1)} %param.12) | copy-start | bytes 3538948
  7.2 13.6 %copy-start.34 = (bf16[768]{0:T(1024)(128)(2,1)S(1)}, bf16[768]{0:T(1024)(128)(2,1)}, u32[]{:S(2)}) copy-start(bf16[768]{0:T(1024)(128)(2,1)} %param.10) | copy-start | bytes 4612
  7.2 421.8 %all-reduce.7.cloned.1.call-start = ((), (), s32[]{:S(2)}) async-start(), calls=%async_computation | async-start | bytes 25165824
  8.2 12.7 %collective-permute-start = (bf16[16,1024]{1,0:T(8,128)(2,1)S(1)}, bf16[16,1024]{1,0:T(8,128)(2,1)S(1)}, u32[]{:S(2)}, u32[]{:S(2)}) collective-permute-start(bf16[16,1024]{1,0:T(8,128)(2,1)S(1)} %slice_bitcast_fusion.73), channel_id=1, source_target_pairs={{1,0},{2,1},{3,2},{5,4},{6,5},{7,6},{9,8},{10,9},{11,10},{13,12},{... | collective-permute-start | bytes 98312 | tf_op jit(solution)/shard_map/ppermute | solution.py:15
  14.3 8.5 %copy-start.14 = (bf16[112,1024]{1,0:T(8,128)(2,1)}, bf16[112,1024]{1,0:T(8,128)(2,1)S(1)}, u32[]{:S(2)}) copy-start(bf16[112,1024]{1,0:T(8,128)(2,1)S(1)} %slice_bitcast_fusion) | copy-start | bytes 688132
  20.8 3.2 copy-start.25
  20.8 4.8 %copy-start.31 = (f32[12]{0:T(128)S(1)}, f32[12]{0:T(128)}, u32[]{:S(2)}) copy-start(f32[12]{0:T(128)} %param.13) | copy-start | bytes 148
  20.8 5.4 %copy-start.17 = (bf16[128,768]{1,0:T(8,128)(2,1)S(1)}, bf16[128,768]{1,0:T(8,128)(2,1)}, u32[]{:S(2)}) copy-start(bf16[128,768]{1,0:T(8,128)(2,1)} %convolution_convert_fusion) | copy-start | bytes 589828
  20.9 3.3 copy-start.27
  22.8 0.7 copy-start.3
  22.9 3.3 copy-start.35
  24.0 30.9 %copy-start.1 = (f32[128,1280]{1,0:T(8,128)}, f32[128,1280]{1,0:T(8,128)S(1)}, u32[]{:S(2)}) copy-start(f32[128,1280]{1,0:T(8,128)S(1)} %fusion.77) | copy-start | bytes 1966084
  24.2 0.6 copy-start.29
  24.9 2.2 copy-start.10
  25.6 10.7 %collective-permute-start.1 = (bf16[128,512]{1,0:T(8,128)(2,1)}, bf16[128,512]{1,0:T(8,128)(2,1)}, u32[]{:S(2)}, u32[]{:S(2)}) collective-permute-start(bf16[128,512]{1,0:T(8,128)(2,1)} %pad_maximum_fusion.13), channel_id=1, source_target_pairs={{0,4},{4,8},{8,12},{12,16},{16,20},{20,24},{24,28},{28,32},{32,36}... | collective-permute-start | bytes 393224 | tf_op jit(solution)/shard_map/ppermute | solution.py:20
  36.3 9.3 %collective-permute-start.2 = (bf16[128,512]{1,0:T(8,128)(2,1)}, bf16[128,512]{1,0:T(8,128)(2,1)}, u32[]{:S(2)}, u32[]{:S(2)}) collective-permute-start(bf16[128,512]{1,0:T(8,128)(2,1)} %collective-permute-done.1), channel_id=1, source_target_pairs={{0,4},{4,8},{8,12},{12,16},{16,20},{20,24},{24,28},{28,32},{32,36}... | collective-permute-start | bytes 393224 | tf_op jit(solution)/shard_map/ppermute | solution.py:20
  45.6 8.2 %collective-permute-start.3 = (bf16[128,512]{1,0:T(8,128)(2,1)}, bf16[128,512]{1,0:T(8,128)(2,1)S(1)}, u32[]{:S(2)}, u32[]{:S(2)}) collective-permute-start(bf16[128,512]{1,0:T(8,128)(2,1)} %collective-permute-done.2), channel_id=1, source_target_pairs={{0,4},{4,8},{8,12},{12,16},{16,20},{20,24},{24,28},{28,32},{32,36}... | collective-permute-start | bytes 393224 | tf_op jit(solution)/shard_map/ppermute | solution.py:20
  54.9 5.2 %copy-start.40 = (f32[3]{0:T(128)S(1)}, f32[3]{0:T(128)}, u32[]{:S(2)}) copy-start(f32[3]{0:T(128)} %get-tuple-element.34) | copy-start | bytes 40
  57.5 6.9 %copy-start.13 = (bf16[128,768]{0,1:T(8,128)(2,1)S(1)}, bf16[128,768]{0,1:T(8,128)(2,1)}, u32[]{:S(2)}) copy-start(bf16[128,768]{0,1:T(8,128)(2,1)} %copy.87) | copy-start | bytes 589828
  57.5 7.8 %copy-start.21 = (bf16[128,4,3,64]{0,3,2,1:T(8,128)(2,1)S(1)}, bf16[128,4,3,64]{0,3,2,1:T(8,128)(2,1)}, u32[]{:S(2)}) copy-start(bf16[128,4,3,64]{0,3,2,1:T(8,128)(2,1)} %multiply_convert_fusion) | copy-start | bytes 589828
  57.5 7.8 %copy-start.38 = (f32[3]{0:T(128)S(1)}, f32[3]{0:T(128)}, u32[]{:S(2)}) copy-start(f32[3]{0:T(128)} %get-tuple-element.35) | copy-start | bytes 40
  62.4 8.2 %copy-start.39 = (f32[3]{0:T(128)S(1)}, f32[3]{0:T(128)}, u32[]{:S(2)}) copy-start(f32[3]{0:T(128)} %get-tuple-element.33) | copy-start | bytes 40
  74.0 5.3 %copy-start.20 = (f32[3,128,512]{1,2,0:T(8,128)S(1)}, f32[3,128,512]{1,2,0:T(8,128)}, u32[]{:S(2)}) copy-start(f32[3,128,512]{1,2,0:T(8,128)} %get-tuple-element.37) | copy-start | bytes 2359300
  77.6 3.8 copy-start.19
  79.7 3.8 copy-start.18
  79.7 3.8 copy-start.37
  81.8 3.8 copy-start.22
  81.8 3.8 copy-start.23
  85.6 2.3 copy-start.24
  89.1 12.3 %copy-start.5 = (bf16[1,128,768]{2,1,0:T(8,128)(2,1)S(1)}, bf16[1,128,768]{2,1,0:T(8,128)(2,1)}, u32[]{:S(2)}) copy-start(bf16[1,128,768]{2,1,0:T(8,128)(2,1)} %param.15) | copy-start | bytes 589828
  89.9 5.5 %collective-permute-start.4 = (f32[128,512]{1,0:T(8,128)}, f32[128,512]{1,0:T(8,128)}, u32[]{:S(2)}, u32[]{:S(2)}) collective-permute-start(f32[128,512]{1,0:T(8,128)} %fusion.64), channel_id=1, source_target_pairs={{0,252},{4,0},{8,4},{12,8},{16,12},{20,16},{24,20},{28,24},{32,28}... | collective-permute-start | bytes 786440 | tf_op jit(solution)/shard_map/ppermute | solution.py:20
  92.6 18.4 %copy-start.2 = (f32[128,1280]{1,0:T(8,128)S(1)}, f32[128,1280]{1,0:T(8,128)}, u32[]{:S(2)}) copy-start(f32[128,1280]{1,0:T(8,128)} %copy-done.1) | copy-start | bytes 1966084
  92.6 18.4 %copy-start.6 = (f32[128,768]{1,0:T(8,128)S(1)}, f32[128,768]{1,0:T(8,128)}, u32[]{:S(2)}) copy-start(f32[128,768]{1,0:T(8,128)} %copy.97) | copy-start | bytes 1179652
  92.6 18.4 %copy-start.7 = (f32[128,768]{1,0:T(8,128)S(1)}, f32[128,768]{1,0:T(8,128)}, u32[]{:S(2)}) copy-start(f32[128,768]{1,0:T(8,128)} %copy.96) | copy-start | bytes 1179652
  92.6 18.4 %copy-start.8 = (f32[128,768]{1,0:T(8,128)S(1)}, f32[128,768]{1,0:T(8,128)}, u32[]{:S(2)}) copy-start(f32[128,768]{1,0:T(8,128)} %copy.98) | copy-start | bytes 1179652
  96.4 8.4 %collective-permute-start.5 = (f32[128,512]{1,0:T(8,128)S(1)}, f32[128,512]{1,0:T(8,128)S(1)}, u32[]{:S(2)}, u32[]{:S(2)}) collective-permute-start(f32[128,512]{1,0:T(8,128)S(1)} %fusion.66), channel_id=1, source_target_pairs={{0,252},{4,0},{8,4},{12,8},{16,12},{20,16},{24,20},{28,24},{32,28}... | collective-permute-start | bytes 786440 | tf_op jit(solution)/shard_map/ppermute | solution.py:20
  103.4 13.7 %copy-start.30 = (f32[128,4]{0,1:T(4,128)S(1)}, f32[128,4]{0,1:T(4,128)}, u32[]{:S(2)}) copy-start(f32[128,4]{0,1:T(4,128)} %copy-done.29) | copy-start | bytes 6148
  103.4 13.8 %copy-start.11 = (f32[128,256]{1,0:T(8,128)S(1)}, f32[128,256]{1,0:T(8,128)}, u32[]{:S(2)}) copy-start(f32[128,256]{1,0:T(8,128)} %copy-done.10) | copy-start | bytes 393220
  103.4 14.8 %copy-start.4 = (bf16[128,768]{1,0:T(8,128)(2,1)S(1)}, bf16[128,768]{1,0:T(8,128)(2,1)}, u32[]{:S(2)}) copy-start(bf16[128,768]{1,0:T(8,128)(2,1)} %copy-done.3) | copy-start | bytes 589828
  103.4 14.8 %copy-start.26 = (f32[768]{0:T(1024)S(1)}, f32[768]{0:T(1024)}, u32[]{:S(2)}) copy-start(f32[768]{0:T(1024)} %copy-done.25) | copy-start | bytes 9220
  103.4 14.8 %copy-start.33 = (f32[128]{0:T(128)S(1)}, f32[128]{0:T(128)}, u32[]{:S(2)}) copy-start(f32[128]{0:T(128)} %copy-done.32) | copy-start | bytes 1540
  104.8 9.5 %collective-permute-start.6 = (f32[128,512]{1,0:T(8,128)S(1)}, f32[128,512]{1,0:T(8,128)S(1)}, u32[]{:S(2)}, u32[]{:S(2)}) collective-permute-start(f32[128,512]{1,0:T(8,128)S(1)} %fusion.63), channel_id=1, source_target_pairs={{0,252},{4,0},{8,4},{12,8},{16,12},{20,16},{24,20},{28,24},{32,28}... | collective-permute-start | bytes 786440 | tf_op jit(solution)/shard_map/ppermute | solution.py:20
  115.0 5.0 %copy-start.16 = (bf16[128,768]{1,0:T(8,128)(2,1)S(1)}, bf16[128,768]{1,0:T(8,128)(2,1)}, u32[]{:S(2)}) copy-start(bf16[128,768]{1,0:T(8,128)(2,1)} %fusion.52) | copy-start | bytes 589828
  118.2 4.5 %copy-start.36 = (f32[128]{0:T(128)S(1)}, f32[128]{0:T(128)}, u32[]{:S(2)}) copy-start(f32[128]{0:T(128)} %copy-done.35) | copy-start | bytes 1540
  120.1 2.9 copy-start.12
  122.7 0.9 copy-start.15
  122.7 0.9 copy-start.28
  (1 other events, 0.5 us)
Sparse Core Ops, SparseCore 0:
  138.0 290.9 all-reduce.6
where the time goes:
time: 442 us; the launch traced here: 440 us
  waiting for transfers between devices  238 us (54%)
  blocking collectives  81.7 us (18%)
  matrix products  40.1 us (9%)
  local copies, waits for them, and re-layouts  28.1 us (6%)
  other arithmetic  20.8 us (5%)
  starting transfers between devices  16.4 us (4%)
  between operations  14.8 us (3%)
    unnamed x2, waiting for transfers between devices  209 us
    unnamed x1, blocking collectives  81.7 us
    ppermute x6, waiting for transfers between devices, passed_along(): return lax.ppermute(x, axis, [(i, (i + by) % peers) for i in range(peers)])  29.2 us
    ppermute x6, starting transfers between devices, passed_along(): return lax.ppermute(x, axis, [(i, (i + by) % peers) for i in range(peers)])  11.2 us
    another operation x1, local copies, waits for them, and re-layouts, shards(): jnp.stack([jnp.dot(tiles.T, d_tokens, preferred_element_type=jnp.float32)...  10.3 us
    sub x4, matrix products, shards(): weights = jnp.where(visible, jnp.exp(attention_scores - top), 0.0)  9.18 us
  transfers between devices with their start and end apart: 8, of which 7 were waited for; matrix products, arithmetic and copies ran while one was open for 4% of the time, Pallas kernels for 0%

commit v1 on v0

v1 whole, which is shorter than its diff:
```python
import jax
import jax.numpy as jnp
from jax import lax
from jax.sharding import Mesh, PartitionSpec as P

QUERY_HEADS = 12
KEY_VALUE_HEADS = 4
HEAD_SIZE = 64
TC = 16
BLK = ("yl", "x", "z")
BAND = ("yh", "c")
RING = ("yl", "yh", "c")
REST = ("x", "z")


def passed_along(x, by):
    peers = lax.axis_size(BLK)
    return lax.ppermute(x, BLK, [(i, (i + by) % peers) for i in range(peers)])


def row_norm(values):
    return values * lax.rsqrt(jnp.mean(values * values, axis=-1, keepdims=True) + 1e-05)


def head_norm(values):
    return values * lax.rsqrt(jnp.mean(values * values, axis=-1, keepdims=True) + 1e-06)


def one_hot(sources, size):
    rows = lax.broadcasted_iota(jnp.int32, (sources.shape[0], size, sources.shape[1]), 1)
    return (rows == sources[:, None, :]).astype(jnp.bfloat16)


def spread(x, sources):
    pick = one_hot(sources, x.shape[1])
    return jnp.einsum("tc,qcj->qtj", x, pick, preferred_element_type=jnp.float32).astype(
        jnp.bfloat16
    )


def exchange(x, axes):
    return lax.all_to_all(x, axes, split_axis=0, concat_axis=0, tiled=True)


def shards(patches, stem_weight, norm_gain, w_qkv, w_out, per_head_scale, positions, d_out):
    tiles = patches[0]
    grad_out = d_out[0]
    token_rows = tiles.shape[0]
    group_factor = QUERY_HEADS // KEY_VALUE_HEADS
    query_span_width = QUERY_HEADS * HEAD_SIZE
    key_span_width = KEY_VALUE_HEADS * HEAD_SIZE
    bands = lax.axis_size(BAND)
    arrived = lax.ppermute(tiles[:TC], BAND, [(i, i - 1) for i in range(1, bands)])
    dout_ring = lax.all_gather(grad_out, RING, axis=0, tiled=True)
    tiles_ring = lax.all_gather(tiles, RING, axis=0, tiled=True)
    below = jnp.concatenate([tiles[TC:], arrived], axis=0)
    stem = jnp.dot(tiles, stem_weight[0], preferred_element_type=jnp.float32)
    stem = stem + jnp.dot(below, stem_weight[1], preferred_element_type=jnp.float32)
    token_f = lax.optimization_barrier(stem.astype(jnp.bfloat16)).astype(jnp.float32)
    gain_f = norm_gain.astype(jnp.float32)
    normed = row_norm(token_f)
    hidden = (normed * gain_f).astype(jnp.bfloat16)
    hidden_ring = lax.all_gather(hidden, RING, axis=0, tiled=True)
    query_key_value = jnp.dot(hidden, w_qkv, preferred_element_type=jnp.float32)
    query = query_key_value[:, :query_span_width].reshape(token_rows, QUERY_HEADS, HEAD_SIZE)
    key = query_key_value[:, query_span_width : query_span_width + key_span_width].reshape(
        token_rows, KEY_VALUE_HEADS, HEAD_SIZE
    )
    query_normalized = head_norm(query).astype(jnp.bfloat16)
    key_n = head_norm(key).astype(jnp.bfloat16).reshape(token_rows, key_span_width)
    value = query_key_value[:, query_span_width + key_span_width :].astype(jnp.bfloat16)
    kv_own = jnp.concatenate([key_n, value], axis=1)
    blk_count = lax.axis_size(BLK)
    own_index = lax.axis_index(BLK)
    blocks = [kv_own] + [passed_along(kv_own, offset) for offset in range(1, 4)]
    attention_gradient = jnp.dot(grad_out, w_out.T, preferred_element_type=jnp.float32).astype(
        jnp.bfloat16
    )
    causal_window = jnp.concatenate(blocks, axis=0)
    key_pos = jnp.concatenate(
        [
            lax.dynamic_slice_in_dim(
                positions, (own_index - offset) % blk_count * token_rows, token_rows
            )
            for offset in range(4)
        ]
    )
    query_pos = lax.dynamic_slice_in_dim(positions, own_index * token_rows, token_rows)
    visible = (key_pos[None, :] <= query_pos[:, None])[None]
    every_key = causal_window.shape[0]
    query_cube = query_normalized.reshape(token_rows, KEY_VALUE_HEADS, group_factor, HEAD_SIZE)
    gradient_cube = attention_gradient.reshape(token_rows, KEY_VALUE_HEADS, group_factor, HEAD_SIZE)
    key_cube = causal_window[:, :key_span_width].reshape(every_key, KEY_VALUE_HEADS, HEAD_SIZE)
    value_cube = causal_window[:, key_span_width:].reshape(every_key, KEY_VALUE_HEADS, HEAD_SIZE)
    score_scales = per_head_scale.reshape(KEY_VALUE_HEADS, group_factor)
    attn_list = []
    dquery_list = []
    dkey_list = []
    dvalue_list = []
    f32 = jnp.float32
    for group in range(KEY_VALUE_HEADS):
        scale_col = score_scales[group][:, None, None]
        q_group = query_cube[:, group]
        grad_group = gradient_cube[:, group]
        k_group = key_cube[:, group]
        v_group = value_cube[:, group]
        scores = jnp.einsum("trd,sd->rts", q_group, k_group, preferred_element_type=f32) * scale_col
        scores = jnp.where(visible, scores, -1e30)
        top = jnp.max(scores, axis=-1, keepdims=True)
        weights = jnp.where(visible, jnp.exp(scores - top), 0.0)
        probs = weights / jnp.sum(weights, axis=-1, keepdims=True)
        narrow = probs.astype(jnp.bfloat16)
        attn = jnp.einsum("rts,sd->trd", narrow, v_group, preferred_element_type=f32)
        attn_list.append(attn)
        delta = jnp.sum(grad_group.astype(f32) * attn, axis=-1)
        dprobs = jnp.einsum("trd,sd->rts", grad_group, v_group, preferred_element_type=f32)
        dscores = (scale_col * probs * (dprobs - delta.T[:, :, None])).astype(jnp.bfloat16)
        dquery_list.append(jnp.einsum("rts,sd->trd", dscores, k_group, preferred_element_type=f32))
        dkey_list.append(jnp.einsum("rts,trd->sd", dscores, q_group, preferred_element_type=f32))
        dvalue_list.append(
            jnp.einsum("rts,trd->sd", narrow, grad_group, preferred_element_type=f32)
        )
    attention_output = (
        jnp.stack(attn_list, axis=1).reshape(token_rows, query_span_width).astype(jnp.bfloat16)
    )
    query_gradient = jnp.stack(dquery_list, axis=1).reshape(token_rows, QUERY_HEADS, HEAD_SIZE)
    dkey_all = jnp.stack(dkey_list, axis=1).reshape(every_key, key_span_width)
    dvalue_all = jnp.stack(dvalue_list, axis=1).reshape(every_key, key_span_width)
    partial_terms = jnp.concatenate([dkey_all, dvalue_all], axis=1)
    pieces = [partial_terms[offset * token_rows : (offset + 1) * token_rows] for offset in range(4)]
    returned = [
        passed_along(pieces[offset].astype(jnp.bfloat16), -offset) for offset in (1, 2, 3)
    ]
    pull_query = jax.vjp(head_norm, query)[1]
    pull_key = jax.vjp(head_norm, key)[1]
    d_q = pull_query(query_gradient)[0].reshape(token_rows, query_span_width).astype(jnp.bfloat16)
    members = jnp.arange(8, dtype=jnp.int32)[:, None]
    lane = jnp.arange(192, dtype=jnp.int32)[None, :]
    early = spread(
        jnp.concatenate([attention_output, d_q], axis=1),
        members * 96 + lane % 96 + lane // 96 * query_span_width,
    )
    early_ring = exchange(early, RING).reshape(8 * token_rows, 192)
    carried = pieces[0] + sum(piece.astype(f32) for piece in returned)
    d_key = pull_key(
        carried[:, :key_span_width].reshape(token_rows, KEY_VALUE_HEADS, HEAD_SIZE)
    )[0].reshape(token_rows, key_span_width)
    d_kv = jnp.concatenate([d_key, carried[:, key_span_width:]], axis=1).astype(jnp.bfloat16)
    d_hidden = jnp.dot(
        jnp.concatenate([d_q, d_kv], axis=1), w_qkv.T, preferred_element_type=f32
    )
    gain_term = jnp.sum(d_hidden * normed, axis=0)
    pull_tokens = jax.vjp(row_norm, token_f)[1]
    d_tokens = (grad_out.astype(f32) + pull_tokens(d_hidden * gain_f)[0]).astype(jnp.bfloat16)
    extra = TC
    width = d_tokens.shape[1]
    late_rows = jnp.concatenate(
        [
            jnp.concatenate([d_tokens, d_kv], axis=1),
            jnp.pad(gain_term.astype(jnp.bfloat16)[None], ((0, extra - 1), (0, 2 * key_span_width))),
        ],
        axis=0,
    )
    lane = jnp.arange(160, dtype=jnp.int32)[None, :]
    token_source = members // 4 * 384 + lane // 3 * 12 + members % 4 * 3 + lane % 3
    kv_lane = lane - 96
    kv_source = width + kv_lane // 32 * key_span_width + members * 32 + kv_lane % 32
    late = spread(late_rows, jnp.where(lane < 96, token_source, kv_source))
    late_ring = exchange(late, RING)
    gain_ring = jnp.sum(late_ring[:, token_rows, :96].astype(f32), axis=0)
    late_ring = late_ring[:, :token_rows]
    own_tokens = late_ring[:, :, :96].reshape(2, 4 * token_rows, 96)
    above = jnp.pad(own_tokens, ((0, 0), (TC, 0), (0, 0)))[:, : 4 * token_rows]
    both = jnp.concatenate([own_tokens, above], axis=2).reshape(8 * token_rows, 192)
    stem_part = jnp.dot(both.T, tiles_ring, preferred_element_type=f32).astype(jnp.bfloat16)
    stem_part = stem_part.reshape(2, 32, 3, 1024).transpose(1, 0, 2, 3).reshape(32, 48, 128)
    qkv_columns = jnp.concatenate(
        [early_ring[:, 96:], late_ring[:, :, 96:].reshape(8 * token_rows, 64)], axis=1
    )
    qkv_part = jnp.dot(hidden_ring.T, qkv_columns, preferred_element_type=f32)
    out_part = jnp.dot(dout_ring.T, early_ring[:, :96], preferred_element_type=f32)
    rows_part = jnp.concatenate([qkv_part, out_part], axis=1).astype(jnp.bfloat16)
    rows_part = rows_part.reshape(2, 32, 12, 256).transpose(1, 0, 2, 3).reshape(32, 48, 128)
    gain_part = jnp.pad(
        gain_ring.reshape(32, 1, 3).astype(jnp.bfloat16), ((0, 0), (0, 15), (0, 125))
    )
    terms = exchange(jnp.concatenate([stem_part, rows_part, gain_part], axis=1), REST)
    total = jnp.sum(terms.astype(f32), axis=0)
    d_stem_weight = total[:48].reshape(2, 3, 1024).transpose(0, 2, 1)
    d_norm_gain = total[96, :3]
    rows = exchange(total[48:96].reshape(8, 3, 256), RING)
    d_w_qkv = jnp.concatenate(
        [
            rows[:, :, first:last].transpose(1, 0, 2).reshape(3, -1)
            for first, last in ((0, 96), (96, 128), (128, 160))
        ],
        axis=1,
    )
    d_w_out = rows[:, :, 160:].transpose(0, 2, 1).reshape(query_span_width, 3)
    return (d_stem_weight, d_norm_gain, d_w_qkv, d_w_out)


def solution(mesh):
    fine = Mesh(mesh.devices.reshape(2, 4, 8, 2, 2), BLK + BAND)
    placed = (P(BAND, BLK, None), P(), P(), P(), P(), P(), P(), P(BAND, BLK, None))
    every = BLK + BAND
    return jax.shard_map(
        shards,
        mesh=fine,
        in_specs=placed,
        out_specs=(P(None, None, every), P(every), P(every, None), P(None, every)),
        check_vma=False,
    )
```

time: 442 us -> 202 us (0.46)
  waiting for transfers between devices: 238 us -> 31.9 us
  blocking collectives: 81.7 us -> 29.4 us
  starting transfers between devices: 16.4 us -> 37.1 us
  matrix products: 40.1 us -> 44.8 us
  local copies, waits for them, and re-layouts: 28.1 us -> 23.5 us
    unnamed x2 -> x3, waiting for transfers between devices: 209 us -> 1.38 us
    unnamed x1 -> x0, blocking collectives: 81.7 us -> none
    all_to_all x0 -> x1, blocking collectives: none -> 29.4 us  [exchange(): return lax.all_to_all(x, axes, split_axis=0, concat_axis=0, tiled=True)]
    all_to_all x0 -> x3, starting transfers between devices: none -> 20 us  [exchange(): return lax.all_to_all(x, axes, split_axis=0, concat_axis=0, tiled=True)]
    all_to_all x0 -> x3, waiting for transfers between devices: none -> 12.2 us  [exchange(): return lax.all_to_all(x, axes, split_axis=0, concat_axis=0, tiled=True)]
    ppermute x7, waiting for transfers between devices: 29.2 us -> 18.2 us  [the longest x6 17.6 us: passed_along(): return lax.ppermute(x, BLK, [(i, (i + by) % peers) for i in range(peers)])]
    another operation x1, local copies, waits for them, and re-layouts: 10.3 us -> 0.17 us  [shards(): jnp.stack([jnp.dot(tiles.T, d_tokens, preferred_element_type=jnp.float32)...]
    dot_general x25 -> x26, matrix products: 23.7 us -> 29.1 us  [the longest x2 5.93 us: spread(): jnp.einsum('tc,qcj->qtj', x, pick, preferred_element_type=jnp.float32)]
  transfers between devices with their start and end apart: 8 -> 13, of which waited for: 7 -> 8; matrix products, arithmetic and copies ran while one was open for 4% -> 39% of each run, Pallas kernels for 0% -> 0%
where the time goes in v1:
time: 202 us; the launch traced here: 201 us
  matrix products  44.8 us (22%)
  starting transfers between devices  37.1 us (18%)
  waiting for transfers between devices  31.9 us (16%)
  blocking collectives  29.4 us (15%)
  local copies, waits for them, and re-layouts  23.5 us (12%)
  other arithmetic  19.4 us (10%)
  between operations  14.8 us (7%)
    all_to_all x1, blocking collectives, exchange(): return lax.all_to_all(x, axes, split_axis=0, concat_axis=0, tiled=True)  29.4 us
    all_to_all x3, starting transfers between devices, exchange(): return lax.all_to_all(x, axes, split_axis=0, concat_axis=0, tiled=True)  20 us
    ppermute x6, waiting for transfers between devices, passed_along(): return lax.ppermute(x, BLK, [(i, (i + by) % peers) for i in range(peers)])  17.6 us
    all_to_all x3, waiting for transfers between devices, exchange(): return lax.all_to_all(x, axes, split_axis=0, concat_axis=0, tiled=True)  12.2 us
    ppermute x6, starting transfers between devices, passed_along(): return lax.ppermute(x, BLK, [(i, (i + by) % peers) for i in range(peers)])  11.8 us
    sub x4, matrix products, shards(): weights = jnp.where(visible, jnp.exp(scores - top), 0.0)  9.84 us
    dot_general x2, matrix products, spread(): jnp.einsum('tc,qcj->qtj', x, pick, preferred_element_type=jnp.float32)  5.93 us
    dot_general x4, matrix products, shards(): jnp.einsum('rts,trd->sd', narrow, grad_group, preferred_element_type=f32)  5.17 us
  transfers between devices with their start and end apart: 13, of which 8 were waited for; matrix products, arithmetic and copies ran while one was open for 39% of the time, Pallas kernels for 0%

profile of v1, /device:TPU:1, one launch (start us, length us, event | category | flops | bytes accessed | tf_op | source)
XLA Modules:
  0.0 201.0 jit_solution(5912696209215367656)
XLA Ops:
  8.7 5.1 %collective-permute-start = (bf16[16,1024]{1,0:T(8,128)(2,1)S(1)}, bf16[16,1024]{1,0:T(8,128)(2,1)S(1)}, u32[]{:S(2)}, u32[]{:S(2)}) collective-permute-start(bf16[16,1024]{1,0:T(8,128)(2,1)S(1)} %slice_bitcast_fusion.73), channel_id=1, source_target_pairs={{1,0},{2,1},{3,2},{5,4},{6,5},{7,6},{9,8},{10,9},{11,10},{13,12},{... | collective-permute-start | bytes 98312 | tf_op jit(solution)/shard_map/ppermute | solution.py:53
  13.9 1.9 fusion.15
  16.5 1.8 fusion.61
  21.9 1.8 convolution_convert_fusion.1
  29.5 1.6 collective-permute-start.1
  31.2 3.1 %collective-permute-start.2 = (bf16[128,512]{1,0:T(8,128)(2,1)}, bf16[128,512]{1,0:T(8,128)(2,1)}, u32[]{:S(2)}, u32[]{:S(2)}) collective-permute-start(bf16[128,512]{1,0:T(8,128)(2,1)} %pad_maximum_fusion.6), channel_id=1, source_target_pairs={{0,8},{4,12},{8,16},{12,20},{16,24},{20,28},{24,32},{28,36},{32,40... | collective-permute-start | bytes 393224 | tf_op jit(solution)/shard_map/ppermute | solution.py:18
  34.2 3.8 %collective-permute-start.3 = (bf16[128,512]{1,0:T(8,128)(2,1)}, bf16[128,512]{1,0:T(8,128)(2,1)}, u32[]{:S(2)}, u32[]{:S(2)}) collective-permute-start(bf16[128,512]{1,0:T(8,128)(2,1)} %pad_maximum_fusion.6), channel_id=1, source_target_pairs={{0,12},{4,16},{8,20},{12,24},{16,28},{20,32},{24,36},{28,40},{32,4... | collective-permute-start | bytes 393224 | tf_op jit(solution)/shard_map/ppermute | solution.py:18
  38.9 1.0 copy.105
  39.8 1.4 multiply_convert_fusion
  41.3 1.3 collective-permute-done.1
  42.5 7.8 %collective-permute-done.2 = bf16[128,512]{1,0:T(8,128)(2,1)} collective-permute-done((bf16[128,512]{1,0:T(8,128)(2,1)}, bf16[128,512]{1,0:T(8,128)(2,1)}, u32[]{:S(2)}, u32[]{:S(2)}) %collective-permute-start.2) | collective-permute-done | bytes 131104 | tf_op jit(solution)/shard_map/ppermute | solution.py:18
  50.3 4.5 %collective-permute-done.3 = bf16[128,512]{1,0:T(8,128)(2,1)} collective-permute-done((bf16[128,512]{1,0:T(8,128)(2,1)}, bf16[128,512]{1,0:T(8,128)(2,1)}, u32[]{:S(2)}, u32[]{:S(2)}) %collective-permute-start.3) | collective-permute-done | bytes 131104 | tf_op jit(solution)/shard_map/ppermute | solution.py:18
  54.7 1.1 pad_maximum_fusion.1
  56.7 1.1 copy.94
  57.8 2.3 %fusion.156 = (f32[3,128]{1,0:T(4,128)S(1)}, f32[3,128,512]{1,2,0:T(8,128)}) fusion(f32[3]{0:T(128)S(1)} %copy-done.46, pred[128,512]{0,1:T(8,128)(4,1)} %broadcast_compare_fusion, bf16[512,4,64]{0,2,1:T(8,128)(2,1)S(1)} %bitcast.381, bf16[128,4,3,64]{0,3,2,1:T(8,128)(2,1)} %multiply_convert_fusion), kind=kOutput, calls=%fused_computation.279 | convolution fusion | flops 26149376 | bytes 1034240 | tf_op jit(solution)/shard_map/sub | solution.py:110
  60.1 2.3 %fusion.155 = (f32[3,128]{1,0:T(4,128)S(1)}, f32[3,128,512]{1,2,0:T(8,128)}) fusion(f32[3]{0:T(128)} %get-tuple-element.41, pred[128,512]{0,1:T(8,128)(4,1)} %broadcast_compare_fusion, bf16[512,4,64]{0,2,1:T(8,128)(2,1)S(1)} %bitcast.382, bf16[128,4,3,64]{0,3,2,1:T(8,128)(2,1)} %multiply_convert_fusion), kind=kOutput, calls=%fused_computation.278 | convolution fusion | flops 26149376 | bytes 1034240 | tf_op jit(solution)/shard_map/sub | solution.py:110
  62.4 1.3 fusion.108
  67.2 2.3 %fusion.154 = (f32[3,128]{1,0:T(4,128)S(1)}, f32[3,128,512]{1,2,0:T(8,128)}) fusion(f32[3]{0:T(128)} %get-tuple-element.40, pred[128,512]{0,1:T(8,128)(4,1)} %broadcast_compare_fusion, bf16[512,4,64]{0,2,1:T(8,128)(2,1)S(1)} %bitcast.383, bf16[128,4,3,64]{0,3,2,1:T(8,128)(2,1)} %multiply_convert_fusion), kind=kOutput, calls=%fused_computation.277 | convolution fusion | flops 26149376 | bytes 1034240 | tf_op jit(solution)/shard_map/sub | solution.py:110
  69.5 1.2 fusion.110
  71.6 1.7 convolution_bitcast_fusion.4
  73.3 3.0 %fusion.153 = (f32[3,128]{1,0:T(4,128)}, f32[3,128,512]{1,2,0:T(8,128)}) fusion(f32[3]{0:T(128)} %get-tuple-element.39, pred[128,512]{0,1:T(8,128)(4,1)} %broadcast_compare_fusion, bf16[512,4,64]{0,2,1:T(8,128)(2,1)S(1)} %bitcast.384, bf16[128,4,3,64]{0,3,2,1:T(8,128)(2,1)} %multiply_convert_fusion), kind=kOutput, calls=%fused_computation.276 | convolution fusion | flops 26149376 | bytes 1034240 | tf_op jit(solution)/shard_map/sub | solution.py:110
  76.2 1.3 fusion.107
  77.5 1.7 convolution_bitcast_fusion.7
  79.2 2.1 %multiply_reduce_fusion.4 = (f32[128,3]{0,1:T(4,128)S(1)}, f32[128,3]{0,1:T(4,128)S(1)}, f32[128,3]{0,1:T(4,128)S(1)}, f32[128,3]{0,1:T(4,128)S(1)}, bf16[128,1,...) fusion(bf16[128,4,3,64]{0,3,2,1:T(8,128)(2,1)} %bitcast.401, ...), kind=kOutput, calls=%fused_computation.180 | convolution fusion | flops 25557504 | bytes 1153024 | tf_op jit(solution)/shard_map/rts,sd->trd/dot_general | solution.py:113
  87.6 0.9 copy.106
  88.5 0.9 copy.104
  89.4 1.9 pad_maximum_fusion.3
  91.3 1.2 copy.116
  92.6 1.8 pad_maximum_fusion.2
  94.4 2.1 %copy.115 = f32[512,256]{1,0:T(8,128)} copy(f32[512,256]{0,1:T(8,128)} %bitcast.378) | data formatting | bytes 1048576 | tf_op jit(solution)/shard_map/reshape | solution.py:127
  96.5 1.2 fusion.70
  98.5 3.3 %collective-permute-start.5 = (bf16[128,512]{1,0:T(8,128)(2,1)}, bf16[128,512]{1,0:T(8,128)(2,1)}, u32[]{:S(2)}, u32[]{:S(2)}) collective-permute-start(bf16[128,512]{1,0:T(8,128)(2,1)} %get-tuple-element.20), channel_id=1, source_target_pairs={{0,248},{4,252},{8,0},{12,4},{16,8},{20,12},{24,16},{28,20},{32,24... | collective-permute-start | bytes 393224 | tf_op jit(solution)/shard_map/ppermute | solution.py:18
  102.8 3.4 %fusion.57 = bf16[8,128,192]{1,2,0:T(8,128)(2,1)} fusion(s32[8,192]{1,0:T(8,128)S(1)} %copy-done.34, bf16[128,768]{1,0:T(8,128)(2,1)} %fusion.80, bf16[128,768]{1,0:T(8,128)(2,1)S(1)} %copy.121), kind=kOutput, calls=%fused_computation.70 | convolution fusion | flops 607322112 | bytes 792576 | tf_op jit(solution)/shard_map/tc,qcj->qtj/dot_general | solution.py:36
  106.2 5.4 %all-to-all-start.1 = ((bf16[8,128,192]{1,2,0:T(8,128)(2,1)}), bf16[8,128,192]{1,2,0:T(8,128)(2,1)}, u32[]{:S(2)}, u32[]{:S(2)}) async-start(bf16[8,128,192]{1,2,0:T(8,128)(2,1)} %fusion.57), calls=%async_computation.1 | async-start | bytes 786432 | tf_op jit(solution)/shard_map/all_to_all | solution.py:42
  111.6 3.3 %collective-permute-done.5 = bf16[128,512]{1,0:T(8,128)(2,1)} collective-permute-done((bf16[128,512]{1,0:T(8,128)(2,1)}, bf16[128,512]{1,0:T(8,128)(2,1)}, u32[]{:S(2)}, u32[]{:S(2)}) %collective-permute-start.5) | collective-permute-done | bytes 131104 | tf_op jit(solution)/shard_map/ppermute | solution.py:18
  115.7 1.1 fusion.112
  117.8 1.0 fusion.120
  118.9 1.8 fusion.84
  120.9 2.5 %fusion.52 = bf16[8,144,160]{2,1,0:T(8,128)(2,1)} fusion(s32[8,160]{1,0:T(8,128)S(1)} %copy-done.33, bf16[1,768]{1,0:T(2,128)(2,1)S(1)} %convert_element_type.167, bf16[128,256]{1,0:T(8,128)(2,1)S(1)} %slice.372, bf16[128,256]{1,0:T(8,128)(2,1)S(1)} %fusion.120, bf16[128,768]{1,0:T(8,128)(2,1)S(1)} %fusion.82), kind=kOutput, calls=%fused_computation.64 | convolution fusion | flops 475525120 | bytes 702976 | tf_op jit(solution)/shard_map/tc,qcj->qtj/dot_general | solution.py:36
  123.4 5.5 %all-to-all-start = ((bf16[8,144,160]{2,1,0:T(8,128)(2,1)}), bf16[8,144,160]{2,1,0:T(8,128)(2,1)S(1)}, u32[]{:S(2)}, u32[]{:S(2)}) async-start(bf16[8,144,160]{2,1,0:T(8,128)(2,1)} %fusion.52), calls=%async_computation | async-start | bytes 1179648 | tf_op jit(solution)/shard_map/all_to_all | solution.py:42
  129.0 1.1 copy_bitcast_fusion
  130.7 8.8 %all-to-all-done = bf16[8,144,160]{2,1,0:T(8,128)(2,1)S(1)} async-done(((bf16[8,144,160]{2,1,0:T(8,128)(2,1)}), bf16[8,144,160]{2,1,0:T(8,128)(2,1)S(1)}, u32[]{:S(2)}, u32[]{:S(2)}) %all-to-all-start) | async-done | bytes 368672 | tf_op jit(solution)/shard_map/all_to_all | solution.py:42
  140.8 1.8 fusion.67
  142.8 1.8 convolution_convert_fusion
  145.4 2.4 %fusion.53 = bf16[192,1024]{1,0:T(8,128)(2,1)S(1)} fusion(bf16[1,1024,1024]{2,1,0:T(8,128)(2,1)} %all-gather.8.cloned.1.call-done, bf16[1024,96]{1,0:T(8,128)(2,1)} %bitcast.389, bf16[1024,96]{1,0:T(8,128)(2,1)S(1)} %bitcast.375), kind=kOutput, calls=%fused_computation.65 | convolution fusion | flops 403636224 | bytes 2883584 | tf_op jit(solution)/shard_map/dot_general | solution.py:175
  148.8 29.4 %all_to_all.20 = bf16[32,112,128]{2,1,0:T(8,128)(2,1)S(1)} all-to-all(bf16[32,112,128]{2,1,0:T(8,128)(2,1)S(1)} %fusion.71), channel_id=1, replica_groups=mesh['yl'=2,'x'=4,'z'=8,'yh'=2,'c'=2] {'x','z'}, dimensions={0} | all-to-all | bytes 1835008 | tf_op jit(solution)/shard_map/all_to_all | solution.py:42
  179.0 9.1 %all-to-all-start.3 = ((f32[8,3,256]{2,1,0:T(4,128)}), f32[8,3,256]{2,1,0:T(4,128)S(1)}, u32[]{:S(2)}, u32[]{:S(2)}) async-start(f32[8,3,256]{2,1,0:T(4,128)} %reshape.579), calls=%async_computation.3 | async-start | bytes 65536 | tf_op jit(solution)/shard_map/all_to_all | solution.py:42
  189.2 3.5 %all-to-all-done.3 = f32[8,3,256]{2,1,0:T(4,128)S(1)} async-done(((f32[8,3,256]{2,1,0:T(4,128)}), f32[8,3,256]{2,1,0:T(4,128)S(1)}, u32[]{:S(2)}, u32[]{:S(2)}) %all-to-all-start.3) | async-done | bytes 24608 | tf_op jit(solution)/shard_map/all_to_all | solution.py:42
  (222 shorter events, 34.6 us)
Async XLA Ops:
  7.2 20.3 %copy-start = (bf16[768,1280]{1,0:T(8,128)(2,1)S(1)}, bf16[768,1280]{1,0:T(8,128)(2,1)}, u32[]{:S(2)}) copy-start(bf16[768,1280]{1,0:T(8,128)(2,1)} %param.11) | copy-start | bytes 5898244
  7.2 8.6 %copy-start.12 = (bf16[1,128,1024]{2,1,0:T(8,128)(2,1)S(1)}, bf16[1,128,1024]{2,1,0:T(8,128)(2,1)}, u32[]{:S(2)}) copy-start(bf16[1,128,1024]{2,1,0:T(8,128)(2,1)} %param.8) | copy-start | bytes 786436
  7.2 8.6 %copy-start.41 = (bf16[768]{0:T(1024)(128)(2,1)S(1)}, bf16[768]{0:T(1024)(128)(2,1)}, u32[]{:S(2)}) copy-start(bf16[768]{0:T(1024)(128)(2,1)} %param.10) | copy-start | bytes 4612
  7.2 133.6 %all-gather.10.cloned.1.call-start = ((), (), s32[]{:S(2)}) async-start(), calls=%async_computation.6 | async-start | bytes 1769472 | tf_op jit(solution)/shard_map/all_gather | solution.py:54
  7.9 134.9 %all-gather.6.cloned.1.call-start = ((), (), s32[]{:S(2)}) async-start(), calls=%async_computation.4 | async-start | bytes 1769472 | tf_op jit(solution)/shard_map/all_gather | solution.py:63
  8.7 7.8 %collective-permute-start = (bf16[16,1024]{1,0:T(8,128)(2,1)S(1)}, bf16[16,1024]{1,0:T(8,128)(2,1)S(1)}, u32[]{:S(2)}, u32[]{:S(2)}) collective-permute-start(bf16[16,1024]{1,0:T(8,128)(2,1)S(1)} %slice_bitcast_fusion.73), channel_id=1, source_target_pairs={{1,0},{2,1},{3,2},{5,4},{6,5},{7,6},{9,8},{10,9},{11,10},{13,12},{... | collective-permute-start | bytes 98312 | tf_op jit(solution)/shard_map/ppermute | solution.py:53
  15.8 2.6 %copy-start.29 = (f32[768]{0:T(1024)}, f32[768]{0:T(1024)S(1)}, u32[]{:S(2)}) copy-start(f32[768]{0:T(1024)S(1)} %convert_element_type.144) | copy-start | bytes 9220
  15.8 5.4 %copy-start.35 = (f32[12]{0:T(128)S(1)}, f32[12]{0:T(128)}, u32[]{:S(2)}) copy-start(f32[12]{0:T(128)} %param.13) | copy-start | bytes 148
  15.8 6.0 %copy-start.1 = (bf16[1,128,768]{2,1,0:T(8,128)(2,1)S(1)}, bf16[1,128,768]{2,1,0:T(8,128)(2,1)}, u32[]{:S(2)}) copy-start(bf16[1,128,768]{2,1,0:T(8,128)(2,1)} %param.15) | copy-start | bytes 589828
  20.3 7.2 %copy-start.5 = (bf16[128,768]{1,0:T(8,128)(2,1)S(1)}, bf16[128,768]{1,0:T(8,128)(2,1)}, u32[]{:S(2)}) copy-start(bf16[128,768]{1,0:T(8,128)(2,1)} %fusion.78) | copy-start | bytes 589828
  20.3 125.1 %all-gather.8.cloned.1.call-start = ((), (), s32[]{:S(2)}) async-start(), calls=%async_computation.5 | async-start | bytes 2359296 | tf_op jit(solution)/shard_map/all_gather | solution.py:55
  28.8 9.2 %copy-start.10 = (f32[128,256]{1,0:T(8,128)}, f32[128,256]{1,0:T(8,128)S(1)}, u32[]{:S(2)}) copy-start(f32[128,256]{1,0:T(8,128)S(1)} %copy.90) | copy-start | bytes 393220
  29.5 13.0 %collective-permute-start.1 = (bf16[128,512]{1,0:T(8,128)(2,1)}, bf16[128,512]{1,0:T(8,128)(2,1)}, u32[]{:S(2)}, u32[]{:S(2)}) collective-permute-start(bf16[128,512]{1,0:T(8,128)(2,1)} %pad_maximum_fusion.6), channel_id=1, source_target_pairs={{0,4},{4,8},{8,12},{12,16},{16,20},{20,24},{24,28},{28,32},{32,36}... | collective-permute-start | bytes 393224 | tf_op jit(solution)/shard_map/ppermute | solution.py:18
  31.2 19.1 %collective-permute-start.2 = (bf16[128,512]{1,0:T(8,128)(2,1)}, bf16[128,512]{1,0:T(8,128)(2,1)}, u32[]{:S(2)}, u32[]{:S(2)}) collective-permute-start(bf16[128,512]{1,0:T(8,128)(2,1)} %pad_maximum_fusion.6), channel_id=1, source_target_pairs={{0,8},{4,12},{8,16},{12,20},{16,24},{20,28},{24,32},{28,36},{32,40... | collective-permute-start | bytes 393224 | tf_op jit(solution)/shard_map/ppermute | solution.py:18
  34.2 20.5 %collective-permute-start.3 = (bf16[128,512]{1,0:T(8,128)(2,1)}, bf16[128,512]{1,0:T(8,128)(2,1)}, u32[]{:S(2)}, u32[]{:S(2)}) collective-permute-start(bf16[128,512]{1,0:T(8,128)(2,1)} %pad_maximum_fusion.6), channel_id=1, source_target_pairs={{0,12},{4,16},{8,20},{12,24},{16,28},{20,32},{24,36},{28,40},{32,4... | collective-permute-start | bytes 393224 | tf_op jit(solution)/shard_map/ppermute | solution.py:18
  39.8 18.0 %copy-start.46 = (f32[3]{0:T(128)S(1)}, f32[3]{0:T(128)}, u32[]{:S(2)}) copy-start(f32[3]{0:T(128)} %get-tuple-element.38) | copy-start | bytes 40
  60.1 4.4 %copy-start.36 = (f32[3,128]{1,0:T(4,128)}, f32[3,128]{1,0:T(4,128)S(1)}, u32[]{:S(2)}) copy-start(f32[3,128]{1,0:T(4,128)S(1)} %get-tuple-element.48) | copy-start | bytes 4612
  62.4 2.1 %copy-start.15 = (f32[3,128,512]{1,2,0:T(8,128)S(1)}, f32[3,128,512]{1,2,0:T(8,128)}, u32[]{:S(2)}) copy-start(f32[3,128,512]{1,2,0:T(8,128)} %get-tuple-element.47) | copy-start | bytes 2359300
  62.4 3.1 %copy-start.13 = (bf16[128,768]{0,1:T(8,128)(2,1)S(1)}, bf16[128,768]{0,1:T(8,128)(2,1)}, u32[]{:S(2)}) copy-start(bf16[128,768]{0,1:T(8,128)(2,1)} %copy.95) | copy-start | bytes 589828
  76.2 5.1 %copy-start.14 = (bf16[128,768]{0,1:T(8,128)(2,1)S(1)}, bf16[128,768]{0,1:T(8,128)(2,1)}, u32[]{:S(2)}) copy-start(bf16[128,768]{0,1:T(8,128)(2,1)} %copy.95) | copy-start | bytes 589828
  76.2 5.1 %copy-start.19 = (f32[3,128,512]{1,2,0:T(8,128)S(1)}, f32[3,128,512]{1,2,0:T(8,128)}, u32[]{:S(2)}) copy-start(f32[3,128,512]{1,2,0:T(8,128)} %get-tuple-element.43) | copy-start | bytes 2359300
  76.2 5.1 %copy-start.38 = (f32[3,128]{1,0:T(4,128)S(1)}, f32[3,128]{1,0:T(4,128)}, u32[]{:S(2)}) copy-start(f32[3,128]{1,0:T(4,128)} %get-tuple-element.42) | copy-start | bytes 4612
  76.2 5.1 %copy-start.48 = (f32[3]{0:T(128)S(1)}, f32[3]{0:T(128)}, u32[]{:S(2)}) copy-start(f32[3]{0:T(128)} %get-tuple-element.39) | copy-start | bytes 40
  89.4 3.2 %copy-start.22 = (f32[512,1,64]{0,2,1:T(8,128)S(1)}, f32[512,1,64]{0,2,1:T(8,128)}, u32[]{:S(2)}) copy-start(f32[512,1,64]{0,2,1:T(8,128)} %convolution_bitcast_fusion.11) | copy-start | bytes 393220
  89.4 3.2 %copy-start.23 = (f32[512,1,64]{0,2,1:T(8,128)S(1)}, f32[512,1,64]{0,2,1:T(8,128)}, u32[]{:S(2)}) copy-start(f32[512,1,64]{0,2,1:T(8,128)} %convolution_bitcast_fusion.10) | copy-start | bytes 393220
  94.4 7.4 %copy-start.6 = (f32[128,768]{1,0:T(8,128)S(1)}, f32[128,768]{1,0:T(8,128)}, u32[]{:S(2)}) copy-start(f32[128,768]{1,0:T(8,128)} %copy.105) | copy-start | bytes 1179652
  96.5 5.3 %copy-start.7 = (f32[128,768]{1,0:T(8,128)S(1)}, f32[128,768]{1,0:T(8,128)}, u32[]{:S(2)}) copy-start(f32[128,768]{1,0:T(8,128)} %copy.106) | copy-start | bytes 1179652
  96.5 5.3 %copy-start.8 = (f32[128,768]{1,0:T(8,128)S(1)}, f32[128,768]{1,0:T(8,128)}, u32[]{:S(2)}) copy-start(f32[128,768]{1,0:T(8,128)} %copy.104) | copy-start | bytes 1179652
  96.5 6.1 %copy-start.24 = (bf16[128,1,3,64]{0,3,2,1:T(8,128)(2,1)S(1)}, bf16[128,1,3,64]{0,3,2,1:T(8,128)(2,1)}, u32[]{:S(2)}) copy-start(bf16[128,1,3,64]{0,3,2,1:T(8,128)(2,1)} %get-tuple-element.23) | copy-start | bytes 147460
  96.5 6.1 %copy-start.25 = (bf16[128,1,3,64]{0,3,2,1:T(8,128)(2,1)S(1)}, bf16[128,1,3,64]{0,3,2,1:T(8,128)(2,1)}, u32[]{:S(2)}) copy-start(bf16[128,1,3,64]{0,3,2,1:T(8,128)(2,1)} %get-tuple-element.24) | copy-start | bytes 147460
  96.5 6.1 %copy-start.26 = (bf16[128,1,3,64]{0,3,2,1:T(8,128)(2,1)S(1)}, bf16[128,1,3,64]{0,3,2,1:T(8,128)(2,1)}, u32[]{:S(2)}) copy-start(bf16[128,1,3,64]{0,3,2,1:T(8,128)(2,1)} %get-tuple-element.25) | copy-start | bytes 147460
  96.5 6.0 %copy-start.27 = (bf16[128,1,3,64]{0,3,2,1:T(8,128)(2,1)S(1)}, bf16[128,1,3,64]{0,3,2,1:T(8,128)(2,1)}, u32[]{:S(2)}) copy-start(bf16[128,1,3,64]{0,3,2,1:T(8,128)(2,1)} %get-tuple-element.26) | copy-start | bytes 147460
  97.7 5.1 %copy-start.34 = (s32[8,192]{1,0:T(8,128)S(1)}, s32[8,192]{1,0:T(8,128)}, u32[]{:S(2)}) copy-start(s32[8,192]{1,0:T(8,128)} %add_add_fusion.3) | copy-start | bytes 18436
  98.5 13.1 %collective-permute-start.4 = (bf16[128,512]{1,0:T(8,128)(2,1)}, bf16[128,512]{1,0:T(8,128)(2,1)}, u32[]{:S(2)}, u32[]{:S(2)}) collective-permute-start(bf16[128,512]{1,0:T(8,128)(2,1)} %get-tuple-element.18), channel_id=1, source_target_pairs={{0,252},{4,0},{8,4},{12,8},{16,12},{20,16},{24,20},{28,24},{32,28}... | collective-permute-start | bytes 393224 | tf_op jit(solution)/shard_map/ppermute | solution.py:18
  98.5 16.5 %collective-permute-start.5 = (bf16[128,512]{1,0:T(8,128)(2,1)}, bf16[128,512]{1,0:T(8,128)(2,1)}, u32[]{:S(2)}, u32[]{:S(2)}) collective-permute-start(bf16[128,512]{1,0:T(8,128)(2,1)} %get-tuple-element.20), channel_id=1, source_target_pairs={{0,248},{4,252},{8,0},{12,4},{16,8},{20,12},{24,16},{28,20},{32,24... | collective-permute-start | bytes 393224 | tf_op jit(solution)/shard_map/ppermute | solution.py:18
  101.8 13.9 %collective-permute-start.6 = (bf16[128,512]{1,0:T(8,128)(2,1)}, bf16[128,512]{1,0:T(8,128)(2,1)}, u32[]{:S(2)}, u32[]{:S(2)}) collective-permute-start(bf16[128,512]{1,0:T(8,128)(2,1)} %get-tuple-element.19), channel_id=1, source_target_pairs={{0,244},{4,248},{8,252},{12,0},{16,4},{20,8},{24,12},{28,16},{32,2... | collective-permute-start | bytes 393224 | tf_op jit(solution)/shard_map/ppermute | solution.py:18
  106.2 11.5 %copy-start.32 = (f32[128,4]{0,1:T(4,128)S(1)}, f32[128,4]{0,1:T(4,128)}, u32[]{:S(2)}) copy-start(f32[128,4]{0,1:T(4,128)} %copy-done.31) | copy-start | bytes 6148
  106.2 11.6 %copy-start.11 = (f32[128,256]{1,0:T(8,128)S(1)}, f32[128,256]{1,0:T(8,128)}, u32[]{:S(2)}) copy-start(f32[128,256]{1,0:T(8,128)} %copy-done.10) | copy-start | bytes 393220
  106.2 17.2 %all-to-all-start.1 = ((bf16[8,128,192]{1,2,0:T(8,128)(2,1)}), bf16[8,128,192]{1,2,0:T(8,128)(2,1)}, u32[]{:S(2)}, u32[]{:S(2)}) async-start(bf16[8,128,192]{1,2,0:T(8,128)(2,1)} %fusion.57), calls=%async_computation.1 | async-start | bytes 786432 | tf_op jit(solution)/shard_map/all_to_all | solution.py:42
  111.6 7.3 %copy-start.4 = (bf16[128,768]{1,0:T(8,128)(2,1)S(1)}, bf16[128,768]{1,0:T(8,128)(2,1)}, u32[]{:S(2)}) copy-start(bf16[128,768]{1,0:T(8,128)(2,1)} %copy-done.3) | copy-start | bytes 589828
  111.6 7.3 %copy-start.30 = (f32[768]{0:T(1024)S(1)}, f32[768]{0:T(1024)}, u32[]{:S(2)}) copy-start(f32[768]{0:T(1024)} %copy-done.29) | copy-start | bytes 9220
  111.6 7.3 %copy-start.40 = (f32[128]{0:T(128)S(1)}, f32[128]{0:T(128)}, u32[]{:S(2)}) copy-start(f32[128]{0:T(128)} %copy-done.39) | copy-start | bytes 1540
  117.8 2.9 %copy-start.43 = (f32[128]{0:T(128)S(1)}, f32[128]{0:T(128)}, u32[]{:S(2)}) copy-start(f32[128]{0:T(128)} %copy-done.42) | copy-start | bytes 1540
  117.8 2.9 %copy-start.2 = (bf16[1,128,768]{2,1,0:T(8,128)(2,1)S(1)}, bf16[1,128,768]{2,1,0:T(8,128)(2,1)}, u32[]{:S(2)}) copy-start(bf16[1,128,768]{2,1,0:T(8,128)(2,1)} %param.15) | copy-start | bytes 589828
  118.9 2.1 %copy-start.33 = (s32[8,160]{1,0:T(8,128)S(1)}, s32[8,160]{1,0:T(8,128)}, u32[]{:S(2)}) copy-start(s32[8,160]{1,0:T(8,128)} %add_select_fusion) | copy-start | bytes 15364
  123.4 16.1 %all-to-all-start = ((bf16[8,144,160]{2,1,0:T(8,128)(2,1)}), bf16[8,144,160]{2,1,0:T(8,128)(2,1)S(1)}, u32[]{:S(2)}, u32[]{:S(2)}) async-start(bf16[8,144,160]{2,1,0:T(8,128)(2,1)} %fusion.52), calls=%async_computation | async-start | bytes 1179648 | tf_op jit(solution)/shard_map/all_to_all | solution.py:42
  140.0 2.8 %copy-start.28 = (bf16[1024,96]{0,1:T(8,128)(2,1)S(1)}, bf16[1024,96]{0,1:T(8,128)(2,1)}, u32[]{:S(2)}) copy-start(bf16[1024,96]{0,1:T(8,128)(2,1)} %slice.241) | copy-start | bytes 589828
  179.0 13.8 %all-to-all-start.3 = ((f32[8,3,256]{2,1,0:T(4,128)}), f32[8,3,256]{2,1,0:T(4,128)S(1)}, u32[]{:S(2)}, u32[]{:S(2)}) async-start(f32[8,3,256]{2,1,0:T(4,128)} %reshape.579), calls=%async_computation.3 | async-start | bytes 65536 | tf_op jit(solution)/shard_map/all_to_all | solution.py:42
  (14 other events, 17.1 us)
Sparse Core Ops, SparseCore 0:
  9.8 41.3 all-gather.9
  53.0 36.3 all-gather.5
  91.2 44.0 all-gather.7

commit v2 on v1

v2 whole, which is shorter than its diff:
```python
import jax
import jax.numpy as jnp
import numpy as np
from jax import lax
from jax.experimental import pallas as pl
from jax.experimental.pallas import tpu as pltpu
from jax.sharding import Mesh, PartitionSpec as P

QUERY_HEADS = 12
KEY_VALUE_HEADS = 4
HEAD_SIZE = 64
TC = 16
D = 768
KV = 512
TOK = 128
BLK = ("yl", "x", "z")
BAND = ("yh", "c")
RING = ("yl", "yh", "c")
REST = ("x", "z")
F32 = jnp.float32
B16 = jnp.bfloat16
NN = (((1,), (0,)), ((), ()))
NT = (((1,), (1,)), ((), ()))
TN = (((0,), (0,)), ((), ()))


def dot(a, b, dims=NN):
    return lax.dot_general(a, b, dims, preferred_element_type=F32)


def passed_along(x, by):
    peers = lax.axis_size(BLK)
    return lax.ppermute(x, BLK, [(i, (i + by) % peers) for i in range(peers)])


def exchange(x, axes):
    return lax.all_to_all(x, axes, split_axis=0, concat_axis=0, tiled=True)


def orders():
    column = np.arange(D).reshape(2, 32, 4, 3)
    by_rest = column.transpose(1, 0, 2, 3).reshape(-1)
    by_member = column.transpose(0, 2, 1, 3).reshape(-1)
    eye = np.eye(D, dtype=np.float32)
    place = np.zeros((256, 192), np.float32)
    for j in range(2):
        for r in range(32):
            for k in range(3):
                place[r * 8 + j * 3 + k, j * 96 + r * 3 + k] = 1
    return jnp.asarray(eye[by_rest], B16), jnp.asarray(eye[by_member], B16), jnp.asarray(place, B16)


def call(body, outs, scratch=(), smem=(), count=0, limit=32, flops=10**9):
    specs = [
        pl.BlockSpec(memory_space=pltpu.SMEM if i in smem else pltpu.VMEM) for i in range(count)
    ]
    shapes = [jax.ShapeDtypeStruct(shape, kind) for shape, kind in outs]
    return pl.pallas_call(
        body,
        out_shape=shapes,
        in_specs=specs,
        out_specs=[pl.BlockSpec(memory_space=pltpu.VMEM)] * len(shapes),
        scratch_shapes=list(scratch),
        compiler_params=pltpu.CompilerParams(vmem_limit_bytes=limit * 2**20),
        cost_estimate=pl.CostEstimate(flops=flops, bytes_accessed=4 * 2**20, transcendentals=0),
    )


def stem_body(tiles, arrived, stem_w, gain, w_qkv, tokens_o, hidden_o, key_o, kv_o):
    own = tiles[...]
    below = jnp.concatenate([tiles[TC:, :], arrived[...]], axis=0)
    stem = dot(own, stem_w[0]) + dot(below, stem_w[1])
    low = stem.astype(B16)
    tokens_o[...] = low
    tok = low.astype(F32)
    factor = lax.rsqrt(jnp.mean(tok * tok, axis=1, keepdims=True) + 1e-05)
    hidden = (tok * factor * gain[...].astype(F32)).astype(B16)
    hidden_o[...] = hidden
    kv = dot(hidden, w_qkv[:, D:]).T
    key_o[...] = kv[:256]
    for h in range(KEY_VALUE_HEADS):
        k = kv[h * 64 : h * 64 + 64]
        scale = lax.rsqrt(jnp.mean(k * k, axis=0, keepdims=True) + 1e-06)
        kv_o[h * 64 : h * 64 + 64, :] = (k * scale).astype(B16)
    kv_o[256:, :] = kv[256:].astype(B16)


def query_body(hidden, d_out, w_qkv, w_out, by_rest, query_o, query_n_o, do_o, ring_o):
    h = hidden[...]
    q = dot(h, w_qkv[:, :D]).T
    query_o[...] = q
    for i in range(QUERY_HEADS):
        part = q[i * 64 : i * 64 + 64]
        scale = lax.rsqrt(jnp.mean(part * part, axis=0, keepdims=True) + 1e-06)
        query_n_o[i * 64 : i * 64 + 64, :] = (part * scale).astype(B16)
    g = d_out[...]
    do_o[...] = dot(w_out[...], g, NT).astype(B16)
    ring_o[:, :TOK] = dot(by_rest[...], h, NT).astype(B16)
    ring_o[:, TOK:] = dot(by_rest[...], g, NT).astype(B16)


def attend_body(
    own_block, scales, query, query_n, do, kv0, kv1, kv2, kv3, positions,
    early_o, dq_o, own_o, back1_o, back2_o, back3_o, attn_s,
):
    own = own_block[0]
    blocks = (kv0, kv1, kv2, kv3)
    q_pos = positions[pl.ds(own, 1), :]
    columns = []
    for j in range(4):
        row = positions[pl.ds(lax.rem(own - j + 64, 64), 1), :].astype(F32)
        columns.append(jnp.broadcast_to(row, (TOK, TOK)).T)
    key_pos = jnp.concatenate(columns, axis=0)
    bias = jnp.where(key_pos <= q_pos.astype(F32), 0.0, -1e30)
    bias = jnp.concatenate([bias] * 3, axis=1)
    for g in range(KEY_VALUE_HEADS):
        k = jnp.concatenate([b[g * 64 : g * 64 + 64, :] for b in blocks], axis=1)
        v = jnp.concatenate([b[256 + g * 64 : 320 + g * 64, :] for b in blocks], axis=1)
        heads = [3 * g + i for i in range(3)]
        q = jnp.concatenate([query_n[h * 64 : h * 64 + 64, :] for h in heads], axis=1)
        dy = jnp.concatenate([do[h * 64 : h * 64 + 64, :] for h in heads], axis=1)
        scale = jnp.concatenate([jnp.full((1, TOK), scales[h], F32) for h in heads], axis=1)
        scores = dot(k, q, TN) * scale
        scores = jnp.where(bias < 0.0, -1e30, scores)
        top = jnp.max(scores, axis=0, keepdims=True)
        weights = jnp.exp(scores - top)
        probs = weights * (1.0 / jnp.sum(weights, axis=0, keepdims=True))
        low = probs.astype(B16)
        attn = dot(v, low)
        delta = jnp.sum(dy.astype(F32) * attn, axis=0, keepdims=True)
        dprobs = dot(v, dy, TN)
        dscores = (scale * probs * (dprobs - delta)).astype(B16)
        dq = dot(k, dscores)
        dk = dot(q, dscores, NT)
        dv = dot(dy, low, NT)
        for i, h in enumerate(heads):
            rows = slice(h * 64, h * 64 + 64)
            lanes = slice(i * TOK, i * TOK + TOK)
            attn_s[rows, :] = attn[:, lanes].astype(B16)
            x = query[rows, :]
            dx = dq[:, lanes]
            r = lax.rsqrt(jnp.mean(x * x, axis=0, keepdims=True) + 1e-06)
            inner = jnp.mean(x * dx, axis=0, keepdims=True)
            dq_o[rows, :] = (r * dx - x * (r * r * r * inner)).astype(B16)
        own_o[g * 64 : g * 64 + 64, :] = dk[:, :TOK]
        own_o[256 + g * 64 : 320 + g * 64, :] = dv[:, :TOK]
        for j, back in enumerate((back1_o, back2_o, back3_o)):
            lanes = slice((j + 1) * TOK, (j + 2) * TOK)
            back[g * 64 : g * 64 + 64, :] = dk[:, lanes].astype(B16)
            back[256 + g * 64 : 320 + g * 64, :] = dv[:, lanes].astype(B16)
    for m in range(8):
        early_o[m, :96, :] = attn_s[m * 96 : m * 96 + 96, :]
        early_o[m, 96:, :] = dq_o[m * 96 : m * 96 + 96, :]


def tokens_body(
    own, back1, back2, back3, key, dq, w_qkv, tokens, gain, d_out, by_member, late_o, dkv_s
):
    total = own[...] + back1[...].astype(F32) + back2[...].astype(F32) + back3[...].astype(F32)
    for h in range(KEY_VALUE_HEADS):
        rows = slice(h * 64, h * 64 + 64)
        x = key[rows, :]
        dx = total[rows]
        r = lax.rsqrt(jnp.mean(x * x, axis=0, keepdims=True) + 1e-06)
        inner = jnp.mean(x * dx, axis=0, keepdims=True)
        dkv_s[rows, :] = (r * dx - x * (r * r * r * inner)).astype(B16)
    dkv_s[256:, :] = total[256:].astype(B16)
    d_hidden = (dot(w_qkv[:, :D], dq[...]) + dot(w_qkv[:, D:], dkv_s[...])).T
    tok = tokens[...].astype(F32)
    r = lax.rsqrt(jnp.mean(tok * tok, axis=1, keepdims=True) + 1e-05)
    gain_term = jnp.sum(d_hidden * (tok * r), axis=0, keepdims=True)
    dx = d_hidden * gain[...].astype(F32)
    inner = jnp.mean(tok * dx, axis=1, keepdims=True)
    d_tokens = (d_out[...].astype(F32) + (r * dx - tok * (r * r * r * inner))).astype(B16)
    spread = dot(by_member[...], d_tokens, NT).astype(B16)
    gains = jnp.concatenate(
        [gain_term[:, i * TOK : i * TOK + TOK] for i in range(6)] + [jnp.zeros((10, TOK), F32)],
        axis=0,
    ).astype(B16)
    for m in range(8):
        late_o[m, :96, :] = spread[m * 96 : m * 96 + 96]
        late_o[m, 96:128, :] = dkv_s[m * 32 : m * 32 + 32, :]
        late_o[m, 128:160, :] = dkv_s[256 + m * 32 : 288 + m * 32, :]
        late_o[m, 160:, :] = gains


def terms_body(
    core, early, late, tiles0, tiles1, ring0, ring1, place, stem_o, rows_o, pair_s, rhs_s, both_s
):
    lane = lax.broadcasted_iota(jnp.int32, (96, TOK), 1)
    gain = jnp.zeros((16, TOK), F32)
    zero = jnp.zeros((TOK, TOK), B16)
    for yl in range(2):
        before = jnp.zeros((96, TOK), F32)
        for band in range(4):
            m = yl * 4 + band
            block = late[m, :96, :]
            gain = gain + late[m, 160:, :].astype(F32)
            moved = pltpu.roll(block.astype(F32), TC, 1)
            pair_s[m, :96, :] = block
            pair_s[m, 96:, :] = jnp.where(lane < TC, before, moved).astype(B16)
            before = moved
            rhs_s[m, :96, :TOK] = early[m, 96:, :]
            rhs_s[m, 96:128, :TOK] = late[m, 96:128, :]
            rhs_s[m, :128, TOK:] = zero
            rhs_s[m, 128:224, :TOK] = zero[:96]
            rhs_s[m, 128:224, TOK:] = early[m, :96, :]
            rhs_s[m, 224:, :TOK] = late[m, 128:160, :]
            rhs_s[m, 224:, TOK:] = zero[:32]
    rows = jnp.zeros((D, 256), F32)
    for s, ring in enumerate((ring0, ring1)):
        side = lax.rem(core[0] + s, 2)
        for j in range(4):
            m = (j % 2) * 4 + (j // 2) * 2 + side
            at = s * 4 + j
            both_s[:, at * TOK : at * TOK + TOK] = dot(place[...], pair_s[m]).astype(B16)
            rows = rows + dot(ring[j], rhs_s[m], NT)
    rows_o[...] = rows.astype(B16)
    stem = dot(both_s[:, :512], tiles0[...]) + dot(both_s[:, 512:], tiles1[...])
    gain_row = jnp.concatenate(
        [gain[i : i + 1, :] for i in range(6)] + [jnp.zeros((1, 256), F32)], axis=1
    )
    slot = lax.rem(lax.broadcasted_iota(jnp.int32, (256, 1024), 0), 8)
    stem_o[...] = jnp.where(slot == 6, jnp.broadcast_to(gain_row, (256, 1024)), stem).astype(B16)


def shards(patches, stem_weight, norm_gain, w_qkv, w_out, per_head_scale, positions, d_out):
    tiles = patches[0]
    grad_out = d_out[0]
    by_rest, by_member, place = orders()
    bands = lax.axis_size(BAND)
    arrived = lax.ppermute(tiles[:TC], BAND, [(i, i - 1) for i in range(1, bands)])
    tiles_mine = lax.all_gather(tiles, ("yh", "yl"), axis=0, tiled=True)
    tiles_other = lax.ppermute(tiles_mine, "c", [(0, 1), (1, 0)])
    gain = norm_gain.reshape(1, D)
    tokens, hidden, key, kv_own = call(
        stem_body,
        [((TOK, D), B16), ((TOK, D), B16), ((256, TOK), F32), ((KV, TOK), B16)],
        count=5,
    )(tiles, arrived, stem_weight, gain, w_qkv)
    moved = [passed_along(kv_own, offset) for offset in range(1, 4)]
    query, query_n, do, ring_own = call(
        query_body,
        [((D, TOK), F32), ((D, TOK), B16), ((D, TOK), B16), ((D, 2 * TOK), B16)],
        count=5,
    )(hidden, grad_out, w_qkv, w_out, by_rest)
    ring_mine = lax.all_gather(ring_own, ("yh", "yl"), axis=0, tiled=False)
    ring_other = lax.ppermute(ring_mine, "c", [(0, 1), (1, 0)])
    own_block = lax.axis_index(BLK).astype(jnp.int32).reshape(1)
    early, d_q, own, back1, back2, back3 = call(
        attend_body,
        [((8, 192, TOK), B16), ((D, TOK), B16), ((KV, TOK), F32)] + [((KV, TOK), B16)] * 3,
        scratch=[pltpu.VMEM((D, TOK), B16)],
        smem=(0, 1),
        count=10,
    )(own_block, per_head_scale, query, query_n, do, kv_own, *moved, positions.reshape(64, TOK))
    returned = [passed_along(piece, -(j + 1)) for j, piece in enumerate((back1, back2, back3))]
    early_ring = exchange(early, RING)
    late = call(
        tokens_body,
        [((8, 176, TOK), B16)],
        scratch=[pltpu.VMEM((KV, TOK), B16)],
        count=11,
    )(own, *returned, key, d_q, w_qkv, tokens, gain, grad_out, by_member)[0]
    late_ring = exchange(late, RING)
    core = lax.axis_index("c").astype(jnp.int32).reshape(1)
    stem_terms, row_terms = call(
        terms_body,
        [((256, 1024), B16), ((D, 256), B16)],
        scratch=[
            pltpu.VMEM((8, 192, TOK), B16),
            pltpu.VMEM((8, 256, 256), B16),
            pltpu.VMEM((256, 1024), B16),
        ],
        smem=(0,),
        count=8,
    )(core, early_ring, late_ring, tiles_mine, tiles_other, ring_mine, ring_other, place)
    row_total = jnp.sum(exchange(row_terms.reshape(32, 24, 256), REST).astype(F32), axis=0)
    rows = exchange(row_total.reshape(8, 3, 256), RING)
    stem_total = jnp.sum(exchange(stem_terms.reshape(32, 8, 1024), REST).astype(F32), axis=0)
    d_stem_weight = stem_total[:6].reshape(2, 3, 1024).transpose(0, 2, 1)
    own_column = (lax.axis_index(BLK) * 4 + lax.axis_index(BAND)) * 3
    d_norm_gain = lax.dynamic_slice_in_dim(stem_total[6], own_column, 3)
    d_w_qkv = jnp.concatenate(
        [
            rows[:, :, first:last].transpose(1, 0, 2).reshape(3, -1)
            for first, last in ((0, 96), (96, 128), (224, 256))
        ],
        axis=1,
    )
    d_w_out = rows[:, :, 128:224].transpose(0, 2, 1).reshape(D, 3)
    return (d_stem_weight, d_norm_gain, d_w_qkv, d_w_out)


def solution(mesh):
    fine = Mesh(mesh.devices.reshape(2, 4, 8, 2, 2), BLK + BAND)
    placed = (P(BAND, BLK, None), P(), P(), P(), P(), P(), P(), P(BAND, BLK, None))
    every = BLK + BAND
    return jax.shard_map(
        shards,
        mesh=fine,
        in_specs=placed,
        out_specs=(P(None, None, every), P(every), P(every, None), P(None, every)),
        check_vma=False,
    )
```

time: 202 us -> 239 us (1.18); the launches traced: 201 us -> 235 us
  waiting for transfers between devices: 31.9 us -> 107 us
  matrix products: 44.8 us -> 0 us
  other arithmetic: 19.4 us -> 0.77 us
  Pallas kernels: 0 us -> 15.2 us
  local copies, waits for them, and re-layouts: 23.5 us -> 31.1 us
  blocking collectives: 29.4 us -> 33.4 us
  starting transfers between devices: 37.1 us -> 33.3 us
    all_gather x3 -> x2, waiting for transfers between devices: 0.04 us -> 56 us  [the longest x1 29.1 us: shards(): ring_mine = lax.all_gather(ring_own, ('yh', 'yl'), axis=0, tiled=False)]
    dot_general x30 -> x0, matrix products: 35 us -> none  [the longest x2 5.93 us: spread(): jnp.einsum('tc,qcj->qtj', x, pick, preferred_element_type=jnp.float32)]
    unnamed x99 -> x77, local copies, waits for them, and re-layouts: 3.46 us -> 28 us
    pallas_call x0 -> x5, Pallas kernels: none -> 15.2 us  [the longest x1 4.87 us: shards(): call(attend_body, [((8, 192, TOK), B16), ((D, TOK), B16), ((KV, TOK), F32...]
    ppermute x6, waiting for transfers between devices: 17.6 us -> 28.5 us  [passed_along(): return lax.ppermute(x, BLK, [(i, (i + by) % peers) for i in range(peers)])]
    sub x4 -> x0, matrix products: 9.84 us -> none  [shards(): weights = jnp.where(visible, jnp.exp(scores - top), 0.0)]
    all_to_all x3, waiting for transfers between devices: 12.2 us -> 19.8 us  [exchange(): return lax.all_to_all(x, axes, split_axis=0, concat_axis=0, tiled=True)]
    convert_element_type x10 -> x0, other arithmetic: 7.02 us -> none  [the longest x4 3.84 us: shards(): narrow = probs.astype(jnp.bfloat16)]
  transfers between devices with their start and end apart: 13 -> 14, of which waited for: 8 -> 11; matrix products, arithmetic and copies ran while one was open for 39% -> 1% of each run, Pallas kernels for 0% -> 3%
where the time goes in v2:
time: 239 us; the launch traced here: 235 us
  waiting for transfers between devices  107 us (45%)
  blocking collectives  33.4 us (14%)
  starting transfers between devices  33.3 us (14%)
  local copies, waits for them, and re-layouts  31.1 us (13%)
  Pallas kernels  15.2 us (6%)
  between operations  14.2 us (6%)
    all_to_all x2, blocking collectives, exchange(): return lax.all_to_all(x, axes, split_axis=0, concat_axis=0, tiled=True)  33.4 us
    all_gather x1, waiting for transfers between devices, shards(): ring_mine = lax.all_gather(ring_own, ('yh', 'yl'), axis=0, tiled=False)  29.1 us
    ppermute x6, waiting for transfers between devices, passed_along(): return lax.ppermute(x, BLK, [(i, (i + by) % peers) for i in range(peers)])  28.5 us
    unnamed x77, local copies, waits for them, and re-layouts  28 us
    all_gather x1, waiting for transfers between devices, shards(): tiles_mine = lax.all_gather(tiles, ('yh', 'yl'), axis=0, tiled=True)  26.9 us
    all_to_all x3, waiting for transfers between devices, exchange(): return lax.all_to_all(x, axes, split_axis=0, concat_axis=0, tiled=True)  19.8 us
    all_to_all x3, starting transfers between devices, exchange(): return lax.all_to_all(x, axes, split_axis=0, concat_axis=0, tiled=True)  14.3 us
    ppermute x6, starting transfers between devices, passed_along(): return lax.ppermute(x, BLK, [(i, (i + by) % peers) for i in range(peers)])  11.4 us
  transfers between devices with their start and end apart: 14, of which 11 were waited for; matrix products, arithmetic and copies ran while one was open for 1% of the time, Pallas kernels for 3%

profile of v2, /device:TPU:1, one launch (start us, length us, event | category | flops | bytes accessed | tf_op | source)
XLA Modules:
  0.0 234.8 jit_solution(1036195731866731753)
XLA Ops:
  7.2 0.8 slice_bitcast_fusion
  8.0 5.1 %collective-permute-start = (bf16[16,1024]{1,0:T(8,128)(2,1)S(1)}, bf16[16,1024]{1,0:T(8,128)(2,1)S(1)}, u32[]{:S(2)}, u32[]{:S(2)}) collective-permute-start(bf16[16,1024]{1,0:T(8,128)(2,1)S(1)} %slice_bitcast_fusion), channel_id=1, source_target_pairs={{1,0},{2,1},{3,2},{5,4},{6,5},{7,6},{9,8},{10,9},{11,10},{13,12},{... | collective-permute-start | bytes 98312 | tf_op jit(solution)/shard_map/ppermute | solution.py:232
  13.8 2.0 collective-permute-done.arrived
  15.8 1.5 copy-done
  17.3 1.9 copy-done.2
  19.2 0.9 copy-done.4
  20.2 1.2 shard_map.138
  22.5 2.0 shard_map.139
  26.7 29.1 %all-gather.7.cloned.1.call-done = bf16[3072,256]{1,0:T(8,128)(2,1)} async-done(((bf16[768,256]{1,0:T(8,128)(2,1)}), bf16[3072,256]{1,0:T(8,128)(2,1)}) %all-gather.7.cloned.1.call-update) | async-done | bytes 1572880 | tf_op jit(solution)/shard_map/all_gather | solution.py:247
  56.4 26.9 %all-gather.5.cloned.1.call-done = bf16[1,512,1024]{2,1,0:T(8,128)(2,1)} async-done(((bf16[1,128,1024]{2,1,0:T(8,128)(2,1)}), bf16[1,512,1024]{2,1,0:T(8,128)(2,1)}) %all-gather.5.cloned.1.call-update) | async-done | bytes 1048592 | tf_op jit(solution)/shard_map/all_gather | solution.py:233
  83.3 1.6 collective-permute-start.7
  84.9 3.3 %collective-permute-start.3 = (bf16[512,128]{1,0:T(8,128)(2,1)S(1)}, bf16[512,128]{1,0:T(8,128)(2,1)S(1)}, u32[]{:S(2)}, u32[]{:S(2)}) collective-permute-start(bf16[512,128]{1,0:T(8,128)(2,1)S(1)} %get-tuple-element.24.kv0), channel_id=1, source_target_pairs={{0,12},{4,16},{8,20},{12,24},{16,28},{20,32},{24,36},{28,40},{32,4... | collective-permute-start | bytes 393224 | tf_op jit(solution)/shard_map/ppermute | solution.py:33
  88.2 2.6 %collective-permute-start.2 = (bf16[512,128]{1,0:T(8,128)(2,1)S(1)}, bf16[512,128]{1,0:T(8,128)(2,1)S(1)}, u32[]{:S(2)}, u32[]{:S(2)}) collective-permute-start(bf16[512,128]{1,0:T(8,128)(2,1)S(1)} %get-tuple-element.24.kv0), channel_id=1, source_target_pairs={{0,8},{4,12},{8,16},{12,20},{16,24},{20,28},{24,32},{28,36},{32,40... | collective-permute-start | bytes 393224 | tf_op jit(solution)/shard_map/ppermute | solution.py:33
  91.1 9.7 %collective-permute-done.3.kv3 = bf16[512,128]{1,0:T(8,128)(2,1)S(1)} collective-permute-done((bf16[512,128]{1,0:T(8,128)(2,1)S(1)}, bf16[512,128]{1,0:T(8,128)(2,1)S(1)}, u32[]{:S(2)}, u32[]{:S(2)}) %collective-permute-start.3) | collective-permute-done | bytes 131104 | tf_op jit(solution)/shard_map/ppermute | solution.py:33
  101.5 4.8 %collective-permute-done.2.kv2 = bf16[512,128]{1,0:T(8,128)(2,1)S(1)} collective-permute-done((bf16[512,128]{1,0:T(8,128)(2,1)S(1)}, bf16[512,128]{1,0:T(8,128)(2,1)S(1)}, u32[]{:S(2)}, u32[]{:S(2)}) %collective-permute-start.2) | collective-permute-done | bytes 131104 | tf_op jit(solution)/shard_map/ppermute | solution.py:33
  106.9 3.5 %collective-permute-done.1.kv1 = bf16[512,128]{1,0:T(8,128)(2,1)S(1)} collective-permute-done((bf16[512,128]{1,0:T(8,128)(2,1)S(1)}, bf16[512,128]{1,0:T(8,128)(2,1)S(1)}, u32[]{:S(2)}, u32[]{:S(2)}) %collective-permute-start.1) | collective-permute-done | bytes 131104 | tf_op jit(solution)/shard_map/ppermute | solution.py:33
  111.1 0.9 copy-done.22
  112.0 0.9 copy-done.24
  113.0 0.9 copy-done.26
  113.9 0.9 copy-done.28
  114.8 0.9 copy-done.30
  115.7 0.9 copy-done.32
  116.6 0.8 copy-done.36
  117.3 4.9 %shard_map.140 = (bf16[8,192,128]{2,1,0:T(8,128)(2,1)S(1)}, bf16[768,128]{1,0:T(8,128)(2,1)S(1)}, f32[512,128]{1,0:T(8,128)S(1)}, bf16[512,128]{1,0:T(8,128)(2,1...) custom-call(s32[1]{0:T(128)} %bitcast.1.own_block, f32[12]{0:T(128)S(1)} %copy-done.37, ...), custom_call_target="tpu_custom_call" | custom-call | flops 1000000000 | bytes 4194304 | tf_op jit(solution)/shard_map/pallas_call | solution.py:250
  122.2 0.8 copy-done.11
  123.0 0.7 copy-done.12
  126.3 3.8 %all-to-all-start = ((bf16[8,192,128]{2,1,0:T(8,128)(2,1)}), bf16[8,192,128]{2,1,0:T(8,128)(2,1)S(1)}, u32[]{:S(2)}, u32[]{:S(2)}) async-start(bf16[8,192,128]{2,1,0:T(8,128)(2,1)} %copy-done.11), calls=%async_computation | async-start | bytes 786432 | tf_op jit(solution)/shard_map/all_to_all | solution.py:37
  130.1 1.1 collective-permute-start.4
  131.2 1.5 collective-permute-start.5
  132.7 2.6 %collective-permute-start.6 = (bf16[512,128]{1,0:T(8,128)(2,1)}, bf16[512,128]{1,0:T(8,128)(2,1)S(1)}, u32[]{:S(2)}, u32[]{:S(2)}) collective-permute-start(bf16[512,128]{1,0:T(8,128)(2,1)} %copy-done.33), channel_id=1, source_target_pairs={{0,244},{4,248},{8,252},{12,0},{16,4},{20,8},{24,12},{28,16},{32,2... | collective-permute-start | bytes 393224 | tf_op jit(solution)/shard_map/ppermute | solution.py:33
  135.4 4.5 %collective-permute-done.5.back2 = bf16[512,128]{1,0:T(8,128)(2,1)S(1)} collective-permute-done((bf16[512,128]{1,0:T(8,128)(2,1)}, bf16[512,128]{1,0:T(8,128)(2,1)S(1)}, u32[]{:S(2)}, u32[]{:S(2)}) %collective-permute-start.5) | collective-permute-done | bytes 131104 | tf_op jit(solution)/shard_map/ppermute | solution.py:33
  140.0 5.9 %collective-permute-done.6.back3 = bf16[512,128]{1,0:T(8,128)(2,1)S(1)} collective-permute-done((bf16[512,128]{1,0:T(8,128)(2,1)}, bf16[512,128]{1,0:T(8,128)(2,1)S(1)}, u32[]{:S(2)}, u32[]{:S(2)}) %collective-permute-start.6) | collective-permute-done | bytes 131104 | tf_op jit(solution)/shard_map/ppermute | solution.py:33
  145.9 0.9 copy-done.10
  146.8 0.9 copy-done.13
  147.7 0.9 copy-done.15
  148.7 0.9 copy-done.17
  149.6 0.9 copy-done.20
  150.5 2.7 %shard_map.141 = bf16[8,176,128]{2,1,0:T(8,128)(2,1)} custom-call(f32[512,128]{1,0:T(8,128)S(1)} %copy-done.13, bf16[512,128]{1,0:T(8,128)(2,1)S(1)} %collective-permute-done.4.back1, bf16[512,128]{1,0:T(8,128)(2,1)S(1)} %collective-permute-done.5.back2, bf16[512,128]{1,0:T(8,128)(2,1)S(1)} %collective-permute-done.6.back3, f32[256,128]{1,0:T(8,128)S(1)} %copy-done.20, ...), custom_call_target="tpu_custom_call" | custom-call | flops 1000000000 | bytes 4194304 | tf_op jit(solution)/shard_map/pallas_call | solution.py:259
  153.2 5.7 %all-to-all-start.1 = ((bf16[8,176,128]{2,1,0:T(8,128)(2,1)}), bf16[8,176,128]{2,1,0:T(8,128)(2,1)S(1)}, u32[]{:S(2)}, u32[]{:S(2)}) async-start(bf16[8,176,128]{2,1,0:T(8,128)(2,1)} %shard_map.141), calls=%async_computation.1 | async-start | bytes 720896 | tf_op jit(solution)/shard_map/all_to_all | solution.py:37
  158.9 7.4 %all-to-all-done.1.late = bf16[8,176,128]{2,1,0:T(8,128)(2,1)S(1)} async-done(((bf16[8,176,128]{2,1,0:T(8,128)(2,1)}), bf16[8,176,128]{2,1,0:T(8,128)(2,1)S(1)}, u32[]{:S(2)}, u32[]{:S(2)}) %all-to-all-start.1) | async-done | bytes 360480 | tf_op jit(solution)/shard_map/all_to_all | solution.py:37
  166.3 1.4 copy-done.3
  167.8 1.2 copy-done.8
  169.0 0.9 copy-done.18
  169.9 4.5 %shard_map.142 = (bf16[256,1024]{1,0:T(8,128)(2,1)}, bf16[768,256]{1,0:T(8,128)(2,1)S(1)}) custom-call(s32[1]{0:T(128)} %bitcast.core, bf16[8,192,128]{2,1,0:T(8,128)(2,1)S(1)} %all-to-all-done.early, bf16[8,176,128]{2,1,0:T(8,128)(2,1)S(1)} %all-to-all-done.1.late, bf16[512,1024]{1,0:T(8,128)(2,1)S(1)} %bitcast.29, ...), custom_call_target="tpu_custom_call" | custom-call | flops 1000000000 | bytes 4194304 | tf_op jit(solution)/shard_map/pallas_call | solution.py:267
  174.4 21.7 %all_to_all.25 = bf16[32,24,256]{2,1,0:T(8,128)(2,1)S(1)} all-to-all(bf16[32,24,256]{2,1,0:T(8,128)(2,1)S(1)} %bitcast.32), channel_id=1, replica_groups=mesh['yl'=2,'x'=4,'z'=8,'yh'=2,'c'=2] {'x','z'}, dimensions={0} | all-to-all | bytes 786432 | tf_op jit(solution)/shard_map/all_to_all | solution.py:37
  196.1 11.7 %all_to_all.26 = f32[8,3,256]{2,1,0:T(4,128)S(1)} all-to-all(f32[8,3,256]{2,1,0:T(4,128)S(1)} %reshape.53), channel_id=1, replica_groups=mesh['yl'=2,'x'=4,'z'=8,'yh'=2,'c'=2] {'yl','yh','c'}, dimensions={0} | all-to-all | bytes 49152 | tf_op jit(solution)/shard_map/all_to_all | solution.py:37
  207.9 4.8 %all-to-all-start.2 = ((bf16[32,8,1024]{2,1,0:T(8,128)(2,1)}), bf16[32,8,1024]{2,1,0:T(8,128)(2,1)S(1)}, u32[]{:S(2)}, u32[]{:S(2)}) async-start(bf16[32,8,1024]{2,1,0:T(8,128)(2,1)} %bitcast.8), calls=%async_computation.2 | async-start | bytes 1048576 | tf_op jit(solution)/shard_map/all_to_all | solution.py:37
  214.3 12.3 %all-to-all-done.2 = bf16[32,8,1024]{2,1,0:T(8,128)(2,1)S(1)} async-done(((bf16[32,8,1024]{2,1,0:T(8,128)(2,1)}), bf16[32,8,1024]{2,1,0:T(8,128)(2,1)S(1)}, u32[]{:S(2)}, u32[]{:S(2)}) %all-to-all-start.2) | async-done | bytes 524320 | tf_op jit(solution)/shard_map/all_to_all | solution.py:37
  (85 shorter events, 12.8 us)
Async XLA Ops:
  7.2 48.6 %all-gather.7.cloned.1.call-start = ((), (), s32[]{:S(2)}) async-start(), calls=%async_computation.6 | async-start | bytes 1966080 | tf_op jit(solution)/shard_map/all_gather | solution.py:247
  8.0 7.8 %collective-permute-start = (bf16[16,1024]{1,0:T(8,128)(2,1)S(1)}, bf16[16,1024]{1,0:T(8,128)(2,1)S(1)}, u32[]{:S(2)}, u32[]{:S(2)}) collective-permute-start(bf16[16,1024]{1,0:T(8,128)(2,1)S(1)} %slice_bitcast_fusion), channel_id=1, source_target_pairs={{1,0},{2,1},{3,2},{5,4},{6,5},{7,6},{9,8},{10,9},{11,10},{13,12},{... | collective-permute-start | bytes 98312 | tf_op jit(solution)/shard_map/ppermute | solution.py:232
  15.8 1.5 copy-start
  17.3 1.9 copy-start.2
  19.2 0.9 copy-start.4
  20.2 1.5 copy-start.1
  20.2 1.9 copy-start.6
  20.2 2.4 %copy-start.7 = (bf16[768,768]{1,0:T(8,128)(2,1)S(1)}, bf16[768,768]{1,0:T(8,128)(2,1)}, u32[]{:S(2)}) copy-start(bf16[768,768]{1,0:T(8,128)(2,1)} %constant.43.clone.by_rest) | copy-start | bytes 3538948
  20.2 2.4 %copy-start.9 = (bf16[1,128,768]{2,1,0:T(8,128)(2,1)S(1)}, bf16[1,128,768]{2,1,0:T(8,128)(2,1)}, u32[]{:S(2)}) copy-start(bf16[1,128,768]{2,1,0:T(8,128)(2,1)} %param.18) | copy-start | bytes 589828
  21.3 3.2 %copy-start.14 = (bf16[128,768]{1,0:T(8,128)(2,1)}, bf16[128,768]{1,0:T(8,128)(2,1)S(1)}, u32[]{:S(2)}) copy-start(bf16[128,768]{1,0:T(8,128)(2,1)S(1)} %get-tuple-element.32.tokens) | copy-start | bytes 589828
  21.3 3.2 %copy-start.19 = (f32[256,128]{1,0:T(8,128)}, f32[256,128]{1,0:T(8,128)S(1)}, u32[]{:S(2)}) copy-start(f32[256,128]{1,0:T(8,128)S(1)} %get-tuple-element.30.key) | copy-start | bytes 393220
  21.4 69.4 %copy-start.25 = (bf16[512,128]{1,0:T(8,128)(2,1)}, bf16[512,128]{1,0:T(8,128)(2,1)S(1)}, u32[]{:S(2)}) copy-start(bf16[512,128]{1,0:T(8,128)(2,1)S(1)} %get-tuple-element.24.kv0) | copy-start | bytes 393220
  22.5 88.6 %copy-start.37 = (f32[12]{0:T(128)S(1)}, f32[12]{0:T(128)}, u32[]{:S(2)}) copy-start(f32[12]{0:T(128)} %scales.1) | copy-start | bytes 148
  24.5 0.7 copy-start.21
  25.2 0.7 copy-start.23
  25.9 57.4 %all-gather.5.cloned.1.call-start = ((), (), s32[]{:S(2)}) async-start(), calls=%async_computation.5 | async-start | bytes 1310720 | tf_op jit(solution)/shard_map/all_gather | solution.py:233
  55.8 110.6 %collective-permute-start.8 = (bf16[4,768,256]{2,1,0:T(8,128)(2,1)}, bf16[4,768,256]{2,1,0:T(8,128)(2,1)}, u32[]{:S(2)}, u32[]{:S(2)}) collective-permute-start(bf16[4,768,256]{2,1,0:T(8,128)(2,1)} %bitcast.25), channel_id=1, source_target_pairs={{0,1},{1,0},{2,3},{3,2},{4,5},{5,4},{6,7},{7,6},{8,9},{9,8},{10,11... | collective-permute-start | bytes 4718600 | tf_op jit(solution)/shard_map/ppermute | solution.py:248
  83.3 83.0 %collective-permute-start.7 = (bf16[512,1024]{1,0:T(8,128)(2,1)}, bf16[512,1024]{1,0:T(8,128)(2,1)}, u32[]{:S(2)}, u32[]{:S(2)}) collective-permute-start(bf16[512,1024]{1,0:T(8,128)(2,1)} %bitcast.28), channel_id=1, source_target_pairs={{0,1},{1,0},{2,3},{3,2},{4,5},{5,4},{6,7},{7,6},{8,9},{9,8},{10,11... | collective-permute-start | bytes 3145736 | tf_op jit(solution)/shard_map/ppermute | solution.py:234
  84.9 15.9 %collective-permute-start.3 = (bf16[512,128]{1,0:T(8,128)(2,1)S(1)}, bf16[512,128]{1,0:T(8,128)(2,1)S(1)}, u32[]{:S(2)}, u32[]{:S(2)}) collective-permute-start(bf16[512,128]{1,0:T(8,128)(2,1)S(1)} %get-tuple-element.24.kv0), channel_id=1, source_target_pairs={{0,12},{4,16},{8,20},{12,24},{16,28},{20,32},{24,36},{28,40},{32,4... | collective-permute-start | bytes 393224 | tf_op jit(solution)/shard_map/ppermute | solution.py:33
  88.2 18.1 %collective-permute-start.2 = (bf16[512,128]{1,0:T(8,128)(2,1)S(1)}, bf16[512,128]{1,0:T(8,128)(2,1)S(1)}, u32[]{:S(2)}, u32[]{:S(2)}) collective-permute-start(bf16[512,128]{1,0:T(8,128)(2,1)S(1)} %get-tuple-element.24.kv0), channel_id=1, source_target_pairs={{0,8},{4,12},{8,16},{12,20},{16,24},{20,28},{24,32},{28,36},{32,40... | collective-permute-start | bytes 393224 | tf_op jit(solution)/shard_map/ppermute | solution.py:33
  90.7 19.7 %collective-permute-start.1 = (bf16[512,128]{1,0:T(8,128)(2,1)S(1)}, bf16[512,128]{1,0:T(8,128)(2,1)S(1)}, u32[]{:S(2)}, u32[]{:S(2)}) collective-permute-start(bf16[512,128]{1,0:T(8,128)(2,1)S(1)} %get-tuple-element.24.kv0), channel_id=1, source_target_pairs={{0,4},{4,8},{8,12},{12,16},{16,20},{20,24},{24,28},{28,32},{32,36}... | collective-permute-start | bytes 393224 | tf_op jit(solution)/shard_map/ppermute | solution.py:33
  110.4 0.7 copy-start.31
  111.1 0.9 copy-start.22
  112.0 0.9 copy-start.24
  113.0 0.9 copy-start.26
  113.9 0.9 copy-start.28
  114.8 0.9 copy-start.30
  115.7 0.9 copy-start.32
  116.6 0.8 copy-start.36
  117.3 28.5 %copy-start.5 = (bf16[768,768]{1,0:T(8,128)(2,1)S(1)}, bf16[768,768]{1,0:T(8,128)(2,1)}, u32[]{:S(2)}) copy-start(bf16[768,768]{1,0:T(8,128)(2,1)} %constant.44.clone.by_member) | copy-start | bytes 3538948
  122.2 0.8 copy-start.11
  123.0 0.7 copy-start.12
  123.7 0.7 copy-start.16
  125.7 0.7 copy-start.35
  126.3 26.9 %all-to-all-start = ((bf16[8,192,128]{2,1,0:T(8,128)(2,1)}), bf16[8,192,128]{2,1,0:T(8,128)(2,1)S(1)}, u32[]{:S(2)}, u32[]{:S(2)}) async-start(bf16[8,192,128]{2,1,0:T(8,128)(2,1)} %copy-done.11), calls=%async_computation | async-start | bytes 786432 | tf_op jit(solution)/shard_map/all_to_all | solution.py:37
  130.1 5.3 %collective-permute-start.4 = (bf16[512,128]{1,0:T(8,128)(2,1)}, bf16[512,128]{1,0:T(8,128)(2,1)S(1)}, u32[]{:S(2)}, u32[]{:S(2)}) collective-permute-start(bf16[512,128]{1,0:T(8,128)(2,1)} %copy-done.35), channel_id=1, source_target_pairs={{0,252},{4,0},{8,4},{12,8},{16,12},{20,16},{24,20},{28,24},{32,28}... | collective-permute-start | bytes 393224 | tf_op jit(solution)/shard_map/ppermute | solution.py:33
  131.2 8.7 %collective-permute-start.5 = (bf16[512,128]{1,0:T(8,128)(2,1)}, bf16[512,128]{1,0:T(8,128)(2,1)S(1)}, u32[]{:S(2)}, u32[]{:S(2)}) collective-permute-start(bf16[512,128]{1,0:T(8,128)(2,1)} %copy-done.34), channel_id=1, source_target_pairs={{0,248},{4,252},{8,0},{12,4},{16,8},{20,12},{24,16},{28,20},{32,24... | collective-permute-start | bytes 393224 | tf_op jit(solution)/shard_map/ppermute | solution.py:33
  132.7 13.2 %collective-permute-start.6 = (bf16[512,128]{1,0:T(8,128)(2,1)}, bf16[512,128]{1,0:T(8,128)(2,1)S(1)}, u32[]{:S(2)}, u32[]{:S(2)}) collective-permute-start(bf16[512,128]{1,0:T(8,128)(2,1)} %copy-done.33), channel_id=1, source_target_pairs={{0,244},{4,248},{8,252},{12,0},{16,4},{20,8},{24,12},{28,16},{32,2... | collective-permute-start | bytes 393224 | tf_op jit(solution)/shard_map/ppermute | solution.py:33
  145.9 0.9 copy-start.10
  146.8 0.9 copy-start.13
  147.7 0.9 copy-start.15
  148.7 0.9 copy-start.17
  149.6 0.9 copy-start.20
  153.2 13.2 %all-to-all-start.1 = ((bf16[8,176,128]{2,1,0:T(8,128)(2,1)}), bf16[8,176,128]{2,1,0:T(8,128)(2,1)S(1)}, u32[]{:S(2)}, u32[]{:S(2)}) async-start(bf16[8,176,128]{2,1,0:T(8,128)(2,1)} %shard_map.141), calls=%async_computation.1 | async-start | bytes 720896 | tf_op jit(solution)/shard_map/all_to_all | solution.py:37
  166.3 1.4 copy-start.3
  167.8 1.2 copy-start.8
  169.0 0.9 copy-start.18
  207.9 18.8 %all-to-all-start.2 = ((bf16[32,8,1024]{2,1,0:T(8,128)(2,1)}), bf16[32,8,1024]{2,1,0:T(8,128)(2,1)S(1)}, u32[]{:S(2)}, u32[]{:S(2)}) async-start(bf16[32,8,1024]{2,1,0:T(8,128)(2,1)} %bitcast.8), calls=%async_computation.2 | async-start | bytes 1048576 | tf_op jit(solution)/shard_map/all_to_all | solution.py:37
  (4 other events, 2.6 us)
Sparse Core Ops, SparseCore 0:
  26.0 29.6 all-gather.6
  57.6 25.7 all-gather.4

commit v3 on v2

--- a/solution.py
+++ b/solution.py
@@ -39,18 +39,24 @@
 
 def orders():
     column = np.arange(D).reshape(2, 32, 4, 3)
-    by_rest = column.transpose(1, 0, 2, 3).reshape(-1)
+    by_rest = column.transpose(1, 0, 2, 3).reshape(32, 24)
+    by_rest = np.concatenate([by_rest[:, :16].reshape(-1), by_rest[:, 16:].reshape(-1)])
     by_member = column.transpose(0, 2, 1, 3).reshape(-1)
     eye = np.eye(D, dtype=np.float32)
-    place = np.zeros((256, 192), np.float32)
-    for j in range(2):
+    place = np.zeros((2, 512, 192), np.float32)
+    fold = np.zeros((2, 512, 256), np.float32)
+    for half in range(2):
         for r in range(32):
-            for k in range(3):
-                place[r * 8 + j * 3 + k, j * 96 + r * 3 + k] = 1
-    return jnp.asarray(eye[by_rest], B16), jnp.asarray(eye[by_member], B16), jnp.asarray(place, B16)
-
-
-def call(body, outs, scratch=(), smem=(), count=0, limit=32, flops=10**9):
+            for j in range(2):
+                for k in range(3):
+                    place[half, r * 16 + half * 6 + j * 3 + k, j * 96 + r * 3 + k] = 1
+            for i in range(8):
+                fold[half, r * 16 + half * 8 + i, r * 8 + i] = 1
+    tables = (eye[by_rest], eye[by_member], place, fold)
+    return [jnp.asarray(table, B16) for table in tables]
+
+
+def call(body, outs, scratch=(), smem=(), count=0, limit=60, flops=10**9):
     specs = [
         pl.BlockSpec(memory_space=pltpu.SMEM if i in smem else pltpu.VMEM) for i in range(count)
     ]
@@ -185,7 +191,7 @@
 
 
 def terms_body(
-    core, early, late, tiles0, tiles1, ring0, ring1, place, stem_o, rows_o, pair_s, rhs_s, both_s
+    core, early, late, tiles0, tiles1, ring0, ring1, place, fold, terms_o, pair_s, rhs_s, both_s
 ):
     lane = lax.broadcasted_iota(jnp.int32, (96, TOK), 1)
     gain = jnp.zeros((16, TOK), F32)
@@ -213,25 +219,54 @@
         for j in range(4):
             m = (j % 2) * 4 + (j // 2) * 2 + side
             at = s * 4 + j
-            both_s[:, at * TOK : at * TOK + TOK] = dot(place[...], pair_s[m]).astype(B16)
+            for half in range(2):
+                both_s[half, :, at * TOK : at * TOK + TOK] = dot(place[half], pair_s[m]).astype(B16)
             rows = rows + dot(ring[j], rhs_s[m], NT)
-    rows_o[...] = rows.astype(B16)
-    stem = dot(both_s[:, :512], tiles0[...]) + dot(both_s[:, 512:], tiles1[...])
-    gain_row = jnp.concatenate(
-        [gain[i : i + 1, :] for i in range(6)] + [jnp.zeros((1, 256), F32)], axis=1
-    )
-    slot = lax.rem(lax.broadcasted_iota(jnp.int32, (256, 1024), 0), 8)
-    stem_o[...] = jnp.where(slot == 6, jnp.broadcast_to(gain_row, (256, 1024)), stem).astype(B16)
+    low = rows.astype(B16)
+    terms_o[:, 512:768] = low[:512]
+    terms_o[:, 768:] = (dot(fold[0], low[512:, :TOK]) + dot(fold[1], low[512:, TOK:])).astype(B16)
+    stem = dot(both_s[0, :, :512], tiles0[:, :512]) + dot(both_s[0, :, 512:], tiles1[:, :512])
+    stem = stem + dot(both_s[1, :, :512], tiles0[:, 512:])
+    stem = stem + dot(both_s[1, :, 512:], tiles1[:, 512:])
+    slot = lax.rem(lax.broadcasted_iota(jnp.int32, (512, 512), 0), 16)
+    first = jnp.concatenate([gain[i : i + 1, :] for i in range(4)], axis=1)
+    second = jnp.concatenate([gain[4:5, :], gain[5:6, :], jnp.zeros((1, 256), F32)], axis=1)
+    stem = jnp.where(slot == 12, jnp.broadcast_to(first, (512, 512)), stem)
+    stem = jnp.where(slot == 13, jnp.broadcast_to(second, (512, 512)), stem)
+    terms_o[:, :512] = stem.astype(B16)
+
+
+def total_body(terms, stem_o, gain_o, rows_o):
+    total = terms[0].astype(F32)
+    for r in range(1, 32):
+        total = total + terms[r].astype(F32)
+    stem_o[:, :512] = total[:6, :512]
+    stem_o[:, 512:] = total[6:12, :512]
+    gain_o[:, :512] = total[12:13, :512]
+    gain_o[:, 512:] = total[13:14, :256]
+    last = jnp.concatenate([total[:8, 768:], total[8:, 768:]], axis=1)
+    rows = jnp.concatenate([total[:, 512:768], last], axis=0)
+    for m in range(8):
+        rows_o[m, :3, :] = rows[m * 3 : m * 3 + 3]
+        rows_o[m, 3:, :] = jnp.zeros((5, 256), F32)
+
+
+def final_body(rows, qkv_o, out_o):
+    for first, last, to in ((0, 96, 0), (96, 128, D), (224, 256, D + 256)):
+        width = last - first
+        for m in range(8):
+            qkv_o[:, to + m * width : to + m * width + width] = rows[m, :3, first:last]
+    for m in range(8):
+        out_o[:, m * 96 : m * 96 + 96] = rows[m, :3, 128:224]
 
 
 def shards(patches, stem_weight, norm_gain, w_qkv, w_out, per_head_scale, positions, d_out):
     tiles = patches[0]
     grad_out = d_out[0]
-    by_rest, by_member, place = orders()
+    by_rest, by_member, place, fold = orders()
     bands = lax.axis_size(BAND)
     arrived = lax.ppermute(tiles[:TC], BAND, [(i, i - 1) for i in range(1, bands)])
     tiles_mine = lax.all_gather(tiles, ("yh", "yl"), axis=0, tiled=True)
-    tiles_other = lax.ppermute(tiles_mine, "c", [(0, 1), (1, 0)])
     gain = norm_gain.reshape(1, D)
     tokens, hidden, key, kv_own = call(
         stem_body,
@@ -245,7 +280,6 @@
         count=5,
     )(hidden, grad_out, w_qkv, w_out, by_rest)
     ring_mine = lax.all_gather(ring_own, ("yh", "yl"), axis=0, tiled=False)
-    ring_other = lax.ppermute(ring_mine, "c", [(0, 1), (1, 0)])
     own_block = lax.axis_index(BLK).astype(jnp.int32).reshape(1)
     early, d_q, own, back1, back2, back3 = call(
         attend_body,
@@ -263,33 +297,31 @@
         count=11,
     )(own, *returned, key, d_q, w_qkv, tokens, gain, grad_out, by_member)[0]
     late_ring = exchange(late, RING)
+    tiles_mine, ring_mine, late = lax.optimization_barrier((tiles_mine, ring_mine, late))
+    tiles_other = lax.ppermute(tiles_mine, "c", [(0, 1), (1, 0)])
+    ring_other = lax.ppermute(ring_mine, "c", [(0, 1), (1, 0)])
     core = lax.axis_index("c").astype(jnp.int32).reshape(1)
-    stem_terms, row_terms = call(
+    terms = call(
         terms_body,
-        [((256, 1024), B16), ((D, 256), B16)],
+        [((512, 896), B16)],
         scratch=[
             pltpu.VMEM((8, 192, TOK), B16),
             pltpu.VMEM((8, 256, 256), B16),
-            pltpu.VMEM((256, 1024), B16),
+            pltpu.VMEM((2, 512, 1024), B16),
         ],
         smem=(0,),
-        count=8,
-    )(core, early_ring, late_ring, tiles_mine, tiles_other, ring_mine, ring_other, place)
-    row_total = jnp.sum(exchange(row_terms.reshape(32, 24, 256), REST).astype(F32), axis=0)
-    rows = exchange(row_total.reshape(8, 3, 256), RING)
-    stem_total = jnp.sum(exchange(stem_terms.reshape(32, 8, 1024), REST).astype(F32), axis=0)
-    d_stem_weight = stem_total[:6].reshape(2, 3, 1024).transpose(0, 2, 1)
+        count=9,
+    )(core, early_ring, late_ring, tiles_mine, tiles_other, ring_mine, ring_other, place, fold)[0]
+    stem_total, gain_total, row_total = call(
+        total_body, [((6, 1024), F32), ((1, D), F32), ((8, 8, 256), F32)], count=1
+    )(exchange(terms.reshape(32, 16, 896), REST))
+    d_w_qkv, d_w_out = call(final_body, [((3, 1280), F32), ((3, D), F32)], count=1)(
+        exchange(row_total, RING)
+    )
     own_column = (lax.axis_index(BLK) * 4 + lax.axis_index(BAND)) * 3
-    d_norm_gain = lax.dynamic_slice_in_dim(stem_total[6], own_column, 3)
-    d_w_qkv = jnp.concatenate(
-        [
-            rows[:, :, first:last].transpose(1, 0, 2).reshape(3, -1)
-            for first, last in ((0, 96), (96, 128), (224, 256))
-        ],
-        axis=1,
-    )
-    d_w_out = rows[:, :, 128:224].transpose(0, 2, 1).reshape(D, 3)
-    return (d_stem_weight, d_norm_gain, d_w_qkv, d_w_out)
+    d_norm_gain = lax.dynamic_slice_in_dim(gain_total[0], own_column, 3)
+    d_stem_weight = stem_total.reshape(2, 3, 1024).transpose(0, 2, 1)
+    return (d_stem_weight, d_norm_gain, d_w_qkv, d_w_out.T)
 
 
 def solution(mesh):

time: 239 us -> 173 us (0.72); the launches traced: 235 us -> 173 us
  waiting for transfers between devices: 107 us -> 59.8 us
  local copies, waits for them, and re-layouts: 31.1 us -> 9.8 us
  blocking collectives: 33.4 us -> 12.9 us
  Pallas kernels: 15.2 us -> 32 us
  starting transfers between devices: 33.3 us -> 44 us
    all_gather x1, waiting for transfers between devices: 29.1 us -> 0.01 us  [shards(): ring_mine = lax.all_gather(ring_own, ('yh', 'yl'), axis=0, tiled=False)]
    all_gather x1, waiting for transfers between devices: 26.9 us -> 0.01 us  [shards(): tiles_mine = lax.all_gather(tiles, ('yh', 'yl'), axis=0, tiled=True)]
    unnamed x77 -> x29, local copies, waits for them, and re-layouts: 28 us -> 5.74 us
    all_to_all x2 -> x1, blocking collectives: 33.4 us -> 12.9 us  [exchange(): return lax.all_to_all(x, axes, split_axis=0, concat_axis=0, tiled=True)]
    all_to_all x3, waiting for transfers between devices: 19.8 us -> 32.8 us  [exchange(): return lax.all_to_all(x, axes, split_axis=0, concat_axis=0, tiled=True)]
    all_to_all x3, starting transfers between devices: 14.3 us -> 23.2 us  [exchange(): return lax.all_to_all(x, axes, split_axis=0, concat_axis=0, tiled=True)]
    pallas_call x1 -> x3, Pallas kernels: 4.51 us -> 11.2 us  [the longest x1 7.77 us: shards(): call(terms_body, [((512, 896), B16)], scratch=[pltpu.VMEM((8, 192, TOK),...]
    ppermute x6, waiting for transfers between devices: 28.5 us -> 25 us  [passed_along(): return lax.ppermute(x, BLK, [(i, (i + by) % peers) for i in range(peers)])]
  transfers between devices with their start and end apart: 14 -> 14, of which waited for: 11 -> 10; matrix products, arithmetic and copies ran while one was open for 1% -> 2% of each run, Pallas kernels for 3% -> 12%
where the time goes in v3:
time: 173 us
  waiting for transfers between devices  59.8 us (35%)
  starting transfers between devices  44 us (25%)
  Pallas kernels  32 us (18%)
  between operations  14.1 us (8%)
  blocking collectives  12.9 us (7%)
  local copies, waits for them, and re-layouts  9.8 us (6%)
    all_to_all x3, waiting for transfers between devices, exchange(): return lax.all_to_all(x, axes, split_axis=0, concat_axis=0, tiled=True)  32.8 us
    ppermute x6, waiting for transfers between devices, passed_along(): return lax.ppermute(x, BLK, [(i, (i + by) % peers) for i in range(peers)])  25 us
    all_to_all x3, starting transfers between devices, exchange(): return lax.all_to_all(x, axes, split_axis=0, concat_axis=0, tiled=True)  23.2 us
    ppermute x6, starting transfers between devices, passed_along(): return lax.ppermute(x, BLK, [(i, (i + by) % peers) for i in range(peers)])  14 us
    all_to_all x1, blocking collectives, exchange(): return lax.all_to_all(x, axes, split_axis=0, concat_axis=0, tiled=True)  12.9 us
    pallas_call x1, Pallas kernels, shards(): call(terms_body, [((512, 896), B16)], scratch=[pltpu.VMEM((8, 192, TOK),...  7.77 us
    pallas_call x1, Pallas kernels, shards(): call(attend_body, [((8, 192, TOK), B16), ((D, TOK), B16), ((KV, TOK), F32...  6.56 us
    unnamed x29, local copies, waits for them, and re-layouts  5.74 us
  transfers between devices with their start and end apart: 14, of which 10 were waited for; matrix products, arithmetic and copies ran while one was open for 2% of the time, Pallas kernels for 12%

profile of v3, /device:TPU:1, one launch (start us, length us, event | category | flops | bytes accessed | tf_op | source)
XLA Modules:
  0.0 172.7 jit_solution(7960617344421918405)
XLA Ops:
  7.2 0.0 all-gather.5.cloned.1.call-start
  7.2 0.7 all-gather.5.cloned.1.call-update
  7.9 0.0 all-gather.7.cloned.1.call-start
  7.9 0.8 slice_bitcast_fusion
  8.7 5.1 %collective-permute-start = (bf16[16,1024]{1,0:T(8,128)(2,1)S(1)}, bf16[16,1024]{1,0:T(8,128)(2,1)S(1)}, u32[]{:S(2)}, u32[]{:S(2)}) collective-permute-start(bf16[16,1024]{1,0:T(8,128)(2,1)S(1)} %slice_bitcast_fusion), channel_id=1, source_target_pairs={{1,0},{2,1},{3,2},{5,4},{6,5},{7,6},{9,8},{10,9},{11,10},{13,12},{... | collective-permute-start | bytes 98312 | tf_op jit(solution)/shard_map/ppermute | solution.py:268
  13.9 1.3 reshape.30.gain
  15.1 1.4 collective-permute-done.arrived
  16.5 0.6 copy-done.9
  17.1 4.4 %shard_map.147 = (bf16[128,768]{1,0:T(8,128)(2,1)}, bf16[128,768]{1,0:T(8,128)(2,1)}, f32[256,128]{1,0:T(8,128)}, bf16[512,128]{1,0:T(8,128)(2,1)}) custom-call(bf16[128,1024]{1,0:T(8,128)(2,1)} %bitcast.17, bf16[16,1024]{1,0:T(8,128)(2,1)} %copy-done.9, bf16[2,1024,768]{2,1,0:T(8,128)(2,1)} %stem_w.1, bf16[1,768]{1,0:T(2,128)(2,1)} %reshape.30.gain, ...), custom_call_target="tpu_custom_call" | custom-call | flops 1000000000 | bytes 4194304 | tf_op jit(solution)/shard_map/pallas_call | solution.py:271
  21.5 4.6 %shard_map.148 = (f32[768,128]{1,0:T(8,128)}, bf16[768,128]{1,0:T(8,128)(2,1)}, bf16[768,128]{1,0:T(8,128)(2,1)}, bf16[768,256]{1,0:T(8,128)(2,1)}) custom-call(bf16[128,768]{1,0:T(8,128)(2,1)} %get-tuple-element.25.hidden, bf16[128,768]{1,0:T(8,128)(2,1)} %bitcast.20, bf16[768,1280]{1,0:T(8,128)(2,1)} %w_qkv.5, bf16[768,768]{1,0:T(8,128)(2,1)} %w_out.1, ...), custom_call_target="tpu_custom_call" | custom-call | flops 1000000000 | bytes 4194304 | tf_op jit(solution)/shard_map/pallas_call | solution.py:277
  26.2 0.0 all-gather.7.cloned.1.call-update
  26.2 4.4 %collective-permute-start.3 = (bf16[512,128]{1,0:T(8,128)(2,1)S(1)}, bf16[512,128]{1,0:T(8,128)(2,1)S(1)}, u32[]{:S(2)}, u32[]{:S(2)}) collective-permute-start(bf16[512,128]{1,0:T(8,128)(2,1)S(1)} %copy-done.10), channel_id=1, source_target_pairs={{0,12},{4,16},{8,20},{12,24},{16,28},{20,32},{24,36},{28,40},{32,4... | collective-permute-start | bytes 393224 | tf_op jit(solution)/shard_map/ppermute | solution.py:33
  30.6 3.4 %collective-permute-start.2 = (bf16[512,128]{1,0:T(8,128)(2,1)S(1)}, bf16[512,128]{1,0:T(8,128)(2,1)S(1)}, u32[]{:S(2)}, u32[]{:S(2)}) collective-permute-start(bf16[512,128]{1,0:T(8,128)(2,1)S(1)} %copy-done.10), channel_id=1, source_target_pairs={{0,8},{4,12},{8,16},{12,20},{16,24},{20,28},{24,32},{28,36},{32,40... | collective-permute-start | bytes 393224 | tf_op jit(solution)/shard_map/ppermute | solution.py:33
  34.0 0.8 collective-permute-start.1
  34.8 9.9 %collective-permute-done.3.kv3 = bf16[512,128]{1,0:T(8,128)(2,1)S(1)} collective-permute-done((bf16[512,128]{1,0:T(8,128)(2,1)S(1)}, bf16[512,128]{1,0:T(8,128)(2,1)S(1)}, u32[]{:S(2)}, u32[]{:S(2)}) %collective-permute-start.3) | collective-permute-done | bytes 131104 | tf_op jit(solution)/shard_map/ppermute | solution.py:33
  44.6 3.5 %collective-permute-done.2.kv2 = bf16[512,128]{1,0:T(8,128)(2,1)S(1)} collective-permute-done((bf16[512,128]{1,0:T(8,128)(2,1)S(1)}, bf16[512,128]{1,0:T(8,128)(2,1)S(1)}, u32[]{:S(2)}, u32[]{:S(2)}) %collective-permute-start.2) | collective-permute-done | bytes 131104 | tf_op jit(solution)/shard_map/ppermute | solution.py:33
  48.1 1.8 %collective-permute-done.1.kv1 = bf16[512,128]{1,0:T(8,128)(2,1)S(1)} collective-permute-done((bf16[512,128]{1,0:T(8,128)(2,1)S(1)}, bf16[512,128]{1,0:T(8,128)(2,1)S(1)}, u32[]{:S(2)}, u32[]{:S(2)}) %collective-permute-start.1) | collective-permute-done | bytes 131104 | tf_op jit(solution)/shard_map/ppermute | solution.py:33
  49.9 0.6 copy-done.13
  50.6 6.6 %shard_map.149 = (bf16[8,192,128]{2,1,0:T(8,128)(2,1)}, bf16[768,128]{1,0:T(8,128)(2,1)}, f32[512,128]{1,0:T(8,128)}, bf16[512,128]{1,0:T(8,128)(2,1)}, bf16[512...) custom-call(s32[1]{0:T(128)} %bitcast.1.own_block, f32[12]{0:T(128)} %scales.1, f32[768,128]{1,0:T(8,128)} %get-tuple-element.26.query, ...), custom_call_target="tpu_custom_call" | custom-call | flops 1000000000 | bytes 4194304 | tf_op jit(solution)/shard_map/pallas_call | solution.py:284
  57.1 0.7 collective-permute-start.4
  57.8 3.3 %collective-permute-start.5 = (bf16[512,128]{1,0:T(8,128)(2,1)}, bf16[512,128]{1,0:T(8,128)(2,1)S(1)}, u32[]{:S(2)}, u32[]{:S(2)}) collective-permute-start(bf16[512,128]{1,0:T(8,128)(2,1)} %get-tuple-element.33), channel_id=1, source_target_pairs={{0,248},{4,252},{8,0},{12,4},{16,8},{20,12},{24,16},{28,20},{32,24... | collective-permute-start | bytes 393224 | tf_op jit(solution)/shard_map/ppermute | solution.py:33
  61.2 1.4 collective-permute-start.6
  62.5 0.2 collective-permute-done.4.back1
  62.8 2.4 %collective-permute-done.5.back2 = bf16[512,128]{1,0:T(8,128)(2,1)S(1)} collective-permute-done((bf16[512,128]{1,0:T(8,128)(2,1)}, bf16[512,128]{1,0:T(8,128)(2,1)S(1)}, u32[]{:S(2)}, u32[]{:S(2)}) %collective-permute-start.5) | collective-permute-done | bytes 131104 | tf_op jit(solution)/shard_map/ppermute | solution.py:33
  65.1 7.2 %collective-permute-done.6.back3 = bf16[512,128]{1,0:T(8,128)(2,1)S(1)} collective-permute-done((bf16[512,128]{1,0:T(8,128)(2,1)}, bf16[512,128]{1,0:T(8,128)(2,1)S(1)}, u32[]{:S(2)}, u32[]{:S(2)}) %collective-permute-start.6) | collective-permute-done | bytes 131104 | tf_op jit(solution)/shard_map/ppermute | solution.py:33
  72.4 0.7 copy-done.7
  73.0 5.1 %shard_map.150 = bf16[8,176,128]{2,1,0:T(8,128)(2,1)} custom-call(f32[512,128]{1,0:T(8,128)} %get-tuple-element.31.own, bf16[512,128]{1,0:T(8,128)(2,1)} %copy-done.5, bf16[512,128]{1,0:T(8,128)(2,1)} %copy-done.6, bf16[512,128]{1,0:T(8,128)(2,1)} %copy-done.7, f32[256,128]{1,0:T(8,128)} %get-tuple-element.35.key, bf16[768,128]{1,0:T(8,128)(2,1)} %get-tuple-element.36.dq, ...), custom_call_target="tpu_custom_call" | custom-call | flops 1000000000 | bytes 4194304 | tf_op jit(solution)/shard_map/pallas_call | solution.py:293
  78.2 1.5 collective-permute-start.8
  79.7 0.1 collective-permute-start.7
  79.8 12.9 %all_to_all.20.early = bf16[8,192,128]{2,1,0:T(8,128)(2,1)} all-to-all(bf16[8,192,128]{2,1,0:T(8,128)(2,1)S(1)} %copy-done.4), channel_id=1, replica_groups=mesh['yl'=2,'x'=4,'z'=8,'yh'=2,'c'=2] {'yl','yh','c'}, dimensions={0} | all-to-all | bytes 786432 | tf_op jit(solution)/shard_map/all_to_all | solution.py:37
  92.7 4.2 %all-to-all-start.1 = ((bf16[8,176,128]{2,1,0:T(8,128)(2,1)}), bf16[8,176,128]{2,1,0:T(8,128)(2,1)S(1)}, u32[]{:S(2)}, u32[]{:S(2)}) async-start(bf16[8,176,128]{2,1,0:T(8,128)(2,1)} %shard_map.150), calls=%async_computation.1 | async-start | bytes 720896 | tf_op jit(solution)/shard_map/all_to_all | solution.py:37
  96.9 7.4 %all-to-all-done.1.late = bf16[8,176,128]{2,1,0:T(8,128)(2,1)S(1)} async-done(((bf16[8,176,128]{2,1,0:T(8,128)(2,1)}), bf16[8,176,128]{2,1,0:T(8,128)(2,1)S(1)}, u32[]{:S(2)}, u32[]{:S(2)}) %all-to-all-start.1) | async-done | bytes 360480 | tf_op jit(solution)/shard_map/all_to_all | solution.py:37
  104.3 0.0 collective-permute-done.7.tiles1
  104.4 0.7 copy-done.1
  105.1 0.4 copy-done.2
  105.5 0.5 copy-done
  106.0 7.8 %shard_map.151 = bf16[512,896]{1,0:T(8,128)(2,1)} custom-call(s32[1]{0:T(128)} %bitcast.core, bf16[8,192,128]{2,1,0:T(8,128)(2,1)} %all_to_all.20.early, bf16[8,176,128]{2,1,0:T(8,128)(2,1)} %copy-done.1, bf16[512,1024]{1,0:T(8,128)(2,1)} %bitcast.19, bf16[512,1024]{1,0:T(8,128)(2,1)} %copy-done.2, bf16[4,768,256]{2,1,0:T(8,128)(2,1)} %bitcast.16, ...), custom_call_target="tpu_custom_call" | custom-call | flops 1000000000 | bytes 4194304 | tf_op jit(solution)/shard_map/pallas_call | solution.py:304
  113.7 10.6 %all-to-all-start.2 = ((bf16[32,16,896]{2,1,0:T(8,128)(2,1)}), bf16[32,16,896]{2,1,0:T(8,128)(2,1)S(1)}, u32[]{:S(2)}, u32[]{:S(2)}) async-start(bf16[32,16,896]{2,1,0:T(8,128)(2,1)} %bitcast.14), calls=%async_computation.2 | async-start | bytes 1835008 | tf_op jit(solution)/shard_map/all_to_all | solution.py:37
  124.3 21.9 %all-to-all-done.2.terms = bf16[32,16,896]{2,1,0:T(8,128)(2,1)S(1)} async-done(((bf16[32,16,896]{2,1,0:T(8,128)(2,1)}), bf16[32,16,896]{2,1,0:T(8,128)(2,1)S(1)}, u32[]{:S(2)}, u32[]{:S(2)}) %all-to-all-start.2) | async-done | bytes 917536 | tf_op jit(solution)/shard_map/all_to_all | solution.py:37
  146.2 0.9 copy-done.3
  147.2 1.9 %shard_map.152 = (f32[6,1024]{1,0:T(8,128)}, f32[1,768]{1,0:T(1,128)}, f32[8,8,256]{2,1,0:T(8,128)}) custom-call(bf16[32,16,896]{2,1,0:T(8,128)(2,1)} %copy-done.3), custom_call_target="tpu_custom_call" | custom-call | flops 1000000000 | bytes 4194304 | tf_op jit(solution)/shard_map/pallas_call | solution.py:315
  149.1 0.8 reshape.33
  149.9 0.6 copy.17
  150.5 8.5 %all-to-all-start.3 = ((f32[8,8,256]{2,1,0:T(8,128)}), f32[8,8,256]{2,1,0:T(8,128)S(1)}, u32[]{:S(2)}, u32[]{:S(2)}) async-start(f32[8,8,256]{2,1,0:T(8,128)} %get-tuple-element.43), calls=%async_computation.3 | async-start | bytes 131072 | tf_op jit(solution)/shard_map/all_to_all | solution.py:37
  159.0 1.3 dynamic-slice_bitcast_fusion
  160.2 3.4 %all-to-all-done.3.rows = f32[8,8,256]{2,1,0:T(8,128)S(1)} async-done(((f32[8,8,256]{2,1,0:T(8,128)}), f32[8,8,256]{2,1,0:T(8,128)S(1)}, u32[]{:S(2)}, u32[]{:S(2)}) %all-to-all-start.3) | async-done | bytes 65568 | tf_op jit(solution)/shard_map/all_to_all | solution.py:37
  163.7 0.6 copy-done.8
  164.3 1.5 shard_map.153
  (23 shorter events, 0.0 us)
Async XLA Ops:
  7.2 71.0 %all-gather.5.cloned.1.call-start = ((), (), s32[]{:S(2)}) async-start(), calls=%async_computation.4 | async-start | bytes 1310720 | tf_op jit(solution)/shard_map/all_gather | solution.py:269
  7.9 70.3 %all-gather.7.cloned.1.call-start = ((), (), s32[]{:S(2)}) async-start(), calls=%async_computation.5 | async-start | bytes 1966080 | tf_op jit(solution)/shard_map/all_gather | solution.py:282
  8.7 7.8 %collective-permute-start = (bf16[16,1024]{1,0:T(8,128)(2,1)S(1)}, bf16[16,1024]{1,0:T(8,128)(2,1)S(1)}, u32[]{:S(2)}, u32[]{:S(2)}) collective-permute-start(bf16[16,1024]{1,0:T(8,128)(2,1)S(1)} %slice_bitcast_fusion), channel_id=1, source_target_pairs={{1,0},{2,1},{3,2},{5,4},{6,5},{7,6},{9,8},{10,9},{11,10},{13,12},{... | collective-permute-start | bytes 98312 | tf_op jit(solution)/shard_map/ppermute | solution.py:268
  16.5 0.6 copy-start.9
  21.5 4.6 %copy-start.10 = (bf16[512,128]{1,0:T(8,128)(2,1)S(1)}, bf16[512,128]{1,0:T(8,128)(2,1)}, u32[]{:S(2)}) copy-start(bf16[512,128]{1,0:T(8,128)(2,1)} %get-tuple-element.29.kv0) | copy-start | bytes 393220
  26.2 18.4 %collective-permute-start.3 = (bf16[512,128]{1,0:T(8,128)(2,1)S(1)}, bf16[512,128]{1,0:T(8,128)(2,1)S(1)}, u32[]{:S(2)}, u32[]{:S(2)}) collective-permute-start(bf16[512,128]{1,0:T(8,128)(2,1)S(1)} %copy-done.10), channel_id=1, source_target_pairs={{0,12},{4,16},{8,20},{12,24},{16,28},{20,32},{24,36},{28,40},{32,4... | collective-permute-start | bytes 393224 | tf_op jit(solution)/shard_map/ppermute | solution.py:33
  30.6 17.5 %collective-permute-start.2 = (bf16[512,128]{1,0:T(8,128)(2,1)S(1)}, bf16[512,128]{1,0:T(8,128)(2,1)S(1)}, u32[]{:S(2)}, u32[]{:S(2)}) collective-permute-start(bf16[512,128]{1,0:T(8,128)(2,1)S(1)} %copy-done.10), channel_id=1, source_target_pairs={{0,8},{4,12},{8,16},{12,20},{16,24},{20,28},{24,32},{28,36},{32,40... | collective-permute-start | bytes 393224 | tf_op jit(solution)/shard_map/ppermute | solution.py:33
  34.0 15.9 %collective-permute-start.1 = (bf16[512,128]{1,0:T(8,128)(2,1)S(1)}, bf16[512,128]{1,0:T(8,128)(2,1)S(1)}, u32[]{:S(2)}, u32[]{:S(2)}) collective-permute-start(bf16[512,128]{1,0:T(8,128)(2,1)S(1)} %copy-done.10), channel_id=1, source_target_pairs={{0,4},{4,8},{8,12},{12,16},{16,20},{20,24},{24,28},{28,32},{32,36}... | collective-permute-start | bytes 393224 | tf_op jit(solution)/shard_map/ppermute | solution.py:33
  44.6 5.3 %copy-start.11 = (bf16[512,128]{1,0:T(8,128)(2,1)}, bf16[512,128]{1,0:T(8,128)(2,1)S(1)}, u32[]{:S(2)}) copy-start(bf16[512,128]{1,0:T(8,128)(2,1)S(1)} %collective-permute-done.3.kv3) | copy-start | bytes 393220
  48.1 1.8 %copy-start.12 = (bf16[512,128]{1,0:T(8,128)(2,1)}, bf16[512,128]{1,0:T(8,128)(2,1)S(1)}, u32[]{:S(2)}) copy-start(bf16[512,128]{1,0:T(8,128)(2,1)S(1)} %collective-permute-done.2.kv2) | copy-start | bytes 393220
  49.9 0.7 copy-start.13
  57.1 5.6 %collective-permute-start.4 = (bf16[512,128]{1,0:T(8,128)(2,1)}, bf16[512,128]{1,0:T(8,128)(2,1)S(1)}, u32[]{:S(2)}, u32[]{:S(2)}) collective-permute-start(bf16[512,128]{1,0:T(8,128)(2,1)} %get-tuple-element.32), channel_id=1, source_target_pairs={{0,252},{4,0},{8,4},{12,8},{16,12},{20,16},{24,20},{28,24},{32,28}... | collective-permute-start | bytes 393224 | tf_op jit(solution)/shard_map/ppermute | solution.py:33
  57.8 7.3 %collective-permute-start.5 = (bf16[512,128]{1,0:T(8,128)(2,1)}, bf16[512,128]{1,0:T(8,128)(2,1)S(1)}, u32[]{:S(2)}, u32[]{:S(2)}) collective-permute-start(bf16[512,128]{1,0:T(8,128)(2,1)} %get-tuple-element.33), channel_id=1, source_target_pairs={{0,248},{4,252},{8,0},{12,4},{16,8},{20,12},{24,16},{28,20},{32,24... | collective-permute-start | bytes 393224 | tf_op jit(solution)/shard_map/ppermute | solution.py:33
  61.2 11.2 %collective-permute-start.6 = (bf16[512,128]{1,0:T(8,128)(2,1)}, bf16[512,128]{1,0:T(8,128)(2,1)S(1)}, u32[]{:S(2)}, u32[]{:S(2)}) collective-permute-start(bf16[512,128]{1,0:T(8,128)(2,1)} %get-tuple-element.34), channel_id=1, source_target_pairs={{0,244},{4,248},{8,252},{12,0},{16,4},{20,8},{24,12},{28,16},{32,2... | collective-permute-start | bytes 393224 | tf_op jit(solution)/shard_map/ppermute | solution.py:33
  62.8 9.6 %copy-start.5 = (bf16[512,128]{1,0:T(8,128)(2,1)}, bf16[512,128]{1,0:T(8,128)(2,1)S(1)}, u32[]{:S(2)}) copy-start(bf16[512,128]{1,0:T(8,128)(2,1)S(1)} %collective-permute-done.4.back1) | copy-start | bytes 393220
  65.1 7.2 %copy-start.6 = (bf16[512,128]{1,0:T(8,128)(2,1)}, bf16[512,128]{1,0:T(8,128)(2,1)S(1)}, u32[]{:S(2)}) copy-start(bf16[512,128]{1,0:T(8,128)(2,1)S(1)} %collective-permute-done.5.back2) | copy-start | bytes 393220
  72.4 0.7 copy-start.7
  73.0 6.7 %copy-start.4 = (bf16[8,192,128]{2,1,0:T(8,128)(2,1)S(1)}, bf16[8,192,128]{2,1,0:T(8,128)(2,1)}, u32[]{:S(2)}) copy-start(bf16[8,192,128]{2,1,0:T(8,128)(2,1)} %get-tuple-element.30) | copy-start | bytes 1179652
  78.2 26.2 %collective-permute-start.8 = (bf16[4,768,256]{2,1,0:T(8,128)(2,1)}, bf16[4,768,256]{2,1,0:T(8,128)(2,1)S(1)}, u32[]{:S(2)}, u32[]{:S(2)}) collective-permute-start(bf16[4,768,256]{2,1,0:T(8,128)(2,1)} %bitcast.15), channel_id=1, source_target_pairs={{0,1},{1,0},{2,3},{3,2},{4,5},{5,4},{6,7},{7,6},{8,9},{9,8},{10,11... | collective-permute-start | bytes 4718600 | tf_op jit(solution)/shard_map/ppermute | solution.py:302
  79.7 24.7 %collective-permute-start.7 = (bf16[512,1024]{1,0:T(8,128)(2,1)}, bf16[512,1024]{1,0:T(8,128)(2,1)S(1)}, u32[]{:S(2)}, u32[]{:S(2)}) collective-permute-start(bf16[512,1024]{1,0:T(8,128)(2,1)} %bitcast.18), channel_id=1, source_target_pairs={{0,1},{1,0},{2,3},{3,2},{4,5},{5,4},{6,7},{7,6},{8,9},{9,8},{10,11... | collective-permute-start | bytes 3145736 | tf_op jit(solution)/shard_map/ppermute | solution.py:301
  92.7 11.6 %all-to-all-start.1 = ((bf16[8,176,128]{2,1,0:T(8,128)(2,1)}), bf16[8,176,128]{2,1,0:T(8,128)(2,1)S(1)}, u32[]{:S(2)}, u32[]{:S(2)}) async-start(bf16[8,176,128]{2,1,0:T(8,128)(2,1)} %shard_map.150), calls=%async_computation.1 | async-start | bytes 720896 | tf_op jit(solution)/shard_map/all_to_all | solution.py:37
  104.3 0.7 copy-start.1
  104.3 1.1 copy-start.2
  104.3 1.6 copy-start
  113.7 32.5 %all-to-all-start.2 = ((bf16[32,16,896]{2,1,0:T(8,128)(2,1)}), bf16[32,16,896]{2,1,0:T(8,128)(2,1)S(1)}, u32[]{:S(2)}, u32[]{:S(2)}) async-start(bf16[32,16,896]{2,1,0:T(8,128)(2,1)} %bitcast.14), calls=%async_computation.2 | async-start | bytes 1835008 | tf_op jit(solution)/shard_map/all_to_all | solution.py:37
  146.2 0.9 copy-start.3
  150.5 13.2 %all-to-all-start.3 = ((f32[8,8,256]{2,1,0:T(8,128)}), f32[8,8,256]{2,1,0:T(8,128)S(1)}, u32[]{:S(2)}, u32[]{:S(2)}) async-start(f32[8,8,256]{2,1,0:T(8,128)} %get-tuple-element.43), calls=%async_computation.3 | async-start | bytes 131072 | tf_op jit(solution)/shard_map/all_to_all | solution.py:37
  163.7 0.6 copy-start.8
Sparse Core Ops, SparseCore 0:
  9.8 30.5 all-gather.4
  42.2 29.1 all-gather.6

commit v4 on v3

--- a/solution.py
+++ b/solution.py
@@ -56,65 +56,138 @@
     return [jnp.asarray(table, B16) for table in tables]
 
 
-def call(body, outs, scratch=(), smem=(), count=0, limit=60, flops=10**9):
-    specs = [
-        pl.BlockSpec(memory_space=pltpu.SMEM if i in smem else pltpu.VMEM) for i in range(count)
-    ]
-    shapes = [jax.ShapeDtypeStruct(shape, kind) for shape, kind in outs]
-    return pl.pallas_call(
-        body,
-        out_shape=shapes,
-        in_specs=specs,
-        out_specs=[pl.BlockSpec(memory_space=pltpu.VMEM)] * len(shapes),
-        scratch_shapes=list(scratch),
-        compiler_params=pltpu.CompilerParams(vmem_limit_bytes=limit * 2**20),
-        cost_estimate=pl.CostEstimate(flops=flops, bytes_accessed=4 * 2**20, transcendentals=0),
-    )
-
-
-def stem_body(tiles, arrived, stem_w, gain, w_qkv, tokens_o, hidden_o, key_o, kv_o):
+class Loaded:
+    def __init__(self, ref, pieces):
+        self.ref, self.pieces = ref, pieces
+
+    def piece(self, i):
+        copy, place = self.pieces[i]
+        if copy is not None:
+            copy.wait()
+            self.pieces[i] = (None, place)
+        return self.ref.at[place]
+
+    def __getitem__(self, index):
+        for i in range(len(self.pieces)):
+            self.piece(i)
+        return self.ref[index]
+
+
+def split(shape, count):
+    rows = shape[0] // count
+    return [slice(i * rows, i * rows + rows) for i in range(count)]
+
+
+def call(body, outs, scratch=(), smem=(), pieces=None, columns=None, flops=10**9):
+    pieces, columns = pieces or {}, columns or {}
+
+    def run(*operands):
+        held, parts, total = [], [], 0
+        for i, operand in enumerate(operands):
+            if i in smem:
+                continue
+            shape = operand.shape
+            if i in columns:
+                shape = (shape[0], columns[i][1] - columns[i][0])
+            held.append(pltpu.VMEM(shape, operand.dtype))
+            parts.append((i, split(shape, pieces.get(i, 1))))
+            total += pieces.get(i, 1)
+
+        def kernel(*refs):
+            inputs = list(refs[: len(operands)])
+            others = refs[len(operands) : len(refs) - len(held) - 1]
+            stores, sems = refs[len(refs) - len(held) - 1 : -1], refs[-1]
+            used = 0
+            for (i, places), store in zip(parts, stores):
+                source = inputs[i]
+                if i in columns:
+                    source = source.at[:, columns[i][0] : columns[i][1]]
+                made = []
+                for place in places:
+                    copy = pltpu.make_async_copy(
+                        source.at[place], store.at[place], sems.at[used]
+                    )
+                    copy.start()
+                    made.append((copy, place))
+                    used += 1
+                inputs[i] = Loaded(store, made)
+            body(*inputs, *others)
+            for value in inputs:
+                if isinstance(value, Loaded):
+                    for j in range(len(value.pieces)):
+                        value.piece(j)
+
+        shapes = [jax.ShapeDtypeStruct(shape, kind) for shape, kind in outs]
+        return pl.pallas_call(
+            kernel,
+            out_shape=shapes,
+            in_specs=[
+                pl.BlockSpec(memory_space=pltpu.SMEM if i in smem else pl.ANY)
+                for i in range(len(operands))
+            ],
+            out_specs=[pl.BlockSpec(memory_space=pltpu.VMEM)] * len(shapes),
+            scratch_shapes=[*scratch, *held, pltpu.SemaphoreType.DMA((total,))],
+            compiler_params=pltpu.CompilerParams(vmem_limit_bytes=64 * 2**20),
+            cost_estimate=pl.CostEstimate(
+                flops=flops, bytes_accessed=4 * 2**20, transcendentals=0
+            ),
+        )(*operands)
+
+    return run
+
+
+def stem_body(
+    tiles, stem_w, arrived, w_kv, gain, d_out, by_rest, tokens_o, hidden_o, key_o, kv_o, ring_o
+):
     own = tiles[...]
-    below = jnp.concatenate([tiles[TC:, :], arrived[...]], axis=0)
-    stem = dot(own, stem_w[0]) + dot(below, stem_w[1])
+    deep = own.shape[1] // 4
+    below = jnp.concatenate([own[TC:], arrived[...]], axis=0)
+    stem = jnp.zeros((TOK, D), F32)
+    for j, rows in enumerate((own, below)):
+        for i in range(4):
+            columns = rows[:, i * deep : i * deep + deep]
+            stem = stem + dot(columns, stem_w.piece(4 * j + i)[...])
     low = stem.astype(B16)
     tokens_o[...] = low
     tok = low.astype(F32)
     factor = lax.rsqrt(jnp.mean(tok * tok, axis=1, keepdims=True) + 1e-05)
     hidden = (tok * factor * gain[...].astype(F32)).astype(B16)
     hidden_o[...] = hidden
-    kv = dot(hidden, w_qkv[:, D:]).T
+    kv = dot(hidden, w_kv[...]).T
     key_o[...] = kv[:256]
     for h in range(KEY_VALUE_HEADS):
         k = kv[h * 64 : h * 64 + 64]
         scale = lax.rsqrt(jnp.mean(k * k, axis=0, keepdims=True) + 1e-06)
         kv_o[h * 64 : h * 64 + 64, :] = (k * scale).astype(B16)
     kv_o[256:, :] = kv[256:].astype(B16)
-
-
-def query_body(hidden, d_out, w_qkv, w_out, by_rest, query_o, query_n_o, do_o, ring_o):
+    ring_o[:, :TOK] = dot(by_rest[...], hidden, NT).astype(B16)
+    ring_o[:, TOK:] = dot(by_rest[...], d_out[...], NT).astype(B16)
+
+
+def query_body(hidden, d_out, w_q, w_out, query_o, query_n_o, do_o):
     h = hidden[...]
-    q = dot(h, w_qkv[:, :D]).T
+    g = d_out[...]
+    q = dot(h, w_q[...]).T
     query_o[...] = q
     for i in range(QUERY_HEADS):
         part = q[i * 64 : i * 64 + 64]
         scale = lax.rsqrt(jnp.mean(part * part, axis=0, keepdims=True) + 1e-06)
         query_n_o[i * 64 : i * 64 + 64, :] = (part * scale).astype(B16)
-    g = d_out[...]
     do_o[...] = dot(w_out[...], g, NT).astype(B16)
-    ring_o[:, :TOK] = dot(by_rest[...], h, NT).astype(B16)
-    ring_o[:, TOK:] = dot(by_rest[...], g, NT).astype(B16)
 
 
 def attend_body(
-    own_block, scales, query, query_n, do, kv0, kv1, kv2, kv3, positions,
-    early_o, dq_o, own_o, back1_o, back2_o, back3_o, attn_s,
+    own_block, scales, positions, kv0, kv1, kv2, kv3, query_n, do, query,
+    attn_o, dq_o, own_o, back1_o, back2_o, back3_o,
 ):
     own = own_block[0]
     blocks = (kv0, kv1, kv2, kv3)
-    q_pos = positions[pl.ds(own, 1), :]
+    positions[:8]
+    rows = positions.ref
+    q_pos = rows[pl.ds(own, 1), :]
     columns = []
     for j in range(4):
-        row = positions[pl.ds(lax.rem(own - j + 64, 64), 1), :].astype(F32)
+        row = rows[pl.ds(lax.rem(own - j + 64, 64), 1), :].astype(F32)
         columns.append(jnp.broadcast_to(row, (TOK, TOK)).T)
     key_pos = jnp.concatenate(columns, axis=0)
     bias = jnp.where(key_pos <= q_pos.astype(F32), 0.0, -1e30)
@@ -142,7 +215,7 @@
         for i, h in enumerate(heads):
             rows = slice(h * 64, h * 64 + 64)
             lanes = slice(i * TOK, i * TOK + TOK)
-            attn_s[rows, :] = attn[:, lanes].astype(B16)
+            attn_o[rows, :] = attn[:, lanes].astype(B16)
             x = query[rows, :]
             dx = dq[:, lanes]
             r = lax.rsqrt(jnp.mean(x * x, axis=0, keepdims=True) + 1e-06)
@@ -154,13 +227,15 @@
             lanes = slice((j + 1) * TOK, (j + 2) * TOK)
             back[g * 64 : g * 64 + 64, :] = dk[:, lanes].astype(B16)
             back[256 + g * 64 : 320 + g * 64, :] = dv[:, lanes].astype(B16)
-    for m in range(8):
-        early_o[m, :96, :] = attn_s[m * 96 : m * 96 + 96, :]
-        early_o[m, 96:, :] = dq_o[m * 96 : m * 96 + 96, :]
+
+
+def part_body(w_q, dq, part_o):
+    part_o[...] = dot(w_q[...], dq[...]).T
 
 
 def tokens_body(
-    own, back1, back2, back3, key, dq, w_qkv, tokens, gain, d_out, by_member, late_o, dkv_s
+    own, back1, back2, back3, key, w_kv, tokens, gain, part, d_out, by_member, attn, dq,
+    late_o, dkv_s,
 ):
     total = own[...] + back1[...].astype(F32) + back2[...].astype(F32) + back3[...].astype(F32)
     for h in range(KEY_VALUE_HEADS):
@@ -171,7 +246,7 @@
         inner = jnp.mean(x * dx, axis=0, keepdims=True)
         dkv_s[rows, :] = (r * dx - x * (r * r * r * inner)).astype(B16)
     dkv_s[256:, :] = total[256:].astype(B16)
-    d_hidden = (dot(w_qkv[:, :D], dq[...]) + dot(w_qkv[:, D:], dkv_s[...])).T
+    d_hidden = part[...] + dot(w_kv[...], dkv_s[...]).T
     tok = tokens[...].astype(F32)
     r = lax.rsqrt(jnp.mean(tok * tok, axis=1, keepdims=True) + 1e-05)
     gain_term = jnp.sum(d_hidden * (tok * r), axis=0, keepdims=True)
@@ -187,11 +262,13 @@
         late_o[m, :96, :] = spread[m * 96 : m * 96 + 96]
         late_o[m, 96:128, :] = dkv_s[m * 32 : m * 32 + 32, :]
         late_o[m, 128:160, :] = dkv_s[256 + m * 32 : 288 + m * 32, :]
-        late_o[m, 160:, :] = gains
+        late_o[m, 160:176, :] = gains
+        late_o[m, 176:272, :] = attn[m * 96 : m * 96 + 96, :]
+        late_o[m, 272:, :] = dq[m * 96 : m * 96 + 96, :]
 
 
 def terms_body(
-    core, early, late, tiles0, tiles1, ring0, ring1, place, fold, terms_o, pair_s, rhs_s, both_s
+    core, late, place, ring0, ring1, tiles0, tiles1, fold, terms_o, pair_s, rhs_s, both_s
 ):
     lane = lax.broadcasted_iota(jnp.int32, (96, TOK), 1)
     gain = jnp.zeros((16, TOK), F32)
@@ -201,16 +278,16 @@
         for band in range(4):
             m = yl * 4 + band
             block = late[m, :96, :]
-            gain = gain + late[m, 160:, :].astype(F32)
+            gain = gain + late[m, 160:176, :].astype(F32)
             moved = pltpu.roll(block.astype(F32), TC, 1)
             pair_s[m, :96, :] = block
             pair_s[m, 96:, :] = jnp.where(lane < TC, before, moved).astype(B16)
             before = moved
-            rhs_s[m, :96, :TOK] = early[m, 96:, :]
+            rhs_s[m, :96, :TOK] = late[m, 272:, :]
             rhs_s[m, 96:128, :TOK] = late[m, 96:128, :]
             rhs_s[m, :128, TOK:] = zero
             rhs_s[m, 128:224, :TOK] = zero[:96]
-            rhs_s[m, 128:224, TOK:] = early[m, :96, :]
+            rhs_s[m, 128:224, TOK:] = late[m, 176:272, :]
             rhs_s[m, 224:, :TOK] = late[m, 128:160, :]
             rhs_s[m, 224:, TOK:] = zero[:32]
     rows = jnp.zeros((D, 256), F32)
@@ -221,12 +298,12 @@
             at = s * 4 + j
             for half in range(2):
                 both_s[half, :, at * TOK : at * TOK + TOK] = dot(place[half], pair_s[m]).astype(B16)
-            rows = rows + dot(ring[j], rhs_s[m], NT)
+            rows = rows + dot(ring.piece(j)[0], rhs_s[m], NT)
     low = rows.astype(B16)
     terms_o[:, 512:768] = low[:512]
     terms_o[:, 768:] = (dot(fold[0], low[512:, :TOK]) + dot(fold[1], low[512:, TOK:])).astype(B16)
-    stem = dot(both_s[0, :, :512], tiles0[:, :512]) + dot(both_s[0, :, 512:], tiles1[:, :512])
-    stem = stem + dot(both_s[1, :, :512], tiles0[:, 512:])
+    stem = dot(both_s[0, :, :512], tiles0[:, :512]) + dot(both_s[1, :, :512], tiles0[:, 512:])
+    stem = stem + dot(both_s[0, :, 512:], tiles1[:, :512])
     stem = stem + dot(both_s[1, :, 512:], tiles1[:, 512:])
     slot = lax.rem(lax.broadcasted_iota(jnp.int32, (512, 512), 0), 16)
     first = jnp.concatenate([gain[i : i + 1, :] for i in range(4)], axis=1)
@@ -237,11 +314,16 @@
 
 
 def total_body(terms, stem_o, gain_o, rows_o):
-    total = terms[0].astype(F32)
-    for r in range(1, 32):
-        total = total + terms[r].astype(F32)
-    stem_o[:, :512] = total[:6, :512]
-    stem_o[:, 512:] = total[6:12, :512]
+    total = jnp.zeros((16, 896), F32)
+    for piece in range(4):
+        block = terms.piece(piece)
+        for r in range(8):
+            total = total + block[r].astype(F32)
+    for j in range(2):
+        for k in range(3):
+            at = j * 3 + k
+            stem_o[k, j : j + 1, :512] = total[at : at + 1, :512]
+            stem_o[k, j : j + 1, 512:] = total[at + 6 : at + 7, :512]
     gain_o[:, :512] = total[12:13, :512]
     gain_o[:, 512:] = total[13:14, :256]
     last = jnp.concatenate([total[:8, 768:], total[8:, 768:]], axis=1)
@@ -268,34 +350,43 @@
     arrived = lax.ppermute(tiles[:TC], BAND, [(i, i - 1) for i in range(1, bands)])
     tiles_mine = lax.all_gather(tiles, ("yh", "yl"), axis=0, tiled=True)
     gain = norm_gain.reshape(1, D)
-    tokens, hidden, key, kv_own = call(
+    tokens, hidden, key, kv_own, ring_own = call(
         stem_body,
-        [((TOK, D), B16), ((TOK, D), B16), ((256, TOK), F32), ((KV, TOK), B16)],
-        count=5,
-    )(tiles, arrived, stem_weight, gain, w_qkv)
+        [
+            ((TOK, D), B16),
+            ((TOK, D), B16),
+            ((256, TOK), F32),
+            ((KV, TOK), B16),
+            ((D, 2 * TOK), B16),
+        ],
+        pieces={1: 8, 3: 2, 6: 2},
+        columns={3: (D, D + KV)},
+    )(tiles, stem_weight.reshape(-1, D), arrived, w_qkv, gain, grad_out, by_rest)
     moved = [passed_along(kv_own, offset) for offset in range(1, 4)]
-    query, query_n, do, ring_own = call(
+    moved[0], hidden = lax.optimization_barrier((moved[0], hidden))
+    query, query_n, do = call(
         query_body,
-        [((D, TOK), F32), ((D, TOK), B16), ((D, TOK), B16), ((D, 2 * TOK), B16)],
-        count=5,
-    )(hidden, grad_out, w_qkv, w_out, by_rest)
+        [((D, TOK), F32), ((D, TOK), B16), ((D, TOK), B16)],
+        pieces={2: 2, 3: 2},
+        columns={2: (0, D)},
+    )(hidden, grad_out, w_qkv, w_out)
     ring_mine = lax.all_gather(ring_own, ("yh", "yl"), axis=0, tiled=False)
     own_block = lax.axis_index(BLK).astype(jnp.int32).reshape(1)
-    early, d_q, own, back1, back2, back3 = call(
+    attn, d_q, own, back1, back2, back3 = call(
         attend_body,
-        [((8, 192, TOK), B16), ((D, TOK), B16), ((KV, TOK), F32)] + [((KV, TOK), B16)] * 3,
-        scratch=[pltpu.VMEM((D, TOK), B16)],
+        [((D, TOK), B16), ((D, TOK), B16), ((KV, TOK), F32)] + [((KV, TOK), B16)] * 3,
         smem=(0, 1),
-        count=10,
-    )(own_block, per_head_scale, query, query_n, do, kv_own, *moved, positions.reshape(64, TOK))
+    )(own_block, per_head_scale, positions.reshape(64, TOK), kv_own, *moved, query_n, do, query)
     returned = [passed_along(piece, -(j + 1)) for j, piece in enumerate((back1, back2, back3))]
-    early_ring = exchange(early, RING)
+    returned[0], d_q = lax.optimization_barrier((returned[0], d_q))
+    part = call(part_body, [((TOK, D), F32)], pieces={0: 2}, columns={0: (0, D)})(w_qkv, d_q)[0]
     late = call(
         tokens_body,
-        [((8, 176, TOK), B16)],
+        [((8, 368, TOK), B16)],
         scratch=[pltpu.VMEM((KV, TOK), B16)],
-        count=11,
-    )(own, *returned, key, d_q, w_qkv, tokens, gain, grad_out, by_member)[0]
+        pieces={5: 2, 10: 2},
+        columns={5: (D, D + KV)},
+    )(own, *returned, key, w_qkv, tokens, gain, part, grad_out, by_member, attn, d_q)[0]
     late_ring = exchange(late, RING)
     tiles_mine, ring_mine, late = lax.optimization_barrier((tiles_mine, ring_mine, late))
     tiles_other = lax.ppermute(tiles_mine, "c", [(0, 1), (1, 0)])
@@ -310,17 +401,17 @@
             pltpu.VMEM((2, 512, 1024), B16),
         ],
         smem=(0,),
-        count=9,
-    )(core, early_ring, late_ring, tiles_mine, tiles_other, ring_mine, ring_other, place, fold)[0]
+        pieces={1: 2, 3: 4, 4: 4, 5: 2, 6: 2},
+    )(core, late_ring, place, ring_mine, ring_other, tiles_mine, tiles_other, fold)[0]
     stem_total, gain_total, row_total = call(
-        total_body, [((6, 1024), F32), ((1, D), F32), ((8, 8, 256), F32)], count=1
+        total_body, [((3, 2, 1024), F32), ((1, D), F32), ((8, 8, 256), F32)], pieces={0: 4}
     )(exchange(terms.reshape(32, 16, 896), REST))
-    d_w_qkv, d_w_out = call(final_body, [((3, 1280), F32), ((3, D), F32)], count=1)(
+    d_w_qkv, d_w_out = call(final_body, [((3, 1280), F32), ((3, D), F32)])(
         exchange(row_total, RING)
     )
     own_column = (lax.axis_index(BLK) * 4 + lax.axis_index(BAND)) * 3
     d_norm_gain = lax.dynamic_slice_in_dim(gain_total[0], own_column, 3)
-    d_stem_weight = stem_total.reshape(2, 3, 1024).transpose(0, 2, 1)
+    d_stem_weight = stem_total.transpose(1, 2, 0)
     return (d_stem_weight, d_norm_gain, d_w_qkv, d_w_out.T)
 
 

time: 173 us -> 158 us (0.913)
  blocking collectives: 12.9 us -> 0 us
  local copies, waits for them, and re-layouts: 9.8 us -> 3.29 us
  waiting for transfers between devices: 59.8 us -> 62.6 us
  Pallas kernels: 32 us -> 34.8 us
    all_to_all x1 -> x0, blocking collectives: 12.9 us -> none  [exchange(): return lax.all_to_all(x, axes, split_axis=0, concat_axis=0, tiled=True)]
    unnamed x29 -> x0, local copies, waits for them, and re-layouts: 5.74 us -> none
    all_to_all x3, waiting for transfers between devices: 32.8 us -> 35.8 us  [exchange(): return lax.all_to_all(x, axes, split_axis=0, concat_axis=0, tiled=True)]
    pallas_call x7 -> x8, Pallas kernels: 32 us -> 34.8 us  [run(): pl.pallas_call(kernel, out_shape=shapes, in_specs=[pl.BlockSpec(memory_sp...]
    ppermute x6, starting transfers between devices: 14 us -> 12.2 us  [passed_along(): return lax.ppermute(x, BLK, [(i, (i + by) % peers) for i in range(peers)])]
  transfers between devices with their start and end apart: 14 -> 14, of which waited for: 10 -> 10; matrix products, arithmetic and copies ran while one was open for 2% -> 2% of each run, Pallas kernels for 12% -> 15%
where the time goes in v4:
time: 158 us
  waiting for transfers between devices  62.6 us (40%)
  starting transfers between devices  42.7 us (27%)
  Pallas kernels  34.8 us (22%)
  between operations  14.2 us (9%)
  local copies, waits for them, and re-layouts  3.29 us (2%)
    all_to_all x3, waiting for transfers between devices, exchange(): return lax.all_to_all(x, axes, split_axis=0, concat_axis=0, tiled=True)  35.8 us
    pallas_call x8, Pallas kernels, run(): pl.pallas_call(kernel, out_shape=shapes, in_specs=[pl.BlockSpec(memory_sp...  34.8 us
    all_to_all x3, starting transfers between devices, exchange(): return lax.all_to_all(x, axes, split_axis=0, concat_axis=0, tiled=True)  24.7 us
    ppermute x6, waiting for transfers between devices, passed_along(): return lax.ppermute(x, BLK, [(i, (i + by) % peers) for i in range(peers)])  24.6 us
    ppermute x6, starting transfers between devices, passed_along(): return lax.ppermute(x, BLK, [(i, (i + by) % peers) for i in range(peers)])  12.2 us
    ppermute x1, starting transfers between devices, shards(): lax.ppermute(tiles[:TC], BAND, [(i, i - 1) for i in range(1, bands)])  5.14 us
  transfers between devices with their start and end apart: 14, of which 10 were waited for; matrix products, arithmetic and copies ran while one was open for 2% of the time, Pallas kernels for 15%

profile of v4, /device:TPU:1, one launch (start us, length us, event | category | flops | bytes accessed | tf_op | source)
XLA Modules:
  0.0 157.6 jit_solution(8997807273914003423)
XLA Ops:
  7.2 0.0 all-gather.5.cloned.1.call-start
  7.2 0.7 all-gather.5.cloned.1.call-update
  7.9 0.0 all-gather.7.cloned.1.call-start
  7.9 0.8 slice_bitcast_fusion
  8.7 5.1 %collective-permute-start = (bf16[16,1024]{1,0:T(8,128)(2,1)S(1)}, bf16[16,1024]{1,0:T(8,128)(2,1)}, u32[]{:S(2)}, u32[]{:S(2)}) collective-permute-start(bf16[16,1024]{1,0:T(8,128)(2,1)S(1)} %slice_bitcast_fusion), channel_id=1, source_target_pairs={{1,0},{2,1},{3,2},{5,4},{6,5},{7,6},{9,8},{10,9},{11,10},{13,12},{... | collective-permute-start | bytes 98312 | tf_op jit(solution)/shard_map/ppermute | solution.py:350
  13.9 1.3 reshape.32.refs_4_.refs_7_
  15.1 1.5 collective-permute-done.refs_2_
  16.6 5.9 %shard_map.147 = (bf16[128,768]{1,0:T(8,128)(2,1)}, bf16[128,768]{1,0:T(8,128)(2,1)}, f32[256,128]{1,0:T(8,128)}, bf16[512,128]{1,0:T(8,128)(2,1)}, bf16[768,256]{1,0:T(8,128)(2,1)}) custom-call(bf16[128,1024]{1,0:T(8,128)(2,1)} %bitcast.19, bf16[2048,768]{1,0:T(8,128)(2,1)} %bitcast.16, bf16[16,1024]{1,0:T(8,128)(2,1)} %collective-permute-done.refs_2_, ...), custom_call_target="tpu_custom_call" | custom-call | flops 1000000000 | bytes 4194304 | tf_op jit(solution)/shard_map/pallas_call | solution.py:121
  22.5 0.0 all-gather.7.cloned.1.call-update
  22.5 1.7 %collective-permute-start.1 = (bf16[512,128]{1,0:T(8,128)(2,1)}, bf16[512,128]{1,0:T(8,128)(2,1)}, u32[]{:S(2)}, u32[]{:S(2)}) collective-permute-start(bf16[512,128]{1,0:T(8,128)(2,1)} %get-tuple-element.29.refs_3_), channel_id=1, source_target_pairs={{0,4},{4,8},{8,12},{12,16},{16,20},{20,24},{24,28},{28,32},{32,36}... | collective-permute-start | bytes 393224 | tf_op jit(solution)/shard_map/ppermute | solution.py:33
  24.2 5.6 %collective-permute-start.3 = (bf16[512,128]{1,0:T(8,128)(2,1)}, bf16[512,128]{1,0:T(8,128)(2,1)}, u32[]{:S(2)}, u32[]{:S(2)}) collective-permute-start(bf16[512,128]{1,0:T(8,128)(2,1)} %get-tuple-element.29.refs_3_), channel_id=1, source_target_pairs={{0,12},{4,16},{8,20},{12,24},{16,28},{20,32},{24,36},{28,40},{32,4... | collective-permute-start | bytes 393224 | tf_op jit(solution)/shard_map/ppermute | solution.py:33
  29.8 1.2 collective-permute-start.2
  31.0 6.2 %collective-permute-done.1.refs_4_ = bf16[512,128]{1,0:T(8,128)(2,1)} collective-permute-done((bf16[512,128]{1,0:T(8,128)(2,1)}, bf16[512,128]{1,0:T(8,128)(2,1)}, u32[]{:S(2)}, u32[]{:S(2)}) %collective-permute-start.1) | collective-permute-done | bytes 131104 | tf_op jit(solution)/shard_map/ppermute | solution.py:33
  37.2 3.2 %shard_map.148 = (f32[768,128]{1,0:T(8,128)}, bf16[768,128]{1,0:T(8,128)(2,1)}, bf16[768,128]{1,0:T(8,128)(2,1)}) custom-call(bf16[128,768]{1,0:T(8,128)(2,1)} %get-tuple-element.32.refs_0_, bf16[128,768]{1,0:T(8,128)(2,1)} %bitcast.23, bf16[768,1280]{1,0:T(8,128)(2,1)} %refs_5_.1, bf16[768,768]{1,0:T(8,128)(2,1)} %refs_3_.3), custom_call_target="tpu_custom_call" | custom-call | flops 1000000000 | bytes 4194304 | tf_op jit(solution)/shard_map/pallas_call | solution.py:121
  40.4 5.6 %collective-permute-done.3.refs_6_ = bf16[512,128]{1,0:T(8,128)(2,1)} collective-permute-done((bf16[512,128]{1,0:T(8,128)(2,1)}, bf16[512,128]{1,0:T(8,128)(2,1)}, u32[]{:S(2)}, u32[]{:S(2)}) %collective-permute-start.3) | collective-permute-done | bytes 131104 | tf_op jit(solution)/shard_map/ppermute | solution.py:33
  46.0 2.0 %collective-permute-done.2.refs_5_ = bf16[512,128]{1,0:T(8,128)(2,1)} collective-permute-done((bf16[512,128]{1,0:T(8,128)(2,1)}, bf16[512,128]{1,0:T(8,128)(2,1)}, u32[]{:S(2)}, u32[]{:S(2)}) %collective-permute-start.2) | collective-permute-done | bytes 131104 | tf_op jit(solution)/shard_map/ppermute | solution.py:33
  48.0 7.4 %shard_map.149 = (bf16[768,128]{1,0:T(8,128)(2,1)}, bf16[768,128]{1,0:T(8,128)(2,1)}, f32[512,128]{1,0:T(8,128)}, bf16[512,128]{1,0:T(8,128)(2,1)}, bf16[512,128]{1,0:T(8,128)(2,1)}, /*index=5*/bf16[512,128]{1,0:T(8,128)(2,1)}) custom-call(s32[1]{0:T(128)} %bitcast.1.refs_0_, f32[12]{0:T(128)} %refs_1_.1, s32[64,128]{1,0:T(8,128)} %bitcast.25, ...), custom_call_target="tpu_custom_call" | custom-call | flops 1000000000 | bytes 4194304 | tf_op jit(solution)/shard_map/pallas_call | solution.py:121
  55.4 0.2 collective-permute-start.4
  55.6 3.5 %collective-permute-start.5 = (bf16[512,128]{1,0:T(8,128)(2,1)}, bf16[512,128]{1,0:T(8,128)(2,1)}, u32[]{:S(2)}, u32[]{:S(2)}) collective-permute-start(bf16[512,128]{1,0:T(8,128)(2,1)} %get-tuple-element.40), channel_id=1, source_target_pairs={{0,248},{4,252},{8,0},{12,4},{16,8},{20,12},{24,16},{28,20},{32,24... | collective-permute-start | bytes 393224 | tf_op jit(solution)/shard_map/ppermute | solution.py:33
  59.1 0.1 collective-permute-start.6
  59.2 1.7 %collective-permute-done.4.refs_1_ = bf16[512,128]{1,0:T(8,128)(2,1)} collective-permute-done((bf16[512,128]{1,0:T(8,128)(2,1)}, bf16[512,128]{1,0:T(8,128)(2,1)}, u32[]{:S(2)}, u32[]{:S(2)}) %collective-permute-start.4) | collective-permute-done | bytes 131104 | tf_op jit(solution)/shard_map/ppermute | solution.py:33
  60.9 2.6 %shard_map.150.refs_8_ = f32[128,768]{1,0:T(8,128)} custom-call(bf16[768,1280]{1,0:T(8,128)(2,1)} %refs_5_.1, bf16[768,128]{1,0:T(8,128)(2,1)} %get-tuple-element.44.refs_1_.refs_12_), custom_call_target="tpu_custom_call" | custom-call | flops 1000000000 | bytes 4194304 | tf_op jit(solution)/shard_map/pallas_call | solution.py:121
  63.5 5.8 %collective-permute-done.5.refs_2_ = bf16[512,128]{1,0:T(8,128)(2,1)} collective-permute-done((bf16[512,128]{1,0:T(8,128)(2,1)}, bf16[512,128]{1,0:T(8,128)(2,1)}, u32[]{:S(2)}, u32[]{:S(2)}) %collective-permute-start.5) | collective-permute-done | bytes 131104 | tf_op jit(solution)/shard_map/ppermute | solution.py:33
  69.3 3.2 %collective-permute-done.6.refs_3_ = bf16[512,128]{1,0:T(8,128)(2,1)} collective-permute-done((bf16[512,128]{1,0:T(8,128)(2,1)}, bf16[512,128]{1,0:T(8,128)(2,1)}, u32[]{:S(2)}, u32[]{:S(2)}) %collective-permute-start.6) | collective-permute-done | bytes 131104 | tf_op jit(solution)/shard_map/ppermute | solution.py:33
  72.5 4.4 %shard_map.151 = bf16[8,368,128]{2,1,0:T(8,128)(2,1)} custom-call(f32[512,128]{1,0:T(8,128)} %get-tuple-element.36.refs_0_, bf16[512,128]{1,0:T(8,128)(2,1)} %collective-permute-done.4.refs_1_, bf16[512,128]{1,0:T(8,128)(2,1)} %collective-permute-done.5.refs_2_, bf16[512,128]{1,0:T(8,128)(2,1)} %collective-permute-done.6.refs_3_, ...), custom_call_target="tpu_custom_call" | custom-call | flops 1000000000 | bytes 4194304 | tf_op jit(solution)/shard_map/pallas_call | solution.py:121
  76.9 0.0 all-gather.5.cloned.1.call-done
  76.9 0.0 all-gather.7.cloned.1.call-done
  77.0 0.5 collective-permute-start.7
  77.4 0.1 collective-permute-start.8
  77.6 5.4 %all-to-all-start = ((bf16[8,368,128]{2,1,0:T(8,128)(2,1)}), bf16[8,368,128]{2,1,0:T(8,128)(2,1)}, u32[]{:S(2)}, u32[]{:S(2)}) async-start(bf16[8,368,128]{2,1,0:T(8,128)(2,1)} %shard_map.151), calls=%async_computation | async-start | bytes 1507328 | tf_op jit(solution)/shard_map/all_to_all | solution.py:37
  83.0 10.7 %all-to-all-done.refs_1_ = bf16[8,368,128]{2,1,0:T(8,128)(2,1)} async-done(((bf16[8,368,128]{2,1,0:T(8,128)(2,1)}), bf16[8,368,128]{2,1,0:T(8,128)(2,1)}, u32[]{:S(2)}, u32[]{:S(2)}) %all-to-all-start) | async-done | bytes 753696 | tf_op jit(solution)/shard_map/all_to_all | solution.py:37
  93.7 0.0 collective-permute-done.8.refs_6_
  93.7 0.0 collective-permute-done.7.refs_4_
  93.7 7.9 %shard_map.152 = bf16[512,896]{1,0:T(8,128)(2,1)} custom-call(s32[1]{0:T(128)} %bitcast.refs_0_, bf16[8,368,128]{2,1,0:T(8,128)(2,1)} %all-to-all-done.refs_1_, bf16[2,512,192]{2,1,0:T(8,128)(2,1)} %constant.45.clone.refs_2_, bf16[4,768,256]{2,1,0:T(8,128)(2,1)} %bitcast.18, bf16[4,768,256]{2,1,0:T(8,128)(2,1)} %collective-permute-done.7.refs_4_, ...), custom_call_target="tpu_custom_call" | custom-call | flops 1000000000 | bytes 4194304 | tf_op jit(solution)/shard_map/pallas_call | solution.py:121
  101.6 10.0 %all-to-all-start.1 = ((bf16[32,16,896]{2,1,0:T(8,128)(2,1)}), bf16[32,16,896]{2,1,0:T(8,128)(2,1)}, u32[]{:S(2)}, u32[]{:S(2)}) async-start(bf16[32,16,896]{2,1,0:T(8,128)(2,1)} %bitcast.15), calls=%async_computation.1 | async-start | bytes 1835008 | tf_op jit(solution)/shard_map/all_to_all | solution.py:37
  111.6 21.6 %all-to-all-done.1.refs_0_ = bf16[32,16,896]{2,1,0:T(8,128)(2,1)} async-done(((bf16[32,16,896]{2,1,0:T(8,128)(2,1)}), bf16[32,16,896]{2,1,0:T(8,128)(2,1)}, u32[]{:S(2)}, u32[]{:S(2)}) %all-to-all-start.1) | async-done | bytes 917536 | tf_op jit(solution)/shard_map/all_to_all | solution.py:37
  133.1 2.0 %shard_map.153 = (f32[3,2,1024]{2,1,0:T(2,128)}, f32[1,768]{1,0:T(1,128)}, f32[8,8,256]{2,1,0:T(8,128)}) custom-call(bf16[32,16,896]{2,1,0:T(8,128)(2,1)} %all-to-all-done.1.refs_0_), custom_call_target="tpu_custom_call" | custom-call | flops 1000000000 | bytes 4194304 | tf_op jit(solution)/shard_map/pallas_call | solution.py:121
  135.1 9.3 %all-to-all-start.2 = ((f32[8,8,256]{2,1,0:T(8,128)}), f32[8,8,256]{2,1,0:T(8,128)}, u32[]{:S(2)}, u32[]{:S(2)}) async-start(f32[8,8,256]{2,1,0:T(8,128)} %get-tuple-element.51), calls=%async_computation.2 | async-start | bytes 131072 | tf_op jit(solution)/shard_map/all_to_all | solution.py:37
  144.4 1.3 dynamic-slice_bitcast_fusion
  145.7 3.5 %all-to-all-done.2.refs_0_ = f32[8,8,256]{2,1,0:T(8,128)} async-done(((f32[8,8,256]{2,1,0:T(8,128)}), f32[8,8,256]{2,1,0:T(8,128)}, u32[]{:S(2)}, u32[]{:S(2)}) %all-to-all-start.2) | async-done | bytes 65568 | tf_op jit(solution)/shard_map/all_to_all | solution.py:37
  149.2 1.5 shard_map.154
Async XLA Ops:
  7.2 69.8 %all-gather.5.cloned.1.call-start = ((), (), s32[]{:S(2)}) async-start(), calls=%async_computation.3 | async-start | bytes 1310720 | tf_op jit(solution)/shard_map/all_gather | solution.py:351
  7.9 69.1 %all-gather.7.cloned.1.call-start = ((), (), s32[]{:S(2)}) async-start(), calls=%async_computation.4 | async-start | bytes 1966080 | tf_op jit(solution)/shard_map/all_gather | solution.py:373
  8.7 7.9 %collective-permute-start = (bf16[16,1024]{1,0:T(8,128)(2,1)S(1)}, bf16[16,1024]{1,0:T(8,128)(2,1)}, u32[]{:S(2)}, u32[]{:S(2)}) collective-permute-start(bf16[16,1024]{1,0:T(8,128)(2,1)S(1)} %slice_bitcast_fusion), channel_id=1, source_target_pairs={{1,0},{2,1},{3,2},{5,4},{6,5},{7,6},{9,8},{10,9},{11,10},{13,12},{... | collective-permute-start | bytes 98312 | tf_op jit(solution)/shard_map/ppermute | solution.py:350
  22.5 14.7 %collective-permute-start.1 = (bf16[512,128]{1,0:T(8,128)(2,1)}, bf16[512,128]{1,0:T(8,128)(2,1)}, u32[]{:S(2)}, u32[]{:S(2)}) collective-permute-start(bf16[512,128]{1,0:T(8,128)(2,1)} %get-tuple-element.29.refs_3_), channel_id=1, source_target_pairs={{0,4},{4,8},{8,12},{12,16},{16,20},{20,24},{24,28},{28,32},{32,36}... | collective-permute-start | bytes 393224 | tf_op jit(solution)/shard_map/ppermute | solution.py:33
  24.2 21.7 %collective-permute-start.3 = (bf16[512,128]{1,0:T(8,128)(2,1)}, bf16[512,128]{1,0:T(8,128)(2,1)}, u32[]{:S(2)}, u32[]{:S(2)}) collective-permute-start(bf16[512,128]{1,0:T(8,128)(2,1)} %get-tuple-element.29.refs_3_), channel_id=1, source_target_pairs={{0,12},{4,16},{8,20},{12,24},{16,28},{20,32},{24,36},{28,40},{32,4... | collective-permute-start | bytes 393224 | tf_op jit(solution)/shard_map/ppermute | solution.py:33
  29.8 18.2 %collective-permute-start.2 = (bf16[512,128]{1,0:T(8,128)(2,1)}, bf16[512,128]{1,0:T(8,128)(2,1)}, u32[]{:S(2)}, u32[]{:S(2)}) collective-permute-start(bf16[512,128]{1,0:T(8,128)(2,1)} %get-tuple-element.29.refs_3_), channel_id=1, source_target_pairs={{0,8},{4,12},{8,16},{12,20},{16,24},{20,28},{24,32},{28,36},{32,40... | collective-permute-start | bytes 393224 | tf_op jit(solution)/shard_map/ppermute | solution.py:33
  55.4 5.5 %collective-permute-start.4 = (bf16[512,128]{1,0:T(8,128)(2,1)}, bf16[512,128]{1,0:T(8,128)(2,1)}, u32[]{:S(2)}, u32[]{:S(2)}) collective-permute-start(bf16[512,128]{1,0:T(8,128)(2,1)} %get-tuple-element.37), channel_id=1, source_target_pairs={{0,252},{4,0},{8,4},{12,8},{16,12},{20,16},{24,20},{28,24},{32,28}... | collective-permute-start | bytes 393224 | tf_op jit(solution)/shard_map/ppermute | solution.py:33
  55.6 13.8 %collective-permute-start.5 = (bf16[512,128]{1,0:T(8,128)(2,1)}, bf16[512,128]{1,0:T(8,128)(2,1)}, u32[]{:S(2)}, u32[]{:S(2)}) collective-permute-start(bf16[512,128]{1,0:T(8,128)(2,1)} %get-tuple-element.40), channel_id=1, source_target_pairs={{0,248},{4,252},{8,0},{12,4},{16,8},{20,12},{24,16},{28,20},{32,24... | collective-permute-start | bytes 393224 | tf_op jit(solution)/shard_map/ppermute | solution.py:33
  59.1 13.5 %collective-permute-start.6 = (bf16[512,128]{1,0:T(8,128)(2,1)}, bf16[512,128]{1,0:T(8,128)(2,1)}, u32[]{:S(2)}, u32[]{:S(2)}) collective-permute-start(bf16[512,128]{1,0:T(8,128)(2,1)} %get-tuple-element.41), channel_id=1, source_target_pairs={{0,244},{4,248},{8,252},{12,0},{16,4},{20,8},{24,12},{28,16},{32,2... | collective-permute-start | bytes 393224 | tf_op jit(solution)/shard_map/ppermute | solution.py:33
  77.0 16.7 %collective-permute-start.7 = (bf16[4,768,256]{2,1,0:T(8,128)(2,1)}, bf16[4,768,256]{2,1,0:T(8,128)(2,1)}, u32[]{:S(2)}, u32[]{:S(2)}) collective-permute-start(bf16[4,768,256]{2,1,0:T(8,128)(2,1)} %bitcast.17), channel_id=1, source_target_pairs={{0,1},{1,0},{2,3},{3,2},{4,5},{5,4},{6,7},{7,6},{8,9},{9,8},{10,11... | collective-permute-start | bytes 4718600 | tf_op jit(solution)/shard_map/ppermute | solution.py:393
  77.4 16.2 %collective-permute-start.8 = (bf16[512,1024]{1,0:T(8,128)(2,1)}, bf16[512,1024]{1,0:T(8,128)(2,1)}, u32[]{:S(2)}, u32[]{:S(2)}) collective-permute-start(bf16[512,1024]{1,0:T(8,128)(2,1)} %bitcast.20), channel_id=1, source_target_pairs={{0,1},{1,0},{2,3},{3,2},{4,5},{5,4},{6,7},{7,6},{8,9},{9,8},{10,11... | collective-permute-start | bytes 3145736 | tf_op jit(solution)/shard_map/ppermute | solution.py:392
  77.6 16.1 %all-to-all-start = ((bf16[8,368,128]{2,1,0:T(8,128)(2,1)}), bf16[8,368,128]{2,1,0:T(8,128)(2,1)}, u32[]{:S(2)}, u32[]{:S(2)}) async-start(bf16[8,368,128]{2,1,0:T(8,128)(2,1)} %shard_map.151), calls=%async_computation | async-start | bytes 1507328 | tf_op jit(solution)/shard_map/all_to_all | solution.py:37
  101.6 31.6 %all-to-all-start.1 = ((bf16[32,16,896]{2,1,0:T(8,128)(2,1)}), bf16[32,16,896]{2,1,0:T(8,128)(2,1)}, u32[]{:S(2)}, u32[]{:S(2)}) async-start(bf16[32,16,896]{2,1,0:T(8,128)(2,1)} %bitcast.15), calls=%async_computation.1 | async-start | bytes 1835008 | tf_op jit(solution)/shard_map/all_to_all | solution.py:37
  135.1 14.1 %all-to-all-start.2 = ((f32[8,8,256]{2,1,0:T(8,128)}), f32[8,8,256]{2,1,0:T(8,128)}, u32[]{:S(2)}, u32[]{:S(2)}) async-start(f32[8,8,256]{2,1,0:T(8,128)} %get-tuple-element.51), calls=%async_computation.2 | async-start | bytes 131072 | tf_op jit(solution)/shard_map/all_to_all | solution.py:37
Sparse Core Ops, SparseCore 0:
  9.8 33.0 all-gather.4
  44.7 26.6 all-gather.6

commit v5 on v4

--- a/solution.py
+++ b/solution.py
@@ -37,23 +37,9 @@
     return lax.all_to_all(x, axes, split_axis=0, concat_axis=0, tiled=True)
 
 
-def orders():
-    column = np.arange(D).reshape(2, 32, 4, 3)
-    by_rest = column.transpose(1, 0, 2, 3).reshape(32, 24)
-    by_rest = np.concatenate([by_rest[:, :16].reshape(-1), by_rest[:, 16:].reshape(-1)])
-    by_member = column.transpose(0, 2, 1, 3).reshape(-1)
-    eye = np.eye(D, dtype=np.float32)
-    place = np.zeros((2, 512, 192), np.float32)
-    fold = np.zeros((2, 512, 256), np.float32)
-    for half in range(2):
-        for r in range(32):
-            for j in range(2):
-                for k in range(3):
-                    place[half, r * 16 + half * 6 + j * 3 + k, j * 96 + r * 3 + k] = 1
-            for i in range(8):
-                fold[half, r * 16 + half * 8 + i, r * 8 + i] = 1
-    tables = (eye[by_rest], eye[by_member], place, fold)
-    return [jnp.asarray(table, B16) for table in tables]
+def member_order():
+    column = np.arange(D).reshape(2, 32, 4, 3).transpose(0, 2, 1, 3).reshape(-1)
+    return jnp.asarray(np.eye(D, dtype=np.float32)[column], B16)
 
 
 class Loaded:
@@ -78,7 +64,7 @@
     return [slice(i * rows, i * rows + rows) for i in range(count)]
 
 
-def call(body, outs, scratch=(), smem=(), pieces=None, columns=None, flops=10**9):
+def call(body, outs, scratch=(), smem=(), pieces=None, columns=None, limit=64, flops=10**9):
     pieces, columns = pieces or {}, columns or {}
 
     def run(*operands):
@@ -127,7 +113,7 @@
             ],
             out_specs=[pl.BlockSpec(memory_space=pltpu.VMEM)] * len(shapes),
             scratch_shapes=[*scratch, *held, pltpu.SemaphoreType.DMA((total,))],
-            compiler_params=pltpu.CompilerParams(vmem_limit_bytes=64 * 2**20),
+            compiler_params=pltpu.CompilerParams(vmem_limit_bytes=limit * 2**20),
             cost_estimate=pl.CostEstimate(
                 flops=flops, bytes_accessed=4 * 2**20, transcendentals=0
             ),
@@ -137,7 +123,7 @@
 
 
 def stem_body(
-    tiles, stem_w, arrived, w_kv, gain, d_out, by_rest, tokens_o, hidden_o, key_o, kv_o, ring_o
+    tiles, stem_w, arrived, w_kv, gain, d_out, tokens_o, hidden_o, key_o, kv_o, ring_o
 ):
     own = tiles[...]
     deep = own.shape[1] // 4
@@ -160,8 +146,8 @@
         scale = lax.rsqrt(jnp.mean(k * k, axis=0, keepdims=True) + 1e-06)
         kv_o[h * 64 : h * 64 + 64, :] = (k * scale).astype(B16)
     kv_o[256:, :] = kv[256:].astype(B16)
-    ring_o[:, :TOK] = dot(by_rest[...], hidden, NT).astype(B16)
-    ring_o[:, TOK:] = dot(by_rest[...], d_out[...], NT).astype(B16)
+    ring_o[:, :TOK] = hidden.astype(F32).T.astype(B16)
+    ring_o[:, TOK:] = d_out[...].astype(F32).T.astype(B16)
 
 
 def query_body(hidden, d_out, w_q, w_out, query_o, query_n_o, do_o):
@@ -268,7 +254,7 @@
 
 
 def terms_body(
-    core, late, place, ring0, ring1, tiles0, tiles1, fold, terms_o, pair_s, rhs_s, both_s
+    core, late, ring0, ring1, tiles0, tiles1, terms_o, pair_s, rhs_s, both_s, sums_s, all_s
 ):
     lane = lax.broadcasted_iota(jnp.int32, (96, TOK), 1)
     gain = jnp.zeros((16, TOK), F32)
@@ -296,41 +282,44 @@
         for j in range(4):
             m = (j % 2) * 4 + (j // 2) * 2 + side
             at = s * 4 + j
-            for half in range(2):
-                both_s[half, :, at * TOK : at * TOK + TOK] = dot(place[half], pair_s[m]).astype(B16)
+            both_s[:, at * TOK : at * TOK + TOK] = pair_s[m]
             rows = rows + dot(ring.piece(j)[0], rhs_s[m], NT)
-    low = rows.astype(B16)
-    terms_o[:, 512:768] = low[:512]
-    terms_o[:, 768:] = (dot(fold[0], low[512:, :TOK]) + dot(fold[1], low[512:, TOK:])).astype(B16)
-    stem = dot(both_s[0, :, :512], tiles0[:, :512]) + dot(both_s[1, :, :512], tiles0[:, 512:])
-    stem = stem + dot(both_s[0, :, 512:], tiles1[:, :512])
-    stem = stem + dot(both_s[1, :, 512:], tiles1[:, 512:])
-    slot = lax.rem(lax.broadcasted_iota(jnp.int32, (512, 512), 0), 16)
-    first = jnp.concatenate([gain[i : i + 1, :] for i in range(4)], axis=1)
-    second = jnp.concatenate([gain[4:5, :], gain[5:6, :], jnp.zeros((1, 256), F32)], axis=1)
-    stem = jnp.where(slot == 12, jnp.broadcast_to(first, (512, 512)), stem)
-    stem = jnp.where(slot == 13, jnp.broadcast_to(second, (512, 512)), stem)
-    terms_o[:, :512] = stem.astype(B16)
+    for half in range(2):
+        sums_s[half] = rows[:, half * TOK : half * TOK + TOK]
+        for i in range(24):
+            picked = sums_s[half, pl.ds(i // 12 * 384 + i % 12, 32, stride=12), :]
+            all_s[pl.ds(48 + half * 24 + i, 32, stride=104), :] = picked
+    for i in range(8):
+        row = gain[i : i + 1, :]
+        all_s[pl.ds(96 + i, 32, stride=104), :] = jnp.broadcast_to(row, (32, TOK))
+    stem = dot(both_s[:, :512], tiles0[...]) + dot(both_s[:, 512:], tiles1[...])
+    for c in range(8):
+        sums_s[0, :192, :] = stem[:, c * TOK : c * TOK + TOK]
+        for i in range(6):
+            picked = sums_s[0, pl.ds(i // 3 * 96 + i % 3, 32, stride=3), :]
+            all_s[pl.ds(i * 8 + c, 32, stride=104), :] = picked
+    terms_o[...] = all_s[...].astype(B16)
 
 
 def total_body(terms, stem_o, gain_o, rows_o):
-    total = jnp.zeros((16, 896), F32)
+    total = jnp.zeros((104, TOK), F32)
     for piece in range(4):
         block = terms.piece(piece)
         for r in range(8):
             total = total + block[r].astype(F32)
     for j in range(2):
         for k in range(3):
-            at = j * 3 + k
-            stem_o[k, j : j + 1, :512] = total[at : at + 1, :512]
-            stem_o[k, j : j + 1, 512:] = total[at + 6 : at + 7, :512]
-    gain_o[:, :512] = total[12:13, :512]
-    gain_o[:, 512:] = total[13:14, :256]
-    last = jnp.concatenate([total[:8, 768:], total[8:, 768:]], axis=1)
-    rows = jnp.concatenate([total[:, 512:768], last], axis=0)
-    for m in range(8):
-        rows_o[m, :3, :] = rows[m * 3 : m * 3 + 3]
-        rows_o[m, 3:, :] = jnp.zeros((5, 256), F32)
+            for c in range(8):
+                at = (j * 3 + k) * 8 + c
+                stem_o[k, j : j + 1, c * TOK : c * TOK + TOK] = total[at : at + 1]
+    for c in range(6):
+        gain_o[:, c * TOK : c * TOK + TOK] = total[96 + c : 97 + c]
+    for half in range(2):
+        lanes = slice(half * TOK, half * TOK + TOK)
+        for m in range(8):
+            at = 48 + half * 24 + m * 3
+            rows_o[m, :3, lanes] = total[at : at + 3]
+            rows_o[m, 3:, lanes] = jnp.zeros((5, TOK), F32)
 
 
 def final_body(rows, qkv_o, out_o):
@@ -345,7 +334,7 @@
 def shards(patches, stem_weight, norm_gain, w_qkv, w_out, per_head_scale, positions, d_out):
     tiles = patches[0]
     grad_out = d_out[0]
-    by_rest, by_member, place, fold = orders()
+    by_member = member_order()
     bands = lax.axis_size(BAND)
     arrived = lax.ppermute(tiles[:TC], BAND, [(i, i - 1) for i in range(1, bands)])
     tiles_mine = lax.all_gather(tiles, ("yh", "yl"), axis=0, tiled=True)
@@ -359,9 +348,9 @@
             ((KV, TOK), B16),
             ((D, 2 * TOK), B16),
         ],
-        pieces={1: 8, 3: 2, 6: 2},
+        pieces={1: 8, 3: 2},
         columns={3: (D, D + KV)},
-    )(tiles, stem_weight.reshape(-1, D), arrived, w_qkv, gain, grad_out, by_rest)
+    )(tiles, stem_weight.reshape(-1, D), arrived, w_qkv, gain, grad_out)
     moved = [passed_along(kv_own, offset) for offset in range(1, 4)]
     moved[0], hidden = lax.optimization_barrier((moved[0], hidden))
     query, query_n, do = call(
@@ -394,19 +383,24 @@
     core = lax.axis_index("c").astype(jnp.int32).reshape(1)
     terms = call(
         terms_body,
-        [((512, 896), B16)],
+        [((32 * 104, TOK), B16)],
         scratch=[
             pltpu.VMEM((8, 192, TOK), B16),
             pltpu.VMEM((8, 256, 256), B16),
-            pltpu.VMEM((2, 512, 1024), B16),
+            pltpu.VMEM((192, 1024), B16),
+            pltpu.VMEM((2, D, TOK), F32),
+            pltpu.VMEM((32 * 104, TOK), F32),
         ],
         smem=(0,),
-        pieces={1: 2, 3: 4, 4: 4, 5: 2, 6: 2},
-    )(core, late_ring, place, ring_mine, ring_other, tiles_mine, tiles_other, fold)[0]
+        pieces={2: 4, 3: 4, 4: 2, 5: 2},
+    )(core, late_ring, ring_mine, ring_other, tiles_mine, tiles_other)[0]
     stem_total, gain_total, row_total = call(
-        total_body, [((3, 2, 1024), F32), ((1, D), F32), ((8, 8, 256), F32)], pieces={0: 4}
-    )(exchange(terms.reshape(32, 16, 896), REST))
-    d_w_qkv, d_w_out = call(final_body, [((3, 1280), F32), ((3, D), F32)])(
+        total_body,
+        [((3, 2, 1024), F32), ((1, D), F32), ((8, 8, 256), F32)],
+        pieces={0: 4},
+        limit=16,
+    )(exchange(terms.reshape(32, 104, TOK), REST))
+    d_w_qkv, d_w_out = call(final_body, [((3, 1280), F32), ((3, D), F32)], limit=16)(
         exchange(row_total, RING)
     )
     own_column = (lax.axis_index(BLK) * 4 + lax.axis_index(BAND)) * 3

time: 158 us -> 153 us (0.968)
  Pallas kernels: 34.8 us -> 30.8 us
    pallas_call x8, Pallas kernels: 34.8 us -> 30.8 us  [run(): pl.pallas_call(kernel, out_shape=shapes, in_specs=[pl.BlockSpec(memory_sp...]
where the time goes in v5:
time: 153 us; the launch traced here: 152 us
  waiting for transfers between devices  61.8 us (40%)
  starting transfers between devices  42.6 us (28%)
  Pallas kernels  30.8 us (20%)
  between operations  14.2 us (9%)
  local copies, waits for them, and re-layouts  2.61 us (2%)
    all_to_all x3, waiting for transfers between devices, exchange(): return lax.all_to_all(x, axes, split_axis=0, concat_axis=0, tiled=True)  35 us
    pallas_call x8, Pallas kernels, run(): pl.pallas_call(kernel, out_shape=shapes, in_specs=[pl.BlockSpec(memory_sp...  30.8 us
    ppermute x6, waiting for transfers between devices, passed_along(): return lax.ppermute(x, BLK, [(i, (i + by) % peers) for i in range(peers)])  24.6 us
    all_to_all x3, starting transfers between devices, exchange(): return lax.all_to_all(x, axes, split_axis=0, concat_axis=0, tiled=True)  24.6 us
    ppermute x6, starting transfers between devices, passed_along(): return lax.ppermute(x, BLK, [(i, (i + by) % peers) for i in range(peers)])  12.2 us
    ppermute x1, starting transfers between devices, shards(): lax.ppermute(tiles[:TC], BAND, [(i, i - 1) for i in range(1, bands)])  5.14 us
  transfers between devices with their start and end apart: 14, of which 10 were waited for; matrix products, arithmetic and copies ran while one was open for 2% of the time, Pallas kernels for 15%

profile of v5, /device:TPU:1, one launch (start us, length us, event | category | flops | bytes accessed | tf_op | source)
XLA Modules:
  0.0 152.1 jit_solution(10618558346446109090)
XLA Ops:
  7.2 0.0 all-gather.5.cloned.1.call-start
  7.2 0.7 all-gather.5.cloned.1.call-update
  7.9 0.0 all-gather.7.cloned.1.call-start
  7.9 0.8 slice_bitcast_fusion
  8.7 5.1 %collective-permute-start = (bf16[16,1024]{1,0:T(8,128)(2,1)S(1)}, bf16[16,1024]{1,0:T(8,128)(2,1)}, u32[]{:S(2)}, u32[]{:S(2)}) collective-permute-start(bf16[16,1024]{1,0:T(8,128)(2,1)S(1)} %slice_bitcast_fusion), channel_id=1, source_target_pairs={{1,0},{2,1},{3,2},{5,4},{6,5},{7,6},{9,8},{10,9},{11,10},{13,12},{... | collective-permute-start | bytes 98312 | tf_op jit(solution)/shard_map/ppermute | solution.py:339
  13.9 1.3 reshape.32.refs_4_.refs_7_
  15.1 1.5 collective-permute-done.refs_2_
  16.6 4.5 %shard_map.120 = (bf16[128,768]{1,0:T(8,128)(2,1)}, bf16[128,768]{1,0:T(8,128)(2,1)}, f32[256,128]{1,0:T(8,128)}, bf16[512,128]{1,0:T(8,128)(2,1)}, bf16[768,256]{1,0:T(8,128)(2,1)}) custom-call(bf16[128,1024]{1,0:T(8,128)(2,1)} %bitcast.19, bf16[2048,768]{1,0:T(8,128)(2,1)} %bitcast.16, bf16[16,1024]{1,0:T(8,128)(2,1)} %collective-permute-done.refs_2_, ...), custom_call_target="tpu_custom_call" | custom-call | flops 1000000000 | bytes 4194304 | tf_op jit(solution)/shard_map/pallas_call | solution.py:107
  21.2 0.0 all-gather.7.cloned.1.call-update
  21.2 1.7 %collective-permute-start.1 = (bf16[512,128]{1,0:T(8,128)(2,1)}, bf16[512,128]{1,0:T(8,128)(2,1)}, u32[]{:S(2)}, u32[]{:S(2)}) collective-permute-start(bf16[512,128]{1,0:T(8,128)(2,1)} %get-tuple-element.29.refs_3_), channel_id=1, source_target_pairs={{0,4},{4,8},{8,12},{12,16},{16,20},{20,24},{24,28},{28,32},{32,36}... | collective-permute-start | bytes 393224 | tf_op jit(solution)/shard_map/ppermute | solution.py:33
  22.9 5.6 %collective-permute-start.3 = (bf16[512,128]{1,0:T(8,128)(2,1)}, bf16[512,128]{1,0:T(8,128)(2,1)}, u32[]{:S(2)}, u32[]{:S(2)}) collective-permute-start(bf16[512,128]{1,0:T(8,128)(2,1)} %get-tuple-element.29.refs_3_), channel_id=1, source_target_pairs={{0,12},{4,16},{8,20},{12,24},{16,28},{20,32},{24,36},{28,40},{32,4... | collective-permute-start | bytes 393224 | tf_op jit(solution)/shard_map/ppermute | solution.py:33
  28.5 1.2 collective-permute-start.2
  29.6 6.3 %collective-permute-done.1.refs_4_ = bf16[512,128]{1,0:T(8,128)(2,1)} collective-permute-done((bf16[512,128]{1,0:T(8,128)(2,1)}, bf16[512,128]{1,0:T(8,128)(2,1)}, u32[]{:S(2)}, u32[]{:S(2)}) %collective-permute-start.1) | collective-permute-done | bytes 131104 | tf_op jit(solution)/shard_map/ppermute | solution.py:33
  35.9 3.2 %shard_map.121 = (f32[768,128]{1,0:T(8,128)}, bf16[768,128]{1,0:T(8,128)(2,1)}, bf16[768,128]{1,0:T(8,128)(2,1)}) custom-call(bf16[128,768]{1,0:T(8,128)(2,1)} %get-tuple-element.32.refs_0_, bf16[128,768]{1,0:T(8,128)(2,1)} %bitcast.23, bf16[768,1280]{1,0:T(8,128)(2,1)} %refs_5_.1, bf16[768,768]{1,0:T(8,128)(2,1)} %refs_3_.3), custom_call_target="tpu_custom_call" | custom-call | flops 1000000000 | bytes 4194304 | tf_op jit(solution)/shard_map/pallas_call | solution.py:107
  39.1 5.5 %collective-permute-done.3.refs_6_ = bf16[512,128]{1,0:T(8,128)(2,1)} collective-permute-done((bf16[512,128]{1,0:T(8,128)(2,1)}, bf16[512,128]{1,0:T(8,128)(2,1)}, u32[]{:S(2)}, u32[]{:S(2)}) %collective-permute-start.3) | collective-permute-done | bytes 131104 | tf_op jit(solution)/shard_map/ppermute | solution.py:33
  44.6 2.0 %collective-permute-done.2.refs_5_ = bf16[512,128]{1,0:T(8,128)(2,1)} collective-permute-done((bf16[512,128]{1,0:T(8,128)(2,1)}, bf16[512,128]{1,0:T(8,128)(2,1)}, u32[]{:S(2)}, u32[]{:S(2)}) %collective-permute-start.2) | collective-permute-done | bytes 131104 | tf_op jit(solution)/shard_map/ppermute | solution.py:33
  46.7 7.4 %shard_map.122 = (bf16[768,128]{1,0:T(8,128)(2,1)}, bf16[768,128]{1,0:T(8,128)(2,1)}, f32[512,128]{1,0:T(8,128)}, bf16[512,128]{1,0:T(8,128)(2,1)}, bf16[512,128]{1,0:T(8,128)(2,1)}, /*index=5*/bf16[512,128]{1,0:T(8,128)(2,1)}) custom-call(s32[1]{0:T(128)} %bitcast.1.refs_0_, f32[12]{0:T(128)} %refs_1_.1, s32[64,128]{1,0:T(8,128)} %bitcast.25, ...), custom_call_target="tpu_custom_call" | custom-call | flops 1000000000 | bytes 4194304 | tf_op jit(solution)/shard_map/pallas_call | solution.py:107
  54.1 0.2 collective-permute-start.4
  54.2 3.5 %collective-permute-start.5 = (bf16[512,128]{1,0:T(8,128)(2,1)}, bf16[512,128]{1,0:T(8,128)(2,1)}, u32[]{:S(2)}, u32[]{:S(2)}) collective-permute-start(bf16[512,128]{1,0:T(8,128)(2,1)} %get-tuple-element.40), channel_id=1, source_target_pairs={{0,248},{4,252},{8,0},{12,4},{16,8},{20,12},{24,16},{28,20},{32,24... | collective-permute-start | bytes 393224 | tf_op jit(solution)/shard_map/ppermute | solution.py:33
  57.7 0.1 collective-permute-start.6
  57.8 1.8 %collective-permute-done.4.refs_1_ = bf16[512,128]{1,0:T(8,128)(2,1)} collective-permute-done((bf16[512,128]{1,0:T(8,128)(2,1)}, bf16[512,128]{1,0:T(8,128)(2,1)}, u32[]{:S(2)}, u32[]{:S(2)}) %collective-permute-start.4) | collective-permute-done | bytes 131104 | tf_op jit(solution)/shard_map/ppermute | solution.py:33
  59.6 2.6 %shard_map.123.refs_8_ = f32[128,768]{1,0:T(8,128)} custom-call(bf16[768,1280]{1,0:T(8,128)(2,1)} %refs_5_.1, bf16[768,128]{1,0:T(8,128)(2,1)} %get-tuple-element.44.refs_1_.refs_12_), custom_call_target="tpu_custom_call" | custom-call | flops 1000000000 | bytes 4194304 | tf_op jit(solution)/shard_map/pallas_call | solution.py:107
  62.2 5.8 %collective-permute-done.5.refs_2_ = bf16[512,128]{1,0:T(8,128)(2,1)} collective-permute-done((bf16[512,128]{1,0:T(8,128)(2,1)}, bf16[512,128]{1,0:T(8,128)(2,1)}, u32[]{:S(2)}, u32[]{:S(2)}) %collective-permute-start.5) | collective-permute-done | bytes 131104 | tf_op jit(solution)/shard_map/ppermute | solution.py:33
  68.0 3.2 %collective-permute-done.6.refs_3_ = bf16[512,128]{1,0:T(8,128)(2,1)} collective-permute-done((bf16[512,128]{1,0:T(8,128)(2,1)}, bf16[512,128]{1,0:T(8,128)(2,1)}, u32[]{:S(2)}, u32[]{:S(2)}) %collective-permute-start.6) | collective-permute-done | bytes 131104 | tf_op jit(solution)/shard_map/ppermute | solution.py:33
  71.2 4.4 %shard_map.124 = bf16[8,368,128]{2,1,0:T(8,128)(2,1)} custom-call(f32[512,128]{1,0:T(8,128)} %get-tuple-element.36.refs_0_, bf16[512,128]{1,0:T(8,128)(2,1)} %collective-permute-done.4.refs_1_, bf16[512,128]{1,0:T(8,128)(2,1)} %collective-permute-done.5.refs_2_, bf16[512,128]{1,0:T(8,128)(2,1)} %collective-permute-done.6.refs_3_, ...), custom_call_target="tpu_custom_call" | custom-call | flops 1000000000 | bytes 4194304 | tf_op jit(solution)/shard_map/pallas_call | solution.py:107
  75.6 0.0 all-gather.5.cloned.1.call-done
  75.6 0.0 all-gather.7.cloned.1.call-done
  75.6 0.5 collective-permute-start.7
  76.1 0.1 collective-permute-start.8
  76.2 5.4 %all-to-all-start = ((bf16[8,368,128]{2,1,0:T(8,128)(2,1)}), bf16[8,368,128]{2,1,0:T(8,128)(2,1)}, u32[]{:S(2)}, u32[]{:S(2)}) async-start(bf16[8,368,128]{2,1,0:T(8,128)(2,1)} %shard_map.124), calls=%async_computation | async-start | bytes 1507328 | tf_op jit(solution)/shard_map/all_to_all | solution.py:37
  81.6 10.7 %all-to-all-done.refs_1_ = bf16[8,368,128]{2,1,0:T(8,128)(2,1)} async-done(((bf16[8,368,128]{2,1,0:T(8,128)(2,1)}), bf16[8,368,128]{2,1,0:T(8,128)(2,1)}, u32[]{:S(2)}, u32[]{:S(2)}) %all-to-all-start) | async-done | bytes 753696 | tf_op jit(solution)/shard_map/all_to_all | solution.py:37
  92.3 0.0 collective-permute-done.8.refs_5_
  92.3 0.0 collective-permute-done.7.refs_3_
  92.3 6.2 %shard_map.125 = bf16[3328,128]{1,0:T(8,128)(2,1)} custom-call(s32[1]{0:T(128)} %bitcast.refs_0_, bf16[8,368,128]{2,1,0:T(8,128)(2,1)} %all-to-all-done.refs_1_, bf16[4,768,256]{2,1,0:T(8,128)(2,1)} %bitcast.18, bf16[4,768,256]{2,1,0:T(8,128)(2,1)} %collective-permute-done.7.refs_3_, bf16[512,1024]{1,0:T(8,128)(2,1)} %bitcast.21, ...), custom_call_target="tpu_custom_call" | custom-call | flops 1000000000 | bytes 4194304 | tf_op jit(solution)/shard_map/pallas_call | solution.py:107
  98.5 9.9 %all-to-all-start.1 = ((bf16[32,104,128]{2,1,0:T(8,128)(2,1)}), bf16[32,104,128]{2,1,0:T(8,128)(2,1)S(1)}, u32[]{:S(2)}, u32[]{:S(2)}) async-start(bf16[32,104,128]{2,1,0:T(8,128)(2,1)} %bitcast.15), calls=%async_computation.1 | async-start | bytes 1703936 | tf_op jit(solution)/shard_map/all_to_all | solution.py:37
  108.4 20.2 %all-to-all-done.1.refs_0_ = bf16[32,104,128]{2,1,0:T(8,128)(2,1)S(1)} async-done(((bf16[32,104,128]{2,1,0:T(8,128)(2,1)}), bf16[32,104,128]{2,1,0:T(8,128)(2,1)S(1)}, u32[]{:S(2)}, u32[]{:S(2)}) %all-to-all-start.1) | async-done | bytes 852000 | tf_op jit(solution)/shard_map/all_to_all | solution.py:37
  128.5 1.9 %shard_map.126 = (f32[3,2,1024]{2,1,0:T(2,128)}, f32[1,768]{1,0:T(1,128)S(1)}, f32[8,8,256]{2,1,0:T(8,128)}) custom-call(bf16[32,104,128]{2,1,0:T(8,128)(2,1)S(1)} %all-to-all-done.1.refs_0_), custom_call_target="tpu_custom_call" | custom-call | flops 1000000000 | bytes 4194304 | tf_op jit(solution)/shard_map/pallas_call | solution.py:107
  130.4 9.3 %all-to-all-start.2 = ((f32[8,8,256]{2,1,0:T(8,128)}), f32[8,8,256]{2,1,0:T(8,128)S(1)}, u32[]{:S(2)}, u32[]{:S(2)}) async-start(f32[8,8,256]{2,1,0:T(8,128)} %get-tuple-element.51), calls=%async_computation.2 | async-start | bytes 131072 | tf_op jit(solution)/shard_map/all_to_all | solution.py:37
  139.7 0.6 dynamic-slice_bitcast_fusion
  140.3 4.1 %all-to-all-done.2.refs_0_ = f32[8,8,256]{2,1,0:T(8,128)S(1)} async-done(((f32[8,8,256]{2,1,0:T(8,128)}), f32[8,8,256]{2,1,0:T(8,128)S(1)}, u32[]{:S(2)}, u32[]{:S(2)}) %all-to-all-start.2) | async-done | bytes 65568 | tf_op jit(solution)/shard_map/all_to_all | solution.py:37
  144.4 0.8 shard_map.127
Async XLA Ops:
  7.2 68.4 %all-gather.5.cloned.1.call-start = ((), (), s32[]{:S(2)}) async-start(), calls=%async_computation.3 | async-start | bytes 1310720 | tf_op jit(solution)/shard_map/all_gather | solution.py:340
  7.9 67.7 %all-gather.7.cloned.1.call-start = ((), (), s32[]{:S(2)}) async-start(), calls=%async_computation.4 | async-start | bytes 1966080 | tf_op jit(solution)/shard_map/all_gather | solution.py:362
  8.7 7.9 %collective-permute-start = (bf16[16,1024]{1,0:T(8,128)(2,1)S(1)}, bf16[16,1024]{1,0:T(8,128)(2,1)}, u32[]{:S(2)}, u32[]{:S(2)}) collective-permute-start(bf16[16,1024]{1,0:T(8,128)(2,1)S(1)} %slice_bitcast_fusion), channel_id=1, source_target_pairs={{1,0},{2,1},{3,2},{5,4},{6,5},{7,6},{9,8},{10,9},{11,10},{13,12},{... | collective-permute-start | bytes 98312 | tf_op jit(solution)/shard_map/ppermute | solution.py:339
  21.2 14.7 %collective-permute-start.1 = (bf16[512,128]{1,0:T(8,128)(2,1)}, bf16[512,128]{1,0:T(8,128)(2,1)}, u32[]{:S(2)}, u32[]{:S(2)}) collective-permute-start(bf16[512,128]{1,0:T(8,128)(2,1)} %get-tuple-element.29.refs_3_), channel_id=1, source_target_pairs={{0,4},{4,8},{8,12},{12,16},{16,20},{20,24},{24,28},{28,32},{32,36}... | collective-permute-start | bytes 393224 | tf_op jit(solution)/shard_map/ppermute | solution.py:33
  22.9 21.7 %collective-permute-start.3 = (bf16[512,128]{1,0:T(8,128)(2,1)}, bf16[512,128]{1,0:T(8,128)(2,1)}, u32[]{:S(2)}, u32[]{:S(2)}) collective-permute-start(bf16[512,128]{1,0:T(8,128)(2,1)} %get-tuple-element.29.refs_3_), channel_id=1, source_target_pairs={{0,12},{4,16},{8,20},{12,24},{16,28},{20,32},{24,36},{28,40},{32,4... | collective-permute-start | bytes 393224 | tf_op jit(solution)/shard_map/ppermute | solution.py:33
  28.5 18.2 %collective-permute-start.2 = (bf16[512,128]{1,0:T(8,128)(2,1)}, bf16[512,128]{1,0:T(8,128)(2,1)}, u32[]{:S(2)}, u32[]{:S(2)}) collective-permute-start(bf16[512,128]{1,0:T(8,128)(2,1)} %get-tuple-element.29.refs_3_), channel_id=1, source_target_pairs={{0,8},{4,12},{8,16},{12,20},{16,24},{20,28},{24,32},{28,36},{32,40... | collective-permute-start | bytes 393224 | tf_op jit(solution)/shard_map/ppermute | solution.py:33
  54.1 5.5 %collective-permute-start.4 = (bf16[512,128]{1,0:T(8,128)(2,1)}, bf16[512,128]{1,0:T(8,128)(2,1)}, u32[]{:S(2)}, u32[]{:S(2)}) collective-permute-start(bf16[512,128]{1,0:T(8,128)(2,1)} %get-tuple-element.37), channel_id=1, source_target_pairs={{0,252},{4,0},{8,4},{12,8},{16,12},{20,16},{24,20},{28,24},{32,28}... | collective-permute-start | bytes 393224 | tf_op jit(solution)/shard_map/ppermute | solution.py:33
  54.2 13.8 %collective-permute-start.5 = (bf16[512,128]{1,0:T(8,128)(2,1)}, bf16[512,128]{1,0:T(8,128)(2,1)}, u32[]{:S(2)}, u32[]{:S(2)}) collective-permute-start(bf16[512,128]{1,0:T(8,128)(2,1)} %get-tuple-element.40), channel_id=1, source_target_pairs={{0,248},{4,252},{8,0},{12,4},{16,8},{20,12},{24,16},{28,20},{32,24... | collective-permute-start | bytes 393224 | tf_op jit(solution)/shard_map/ppermute | solution.py:33
  57.7 13.5 %collective-permute-start.6 = (bf16[512,128]{1,0:T(8,128)(2,1)}, bf16[512,128]{1,0:T(8,128)(2,1)}, u32[]{:S(2)}, u32[]{:S(2)}) collective-permute-start(bf16[512,128]{1,0:T(8,128)(2,1)} %get-tuple-element.41), channel_id=1, source_target_pairs={{0,244},{4,248},{8,252},{12,0},{16,4},{20,8},{24,12},{28,16},{32,2... | collective-permute-start | bytes 393224 | tf_op jit(solution)/shard_map/ppermute | solution.py:33
  75.6 16.7 %collective-permute-start.7 = (bf16[4,768,256]{2,1,0:T(8,128)(2,1)}, bf16[4,768,256]{2,1,0:T(8,128)(2,1)}, u32[]{:S(2)}, u32[]{:S(2)}) collective-permute-start(bf16[4,768,256]{2,1,0:T(8,128)(2,1)} %bitcast.17), channel_id=1, source_target_pairs={{0,1},{1,0},{2,3},{3,2},{4,5},{5,4},{6,7},{7,6},{8,9},{9,8},{10,11... | collective-permute-start | bytes 4718600 | tf_op jit(solution)/shard_map/ppermute | solution.py:382
  76.1 16.2 %collective-permute-start.8 = (bf16[512,1024]{1,0:T(8,128)(2,1)}, bf16[512,1024]{1,0:T(8,128)(2,1)}, u32[]{:S(2)}, u32[]{:S(2)}) collective-permute-start(bf16[512,1024]{1,0:T(8,128)(2,1)} %bitcast.20), channel_id=1, source_target_pairs={{0,1},{1,0},{2,3},{3,2},{4,5},{5,4},{6,7},{7,6},{8,9},{9,8},{10,11... | collective-permute-start | bytes 3145736 | tf_op jit(solution)/shard_map/ppermute | solution.py:381
  76.2 16.1 %all-to-all-start = ((bf16[8,368,128]{2,1,0:T(8,128)(2,1)}), bf16[8,368,128]{2,1,0:T(8,128)(2,1)}, u32[]{:S(2)}, u32[]{:S(2)}) async-start(bf16[8,368,128]{2,1,0:T(8,128)(2,1)} %shard_map.124), calls=%async_computation | async-start | bytes 1507328 | tf_op jit(solution)/shard_map/all_to_all | solution.py:37
  98.5 30.1 %all-to-all-start.1 = ((bf16[32,104,128]{2,1,0:T(8,128)(2,1)}), bf16[32,104,128]{2,1,0:T(8,128)(2,1)S(1)}, u32[]{:S(2)}, u32[]{:S(2)}) async-start(bf16[32,104,128]{2,1,0:T(8,128)(2,1)} %bitcast.15), calls=%async_computation.1 | async-start | bytes 1703936 | tf_op jit(solution)/shard_map/all_to_all | solution.py:37
  130.4 14.0 %all-to-all-start.2 = ((f32[8,8,256]{2,1,0:T(8,128)}), f32[8,8,256]{2,1,0:T(8,128)S(1)}, u32[]{:S(2)}, u32[]{:S(2)}) async-start(f32[8,8,256]{2,1,0:T(8,128)} %get-tuple-element.51), calls=%async_computation.2 | async-start | bytes 131072 | tf_op jit(solution)/shard_map/all_to_all | solution.py:37
Sparse Core Ops, SparseCore 0:
  9.8 33.8 all-gather.4
  45.5 25.9 all-gather.6

commit v6 on v5

--- a/solution.py
+++ b/solution.py
@@ -16,6 +16,7 @@
 BLK = ("yl", "x", "z")
 BAND = ("yh", "c")
 RING = ("yl", "yh", "c")
+CHIPS = ("yl", "yh")
 REST = ("x", "z")
 F32 = jnp.float32
 B16 = jnp.bfloat16
@@ -31,6 +32,18 @@
 def passed_along(x, by):
     peers = lax.axis_size(BLK)
     return lax.ppermute(x, BLK, [(i, (i + by) % peers) for i in range(peers)])
+
+
+def from_chips(x):
+    order = [0, 2, 1, 3]
+    return [
+        lax.ppermute(x, CHIPS, [(order[i], order[(i + by) % 4]) for i in range(4)])
+        for by in range(1, 4)
+    ]
+
+
+def other_core(x):
+    return lax.ppermute(x, "c", [(0, 1), (1, 0)])
 
 
 def exchange(x, axes):
@@ -254,8 +267,10 @@
 
 
 def terms_body(
-    core, late, ring0, ring1, tiles0, tiles1, terms_o, pair_s, rhs_s, both_s, sums_s, all_s
+    place, late, *rest
 ):
+    rings, tiles = rest[:8], rest[8:16]
+    terms_o, pair_s, rhs_s, sums_s, all_s = rest[16:]
     lane = lax.broadcasted_iota(jnp.int32, (96, TOK), 1)
     gain = jnp.zeros((16, TOK), F32)
     zero = jnp.zeros((TOK, TOK), B16)
@@ -277,13 +292,14 @@
             rhs_s[m, 224:, :TOK] = late[m, 128:160, :]
             rhs_s[m, 224:, TOK:] = zero[:32]
     rows = jnp.zeros((D, 256), F32)
-    for s, ring in enumerate((ring0, ring1)):
-        side = lax.rem(core[0] + s, 2)
-        for j in range(4):
-            m = (j % 2) * 4 + (j // 2) * 2 + side
-            at = s * 4 + j
-            both_s[:, at * TOK : at * TOK + TOK] = pair_s[m]
-            rows = rows + dot(ring.piece(j)[0], rhs_s[m], NT)
+    members = []
+    for side in range(2):
+        for back in range(4):
+            chip = lax.rem(place[0] + 4 - back, 4)
+            core = lax.rem(place[1] + side, 2)
+            members.append(lax.rem(chip, 2) * 4 + lax.div(chip, 2) * 2 + core)
+    for ring, m in zip(rings, members):
+        rows = rows + dot(ring[...], rhs_s[m], NT)
     for half in range(2):
         sums_s[half] = rows[:, half * TOK : half * TOK + TOK]
         for i in range(24):
@@ -292,7 +308,9 @@
     for i in range(8):
         row = gain[i : i + 1, :]
         all_s[pl.ds(96 + i, 32, stride=104), :] = jnp.broadcast_to(row, (32, TOK))
-    stem = dot(both_s[:, :512], tiles0[...]) + dot(both_s[:, 512:], tiles1[...])
+    stem = jnp.zeros((192, 1024), F32)
+    for tile, m in zip(tiles, members):
+        stem = stem + dot(pair_s[m], tile[...])
     for c in range(8):
         sums_s[0, :192, :] = stem[:, c * TOK : c * TOK + TOK]
         for i in range(6):
@@ -337,7 +355,7 @@
     by_member = member_order()
     bands = lax.axis_size(BAND)
     arrived = lax.ppermute(tiles[:TC], BAND, [(i, i - 1) for i in range(1, bands)])
-    tiles_mine = lax.all_gather(tiles, ("yh", "yl"), axis=0, tiled=True)
+    tiles_mine = from_chips(tiles)
     gain = norm_gain.reshape(1, D)
     tokens, hidden, key, kv_own, ring_own = call(
         stem_body,
@@ -359,7 +377,7 @@
         pieces={2: 2, 3: 2},
         columns={2: (0, D)},
     )(hidden, grad_out, w_qkv, w_out)
-    ring_mine = lax.all_gather(ring_own, ("yh", "yl"), axis=0, tiled=False)
+    query_n, tiles_mine = lax.optimization_barrier((query_n, tiles_mine))
     own_block = lax.axis_index(BLK).astype(jnp.int32).reshape(1)
     attn, d_q, own, back1, back2, back3 = call(
         attend_body,
@@ -369,6 +387,8 @@
     returned = [passed_along(piece, -(j + 1)) for j, piece in enumerate((back1, back2, back3))]
     returned[0], d_q = lax.optimization_barrier((returned[0], d_q))
     part = call(part_body, [((TOK, D), F32)], pieces={0: 2}, columns={0: (0, D)})(w_qkv, d_q)[0]
+    ring_mine = from_chips(ring_own)
+    ring_mine, part = lax.optimization_barrier((ring_mine, part))
     late = call(
         tokens_body,
         [((8, 368, TOK), B16)],
@@ -377,23 +397,23 @@
         columns={5: (D, D + KV)},
     )(own, *returned, key, w_qkv, tokens, gain, part, grad_out, by_member, attn, d_q)[0]
     late_ring = exchange(late, RING)
-    tiles_mine, ring_mine, late = lax.optimization_barrier((tiles_mine, ring_mine, late))
-    tiles_other = lax.ppermute(tiles_mine, "c", [(0, 1), (1, 0)])
-    ring_other = lax.ppermute(ring_mine, "c", [(0, 1), (1, 0)])
-    core = lax.axis_index("c").astype(jnp.int32).reshape(1)
+    rings = [ring_own, *ring_mine]
+    blocks = [tiles, *tiles_mine]
+    rings = rings + [other_core(x) for x in rings]
+    blocks = blocks + [other_core(x) for x in blocks]
+    chip = lax.axis_index("yh") * 2 + lax.axis_index("yl")
+    place = jnp.stack([chip, lax.axis_index("c")]).astype(jnp.int32)
     terms = call(
         terms_body,
         [((32 * 104, TOK), B16)],
         scratch=[
             pltpu.VMEM((8, 192, TOK), B16),
             pltpu.VMEM((8, 256, 256), B16),
-            pltpu.VMEM((192, 1024), B16),
             pltpu.VMEM((2, D, TOK), F32),
             pltpu.VMEM((32 * 104, TOK), F32),
         ],
         smem=(0,),
-        pieces={2: 4, 3: 4, 4: 2, 5: 2},
-    )(core, late_ring, ring_mine, ring_other, tiles_mine, tiles_other)[0]
+    )(place, late_ring, *rings, *blocks)[0]
     stem_total, gain_total, row_total = call(
         total_body,
         [((3, 2, 1024), F32), ((1, D), F32), ((8, 8, 256), F32)],

time: 153 us -> 142 us (0.928)
  between operations: 14.2 us -> 0.96 us
  starting transfers between devices: 42.6 us -> 55.8 us
  waiting for transfers between devices: 61.8 us -> 49.5 us
    ppermute x6, waiting for transfers between devices: 24.6 us -> 17.1 us  [passed_along(): return lax.ppermute(x, BLK, [(i, (i + by) % peers) for i in range(peers)])]
    ppermute x2 -> x14, starting transfers between devices: 0.6 us -> 7.39 us  [the longest x6 5.43 us: from_chips(): lax.ppermute(x, CHIPS, [(order[i], order[(i + by) % 4]) for i in range(4)])]
    all_to_all x3, waiting for transfers between devices: 35 us -> 29.7 us  [exchange(): return lax.all_to_all(x, axes, split_axis=0, concat_axis=0, tiled=True)]
    all_to_all x3, starting transfers between devices: 24.6 us -> 27.9 us  [exchange(): return lax.all_to_all(x, axes, split_axis=0, concat_axis=0, tiled=True)]
    ppermute x6, starting transfers between devices: 12.2 us -> 15.4 us  [passed_along(): return lax.ppermute(x, BLK, [(i, (i + by) % peers) for i in range(peers)])]
    ppermute x2 -> x14, waiting for transfers between devices: 0.01 us -> 2.72 us  [the longest x8 2.71 us: other_core(): return lax.ppermute(x, 'c', [(0, 1), (1, 0)])]
  transfers between devices with their start and end apart: 14 -> 24, of which waited for: 10 -> 10; matrix products, arithmetic and copies ran while one was open for 2% -> 2% of each run, Pallas kernels for 15% -> 12%
where the time goes in v6:
time: 142 us
  starting transfers between devices  55.8 us (39%)
  waiting for transfers between devices  49.5 us (35%)
  Pallas kernels  32.2 us (23%)
  local copies, waits for them, and re-layouts  2.61 us (2%)
    pallas_call x8, Pallas kernels, run(): pl.pallas_call(kernel, out_shape=shapes, in_specs=[pl.BlockSpec(memory_sp...  32.2 us
    all_to_all x3, waiting for transfers between devices, exchange(): return lax.all_to_all(x, axes, split_axis=0, concat_axis=0, tiled=True)  29.7 us
    all_to_all x3, starting transfers between devices, exchange(): return lax.all_to_all(x, axes, split_axis=0, concat_axis=0, tiled=True)  27.9 us
    ppermute x6, waiting for transfers between devices, passed_along(): return lax.ppermute(x, BLK, [(i, (i + by) % peers) for i in range(peers)])  17.1 us
    ppermute x6, starting transfers between devices, passed_along(): return lax.ppermute(x, BLK, [(i, (i + by) % peers) for i in range(peers)])  15.4 us
    ppermute x6, starting transfers between devices, from_chips(): lax.ppermute(x, CHIPS, [(order[i], order[(i + by) % 4]) for i in range(4)])  5.43 us
    ppermute x1, starting transfers between devices, shards(): lax.ppermute(tiles[:TC], BAND, [(i, i - 1) for i in range(1, bands)])  5.14 us
  transfers between devices with their start and end apart: 24, of which 10 were waited for; matrix products, arithmetic and copies ran while one was open for 2% of the time, Pallas kernels for 12%

profile of v6, /device:TPU:1, one launch (start us, length us, event | category | flops | bytes accessed | tf_op | source)
XLA Modules:
  0.0 141.7 jit_solution(16978559897491801444)
XLA Ops:
  0.6 0.8 slice_bitcast_fusion
  1.4 5.1 %collective-permute-start = (bf16[16,1024]{1,0:T(8,128)(2,1)S(1)}, bf16[16,1024]{1,0:T(8,128)(2,1)}, u32[]{:S(2)}, u32[]{:S(2)}) collective-permute-start(bf16[16,1024]{1,0:T(8,128)(2,1)S(1)} %slice_bitcast_fusion), channel_id=1, source_target_pairs={{1,0},{2,1},{3,2},{5,4},{6,5},{7,6},{9,8},{10,9},{11,10},{13,12},{... | collective-permute-start | bytes 98312 | tf_op jit(solution)/shard_map/ppermute | solution.py:357
  6.5 1.6 %collective-permute-start.6 = (bf16[128,1024]{1,0:T(8,128)(2,1)}, bf16[128,1024]{1,0:T(8,128)(2,1)}, u32[]{:S(2)}, u32[]{:S(2)}) collective-permute-start(bf16[128,1024]{1,0:T(8,128)(2,1)} %bitcast.16), channel_id=1, source_target_pairs={{0,130},{128,0},{2,128},{130,2},{1,131},{129,1},{3,129},{131,3},{4... | collective-permute-start | bytes 786440 | tf_op jit(solution)/shard_map/ppermute | solution.py:40
  8.1 0.2 collective-permute-start.5
  8.3 0.9 collective-permute-start.4
  9.2 1.3 reshape.28.refs_4_.refs_7_
  10.4 4.5 %shard_map.120 = (bf16[128,768]{1,0:T(8,128)(2,1)}, bf16[128,768]{1,0:T(8,128)(2,1)}, f32[256,128]{1,0:T(8,128)}, bf16[512,128]{1,0:T(8,128)(2,1)}, bf16[768,256]{1,0:T(8,128)(2,1)}) custom-call(bf16[128,1024]{1,0:T(8,128)(2,1)} %bitcast.19, bf16[2048,768]{1,0:T(8,128)(2,1)} %bitcast.15, bf16[16,1024]{1,0:T(8,128)(2,1)} %collective-permute-done.refs_2_, ...), custom_call_target="tpu_custom_call" | custom-call | flops 1000000000 | bytes 4194304 | tf_op jit(solution)/shard_map/pallas_call | solution.py:120
  15.0 1.7 %collective-permute-start.1 = (bf16[512,128]{1,0:T(8,128)(2,1)}, bf16[512,128]{1,0:T(8,128)(2,1)}, u32[]{:S(2)}, u32[]{:S(2)}) collective-permute-start(bf16[512,128]{1,0:T(8,128)(2,1)} %get-tuple-element.35.refs_3_), channel_id=1, source_target_pairs={{0,4},{4,8},{8,12},{12,16},{16,20},{20,24},{24,28},{28,32},{32,36}... | collective-permute-start | bytes 393224 | tf_op jit(solution)/shard_map/ppermute | solution.py:34
  16.7 5.6 %collective-permute-start.3 = (bf16[512,128]{1,0:T(8,128)(2,1)}, bf16[512,128]{1,0:T(8,128)(2,1)}, u32[]{:S(2)}, u32[]{:S(2)}) collective-permute-start(bf16[512,128]{1,0:T(8,128)(2,1)} %get-tuple-element.35.refs_3_), channel_id=1, source_target_pairs={{0,12},{4,16},{8,20},{12,24},{16,28},{20,32},{24,36},{28,40},{32,4... | collective-permute-start | bytes 393224 | tf_op jit(solution)/shard_map/ppermute | solution.py:34
  22.2 5.1 %collective-permute-done.1.refs_4_ = bf16[512,128]{1,0:T(8,128)(2,1)} collective-permute-done((bf16[512,128]{1,0:T(8,128)(2,1)}, bf16[512,128]{1,0:T(8,128)(2,1)}, u32[]{:S(2)}, u32[]{:S(2)}) %collective-permute-start.1) | collective-permute-done | bytes 131104 | tf_op jit(solution)/shard_map/ppermute | solution.py:34
  27.3 0.0 collective-permute-start.2
  27.3 0.0 collective-permute-done.6.refs_13_
  27.3 0.9 collective-permute-start.12
  28.2 0.0 collective-permute-done.5.refs_12_
  28.2 1.5 %collective-permute-start.11 = (bf16[768,256]{1,0:T(8,128)(2,1)}, bf16[768,256]{1,0:T(8,128)(2,1)}, u32[]{:S(2)}, u32[]{:S(2)}) collective-permute-start(bf16[768,256]{1,0:T(8,128)(2,1)} %get-tuple-element.51.refs_2_), channel_id=1, source_target_pairs={{0,2},{128,130},{2,0},{130,128},{1,3},{129,131},{3,1},{131,129},{4... | collective-permute-start | bytes 1179656 | tf_op jit(solution)/shard_map/ppermute | solution.py:40
  29.7 0.4 collective-permute-start.10
  30.1 3.2 %shard_map.121 = (f32[768,128]{1,0:T(8,128)}, bf16[768,128]{1,0:T(8,128)(2,1)}, bf16[768,128]{1,0:T(8,128)(2,1)}) custom-call(bf16[128,768]{1,0:T(8,128)(2,1)} %get-tuple-element.38.refs_0_, bf16[128,768]{1,0:T(8,128)(2,1)} %bitcast.23, bf16[768,1280]{1,0:T(8,128)(2,1)} %refs_5_.1, bf16[768,768]{1,0:T(8,128)(2,1)} %refs_3_.3), custom_call_target="tpu_custom_call" | custom-call | flops 1000000000 | bytes 4194304 | tf_op jit(solution)/shard_map/pallas_call | solution.py:120
  33.3 7.2 %collective-permute-done.2.refs_5_ = bf16[512,128]{1,0:T(8,128)(2,1)} collective-permute-done((bf16[512,128]{1,0:T(8,128)(2,1)}, bf16[512,128]{1,0:T(8,128)(2,1)}, u32[]{:S(2)}, u32[]{:S(2)}) %collective-permute-start.2) | collective-permute-done | bytes 131104 | tf_op jit(solution)/shard_map/ppermute | solution.py:34
  40.5 7.4 %shard_map.122 = (bf16[768,128]{1,0:T(8,128)(2,1)}, bf16[768,128]{1,0:T(8,128)(2,1)}, f32[512,128]{1,0:T(8,128)}, bf16[512,128]{1,0:T(8,128)(2,1)}, bf16[512,128]{1,0:T(8,128)(2,1)}, /*index=5*/bf16[512,128]{1,0:T(8,128)(2,1)}) custom-call(s32[1]{0:T(128)} %bitcast.2.refs_0_, f32[12]{0:T(128)} %refs_1_.1, s32[64,128]{1,0:T(8,128)} %bitcast.25, ...), custom_call_target="tpu_custom_call" | custom-call | flops 1000000000 | bytes 4194304 | tf_op jit(solution)/shard_map/pallas_call | solution.py:120
  47.9 1.0 collective-permute-start.7
  48.9 3.0 %collective-permute-start.8 = (bf16[512,128]{1,0:T(8,128)(2,1)}, bf16[512,128]{1,0:T(8,128)(2,1)}, u32[]{:S(2)}, u32[]{:S(2)}) collective-permute-start(bf16[512,128]{1,0:T(8,128)(2,1)} %get-tuple-element.47), channel_id=1, source_target_pairs={{0,248},{4,252},{8,0},{12,4},{16,8},{20,12},{24,16},{28,20},{32,24... | collective-permute-start | bytes 393224 | tf_op jit(solution)/shard_map/ppermute | solution.py:34
  51.9 0.3 collective-permute-done.7.refs_1_
  52.1 4.2 %collective-permute-start.9 = (bf16[512,128]{1,0:T(8,128)(2,1)}, bf16[512,128]{1,0:T(8,128)(2,1)}, u32[]{:S(2)}, u32[]{:S(2)}) collective-permute-start(bf16[512,128]{1,0:T(8,128)(2,1)} %get-tuple-element.48), channel_id=1, source_target_pairs={{0,244},{4,248},{8,252},{12,0},{16,4},{20,8},{24,12},{28,16},{32,2... | collective-permute-start | bytes 393224 | tf_op jit(solution)/shard_map/ppermute | solution.py:34
  56.3 2.6 %shard_map.123.refs_8_ = f32[128,768]{1,0:T(8,128)} custom-call(bf16[768,1280]{1,0:T(8,128)(2,1)} %refs_5_.1, bf16[768,128]{1,0:T(8,128)(2,1)} %get-tuple-element.52.refs_1_.refs_12_), custom_call_target="tpu_custom_call" | custom-call | flops 1000000000 | bytes 4194304 | tf_op jit(solution)/shard_map/pallas_call | solution.py:120
  59.0 4.5 %collective-permute-done.9.refs_3_ = bf16[512,128]{1,0:T(8,128)(2,1)} collective-permute-done((bf16[512,128]{1,0:T(8,128)(2,1)}, bf16[512,128]{1,0:T(8,128)(2,1)}, u32[]{:S(2)}, u32[]{:S(2)}) %collective-permute-start.9) | collective-permute-done | bytes 131104 | tf_op jit(solution)/shard_map/ppermute | solution.py:34
  63.5 4.4 %shard_map.124 = bf16[8,368,128]{2,1,0:T(8,128)(2,1)} custom-call(f32[512,128]{1,0:T(8,128)} %get-tuple-element.43.refs_0_, bf16[512,128]{1,0:T(8,128)(2,1)} %collective-permute-done.7.refs_1_, bf16[512,128]{1,0:T(8,128)(2,1)} %collective-permute-done.8.refs_2_, bf16[512,128]{1,0:T(8,128)(2,1)} %collective-permute-done.9.refs_3_, ...), custom_call_target="tpu_custom_call" | custom-call | flops 1000000000 | bytes 4194304 | tf_op jit(solution)/shard_map/pallas_call | solution.py:120
  67.9 10.2 %all-to-all-start = ((bf16[8,368,128]{2,1,0:T(8,128)(2,1)}), bf16[8,368,128]{2,1,0:T(8,128)(2,1)}, u32[]{:S(2)}, u32[]{:S(2)}) async-start(bf16[8,368,128]{2,1,0:T(8,128)(2,1)} %shard_map.124), calls=%async_computation | async-start | bytes 1507328 | tf_op jit(solution)/shard_map/all_to_all | solution.py:50
  78.1 0.2 collective-permute-start.13
  78.3 0.3 collective-permute-start.17
  78.6 0.2 collective-permute-start.18
  78.8 0.3 collective-permute-start.14
  79.1 0.2 collective-permute-start.15
  79.3 1.2 collective-permute-done.17.refs_14_
  80.5 0.2 collective-permute-start.16
  80.7 0.3 collective-permute-start.19
  81.0 0.2 collective-permute-start.20
  81.3 0.6 pad_add_fusion.refs_0_
  81.8 1.1 collective-permute-done.19.refs_16_
  83.0 0.4 collective-permute-done.20.refs_17_
  83.3 5.4 %all-to-all-done.refs_1_ = bf16[8,368,128]{2,1,0:T(8,128)(2,1)} async-done(((bf16[8,368,128]{2,1,0:T(8,128)(2,1)}), bf16[8,368,128]{2,1,0:T(8,128)(2,1)}, u32[]{:S(2)}, u32[]{:S(2)}) %all-to-all-start) | async-done | bytes 753696 | tf_op jit(solution)/shard_map/all_to_all | solution.py:50
  88.8 7.5 %shard_map.125 = bf16[3328,128]{1,0:T(8,128)(2,1)} custom-call(s32[2]{0:T(128)} %pad_add_fusion.refs_0_, bf16[8,368,128]{2,1,0:T(8,128)(2,1)} %all-to-all-done.refs_1_, bf16[768,256]{1,0:T(8,128)(2,1)} %get-tuple-element.51.refs_2_, bf16[768,256]{1,0:T(8,128)(2,1)} %collective-permute-done.10.refs_3_, bf16[768,256]{1,0:T(8,128)(2,1)} %collective-permute-done.11.refs_4_, ...), custom_call_target="tpu_custom_call" | custom-call | flops 1000000000 | bytes 4194304 | tf_op jit(solution)/shard_map/pallas_call | solution.py:120
  96.3 8.3 %all-to-all-start.1 = ((bf16[32,104,128]{2,1,0:T(8,128)(2,1)}), bf16[32,104,128]{2,1,0:T(8,128)(2,1)S(1)}, u32[]{:S(2)}, u32[]{:S(2)}) async-start(bf16[32,104,128]{2,1,0:T(8,128)(2,1)} %bitcast.14), calls=%async_computation.1 | async-start | bytes 1703936 | tf_op jit(solution)/shard_map/all_to_all | solution.py:50
  104.7 20.2 %all-to-all-done.1.refs_0_ = bf16[32,104,128]{2,1,0:T(8,128)(2,1)S(1)} async-done(((bf16[32,104,128]{2,1,0:T(8,128)(2,1)}), bf16[32,104,128]{2,1,0:T(8,128)(2,1)S(1)}, u32[]{:S(2)}, u32[]{:S(2)}) %all-to-all-start.1) | async-done | bytes 852000 | tf_op jit(solution)/shard_map/all_to_all | solution.py:50
  124.9 1.9 %shard_map.126 = (f32[3,2,1024]{2,1,0:T(2,128)}, f32[1,768]{1,0:T(1,128)S(1)}, f32[8,8,256]{2,1,0:T(8,128)}) custom-call(bf16[32,104,128]{2,1,0:T(8,128)(2,1)S(1)} %all-to-all-done.1.refs_0_), custom_call_target="tpu_custom_call" | custom-call | flops 1000000000 | bytes 4194304 | tf_op jit(solution)/shard_map/pallas_call | solution.py:120
  126.7 9.3 %all-to-all-start.2 = ((f32[8,8,256]{2,1,0:T(8,128)}), f32[8,8,256]{2,1,0:T(8,128)S(1)}, u32[]{:S(2)}, u32[]{:S(2)}) async-start(f32[8,8,256]{2,1,0:T(8,128)} %get-tuple-element.63), calls=%async_computation.2 | async-start | bytes 131072 | tf_op jit(solution)/shard_map/all_to_all | solution.py:50
  136.1 0.6 dynamic-slice_bitcast_fusion
  136.7 4.1 %all-to-all-done.2.refs_0_ = f32[8,8,256]{2,1,0:T(8,128)S(1)} async-done(((f32[8,8,256]{2,1,0:T(8,128)}), f32[8,8,256]{2,1,0:T(8,128)S(1)}, u32[]{:S(2)}, u32[]{:S(2)}) %all-to-all-start.2) | async-done | bytes 65568 | tf_op jit(solution)/shard_map/all_to_all | solution.py:50
  140.8 0.8 shard_map.127
  (12 shorter events, 0.0 us)
Async XLA Ops:
  1.4 9.1 %collective-permute-start = (bf16[16,1024]{1,0:T(8,128)(2,1)S(1)}, bf16[16,1024]{1,0:T(8,128)(2,1)}, u32[]{:S(2)}, u32[]{:S(2)}) collective-permute-start(bf16[16,1024]{1,0:T(8,128)(2,1)S(1)} %slice_bitcast_fusion), channel_id=1, source_target_pairs={{1,0},{2,1},{3,2},{5,4},{6,5},{7,6},{9,8},{10,9},{11,10},{13,12},{... | collective-permute-start | bytes 98312 | tf_op jit(solution)/shard_map/ppermute | solution.py:357
  6.5 20.8 %collective-permute-start.6 = (bf16[128,1024]{1,0:T(8,128)(2,1)}, bf16[128,1024]{1,0:T(8,128)(2,1)}, u32[]{:S(2)}, u32[]{:S(2)}) collective-permute-start(bf16[128,1024]{1,0:T(8,128)(2,1)} %bitcast.16), channel_id=1, source_target_pairs={{0,130},{128,0},{2,128},{130,2},{1,131},{129,1},{3,129},{131,3},{4... | collective-permute-start | bytes 786440 | tf_op jit(solution)/shard_map/ppermute | solution.py:40
  8.1 20.1 %collective-permute-start.5 = (bf16[128,1024]{1,0:T(8,128)(2,1)}, bf16[128,1024]{1,0:T(8,128)(2,1)}, u32[]{:S(2)}, u32[]{:S(2)}) collective-permute-start(bf16[128,1024]{1,0:T(8,128)(2,1)} %bitcast.17), channel_id=1, source_target_pairs={{0,2},{128,130},{2,0},{130,128},{1,3},{129,131},{3,1},{131,129},{4... | collective-permute-start | bytes 786440 | tf_op jit(solution)/shard_map/ppermute | solution.py:40
  8.3 21.4 %collective-permute-start.4 = (bf16[128,1024]{1,0:T(8,128)(2,1)}, bf16[128,1024]{1,0:T(8,128)(2,1)}, u32[]{:S(2)}, u32[]{:S(2)}) collective-permute-start(bf16[128,1024]{1,0:T(8,128)(2,1)} %bitcast.18), channel_id=1, source_target_pairs={{0,128},{128,2},{2,130},{130,0},{1,129},{129,3},{3,131},{131,1},{4... | collective-permute-start | bytes 786440 | tf_op jit(solution)/shard_map/ppermute | solution.py:40
  15.0 12.3 %collective-permute-start.1 = (bf16[512,128]{1,0:T(8,128)(2,1)}, bf16[512,128]{1,0:T(8,128)(2,1)}, u32[]{:S(2)}, u32[]{:S(2)}) collective-permute-start(bf16[512,128]{1,0:T(8,128)(2,1)} %get-tuple-element.35.refs_3_), channel_id=1, source_target_pairs={{0,4},{4,8},{8,12},{12,16},{16,20},{20,24},{24,28},{28,32},{32,36}... | collective-permute-start | bytes 393224 | tf_op jit(solution)/shard_map/ppermute | solution.py:34
  16.7 16.6 %collective-permute-start.3 = (bf16[512,128]{1,0:T(8,128)(2,1)}, bf16[512,128]{1,0:T(8,128)(2,1)}, u32[]{:S(2)}, u32[]{:S(2)}) collective-permute-start(bf16[512,128]{1,0:T(8,128)(2,1)} %get-tuple-element.35.refs_3_), channel_id=1, source_target_pairs={{0,12},{4,16},{8,20},{12,24},{16,28},{20,32},{24,36},{28,40},{32,4... | collective-permute-start | bytes 393224 | tf_op jit(solution)/shard_map/ppermute | solution.py:34
  27.3 13.2 %collective-permute-start.2 = (bf16[512,128]{1,0:T(8,128)(2,1)}, bf16[512,128]{1,0:T(8,128)(2,1)}, u32[]{:S(2)}, u32[]{:S(2)}) collective-permute-start(bf16[512,128]{1,0:T(8,128)(2,1)} %get-tuple-element.35.refs_3_), channel_id=1, source_target_pairs={{0,8},{4,12},{8,16},{12,20},{16,24},{20,28},{24,32},{28,36},{32,40... | collective-permute-start | bytes 393224 | tf_op jit(solution)/shard_map/ppermute | solution.py:34
  27.3 31.7 %collective-permute-start.12 = (bf16[768,256]{1,0:T(8,128)(2,1)}, bf16[768,256]{1,0:T(8,128)(2,1)}, u32[]{:S(2)}, u32[]{:S(2)}) collective-permute-start(bf16[768,256]{1,0:T(8,128)(2,1)} %get-tuple-element.51.refs_2_), channel_id=1, source_target_pairs={{0,130},{128,0},{2,128},{130,2},{1,131},{129,1},{3,129},{131,3},{4... | collective-permute-start | bytes 1179656 | tf_op jit(solution)/shard_map/ppermute | solution.py:40
  28.2 30.7 %collective-permute-start.11 = (bf16[768,256]{1,0:T(8,128)(2,1)}, bf16[768,256]{1,0:T(8,128)(2,1)}, u32[]{:S(2)}, u32[]{:S(2)}) collective-permute-start(bf16[768,256]{1,0:T(8,128)(2,1)} %get-tuple-element.51.refs_2_), channel_id=1, source_target_pairs={{0,2},{128,130},{2,0},{130,128},{1,3},{129,131},{3,1},{131,129},{4... | collective-permute-start | bytes 1179656 | tf_op jit(solution)/shard_map/ppermute | solution.py:40
  29.7 29.3 %collective-permute-start.10 = (bf16[768,256]{1,0:T(8,128)(2,1)}, bf16[768,256]{1,0:T(8,128)(2,1)}, u32[]{:S(2)}, u32[]{:S(2)}) collective-permute-start(bf16[768,256]{1,0:T(8,128)(2,1)} %get-tuple-element.51.refs_2_), channel_id=1, source_target_pairs={{0,128},{128,2},{2,130},{130,0},{1,129},{129,3},{3,131},{131,1},{4... | collective-permute-start | bytes 1179656 | tf_op jit(solution)/shard_map/ppermute | solution.py:40
  47.9 4.2 %collective-permute-start.7 = (bf16[512,128]{1,0:T(8,128)(2,1)}, bf16[512,128]{1,0:T(8,128)(2,1)}, u32[]{:S(2)}, u32[]{:S(2)}) collective-permute-start(bf16[512,128]{1,0:T(8,128)(2,1)} %get-tuple-element.44), channel_id=1, source_target_pairs={{0,252},{4,0},{8,4},{12,8},{16,12},{20,16},{24,20},{28,24},{32,28}... | collective-permute-start | bytes 393224 | tf_op jit(solution)/shard_map/ppermute | solution.py:34
  48.9 10.1 %collective-permute-start.8 = (bf16[512,128]{1,0:T(8,128)(2,1)}, bf16[512,128]{1,0:T(8,128)(2,1)}, u32[]{:S(2)}, u32[]{:S(2)}) collective-permute-start(bf16[512,128]{1,0:T(8,128)(2,1)} %get-tuple-element.47), channel_id=1, source_target_pairs={{0,248},{4,252},{8,0},{12,4},{16,8},{20,12},{24,16},{28,20},{32,24... | collective-permute-start | bytes 393224 | tf_op jit(solution)/shard_map/ppermute | solution.py:34
  52.1 11.4 %collective-permute-start.9 = (bf16[512,128]{1,0:T(8,128)(2,1)}, bf16[512,128]{1,0:T(8,128)(2,1)}, u32[]{:S(2)}, u32[]{:S(2)}) collective-permute-start(bf16[512,128]{1,0:T(8,128)(2,1)} %get-tuple-element.48), channel_id=1, source_target_pairs={{0,244},{4,248},{8,252},{12,0},{16,4},{20,8},{24,12},{28,16},{32,2... | collective-permute-start | bytes 393224 | tf_op jit(solution)/shard_map/ppermute | solution.py:34
  67.9 20.9 %all-to-all-start = ((bf16[8,368,128]{2,1,0:T(8,128)(2,1)}), bf16[8,368,128]{2,1,0:T(8,128)(2,1)}, u32[]{:S(2)}, u32[]{:S(2)}) async-start(bf16[8,368,128]{2,1,0:T(8,128)(2,1)} %shard_map.124), calls=%async_computation | async-start | bytes 1507328 | tf_op jit(solution)/shard_map/all_to_all | solution.py:50
  78.1 2.7 %collective-permute-start.13 = (bf16[768,256]{1,0:T(8,128)(2,1)}, bf16[768,256]{1,0:T(8,128)(2,1)}, u32[]{:S(2)}, u32[]{:S(2)}) collective-permute-start(bf16[768,256]{1,0:T(8,128)(2,1)} %get-tuple-element.51.refs_2_), channel_id=1, source_target_pairs={{0,1},{1,0},{2,3},{3,2},{4,5},{5,4},{6,7},{7,6},{8,9},{9,8},{10,11... | collective-permute-start | bytes 1179656 | tf_op jit(solution)/shard_map/ppermute | solution.py:46
  78.3 2.2 %collective-permute-start.17 = (bf16[128,1024]{1,0:T(8,128)(2,1)}, bf16[128,1024]{1,0:T(8,128)(2,1)}, u32[]{:S(2)}, u32[]{:S(2)}) collective-permute-start(bf16[128,1024]{1,0:T(8,128)(2,1)} %bitcast.20), channel_id=1, source_target_pairs={{0,1},{1,0},{2,3},{3,2},{4,5},{5,4},{6,7},{7,6},{8,9},{9,8},{10,11... | collective-permute-start | bytes 786440 | tf_op jit(solution)/shard_map/ppermute | solution.py:46
  78.6 2.4 %collective-permute-start.18 = (bf16[128,1024]{1,0:T(8,128)(2,1)}, bf16[128,1024]{1,0:T(8,128)(2,1)}, u32[]{:S(2)}, u32[]{:S(2)}) collective-permute-start(bf16[128,1024]{1,0:T(8,128)(2,1)} %collective-permute-done.4.refs_11_), channel_id=1, source_target_pairs={{0,1},{1,0},{2,3},{3,2},{4,5},{5,4},{6,7},{7,6},{8,9},{9,8},{10,11... | collective-permute-start | bytes 786440 | tf_op jit(solution)/shard_map/ppermute | solution.py:46
  78.8 4.5 %collective-permute-start.14 = (bf16[768,256]{1,0:T(8,128)(2,1)}, bf16[768,256]{1,0:T(8,128)(2,1)}, u32[]{:S(2)}, u32[]{:S(2)}) collective-permute-start(bf16[768,256]{1,0:T(8,128)(2,1)} %collective-permute-done.10.refs_3_), channel_id=1, source_target_pairs={{0,1},{1,0},{2,3},{3,2},{4,5},{5,4},{6,7},{7,6},{8,9},{9,8},{10,11... | collective-permute-start | bytes 1179656 | tf_op jit(solution)/shard_map/ppermute | solution.py:46
  79.1 4.2 %collective-permute-start.15 = (bf16[768,256]{1,0:T(8,128)(2,1)}, bf16[768,256]{1,0:T(8,128)(2,1)}, u32[]{:S(2)}, u32[]{:S(2)}) collective-permute-start(bf16[768,256]{1,0:T(8,128)(2,1)} %collective-permute-done.11.refs_4_), channel_id=1, source_target_pairs={{0,1},{1,0},{2,3},{3,2},{4,5},{5,4},{6,7},{7,6},{8,9},{9,8},{10,11... | collective-permute-start | bytes 1179656 | tf_op jit(solution)/shard_map/ppermute | solution.py:46
  80.5 2.8 %collective-permute-start.16 = (bf16[768,256]{1,0:T(8,128)(2,1)}, bf16[768,256]{1,0:T(8,128)(2,1)}, u32[]{:S(2)}, u32[]{:S(2)}) collective-permute-start(bf16[768,256]{1,0:T(8,128)(2,1)} %collective-permute-done.12.refs_5_), channel_id=1, source_target_pairs={{0,1},{1,0},{2,3},{3,2},{4,5},{5,4},{6,7},{7,6},{8,9},{9,8},{10,11... | collective-permute-start | bytes 1179656 | tf_op jit(solution)/shard_map/ppermute | solution.py:46
  80.7 2.2 %collective-permute-start.19 = (bf16[128,1024]{1,0:T(8,128)(2,1)}, bf16[128,1024]{1,0:T(8,128)(2,1)}, u32[]{:S(2)}, u32[]{:S(2)}) collective-permute-start(bf16[128,1024]{1,0:T(8,128)(2,1)} %collective-permute-done.5.refs_12_), channel_id=1, source_target_pairs={{0,1},{1,0},{2,3},{3,2},{4,5},{5,4},{6,7},{7,6},{8,9},{9,8},{10,11... | collective-permute-start | bytes 786440 | tf_op jit(solution)/shard_map/ppermute | solution.py:46
  81.0 2.3 %collective-permute-start.20 = (bf16[128,1024]{1,0:T(8,128)(2,1)}, bf16[128,1024]{1,0:T(8,128)(2,1)}, u32[]{:S(2)}, u32[]{:S(2)}) collective-permute-start(bf16[128,1024]{1,0:T(8,128)(2,1)} %collective-permute-done.6.refs_13_), channel_id=1, source_target_pairs={{0,1},{1,0},{2,3},{3,2},{4,5},{5,4},{6,7},{7,6},{8,9},{9,8},{10,11... | collective-permute-start | bytes 786440 | tf_op jit(solution)/shard_map/ppermute | solution.py:46
  96.3 28.5 %all-to-all-start.1 = ((bf16[32,104,128]{2,1,0:T(8,128)(2,1)}), bf16[32,104,128]{2,1,0:T(8,128)(2,1)S(1)}, u32[]{:S(2)}, u32[]{:S(2)}) async-start(bf16[32,104,128]{2,1,0:T(8,128)(2,1)} %bitcast.14), calls=%async_computation.1 | async-start | bytes 1703936 | tf_op jit(solution)/shard_map/all_to_all | solution.py:50
  126.7 14.0 %all-to-all-start.2 = ((f32[8,8,256]{2,1,0:T(8,128)}), f32[8,8,256]{2,1,0:T(8,128)S(1)}, u32[]{:S(2)}, u32[]{:S(2)}) async-start(f32[8,8,256]{2,1,0:T(8,128)} %get-tuple-element.63), calls=%async_computation.2 | async-start | bytes 131072 | tf_op jit(solution)/shard_map/all_to_all | solution.py:50

commit v7 on v6

--- a/solution.py
+++ b/solution.py
@@ -1,6 +1,5 @@
 import jax
 import jax.numpy as jnp
-import numpy as np
 from jax import lax
 from jax.experimental import pallas as pl
 from jax.experimental.pallas import tpu as pltpu
@@ -50,11 +49,6 @@
     return lax.all_to_all(x, axes, split_axis=0, concat_axis=0, tiled=True)
 
 
-def member_order():
-    column = np.arange(D).reshape(2, 32, 4, 3).transpose(0, 2, 1, 3).reshape(-1)
-    return jnp.asarray(np.eye(D, dtype=np.float32)[column], B16)
-
-
 class Loaded:
     def __init__(self, ref, pieces):
         self.ref, self.pieces = ref, pieces
@@ -77,12 +71,19 @@
     return [slice(i * rows, i * rows + rows) for i in range(count)]
 
 
-def call(body, outs, scratch=(), smem=(), pieces=None, columns=None, limit=64, flops=10**9):
+def call(
+    body, outs, scratch=(), smem=(), pieces=None, columns=None, joined=None, limit=64, flops=10**9
+):
     pieces, columns = pieces or {}, columns or {}
 
     def run(*operands):
         held, parts, total = [], [], 0
-        for i, operand in enumerate(operands):
+        count = len(operands) if joined is None else joined
+        if joined is not None:
+            rows, width = operands[joined].shape
+            held.append(pltpu.VMEM(((len(operands) - joined) * rows, width), operands[joined].dtype))
+            total += len(operands) - joined
+        for i, operand in enumerate(operands[:count]):
             if i in smem:
                 continue
             shape = operand.shape
@@ -97,6 +98,14 @@
             others = refs[len(operands) : len(refs) - len(held) - 1]
             stores, sems = refs[len(refs) - len(held) - 1 : -1], refs[-1]
             used = 0
+            if joined is not None:
+                used, made = len(operands) - joined, []
+                for i, place in enumerate(split(stores[0].shape, used)):
+                    made.append(
+                        (pltpu.make_async_copy(inputs[joined + i], stores[0].at[place], sems.at[i]), place)
+                    )
+                inputs[joined:] = [Loaded(stores[0], made)]
+                stores = stores[1:]
             for (i, places), store in zip(parts, stores):
                 source = inputs[i]
                 if i in columns:
@@ -110,6 +119,9 @@
                     made.append((copy, place))
                     used += 1
                 inputs[i] = Loaded(store, made)
+            if joined is not None:
+                for copy, _ in inputs[joined].pieces:
+                    copy.start()
             body(*inputs, *others)
             for value in inputs:
                 if isinstance(value, Loaded):
@@ -233,8 +245,8 @@
 
 
 def tokens_body(
-    own, back1, back2, back3, key, w_kv, tokens, gain, part, d_out, by_member, attn, dq,
-    late_o, dkv_s,
+    own, back1, back2, back3, key, w_kv, tokens, gain, part, d_out, attn, dq,
+    late_o, dkv_s, tokens_s,
 ):
     total = own[...] + back1[...].astype(F32) + back2[...].astype(F32) + back3[...].astype(F32)
     for h in range(KEY_VALUE_HEADS):
@@ -251,14 +263,15 @@
     gain_term = jnp.sum(d_hidden * (tok * r), axis=0, keepdims=True)
     dx = d_hidden * gain[...].astype(F32)
     inner = jnp.mean(tok * dx, axis=1, keepdims=True)
-    d_tokens = (d_out[...].astype(F32) + (r * dx - tok * (r * r * r * inner))).astype(B16)
-    spread = dot(by_member[...], d_tokens, NT).astype(B16)
+    tokens_s[...] = (d_out[...].astype(F32) + (r * dx - tok * (r * r * r * inner))).T
     gains = jnp.concatenate(
         [gain_term[:, i * TOK : i * TOK + TOK] for i in range(6)] + [jnp.zeros((10, TOK), F32)],
         axis=0,
     ).astype(B16)
     for m in range(8):
-        late_o[m, :96, :] = spread[m * 96 : m * 96 + 96]
+        for k in range(3):
+            picked = tokens_s[pl.ds(m // 4 * 384 + m % 4 * 3 + k, 32, stride=12), :]
+            late_o[m, k * 32 : k * 32 + 32, :] = picked.astype(B16)
         late_o[m, 96:128, :] = dkv_s[m * 32 : m * 32 + 32, :]
         late_o[m, 128:160, :] = dkv_s[256 + m * 32 : 288 + m * 32, :]
         late_o[m, 160:176, :] = gains
@@ -269,8 +282,8 @@
 def terms_body(
     place, late, *rest
 ):
-    rings, tiles = rest[:8], rest[8:16]
-    terms_o, pair_s, rhs_s, sums_s, all_s = rest[16:]
+    rings, tiles = rest[:8], rest[8]
+    terms_o, both_s, pair_s, rhs_s, sums_s, all_s = rest[9:]
     lane = lax.broadcasted_iota(jnp.int32, (96, TOK), 1)
     gain = jnp.zeros((16, TOK), F32)
     zero = jnp.zeros((TOK, TOK), B16)
@@ -308,13 +321,13 @@
     for i in range(8):
         row = gain[i : i + 1, :]
         all_s[pl.ds(96 + i, 32, stride=104), :] = jnp.broadcast_to(row, (32, TOK))
-    stem = jnp.zeros((192, 1024), F32)
-    for tile, m in zip(tiles, members):
-        stem = stem + dot(pair_s[m], tile[...])
+    for i, m in enumerate(members):
+        both_s[:, i * TOK : i * TOK + TOK] = pair_s[m]
+        tiles.piece(i)
+    stem = dot(both_s[...], tiles[...])
     for c in range(8):
-        sums_s[0, :192, :] = stem[:, c * TOK : c * TOK + TOK]
         for i in range(6):
-            picked = sums_s[0, pl.ds(i // 3 * 96 + i % 3, 32, stride=3), :]
+            picked = stem[i * 32 : i * 32 + 32, c * TOK : c * TOK + TOK]
             all_s[pl.ds(i * 8 + c, 32, stride=104), :] = picked
     terms_o[...] = all_s[...].astype(B16)
 
@@ -352,7 +365,6 @@
 def shards(patches, stem_weight, norm_gain, w_qkv, w_out, per_head_scale, positions, d_out):
     tiles = patches[0]
     grad_out = d_out[0]
-    by_member = member_order()
     bands = lax.axis_size(BAND)
     arrived = lax.ppermute(tiles[:TC], BAND, [(i, i - 1) for i in range(1, bands)])
     tiles_mine = from_chips(tiles)
@@ -392,10 +404,10 @@
     late = call(
         tokens_body,
         [((8, 368, TOK), B16)],
-        scratch=[pltpu.VMEM((KV, TOK), B16)],
-        pieces={5: 2, 10: 2},
+        scratch=[pltpu.VMEM((KV, TOK), B16), pltpu.VMEM((D, TOK), F32)],
+        pieces={5: 2},
         columns={5: (D, D + KV)},
-    )(own, *returned, key, w_qkv, tokens, gain, part, grad_out, by_member, attn, d_q)[0]
+    )(own, *returned, key, w_qkv, tokens, gain, part, grad_out, attn, d_q)[0]
     late_ring = exchange(late, RING)
     rings = [ring_own, *ring_mine]
     blocks = [tiles, *tiles_mine]
@@ -407,12 +419,14 @@
         terms_body,
         [((32 * 104, TOK), B16)],
         scratch=[
+            pltpu.VMEM((192, 1024), B16),
             pltpu.VMEM((8, 192, TOK), B16),
             pltpu.VMEM((8, 256, 256), B16),
             pltpu.VMEM((2, D, TOK), F32),
             pltpu.VMEM((32 * 104, TOK), F32),
         ],
         smem=(0,),
+        joined=10,
     )(place, late_ring, *rings, *blocks)[0]
     stem_total, gain_total, row_total = call(
         total_body,

time: 142 us -> 141 us (level)
  Pallas kernels: 32.2 us -> 30.6 us
    pallas_call x8, Pallas kernels: 32.2 us -> 30.6 us  [run(): pl.pallas_call(kernel, out_shape=shapes, in_specs=[pl.BlockSpec(memory_sp...]
  transfers between devices with their start and end apart: 24 -> 24, of which waited for: 10 -> 10; matrix products, arithmetic and copies ran while one was open for 2% -> 2% of each run, Pallas kernels for 12% -> 13%
where the time goes in v7:
time: 141 us; the launch traced here: 140 us
  starting transfers between devices  55.8 us (40%)
  waiting for transfers between devices  49.5 us (35%)
  Pallas kernels  30.6 us (22%)
  local copies, waits for them, and re-layouts  2.61 us (2%)
    pallas_call x8, Pallas kernels, run(): pl.pallas_call(kernel, out_shape=shapes, in_specs=[pl.BlockSpec(memory_sp...  30.6 us
    all_to_all x3, waiting for transfers between devices, exchange(): return lax.all_to_all(x, axes, split_axis=0, concat_axis=0, tiled=True)  29.7 us
    all_to_all x3, starting transfers between devices, exchange(): return lax.all_to_all(x, axes, split_axis=0, concat_axis=0, tiled=True)  27.9 us
    ppermute x6, waiting for transfers between devices, passed_along(): return lax.ppermute(x, BLK, [(i, (i + by) % peers) for i in range(peers)])  17.1 us
    ppermute x6, starting transfers between devices, passed_along(): return lax.ppermute(x, BLK, [(i, (i + by) % peers) for i in range(peers)])  15.4 us
    ppermute x6, starting transfers between devices, from_chips(): lax.ppermute(x, CHIPS, [(order[i], order[(i + by) % 4]) for i in range(4)])  5.43 us
    ppermute x1, starting transfers between devices, shards(): lax.ppermute(tiles[:TC], BAND, [(i, i - 1) for i in range(1, bands)])  5.14 us
  transfers between devices with their start and end apart: 24, of which 10 were waited for; matrix products, arithmetic and copies ran while one was open for 2% of the time, Pallas kernels for 13%

profile of v7, /device:TPU:1, one launch (start us, length us, event | category | flops | bytes accessed | tf_op | source)
XLA Modules:
  0.0 140.1 jit_solution(1837540830658035178)
XLA Ops:
  0.6 0.8 slice_bitcast_fusion
  1.4 5.1 %collective-permute-start = (bf16[16,1024]{1,0:T(8,128)(2,1)S(1)}, bf16[16,1024]{1,0:T(8,128)(2,1)}, u32[]{:S(2)}, u32[]{:S(2)}) collective-permute-start(bf16[16,1024]{1,0:T(8,128)(2,1)S(1)} %slice_bitcast_fusion), channel_id=1, source_target_pairs={{1,0},{2,1},{3,2},{5,4},{6,5},{7,6},{9,8},{10,9},{11,10},{13,12},{... | collective-permute-start | bytes 98312 | tf_op jit(solution)/shard_map/ppermute | solution.py:369
  6.5 1.6 %collective-permute-start.6 = (bf16[128,1024]{1,0:T(8,128)(2,1)}, bf16[128,1024]{1,0:T(8,128)(2,1)}, u32[]{:S(2)}, u32[]{:S(2)}) collective-permute-start(bf16[128,1024]{1,0:T(8,128)(2,1)} %bitcast.16), channel_id=1, source_target_pairs={{0,130},{128,0},{2,128},{130,2},{1,131},{129,1},{3,129},{131,3},{4... | collective-permute-start | bytes 786440 | tf_op jit(solution)/shard_map/ppermute | solution.py:39
  8.1 0.2 collective-permute-start.5
  8.3 0.9 collective-permute-start.4
  9.2 1.3 reshape.28.refs_4_.refs_7_
  10.4 4.5 %shard_map.111 = (bf16[128,768]{1,0:T(8,128)(2,1)}, bf16[128,768]{1,0:T(8,128)(2,1)}, f32[256,128]{1,0:T(8,128)}, bf16[512,128]{1,0:T(8,128)(2,1)}, bf16[768,256]{1,0:T(8,128)(2,1)}) custom-call(bf16[128,1024]{1,0:T(8,128)(2,1)} %bitcast.19, bf16[2048,768]{1,0:T(8,128)(2,1)} %bitcast.15, bf16[16,1024]{1,0:T(8,128)(2,1)} %collective-permute-done.refs_2_, ...), custom_call_target="tpu_custom_call" | custom-call | flops 1000000000 | bytes 4194304 | tf_op jit(solution)/shard_map/pallas_call | solution.py:132
  15.0 1.7 %collective-permute-start.1 = (bf16[512,128]{1,0:T(8,128)(2,1)}, bf16[512,128]{1,0:T(8,128)(2,1)}, u32[]{:S(2)}, u32[]{:S(2)}) collective-permute-start(bf16[512,128]{1,0:T(8,128)(2,1)} %get-tuple-element.35.refs_3_), channel_id=1, source_target_pairs={{0,4},{4,8},{8,12},{12,16},{16,20},{20,24},{24,28},{28,32},{32,36}... | collective-permute-start | bytes 393224 | tf_op jit(solution)/shard_map/ppermute | solution.py:33
  16.7 5.6 %collective-permute-start.3 = (bf16[512,128]{1,0:T(8,128)(2,1)}, bf16[512,128]{1,0:T(8,128)(2,1)}, u32[]{:S(2)}, u32[]{:S(2)}) collective-permute-start(bf16[512,128]{1,0:T(8,128)(2,1)} %get-tuple-element.35.refs_3_), channel_id=1, source_target_pairs={{0,12},{4,16},{8,20},{12,24},{16,28},{20,32},{24,36},{28,40},{32,4... | collective-permute-start | bytes 393224 | tf_op jit(solution)/shard_map/ppermute | solution.py:33
  22.2 5.1 %collective-permute-done.1.refs_4_ = bf16[512,128]{1,0:T(8,128)(2,1)} collective-permute-done((bf16[512,128]{1,0:T(8,128)(2,1)}, bf16[512,128]{1,0:T(8,128)(2,1)}, u32[]{:S(2)}, u32[]{:S(2)}) %collective-permute-start.1) | collective-permute-done | bytes 131104 | tf_op jit(solution)/shard_map/ppermute | solution.py:33
  27.3 0.0 collective-permute-start.2
  27.3 0.0 collective-permute-done.6.refs_13_
  27.3 0.9 collective-permute-start.12
  28.2 0.0 collective-permute-done.5.refs_12_
  28.2 1.5 %collective-permute-start.11 = (bf16[768,256]{1,0:T(8,128)(2,1)}, bf16[768,256]{1,0:T(8,128)(2,1)}, u32[]{:S(2)}, u32[]{:S(2)}) collective-permute-start(bf16[768,256]{1,0:T(8,128)(2,1)} %get-tuple-element.51.refs_2_), channel_id=1, source_target_pairs={{0,2},{128,130},{2,0},{130,128},{1,3},{129,131},{3,1},{131,129},{4... | collective-permute-start | bytes 1179656 | tf_op jit(solution)/shard_map/ppermute | solution.py:39
  29.7 0.4 collective-permute-start.10
  30.1 3.2 %shard_map.112 = (f32[768,128]{1,0:T(8,128)}, bf16[768,128]{1,0:T(8,128)(2,1)}, bf16[768,128]{1,0:T(8,128)(2,1)}) custom-call(bf16[128,768]{1,0:T(8,128)(2,1)} %get-tuple-element.38.refs_0_, bf16[128,768]{1,0:T(8,128)(2,1)} %bitcast.23, bf16[768,1280]{1,0:T(8,128)(2,1)} %refs_5_.1, bf16[768,768]{1,0:T(8,128)(2,1)} %refs_3_.3), custom_call_target="tpu_custom_call" | custom-call | flops 1000000000 | bytes 4194304 | tf_op jit(solution)/shard_map/pallas_call | solution.py:132
  33.3 7.2 %collective-permute-done.2.refs_5_ = bf16[512,128]{1,0:T(8,128)(2,1)} collective-permute-done((bf16[512,128]{1,0:T(8,128)(2,1)}, bf16[512,128]{1,0:T(8,128)(2,1)}, u32[]{:S(2)}, u32[]{:S(2)}) %collective-permute-start.2) | collective-permute-done | bytes 131104 | tf_op jit(solution)/shard_map/ppermute | solution.py:33
  40.5 7.4 %shard_map.113 = (bf16[768,128]{1,0:T(8,128)(2,1)}, bf16[768,128]{1,0:T(8,128)(2,1)}, f32[512,128]{1,0:T(8,128)}, bf16[512,128]{1,0:T(8,128)(2,1)}, bf16[512,128]{1,0:T(8,128)(2,1)}, /*index=5*/bf16[512,128]{1,0:T(8,128)(2,1)}) custom-call(s32[1]{0:T(128)} %bitcast.2.refs_0_, f32[12]{0:T(128)} %refs_1_.1, s32[64,128]{1,0:T(8,128)} %bitcast.25, ...), custom_call_target="tpu_custom_call" | custom-call | flops 1000000000 | bytes 4194304 | tf_op jit(solution)/shard_map/pallas_call | solution.py:132
  47.9 1.0 collective-permute-start.7
  48.9 3.0 %collective-permute-start.8 = (bf16[512,128]{1,0:T(8,128)(2,1)}, bf16[512,128]{1,0:T(8,128)(2,1)}, u32[]{:S(2)}, u32[]{:S(2)}) collective-permute-start(bf16[512,128]{1,0:T(8,128)(2,1)} %get-tuple-element.47), channel_id=1, source_target_pairs={{0,248},{4,252},{8,0},{12,4},{16,8},{20,12},{24,16},{28,20},{32,24... | collective-permute-start | bytes 393224 | tf_op jit(solution)/shard_map/ppermute | solution.py:33
  51.9 0.3 collective-permute-done.7.refs_1_
  52.1 4.2 %collective-permute-start.9 = (bf16[512,128]{1,0:T(8,128)(2,1)}, bf16[512,128]{1,0:T(8,128)(2,1)}, u32[]{:S(2)}, u32[]{:S(2)}) collective-permute-start(bf16[512,128]{1,0:T(8,128)(2,1)} %get-tuple-element.48), channel_id=1, source_target_pairs={{0,244},{4,248},{8,252},{12,0},{16,4},{20,8},{24,12},{28,16},{32,2... | collective-permute-start | bytes 393224 | tf_op jit(solution)/shard_map/ppermute | solution.py:33
  56.3 2.6 %shard_map.114.refs_8_ = f32[128,768]{1,0:T(8,128)} custom-call(bf16[768,1280]{1,0:T(8,128)(2,1)} %refs_5_.1, bf16[768,128]{1,0:T(8,128)(2,1)} %get-tuple-element.52.refs_1_.refs_11_), custom_call_target="tpu_custom_call" | custom-call | flops 1000000000 | bytes 4194304 | tf_op jit(solution)/shard_map/pallas_call | solution.py:132
  59.0 4.5 %collective-permute-done.9.refs_3_ = bf16[512,128]{1,0:T(8,128)(2,1)} collective-permute-done((bf16[512,128]{1,0:T(8,128)(2,1)}, bf16[512,128]{1,0:T(8,128)(2,1)}, u32[]{:S(2)}, u32[]{:S(2)}) %collective-permute-start.9) | collective-permute-done | bytes 131104 | tf_op jit(solution)/shard_map/ppermute | solution.py:33
  63.5 3.5 %shard_map.115 = bf16[8,368,128]{2,1,0:T(8,128)(2,1)} custom-call(f32[512,128]{1,0:T(8,128)} %get-tuple-element.43.refs_0_, bf16[512,128]{1,0:T(8,128)(2,1)} %collective-permute-done.7.refs_1_, bf16[512,128]{1,0:T(8,128)(2,1)} %collective-permute-done.8.refs_2_, bf16[512,128]{1,0:T(8,128)(2,1)} %collective-permute-done.9.refs_3_, ...), custom_call_target="tpu_custom_call" | custom-call | flops 1000000000 | bytes 4194304 | tf_op jit(solution)/shard_map/pallas_call | solution.py:132
  67.1 10.2 %all-to-all-start = ((bf16[8,368,128]{2,1,0:T(8,128)(2,1)}), bf16[8,368,128]{2,1,0:T(8,128)(2,1)}, u32[]{:S(2)}, u32[]{:S(2)}) async-start(bf16[8,368,128]{2,1,0:T(8,128)(2,1)} %shard_map.115), calls=%async_computation | async-start | bytes 1507328 | tf_op jit(solution)/shard_map/all_to_all | solution.py:49
  77.3 0.2 collective-permute-start.13
  77.5 0.3 collective-permute-start.17
  77.8 0.2 collective-permute-start.18
  78.0 0.3 collective-permute-start.14
  78.3 0.2 collective-permute-start.15
  78.5 1.2 collective-permute-done.17.refs_14_
  79.7 0.2 collective-permute-start.16
  79.9 0.3 collective-permute-start.19
  80.2 0.2 collective-permute-start.20
  80.4 0.6 pad_add_fusion.refs_0_
  81.0 1.1 collective-permute-done.19.refs_16_
  82.1 0.4 collective-permute-done.20.refs_17_
  82.5 5.4 %all-to-all-done.refs_1_ = bf16[8,368,128]{2,1,0:T(8,128)(2,1)} async-done(((bf16[8,368,128]{2,1,0:T(8,128)(2,1)}), bf16[8,368,128]{2,1,0:T(8,128)(2,1)}, u32[]{:S(2)}, u32[]{:S(2)}) %all-to-all-start) | async-done | bytes 753696 | tf_op jit(solution)/shard_map/all_to_all | solution.py:49
  88.0 6.7 %shard_map.116 = bf16[3328,128]{1,0:T(8,128)(2,1)} custom-call(s32[2]{0:T(128)} %pad_add_fusion.refs_0_, bf16[8,368,128]{2,1,0:T(8,128)(2,1)} %all-to-all-done.refs_1_, bf16[768,256]{1,0:T(8,128)(2,1)} %get-tuple-element.51.refs_2_, bf16[768,256]{1,0:T(8,128)(2,1)} %collective-permute-done.10.refs_3_, bf16[768,256]{1,0:T(8,128)(2,1)} %collective-permute-done.11.refs_4_, ...), custom_call_target="tpu_custom_call" | custom-call | flops 1000000000 | bytes 4194304 | tf_op jit(solution)/shard_map/pallas_call | solution.py:132
  94.7 8.3 %all-to-all-start.1 = ((bf16[32,104,128]{2,1,0:T(8,128)(2,1)}), bf16[32,104,128]{2,1,0:T(8,128)(2,1)S(1)}, u32[]{:S(2)}, u32[]{:S(2)}) async-start(bf16[32,104,128]{2,1,0:T(8,128)(2,1)} %bitcast.14), calls=%async_computation.1 | async-start | bytes 1703936 | tf_op jit(solution)/shard_map/all_to_all | solution.py:49
  103.0 20.2 %all-to-all-done.1.refs_0_ = bf16[32,104,128]{2,1,0:T(8,128)(2,1)S(1)} async-done(((bf16[32,104,128]{2,1,0:T(8,128)(2,1)}), bf16[32,104,128]{2,1,0:T(8,128)(2,1)S(1)}, u32[]{:S(2)}, u32[]{:S(2)}) %all-to-all-start.1) | async-done | bytes 852000 | tf_op jit(solution)/shard_map/all_to_all | solution.py:49
  123.2 1.9 %shard_map.117 = (f32[3,2,1024]{2,1,0:T(2,128)}, f32[1,768]{1,0:T(1,128)S(1)}, f32[8,8,256]{2,1,0:T(8,128)}) custom-call(bf16[32,104,128]{2,1,0:T(8,128)(2,1)S(1)} %all-to-all-done.1.refs_0_), custom_call_target="tpu_custom_call" | custom-call | flops 1000000000 | bytes 4194304 | tf_op jit(solution)/shard_map/pallas_call | solution.py:132
  125.1 9.3 %all-to-all-start.2 = ((f32[8,8,256]{2,1,0:T(8,128)}), f32[8,8,256]{2,1,0:T(8,128)S(1)}, u32[]{:S(2)}, u32[]{:S(2)}) async-start(f32[8,8,256]{2,1,0:T(8,128)} %get-tuple-element.63), calls=%async_computation.2 | async-start | bytes 131072 | tf_op jit(solution)/shard_map/all_to_all | solution.py:49
  134.4 0.6 dynamic-slice_bitcast_fusion
  135.0 4.1 %all-to-all-done.2.refs_0_ = f32[8,8,256]{2,1,0:T(8,128)S(1)} async-done(((f32[8,8,256]{2,1,0:T(8,128)}), f32[8,8,256]{2,1,0:T(8,128)S(1)}, u32[]{:S(2)}, u32[]{:S(2)}) %all-to-all-start.2) | async-done | bytes 65568 | tf_op jit(solution)/shard_map/all_to_all | solution.py:49
  139.1 0.8 shard_map.118
  (12 shorter events, 0.0 us)
Async XLA Ops:
  1.4 9.1 %collective-permute-start = (bf16[16,1024]{1,0:T(8,128)(2,1)S(1)}, bf16[16,1024]{1,0:T(8,128)(2,1)}, u32[]{:S(2)}, u32[]{:S(2)}) collective-permute-start(bf16[16,1024]{1,0:T(8,128)(2,1)S(1)} %slice_bitcast_fusion), channel_id=1, source_target_pairs={{1,0},{2,1},{3,2},{5,4},{6,5},{7,6},{9,8},{10,9},{11,10},{13,12},{... | collective-permute-start | bytes 98312 | tf_op jit(solution)/shard_map/ppermute | solution.py:369
  6.5 20.8 %collective-permute-start.6 = (bf16[128,1024]{1,0:T(8,128)(2,1)}, bf16[128,1024]{1,0:T(8,128)(2,1)}, u32[]{:S(2)}, u32[]{:S(2)}) collective-permute-start(bf16[128,1024]{1,0:T(8,128)(2,1)} %bitcast.16), channel_id=1, source_target_pairs={{0,130},{128,0},{2,128},{130,2},{1,131},{129,1},{3,129},{131,3},{4... | collective-permute-start | bytes 786440 | tf_op jit(solution)/shard_map/ppermute | solution.py:39
  8.1 20.1 %collective-permute-start.5 = (bf16[128,1024]{1,0:T(8,128)(2,1)}, bf16[128,1024]{1,0:T(8,128)(2,1)}, u32[]{:S(2)}, u32[]{:S(2)}) collective-permute-start(bf16[128,1024]{1,0:T(8,128)(2,1)} %bitcast.17), channel_id=1, source_target_pairs={{0,2},{128,130},{2,0},{130,128},{1,3},{129,131},{3,1},{131,129},{4... | collective-permute-start | bytes 786440 | tf_op jit(solution)/shard_map/ppermute | solution.py:39
  8.3 21.4 %collective-permute-start.4 = (bf16[128,1024]{1,0:T(8,128)(2,1)}, bf16[128,1024]{1,0:T(8,128)(2,1)}, u32[]{:S(2)}, u32[]{:S(2)}) collective-permute-start(bf16[128,1024]{1,0:T(8,128)(2,1)} %bitcast.18), channel_id=1, source_target_pairs={{0,128},{128,2},{2,130},{130,0},{1,129},{129,3},{3,131},{131,1},{4... | collective-permute-start | bytes 786440 | tf_op jit(solution)/shard_map/ppermute | solution.py:39
  15.0 12.3 %collective-permute-start.1 = (bf16[512,128]{1,0:T(8,128)(2,1)}, bf16[512,128]{1,0:T(8,128)(2,1)}, u32[]{:S(2)}, u32[]{:S(2)}) collective-permute-start(bf16[512,128]{1,0:T(8,128)(2,1)} %get-tuple-element.35.refs_3_), channel_id=1, source_target_pairs={{0,4},{4,8},{8,12},{12,16},{16,20},{20,24},{24,28},{28,32},{32,36}... | collective-permute-start | bytes 393224 | tf_op jit(solution)/shard_map/ppermute | solution.py:33
  16.7 16.6 %collective-permute-start.3 = (bf16[512,128]{1,0:T(8,128)(2,1)}, bf16[512,128]{1,0:T(8,128)(2,1)}, u32[]{:S(2)}, u32[]{:S(2)}) collective-permute-start(bf16[512,128]{1,0:T(8,128)(2,1)} %get-tuple-element.35.refs_3_), channel_id=1, source_target_pairs={{0,12},{4,16},{8,20},{12,24},{16,28},{20,32},{24,36},{28,40},{32,4... | collective-permute-start | bytes 393224 | tf_op jit(solution)/shard_map/ppermute | solution.py:33
  27.3 13.2 %collective-permute-start.2 = (bf16[512,128]{1,0:T(8,128)(2,1)}, bf16[512,128]{1,0:T(8,128)(2,1)}, u32[]{:S(2)}, u32[]{:S(2)}) collective-permute-start(bf16[512,128]{1,0:T(8,128)(2,1)} %get-tuple-element.35.refs_3_), channel_id=1, source_target_pairs={{0,8},{4,12},{8,16},{12,20},{16,24},{20,28},{24,32},{28,36},{32,40... | collective-permute-start | bytes 393224 | tf_op jit(solution)/shard_map/ppermute | solution.py:33
  27.3 31.7 %collective-permute-start.12 = (bf16[768,256]{1,0:T(8,128)(2,1)}, bf16[768,256]{1,0:T(8,128)(2,1)}, u32[]{:S(2)}, u32[]{:S(2)}) collective-permute-start(bf16[768,256]{1,0:T(8,128)(2,1)} %get-tuple-element.51.refs_2_), channel_id=1, source_target_pairs={{0,130},{128,0},{2,128},{130,2},{1,131},{129,1},{3,129},{131,3},{4... | collective-permute-start | bytes 1179656 | tf_op jit(solution)/shard_map/ppermute | solution.py:39
  28.2 30.7 %collective-permute-start.11 = (bf16[768,256]{1,0:T(8,128)(2,1)}, bf16[768,256]{1,0:T(8,128)(2,1)}, u32[]{:S(2)}, u32[]{:S(2)}) collective-permute-start(bf16[768,256]{1,0:T(8,128)(2,1)} %get-tuple-element.51.refs_2_), channel_id=1, source_target_pairs={{0,2},{128,130},{2,0},{130,128},{1,3},{129,131},{3,1},{131,129},{4... | collective-permute-start | bytes 1179656 | tf_op jit(solution)/shard_map/ppermute | solution.py:39
  29.7 29.3 %collective-permute-start.10 = (bf16[768,256]{1,0:T(8,128)(2,1)}, bf16[768,256]{1,0:T(8,128)(2,1)}, u32[]{:S(2)}, u32[]{:S(2)}) collective-permute-start(bf16[768,256]{1,0:T(8,128)(2,1)} %get-tuple-element.51.refs_2_), channel_id=1, source_target_pairs={{0,128},{128,2},{2,130},{130,0},{1,129},{129,3},{3,131},{131,1},{4... | collective-permute-start | bytes 1179656 | tf_op jit(solution)/shard_map/ppermute | solution.py:39
  47.9 4.2 %collective-permute-start.7 = (bf16[512,128]{1,0:T(8,128)(2,1)}, bf16[512,128]{1,0:T(8,128)(2,1)}, u32[]{:S(2)}, u32[]{:S(2)}) collective-permute-start(bf16[512,128]{1,0:T(8,128)(2,1)} %get-tuple-element.44), channel_id=1, source_target_pairs={{0,252},{4,0},{8,4},{12,8},{16,12},{20,16},{24,20},{28,24},{32,28}... | collective-permute-start | bytes 393224 | tf_op jit(solution)/shard_map/ppermute | solution.py:33
  48.9 10.1 %collective-permute-start.8 = (bf16[512,128]{1,0:T(8,128)(2,1)}, bf16[512,128]{1,0:T(8,128)(2,1)}, u32[]{:S(2)}, u32[]{:S(2)}) collective-permute-start(bf16[512,128]{1,0:T(8,128)(2,1)} %get-tuple-element.47), channel_id=1, source_target_pairs={{0,248},{4,252},{8,0},{12,4},{16,8},{20,12},{24,16},{28,20},{32,24... | collective-permute-start | bytes 393224 | tf_op jit(solution)/shard_map/ppermute | solution.py:33
  52.1 11.4 %collective-permute-start.9 = (bf16[512,128]{1,0:T(8,128)(2,1)}, bf16[512,128]{1,0:T(8,128)(2,1)}, u32[]{:S(2)}, u32[]{:S(2)}) collective-permute-start(bf16[512,128]{1,0:T(8,128)(2,1)} %get-tuple-element.48), channel_id=1, source_target_pairs={{0,244},{4,248},{8,252},{12,0},{16,4},{20,8},{24,12},{28,16},{32,2... | collective-permute-start | bytes 393224 | tf_op jit(solution)/shard_map/ppermute | solution.py:33
  67.1 20.9 %all-to-all-start = ((bf16[8,368,128]{2,1,0:T(8,128)(2,1)}), bf16[8,368,128]{2,1,0:T(8,128)(2,1)}, u32[]{:S(2)}, u32[]{:S(2)}) async-start(bf16[8,368,128]{2,1,0:T(8,128)(2,1)} %shard_map.115), calls=%async_computation | async-start | bytes 1507328 | tf_op jit(solution)/shard_map/all_to_all | solution.py:49
  77.3 2.7 %collective-permute-start.13 = (bf16[768,256]{1,0:T(8,128)(2,1)}, bf16[768,256]{1,0:T(8,128)(2,1)}, u32[]{:S(2)}, u32[]{:S(2)}) collective-permute-start(bf16[768,256]{1,0:T(8,128)(2,1)} %get-tuple-element.51.refs_2_), channel_id=1, source_target_pairs={{0,1},{1,0},{2,3},{3,2},{4,5},{5,4},{6,7},{7,6},{8,9},{9,8},{10,11... | collective-permute-start | bytes 1179656 | tf_op jit(solution)/shard_map/ppermute | solution.py:45
  77.5 2.2 %collective-permute-start.17 = (bf16[128,1024]{1,0:T(8,128)(2,1)}, bf16[128,1024]{1,0:T(8,128)(2,1)}, u32[]{:S(2)}, u32[]{:S(2)}) collective-permute-start(bf16[128,1024]{1,0:T(8,128)(2,1)} %bitcast.20), channel_id=1, source_target_pairs={{0,1},{1,0},{2,3},{3,2},{4,5},{5,4},{6,7},{7,6},{8,9},{9,8},{10,11... | collective-permute-start | bytes 786440 | tf_op jit(solution)/shard_map/ppermute | solution.py:45
  77.8 2.4 %collective-permute-start.18 = (bf16[128,1024]{1,0:T(8,128)(2,1)}, bf16[128,1024]{1,0:T(8,128)(2,1)}, u32[]{:S(2)}, u32[]{:S(2)}) collective-permute-start(bf16[128,1024]{1,0:T(8,128)(2,1)} %collective-permute-done.4.refs_11_), channel_id=1, source_target_pairs={{0,1},{1,0},{2,3},{3,2},{4,5},{5,4},{6,7},{7,6},{8,9},{9,8},{10,11... | collective-permute-start | bytes 786440 | tf_op jit(solution)/shard_map/ppermute | solution.py:45
  78.0 4.5 %collective-permute-start.14 = (bf16[768,256]{1,0:T(8,128)(2,1)}, bf16[768,256]{1,0:T(8,128)(2,1)}, u32[]{:S(2)}, u32[]{:S(2)}) collective-permute-start(bf16[768,256]{1,0:T(8,128)(2,1)} %collective-permute-done.10.refs_3_), channel_id=1, source_target_pairs={{0,1},{1,0},{2,3},{3,2},{4,5},{5,4},{6,7},{7,6},{8,9},{9,8},{10,11... | collective-permute-start | bytes 1179656 | tf_op jit(solution)/shard_map/ppermute | solution.py:45
  78.3 4.2 %collective-permute-start.15 = (bf16[768,256]{1,0:T(8,128)(2,1)}, bf16[768,256]{1,0:T(8,128)(2,1)}, u32[]{:S(2)}, u32[]{:S(2)}) collective-permute-start(bf16[768,256]{1,0:T(8,128)(2,1)} %collective-permute-done.11.refs_4_), channel_id=1, source_target_pairs={{0,1},{1,0},{2,3},{3,2},{4,5},{5,4},{6,7},{7,6},{8,9},{9,8},{10,11... | collective-permute-start | bytes 1179656 | tf_op jit(solution)/shard_map/ppermute | solution.py:45
  79.7 2.8 %collective-permute-start.16 = (bf16[768,256]{1,0:T(8,128)(2,1)}, bf16[768,256]{1,0:T(8,128)(2,1)}, u32[]{:S(2)}, u32[]{:S(2)}) collective-permute-start(bf16[768,256]{1,0:T(8,128)(2,1)} %collective-permute-done.12.refs_5_), channel_id=1, source_target_pairs={{0,1},{1,0},{2,3},{3,2},{4,5},{5,4},{6,7},{7,6},{8,9},{9,8},{10,11... | collective-permute-start | bytes 1179656 | tf_op jit(solution)/shard_map/ppermute | solution.py:45
  79.9 2.2 %collective-permute-start.19 = (bf16[128,1024]{1,0:T(8,128)(2,1)}, bf16[128,1024]{1,0:T(8,128)(2,1)}, u32[]{:S(2)}, u32[]{:S(2)}) collective-permute-start(bf16[128,1024]{1,0:T(8,128)(2,1)} %collective-permute-done.5.refs_12_), channel_id=1, source_target_pairs={{0,1},{1,0},{2,3},{3,2},{4,5},{5,4},{6,7},{7,6},{8,9},{9,8},{10,11... | collective-permute-start | bytes 786440 | tf_op jit(solution)/shard_map/ppermute | solution.py:45
  80.2 2.3 %collective-permute-start.20 = (bf16[128,1024]{1,0:T(8,128)(2,1)}, bf16[128,1024]{1,0:T(8,128)(2,1)}, u32[]{:S(2)}, u32[]{:S(2)}) collective-permute-start(bf16[128,1024]{1,0:T(8,128)(2,1)} %collective-permute-done.6.refs_13_), channel_id=1, source_target_pairs={{0,1},{1,0},{2,3},{3,2},{4,5},{5,4},{6,7},{7,6},{8,9},{9,8},{10,11... | collective-permute-start | bytes 786440 | tf_op jit(solution)/shard_map/ppermute | solution.py:45
  94.7 28.5 %all-to-all-start.1 = ((bf16[32,104,128]{2,1,0:T(8,128)(2,1)}), bf16[32,104,128]{2,1,0:T(8,128)(2,1)S(1)}, u32[]{:S(2)}, u32[]{:S(2)}) async-start(bf16[32,104,128]{2,1,0:T(8,128)(2,1)} %bitcast.14), calls=%async_computation.1 | async-start | bytes 1703936 | tf_op jit(solution)/shard_map/all_to_all | solution.py:49
  125.1 14.0 %all-to-all-start.2 = ((f32[8,8,256]{2,1,0:T(8,128)}), f32[8,8,256]{2,1,0:T(8,128)S(1)}, u32[]{:S(2)}, u32[]{:S(2)}) async-start(f32[8,8,256]{2,1,0:T(8,128)} %get-tuple-element.63), calls=%async_computation.2 | async-start | bytes 131072 | tf_op jit(solution)/shard_map/all_to_all | solution.py:49

commit v8 on v7

--- a/solution.py
+++ b/solution.py
@@ -33,12 +33,9 @@
     return lax.ppermute(x, BLK, [(i, (i + by) % peers) for i in range(peers)])
 
 
-def from_chips(x):
+def along_ring(x, by):
     order = [0, 2, 1, 3]
-    return [
-        lax.ppermute(x, CHIPS, [(order[i], order[(i + by) % 4]) for i in range(4)])
-        for by in range(1, 4)
-    ]
+    return lax.ppermute(x, CHIPS, [(order[i], order[(i + by) % 4]) for i in range(4)])
 
 
 def other_core(x):
@@ -210,8 +207,7 @@
         q = jnp.concatenate([query_n[h * 64 : h * 64 + 64, :] for h in heads], axis=1)
         dy = jnp.concatenate([do[h * 64 : h * 64 + 64, :] for h in heads], axis=1)
         scale = jnp.concatenate([jnp.full((1, TOK), scales[h], F32) for h in heads], axis=1)
-        scores = dot(k, q, TN) * scale
-        scores = jnp.where(bias < 0.0, -1e30, scores)
+        scores = dot(k, q, TN) * scale + bias
         top = jnp.max(scores, axis=0, keepdims=True)
         weights = jnp.exp(scores - top)
         probs = weights * (1.0 / jnp.sum(weights, axis=0, keepdims=True))
@@ -334,9 +330,9 @@
 
 def total_body(terms, stem_o, gain_o, rows_o):
     total = jnp.zeros((104, TOK), F32)
-    for piece in range(4):
+    for piece in range(8):
         block = terms.piece(piece)
-        for r in range(8):
+        for r in range(4):
             total = total + block[r].astype(F32)
     for j in range(2):
         for k in range(3):
@@ -367,7 +363,7 @@
     grad_out = d_out[0]
     bands = lax.axis_size(BAND)
     arrived = lax.ppermute(tiles[:TC], BAND, [(i, i - 1) for i in range(1, bands)])
-    tiles_mine = from_chips(tiles)
+    tiles_mine = [along_ring(tiles, 1), None, along_ring(tiles, 3)]
     gain = norm_gain.reshape(1, D)
     tokens, hidden, key, kv_own, ring_own = call(
         stem_body,
@@ -389,7 +385,11 @@
         pieces={2: 2, 3: 2},
         columns={2: (0, D)},
     )(hidden, grad_out, w_qkv, w_out)
-    query_n, tiles_mine = lax.optimization_barrier((query_n, tiles_mine))
+    query_n, tiles_late = lax.optimization_barrier((query_n, tiles_mine[0]))
+    tiles_mine[1] = along_ring(tiles_late, 1)
+    query_n, tiles_mine[0], tiles_mine[2] = lax.optimization_barrier(
+        (query_n, tiles_mine[0], tiles_mine[2])
+    )
     own_block = lax.axis_index(BLK).astype(jnp.int32).reshape(1)
     attn, d_q, own, back1, back2, back3 = call(
         attend_body,
@@ -399,8 +399,10 @@
     returned = [passed_along(piece, -(j + 1)) for j, piece in enumerate((back1, back2, back3))]
     returned[0], d_q = lax.optimization_barrier((returned[0], d_q))
     part = call(part_body, [((TOK, D), F32)], pieces={0: 2}, columns={0: (0, D)})(w_qkv, d_q)[0]
-    ring_mine = from_chips(ring_own)
-    ring_mine, part = lax.optimization_barrier((ring_mine, part))
+    ring_mine = [along_ring(ring_own, by) for by in (1, 2, 3)]
+    ring_mine[0], ring_mine[2], tiles_mine[1], part = lax.optimization_barrier(
+        (ring_mine[0], ring_mine[2], tiles_mine[1], part)
+    )
     late = call(
         tokens_body,
         [((8, 368, TOK), B16)],
@@ -431,7 +433,7 @@
     stem_total, gain_total, row_total = call(
         total_body,
         [((3, 2, 1024), F32), ((1, D), F32), ((8, 8, 256), F32)],
-        pieces={0: 4},
+        pieces={0: 8},
         limit=16,
     )(exchange(terms.reshape(32, 104, TOK), REST))
     d_w_qkv, d_w_out = call(final_body, [((3, 1280), F32), ((3, D), F32)], limit=16)(

time: 141 us -> 140 us (level)
    all_to_all x3, starting transfers between devices: 27.9 us -> 25.7 us  [exchange(): return lax.all_to_all(x, axes, split_axis=0, concat_axis=0, tiled=True)]
  transfers between devices with their start and end apart: 24 -> 24, of which waited for: 10 -> 11; matrix products, arithmetic and copies ran while one was open for 2% -> 2% of each run, Pallas kernels for 13% -> 15%
where the time goes in v8:
time: 140 us
  starting transfers between devices  54.6 us (39%)
  waiting for transfers between devices  50.3 us (36%)
  Pallas kernels  30.5 us (22%)
  local copies, waits for them, and re-layouts  2.61 us (2%)
    pallas_call x8, Pallas kernels, run(): pl.pallas_call(kernel, out_shape=shapes, in_specs=[pl.BlockSpec(memory_sp...  30.5 us
    all_to_all x3, waiting for transfers between devices, exchange(): return lax.all_to_all(x, axes, split_axis=0, concat_axis=0, tiled=True)  29.7 us
    all_to_all x3, starting transfers between devices, exchange(): return lax.all_to_all(x, axes, split_axis=0, concat_axis=0, tiled=True)  25.7 us
    ppermute x6, waiting for transfers between devices, passed_along(): return lax.ppermute(x, BLK, [(i, (i + by) % peers) for i in range(peers)])  17.6 us
    ppermute x6, starting transfers between devices, passed_along(): return lax.ppermute(x, BLK, [(i, (i + by) % peers) for i in range(peers)])  16.6 us
    ppermute x6, starting transfers between devices, along_ring(): lax.ppermute(x, CHIPS, [(order[i], order[(i + by) % 4]) for i in range(4)])  5.57 us
    ppermute x1, starting transfers between devices, shards(): lax.ppermute(tiles[:TC], BAND, [(i, i - 1) for i in range(1, bands)])  5.14 us
    ppermute x8, waiting for transfers between devices, other_core(): return lax.ppermute(x, 'c', [(0, 1), (1, 0)])  3 us
  transfers between devices with their start and end apart: 24, of which 11 were waited for; matrix products, arithmetic and copies ran while one was open for 2% of the time, Pallas kernels for 15%

profile of v8, /device:TPU:1, one launch (start us, length us, event | category | flops | bytes accessed | tf_op | source)
XLA Modules:
  0.0 139.6 jit_solution(11203081003771557695)
XLA Ops:
  0.6 0.8 slice_bitcast_fusion
  1.4 5.1 %collective-permute-start = (bf16[16,1024]{1,0:T(8,128)(2,1)S(1)}, bf16[16,1024]{1,0:T(8,128)(2,1)}, u32[]{:S(2)}, u32[]{:S(2)}) collective-permute-start(bf16[16,1024]{1,0:T(8,128)(2,1)S(1)} %slice_bitcast_fusion), channel_id=1, source_target_pairs={{1,0},{2,1},{3,2},{5,4},{6,5},{7,6},{9,8},{10,9},{11,10},{13,12},{... | collective-permute-start | bytes 98312 | tf_op jit(solution)/shard_map/ppermute | solution.py:365
  6.5 0.1 collective-permute-start.4
  6.6 2.7 %collective-permute-start.5 = (bf16[128,1024]{1,0:T(8,128)(2,1)}, bf16[128,1024]{1,0:T(8,128)(2,1)}, u32[]{:S(2)}, u32[]{:S(2)}) collective-permute-start(bf16[128,1024]{1,0:T(8,128)(2,1)} %bitcast.17), channel_id=1, source_target_pairs={{0,130},{128,0},{2,128},{130,2},{1,131},{129,1},{3,129},{131,3},{4... | collective-permute-start | bytes 786440 | tf_op jit(solution)/shard_map/ppermute | solution.py:38
  9.3 1.3 reshape.28.refs_4_.refs_7_
  10.6 0.0 collective-permute-done.refs_2_
  10.6 4.5 %shard_map.111 = (bf16[128,768]{1,0:T(8,128)(2,1)}, bf16[128,768]{1,0:T(8,128)(2,1)}, f32[256,128]{1,0:T(8,128)}, bf16[512,128]{1,0:T(8,128)(2,1)}, bf16[768,256]{1,0:T(8,128)(2,1)}) custom-call(bf16[128,1024]{1,0:T(8,128)(2,1)} %bitcast.18, bf16[2048,768]{1,0:T(8,128)(2,1)} %bitcast.15, bf16[16,1024]{1,0:T(8,128)(2,1)} %collective-permute-done.refs_2_, ...), custom_call_target="tpu_custom_call" | custom-call | flops 1000000000 | bytes 4194304 | tf_op jit(solution)/shard_map/pallas_call | solution.py:129
  15.1 0.5 collective-permute-start.1
  15.6 5.6 %collective-permute-start.3 = (bf16[512,128]{1,0:T(8,128)(2,1)}, bf16[512,128]{1,0:T(8,128)(2,1)}, u32[]{:S(2)}, u32[]{:S(2)}) collective-permute-start(bf16[512,128]{1,0:T(8,128)(2,1)} %get-tuple-element.36.refs_3_), channel_id=1, source_target_pairs={{0,12},{4,16},{8,20},{12,24},{16,28},{20,32},{24,36},{28,40},{32,4... | collective-permute-start | bytes 393224 | tf_op jit(solution)/shard_map/ppermute | solution.py:33
  21.2 1.2 collective-permute-start.2
  22.4 3.0 %collective-permute-done.1.refs_4_ = bf16[512,128]{1,0:T(8,128)(2,1)} collective-permute-done((bf16[512,128]{1,0:T(8,128)(2,1)}, bf16[512,128]{1,0:T(8,128)(2,1)}, u32[]{:S(2)}, u32[]{:S(2)}) %collective-permute-start.1) | collective-permute-done | bytes 131104 | tf_op jit(solution)/shard_map/ppermute | solution.py:33
  25.4 2.2 %collective-permute-start.10 = (bf16[768,256]{1,0:T(8,128)(2,1)}, bf16[768,256]{1,0:T(8,128)(2,1)}, u32[]{:S(2)}, u32[]{:S(2)}) collective-permute-start(bf16[768,256]{1,0:T(8,128)(2,1)} %get-tuple-element.53.refs_2_), channel_id=1, source_target_pairs={{0,130},{128,0},{2,128},{130,2},{1,131},{129,1},{3,129},{131,3},{4... | collective-permute-start | bytes 1179656 | tf_op jit(solution)/shard_map/ppermute | solution.py:38
  27.6 0.0 collective-permute-start.9
  27.6 3.2 %shard_map.112 = (f32[768,128]{1,0:T(8,128)}, bf16[768,128]{1,0:T(8,128)(2,1)}, bf16[768,128]{1,0:T(8,128)(2,1)}) custom-call(bf16[128,768]{1,0:T(8,128)(2,1)} %get-tuple-element.39.refs_0_, bf16[128,768]{1,0:T(8,128)(2,1)} %bitcast.22, bf16[768,1280]{1,0:T(8,128)(2,1)} %refs_5_.1, bf16[768,768]{1,0:T(8,128)(2,1)} %refs_3_.3), custom_call_target="tpu_custom_call" | custom-call | flops 1000000000 | bytes 4194304 | tf_op jit(solution)/shard_map/pallas_call | solution.py:129
  30.7 0.6 collective-permute-start.11
  31.4 7.0 %collective-permute-done.3.refs_6_ = bf16[512,128]{1,0:T(8,128)(2,1)} collective-permute-done((bf16[512,128]{1,0:T(8,128)(2,1)}, bf16[512,128]{1,0:T(8,128)(2,1)}, u32[]{:S(2)}, u32[]{:S(2)}) %collective-permute-start.3) | collective-permute-done | bytes 131104 | tf_op jit(solution)/shard_map/ppermute | solution.py:33
  38.3 1.5 %collective-permute-done.2.refs_5_ = bf16[512,128]{1,0:T(8,128)(2,1)} collective-permute-done((bf16[512,128]{1,0:T(8,128)(2,1)}, bf16[512,128]{1,0:T(8,128)(2,1)}, u32[]{:S(2)}, u32[]{:S(2)}) %collective-permute-start.2) | collective-permute-done | bytes 131104 | tf_op jit(solution)/shard_map/ppermute | solution.py:33
  39.9 7.3 %shard_map.113 = (bf16[768,128]{1,0:T(8,128)(2,1)}, bf16[768,128]{1,0:T(8,128)(2,1)}, f32[512,128]{1,0:T(8,128)}, bf16[512,128]{1,0:T(8,128)(2,1)}, bf16[512,128]{1,0:T(8,128)(2,1)}, /*index=5*/bf16[512,128]{1,0:T(8,128)(2,1)}) custom-call(s32[1]{0:T(128)} %bitcast.2.refs_0_, f32[12]{0:T(128)} %refs_1_.1, s32[64,128]{1,0:T(8,128)} %bitcast.24, ...), custom_call_target="tpu_custom_call" | custom-call | flops 1000000000 | bytes 4194304 | tf_op jit(solution)/shard_map/pallas_call | solution.py:129
  47.2 2.0 %collective-permute-start.6 = (bf16[512,128]{1,0:T(8,128)(2,1)}, bf16[512,128]{1,0:T(8,128)(2,1)}, u32[]{:S(2)}, u32[]{:S(2)}) collective-permute-start(bf16[512,128]{1,0:T(8,128)(2,1)} %get-tuple-element.46), channel_id=1, source_target_pairs={{0,252},{4,0},{8,4},{12,8},{16,12},{20,16},{24,20},{28,24},{32,28}... | collective-permute-start | bytes 393224 | tf_op jit(solution)/shard_map/ppermute | solution.py:33
  49.2 2.4 %collective-permute-start.7 = (bf16[512,128]{1,0:T(8,128)(2,1)}, bf16[512,128]{1,0:T(8,128)(2,1)}, u32[]{:S(2)}, u32[]{:S(2)}) collective-permute-start(bf16[512,128]{1,0:T(8,128)(2,1)} %get-tuple-element.49), channel_id=1, source_target_pairs={{0,248},{4,252},{8,0},{12,4},{16,8},{20,12},{24,16},{28,20},{32,24... | collective-permute-start | bytes 393224 | tf_op jit(solution)/shard_map/ppermute | solution.py:33
  51.6 2.9 %collective-permute-done.6.refs_1_ = bf16[512,128]{1,0:T(8,128)(2,1)} collective-permute-done((bf16[512,128]{1,0:T(8,128)(2,1)}, bf16[512,128]{1,0:T(8,128)(2,1)}, u32[]{:S(2)}, u32[]{:S(2)}) %collective-permute-start.6) | collective-permute-done | bytes 131104 | tf_op jit(solution)/shard_map/ppermute | solution.py:33
  54.5 4.9 %collective-permute-start.8 = (bf16[512,128]{1,0:T(8,128)(2,1)}, bf16[512,128]{1,0:T(8,128)(2,1)}, u32[]{:S(2)}, u32[]{:S(2)}) collective-permute-start(bf16[512,128]{1,0:T(8,128)(2,1)} %get-tuple-element.50), channel_id=1, source_target_pairs={{0,244},{4,248},{8,252},{12,0},{16,4},{20,8},{24,12},{28,16},{32,2... | collective-permute-start | bytes 393224 | tf_op jit(solution)/shard_map/ppermute | solution.py:33
  59.4 0.0 collective-permute-done.10.refs_5_
  59.4 2.6 %shard_map.114.refs_8_ = f32[128,768]{1,0:T(8,128)} custom-call(bf16[768,1280]{1,0:T(8,128)(2,1)} %refs_5_.1, bf16[768,128]{1,0:T(8,128)(2,1)} %get-tuple-element.55.refs_1_.refs_11_), custom_call_target="tpu_custom_call" | custom-call | flops 1000000000 | bytes 4194304 | tf_op jit(solution)/shard_map/pallas_call | solution.py:129
  62.1 3.2 %collective-permute-done.8.refs_3_ = bf16[512,128]{1,0:T(8,128)(2,1)} collective-permute-done((bf16[512,128]{1,0:T(8,128)(2,1)}, bf16[512,128]{1,0:T(8,128)(2,1)}, u32[]{:S(2)}, u32[]{:S(2)}) %collective-permute-start.8) | collective-permute-done | bytes 131104 | tf_op jit(solution)/shard_map/ppermute | solution.py:33
  65.3 3.5 %shard_map.115 = bf16[8,368,128]{2,1,0:T(8,128)(2,1)} custom-call(f32[512,128]{1,0:T(8,128)} %get-tuple-element.45.refs_0_, bf16[512,128]{1,0:T(8,128)(2,1)} %collective-permute-done.6.refs_1_, bf16[512,128]{1,0:T(8,128)(2,1)} %collective-permute-done.7.refs_2_, bf16[512,128]{1,0:T(8,128)(2,1)} %collective-permute-done.8.refs_3_, ...), custom_call_target="tpu_custom_call" | custom-call | flops 1000000000 | bytes 4194304 | tf_op jit(solution)/shard_map/pallas_call | solution.py:129
  68.8 6.6 %all-to-all-start = ((bf16[8,368,128]{2,1,0:T(8,128)(2,1)}), bf16[8,368,128]{2,1,0:T(8,128)(2,1)}, u32[]{:S(2)}, u32[]{:S(2)}) async-start(bf16[8,368,128]{2,1,0:T(8,128)(2,1)} %shard_map.115), calls=%async_computation | async-start | bytes 1507328 | tf_op jit(solution)/shard_map/all_to_all | solution.py:46
  75.4 0.0 collective-permute-start.13
  75.4 0.5 collective-permute-start.17
  75.9 0.0 collective-permute-start.18
  75.9 0.5 collective-permute-start.15
  76.4 0.0 collective-permute-start.14
  76.4 1.4 %collective-permute-done.17.refs_14_ = bf16[128,1024]{1,0:T(8,128)(2,1)} collective-permute-done((bf16[128,1024]{1,0:T(8,128)(2,1)}, bf16[128,1024]{1,0:T(8,128)(2,1)}, u32[]{:S(2)}, u32[]{:S(2)}) %collective-permute-start.17) | collective-permute-done | bytes 262176 | tf_op jit(solution)/shard_map/ppermute | solution.py:42
  77.8 0.1 collective-permute-start.16
  78.0 0.4 collective-permute-start.20
  78.4 0.1 collective-permute-start.19
  78.5 0.6 pad_add_fusion.refs_0_
  79.1 1.2 collective-permute-done.20.refs_17_
  80.3 0.4 collective-permute-done.19.refs_16_
  80.7 5.4 %all-to-all-done.refs_1_ = bf16[8,368,128]{2,1,0:T(8,128)(2,1)} async-done(((bf16[8,368,128]{2,1,0:T(8,128)(2,1)}), bf16[8,368,128]{2,1,0:T(8,128)(2,1)}, u32[]{:S(2)}, u32[]{:S(2)}) %all-to-all-start) | async-done | bytes 753696 | tf_op jit(solution)/shard_map/all_to_all | solution.py:46
  86.1 6.7 %shard_map.116 = bf16[3328,128]{1,0:T(8,128)(2,1)} custom-call(s32[2]{0:T(128)} %pad_add_fusion.refs_0_, bf16[8,368,128]{2,1,0:T(8,128)(2,1)} %all-to-all-done.refs_1_, bf16[768,256]{1,0:T(8,128)(2,1)} %get-tuple-element.53.refs_2_, bf16[768,256]{1,0:T(8,128)(2,1)} %collective-permute-done.9.refs_3_, bf16[768,256]{1,0:T(8,128)(2,1)} %collective-permute-done.12.refs_4_, ...), custom_call_target="tpu_custom_call" | custom-call | flops 1000000000 | bytes 4194304 | tf_op jit(solution)/shard_map/pallas_call | solution.py:129
  92.8 9.8 %all-to-all-start.1 = ((bf16[32,104,128]{2,1,0:T(8,128)(2,1)}), bf16[32,104,128]{2,1,0:T(8,128)(2,1)S(1)}, u32[]{:S(2)}, u32[]{:S(2)}) async-start(bf16[32,104,128]{2,1,0:T(8,128)(2,1)} %bitcast.14), calls=%async_computation.1 | async-start | bytes 1703936 | tf_op jit(solution)/shard_map/all_to_all | solution.py:46
  102.6 20.2 %all-to-all-done.1.refs_0_ = bf16[32,104,128]{2,1,0:T(8,128)(2,1)S(1)} async-done(((bf16[32,104,128]{2,1,0:T(8,128)(2,1)}), bf16[32,104,128]{2,1,0:T(8,128)(2,1)S(1)}, u32[]{:S(2)}, u32[]{:S(2)}) %all-to-all-start.1) | async-done | bytes 852000 | tf_op jit(solution)/shard_map/all_to_all | solution.py:46
  122.7 1.9 %shard_map.117 = (f32[3,2,1024]{2,1,0:T(2,128)}, f32[1,768]{1,0:T(1,128)S(1)}, f32[8,8,256]{2,1,0:T(8,128)}) custom-call(bf16[32,104,128]{2,1,0:T(8,128)(2,1)S(1)} %all-to-all-done.1.refs_0_), custom_call_target="tpu_custom_call" | custom-call | flops 1000000000 | bytes 4194304 | tf_op jit(solution)/shard_map/pallas_call | solution.py:129
  124.7 9.3 %all-to-all-start.2 = ((f32[8,8,256]{2,1,0:T(8,128)}), f32[8,8,256]{2,1,0:T(8,128)S(1)}, u32[]{:S(2)}, u32[]{:S(2)}) async-start(f32[8,8,256]{2,1,0:T(8,128)} %get-tuple-element.65), calls=%async_computation.2 | async-start | bytes 131072 | tf_op jit(solution)/shard_map/all_to_all | solution.py:46
  134.0 0.6 dynamic-slice_bitcast_fusion
  134.6 4.1 %all-to-all-done.2.refs_0_ = f32[8,8,256]{2,1,0:T(8,128)S(1)} async-done(((f32[8,8,256]{2,1,0:T(8,128)}), f32[8,8,256]{2,1,0:T(8,128)S(1)}, u32[]{:S(2)}, u32[]{:S(2)}) %all-to-all-start.2) | async-done | bytes 65568 | tf_op jit(solution)/shard_map/all_to_all | solution.py:46
  138.7 0.8 shard_map.118
  (12 shorter events, 0.0 us)
Async XLA Ops:
  1.4 9.2 %collective-permute-start = (bf16[16,1024]{1,0:T(8,128)(2,1)S(1)}, bf16[16,1024]{1,0:T(8,128)(2,1)}, u32[]{:S(2)}, u32[]{:S(2)}) collective-permute-start(bf16[16,1024]{1,0:T(8,128)(2,1)S(1)} %slice_bitcast_fusion), channel_id=1, source_target_pairs={{1,0},{2,1},{3,2},{5,4},{6,5},{7,6},{9,8},{10,9},{11,10},{13,12},{... | collective-permute-start | bytes 98312 | tf_op jit(solution)/shard_map/ppermute | solution.py:365
  6.5 21.0 %collective-permute-start.4 = (bf16[128,1024]{1,0:T(8,128)(2,1)}, bf16[128,1024]{1,0:T(8,128)(2,1)}, u32[]{:S(2)}, u32[]{:S(2)}) collective-permute-start(bf16[128,1024]{1,0:T(8,128)(2,1)} %bitcast.16), channel_id=1, source_target_pairs={{0,128},{128,2},{2,130},{130,0},{1,129},{129,3},{3,131},{131,1},{4... | collective-permute-start | bytes 786440 | tf_op jit(solution)/shard_map/ppermute | solution.py:38
  6.6 24.1 %collective-permute-start.5 = (bf16[128,1024]{1,0:T(8,128)(2,1)}, bf16[128,1024]{1,0:T(8,128)(2,1)}, u32[]{:S(2)}, u32[]{:S(2)}) collective-permute-start(bf16[128,1024]{1,0:T(8,128)(2,1)} %bitcast.17), channel_id=1, source_target_pairs={{0,130},{128,0},{2,128},{130,2},{1,131},{129,1},{3,129},{131,3},{4... | collective-permute-start | bytes 786440 | tf_op jit(solution)/shard_map/ppermute | solution.py:38
  15.1 10.3 %collective-permute-start.1 = (bf16[512,128]{1,0:T(8,128)(2,1)}, bf16[512,128]{1,0:T(8,128)(2,1)}, u32[]{:S(2)}, u32[]{:S(2)}) collective-permute-start(bf16[512,128]{1,0:T(8,128)(2,1)} %get-tuple-element.36.refs_3_), channel_id=1, source_target_pairs={{0,4},{4,8},{8,12},{12,16},{16,20},{20,24},{24,28},{28,32},{32,36}... | collective-permute-start | bytes 393224 | tf_op jit(solution)/shard_map/ppermute | solution.py:33
  15.6 22.7 %collective-permute-start.3 = (bf16[512,128]{1,0:T(8,128)(2,1)}, bf16[512,128]{1,0:T(8,128)(2,1)}, u32[]{:S(2)}, u32[]{:S(2)}) collective-permute-start(bf16[512,128]{1,0:T(8,128)(2,1)} %get-tuple-element.36.refs_3_), channel_id=1, source_target_pairs={{0,12},{4,16},{8,20},{12,24},{16,28},{20,32},{24,36},{28,40},{32,4... | collective-permute-start | bytes 393224 | tf_op jit(solution)/shard_map/ppermute | solution.py:33
  21.2 18.7 %collective-permute-start.2 = (bf16[512,128]{1,0:T(8,128)(2,1)}, bf16[512,128]{1,0:T(8,128)(2,1)}, u32[]{:S(2)}, u32[]{:S(2)}) collective-permute-start(bf16[512,128]{1,0:T(8,128)(2,1)} %get-tuple-element.36.refs_3_), channel_id=1, source_target_pairs={{0,8},{4,12},{8,16},{12,20},{16,24},{20,28},{24,32},{28,36},{32,40... | collective-permute-start | bytes 393224 | tf_op jit(solution)/shard_map/ppermute | solution.py:33
  25.4 34.1 %collective-permute-start.10 = (bf16[768,256]{1,0:T(8,128)(2,1)}, bf16[768,256]{1,0:T(8,128)(2,1)}, u32[]{:S(2)}, u32[]{:S(2)}) collective-permute-start(bf16[768,256]{1,0:T(8,128)(2,1)} %get-tuple-element.53.refs_2_), channel_id=1, source_target_pairs={{0,130},{128,0},{2,128},{130,2},{1,131},{129,1},{3,129},{131,3},{4... | collective-permute-start | bytes 1179656 | tf_op jit(solution)/shard_map/ppermute | solution.py:38
  27.6 34.5 %collective-permute-start.9 = (bf16[768,256]{1,0:T(8,128)(2,1)}, bf16[768,256]{1,0:T(8,128)(2,1)}, u32[]{:S(2)}, u32[]{:S(2)}) collective-permute-start(bf16[768,256]{1,0:T(8,128)(2,1)} %get-tuple-element.53.refs_2_), channel_id=1, source_target_pairs={{0,128},{128,2},{2,130},{130,0},{1,129},{129,3},{3,131},{131,1},{4... | collective-permute-start | bytes 1179656 | tf_op jit(solution)/shard_map/ppermute | solution.py:38
  30.7 31.4 %collective-permute-start.11 = (bf16[128,1024]{1,0:T(8,128)(2,1)}, bf16[128,1024]{1,0:T(8,128)(2,1)}, u32[]{:S(2)}, u32[]{:S(2)}) collective-permute-start(bf16[128,1024]{1,0:T(8,128)(2,1)} %collective-permute-done.4.refs_11_), channel_id=1, source_target_pairs={{0,128},{128,2},{2,130},{130,0},{1,129},{129,3},{3,131},{131,1},{4... | collective-permute-start | bytes 786440 | tf_op jit(solution)/shard_map/ppermute | solution.py:38
  47.2 7.3 %collective-permute-start.6 = (bf16[512,128]{1,0:T(8,128)(2,1)}, bf16[512,128]{1,0:T(8,128)(2,1)}, u32[]{:S(2)}, u32[]{:S(2)}) collective-permute-start(bf16[512,128]{1,0:T(8,128)(2,1)} %get-tuple-element.46), channel_id=1, source_target_pairs={{0,252},{4,0},{8,4},{12,8},{16,12},{20,16},{24,20},{28,24},{32,28}... | collective-permute-start | bytes 393224 | tf_op jit(solution)/shard_map/ppermute | solution.py:33
  49.2 12.9 %collective-permute-start.7 = (bf16[512,128]{1,0:T(8,128)(2,1)}, bf16[512,128]{1,0:T(8,128)(2,1)}, u32[]{:S(2)}, u32[]{:S(2)}) collective-permute-start(bf16[512,128]{1,0:T(8,128)(2,1)} %get-tuple-element.49), channel_id=1, source_target_pairs={{0,248},{4,252},{8,0},{12,4},{16,8},{20,12},{24,16},{28,20},{32,24... | collective-permute-start | bytes 393224 | tf_op jit(solution)/shard_map/ppermute | solution.py:33
  54.5 10.8 %collective-permute-start.8 = (bf16[512,128]{1,0:T(8,128)(2,1)}, bf16[512,128]{1,0:T(8,128)(2,1)}, u32[]{:S(2)}, u32[]{:S(2)}) collective-permute-start(bf16[512,128]{1,0:T(8,128)(2,1)} %get-tuple-element.50), channel_id=1, source_target_pairs={{0,244},{4,248},{8,252},{12,0},{16,4},{20,8},{24,12},{28,16},{32,2... | collective-permute-start | bytes 393224 | tf_op jit(solution)/shard_map/ppermute | solution.py:33
  59.4 16.5 %collective-permute-start.12 = (bf16[768,256]{1,0:T(8,128)(2,1)}, bf16[768,256]{1,0:T(8,128)(2,1)}, u32[]{:S(2)}, u32[]{:S(2)}) collective-permute-start(bf16[768,256]{1,0:T(8,128)(2,1)} %get-tuple-element.53.refs_2_), channel_id=1, source_target_pairs={{0,2},{128,130},{2,0},{130,128},{1,3},{129,131},{3,1},{131,129},{4... | collective-permute-start | bytes 1179656 | tf_op jit(solution)/shard_map/ppermute | solution.py:38
  68.8 17.2 %all-to-all-start = ((bf16[8,368,128]{2,1,0:T(8,128)(2,1)}), bf16[8,368,128]{2,1,0:T(8,128)(2,1)}, u32[]{:S(2)}, u32[]{:S(2)}) async-start(bf16[8,368,128]{2,1,0:T(8,128)(2,1)} %shard_map.115), calls=%async_computation | async-start | bytes 1507328 | tf_op jit(solution)/shard_map/all_to_all | solution.py:46
  75.4 2.6 %collective-permute-start.13 = (bf16[768,256]{1,0:T(8,128)(2,1)}, bf16[768,256]{1,0:T(8,128)(2,1)}, u32[]{:S(2)}, u32[]{:S(2)}) collective-permute-start(bf16[768,256]{1,0:T(8,128)(2,1)} %get-tuple-element.53.refs_2_), channel_id=1, source_target_pairs={{0,1},{1,0},{2,3},{3,2},{4,5},{5,4},{6,7},{7,6},{8,9},{9,8},{10,11... | collective-permute-start | bytes 1179656 | tf_op jit(solution)/shard_map/ppermute | solution.py:42
  75.4 2.4 %collective-permute-start.17 = (bf16[128,1024]{1,0:T(8,128)(2,1)}, bf16[128,1024]{1,0:T(8,128)(2,1)}, u32[]{:S(2)}, u32[]{:S(2)}) collective-permute-start(bf16[128,1024]{1,0:T(8,128)(2,1)} %bitcast.19), channel_id=1, source_target_pairs={{0,1},{1,0},{2,3},{3,2},{4,5},{5,4},{6,7},{7,6},{8,9},{9,8},{10,11... | collective-permute-start | bytes 786440 | tf_op jit(solution)/shard_map/ppermute | solution.py:42
  75.9 2.4 %collective-permute-start.18 = (bf16[128,1024]{1,0:T(8,128)(2,1)}, bf16[128,1024]{1,0:T(8,128)(2,1)}, u32[]{:S(2)}, u32[]{:S(2)}) collective-permute-start(bf16[128,1024]{1,0:T(8,128)(2,1)} %collective-permute-done.4.refs_11_), channel_id=1, source_target_pairs={{0,1},{1,0},{2,3},{3,2},{4,5},{5,4},{6,7},{7,6},{8,9},{9,8},{10,11... | collective-permute-start | bytes 786440 | tf_op jit(solution)/shard_map/ppermute | solution.py:42
  75.9 4.7 %collective-permute-start.15 = (bf16[768,256]{1,0:T(8,128)(2,1)}, bf16[768,256]{1,0:T(8,128)(2,1)}, u32[]{:S(2)}, u32[]{:S(2)}) collective-permute-start(bf16[768,256]{1,0:T(8,128)(2,1)} %collective-permute-done.12.refs_4_), channel_id=1, source_target_pairs={{0,1},{1,0},{2,3},{3,2},{4,5},{5,4},{6,7},{7,6},{8,9},{9,8},{10,11... | collective-permute-start | bytes 1179656 | tf_op jit(solution)/shard_map/ppermute | solution.py:42
  76.4 4.2 %collective-permute-start.14 = (bf16[768,256]{1,0:T(8,128)(2,1)}, bf16[768,256]{1,0:T(8,128)(2,1)}, u32[]{:S(2)}, u32[]{:S(2)}) collective-permute-start(bf16[768,256]{1,0:T(8,128)(2,1)} %collective-permute-done.9.refs_3_), channel_id=1, source_target_pairs={{0,1},{1,0},{2,3},{3,2},{4,5},{5,4},{6,7},{7,6},{8,9},{9,8},{10,11... | collective-permute-start | bytes 1179656 | tf_op jit(solution)/shard_map/ppermute | solution.py:42
  77.8 2.8 %collective-permute-start.16 = (bf16[768,256]{1,0:T(8,128)(2,1)}, bf16[768,256]{1,0:T(8,128)(2,1)}, u32[]{:S(2)}, u32[]{:S(2)}) collective-permute-start(bf16[768,256]{1,0:T(8,128)(2,1)} %collective-permute-done.10.refs_5_), channel_id=1, source_target_pairs={{0,1},{1,0},{2,3},{3,2},{4,5},{5,4},{6,7},{7,6},{8,9},{9,8},{10,11... | collective-permute-start | bytes 1179656 | tf_op jit(solution)/shard_map/ppermute | solution.py:42
  78.0 2.3 %collective-permute-start.20 = (bf16[128,1024]{1,0:T(8,128)(2,1)}, bf16[128,1024]{1,0:T(8,128)(2,1)}, u32[]{:S(2)}, u32[]{:S(2)}) collective-permute-start(bf16[128,1024]{1,0:T(8,128)(2,1)} %collective-permute-done.5.refs_13_), channel_id=1, source_target_pairs={{0,1},{1,0},{2,3},{3,2},{4,5},{5,4},{6,7},{7,6},{8,9},{9,8},{10,11... | collective-permute-start | bytes 786440 | tf_op jit(solution)/shard_map/ppermute | solution.py:42
  78.4 2.3 %collective-permute-start.19 = (bf16[128,1024]{1,0:T(8,128)(2,1)}, bf16[128,1024]{1,0:T(8,128)(2,1)}, u32[]{:S(2)}, u32[]{:S(2)}) collective-permute-start(bf16[128,1024]{1,0:T(8,128)(2,1)} %collective-permute-done.11.refs_12_), channel_id=1, source_target_pairs={{0,1},{1,0},{2,3},{3,2},{4,5},{5,4},{6,7},{7,6},{8,9},{9,8},{10,11... | collective-permute-start | bytes 786440 | tf_op jit(solution)/shard_map/ppermute | solution.py:42
  92.8 30.0 %all-to-all-start.1 = ((bf16[32,104,128]{2,1,0:T(8,128)(2,1)}), bf16[32,104,128]{2,1,0:T(8,128)(2,1)S(1)}, u32[]{:S(2)}, u32[]{:S(2)}) async-start(bf16[32,104,128]{2,1,0:T(8,128)(2,1)} %bitcast.14), calls=%async_computation.1 | async-start | bytes 1703936 | tf_op jit(solution)/shard_map/all_to_all | solution.py:46
  124.7 14.0 %all-to-all-start.2 = ((f32[8,8,256]{2,1,0:T(8,128)}), f32[8,8,256]{2,1,0:T(8,128)S(1)}, u32[]{:S(2)}, u32[]{:S(2)}) async-start(f32[8,8,256]{2,1,0:T(8,128)} %get-tuple-element.65), calls=%async_computation.2 | async-start | bytes 131072 | tf_op jit(solution)/shard_map/all_to_all | solution.py:46

commit v9 on v8

--- a/solution.py
+++ b/solution.py
@@ -145,7 +145,7 @@
 
 
 def stem_body(
-    tiles, stem_w, arrived, w_kv, gain, d_out, tokens_o, hidden_o, key_o, kv_o, ring_o
+    tiles, stem_w, arrived, w_kv, gain, tokens_o, hidden_o, key_o, kv_o
 ):
     own = tiles[...]
     deep = own.shape[1] // 4
@@ -168,11 +168,9 @@
         scale = lax.rsqrt(jnp.mean(k * k, axis=0, keepdims=True) + 1e-06)
         kv_o[h * 64 : h * 64 + 64, :] = (k * scale).astype(B16)
     kv_o[256:, :] = kv[256:].astype(B16)
-    ring_o[:, :TOK] = hidden.astype(F32).T.astype(B16)
-    ring_o[:, TOK:] = d_out[...].astype(F32).T.astype(B16)
-
-
-def query_body(hidden, d_out, w_q, w_out, query_o, query_n_o, do_o):
+
+
+def query_body(hidden, d_out, w_q, w_out, query_o, query_n_o, do_o, ring_o):
     h = hidden[...]
     g = d_out[...]
     q = dot(h, w_q[...]).T
@@ -182,10 +180,12 @@
         scale = lax.rsqrt(jnp.mean(part * part, axis=0, keepdims=True) + 1e-06)
         query_n_o[i * 64 : i * 64 + 64, :] = (part * scale).astype(B16)
     do_o[...] = dot(w_out[...], g, NT).astype(B16)
+    ring_o[:, :TOK] = h.astype(F32).T.astype(B16)
+    ring_o[:, TOK:] = g.astype(F32).T.astype(B16)
 
 
 def attend_body(
-    own_block, scales, positions, kv0, kv1, kv2, kv3, query_n, do, query,
+    own_block, scales, positions, kv0, kv1, kv2, kv3, query_n, do,
     attn_o, dq_o, own_o, back1_o, back2_o, back3_o,
 ):
     own = own_block[0]
@@ -223,11 +223,7 @@
             rows = slice(h * 64, h * 64 + 64)
             lanes = slice(i * TOK, i * TOK + TOK)
             attn_o[rows, :] = attn[:, lanes].astype(B16)
-            x = query[rows, :]
-            dx = dq[:, lanes]
-            r = lax.rsqrt(jnp.mean(x * x, axis=0, keepdims=True) + 1e-06)
-            inner = jnp.mean(x * dx, axis=0, keepdims=True)
-            dq_o[rows, :] = (r * dx - x * (r * r * r * inner)).astype(B16)
+            dq_o[rows, :] = dq[:, lanes]
         own_o[g * 64 : g * 64 + 64, :] = dk[:, :TOK]
         own_o[256 + g * 64 : 320 + g * 64, :] = dv[:, :TOK]
         for j, back in enumerate((back1_o, back2_o, back3_o)):
@@ -236,8 +232,15 @@
             back[256 + g * 64 : 320 + g * 64, :] = dv[:, lanes].astype(B16)
 
 
-def part_body(w_q, dq, part_o):
-    part_o[...] = dot(w_q[...], dq[...]).T
+def part_body(dq_n, query, w_q, dq_o, part_o):
+    for h in range(QUERY_HEADS):
+        rows = slice(h * 64, h * 64 + 64)
+        x = query[rows, :]
+        dx = dq_n[rows, :]
+        r = lax.rsqrt(jnp.mean(x * x, axis=0, keepdims=True) + 1e-06)
+        inner = jnp.mean(x * dx, axis=0, keepdims=True)
+        dq_o[rows, :] = (r * dx - x * (r * r * r * inner)).astype(B16)
+    part_o[...] = dot(w_q[...], dq_o[...]).T
 
 
 def tokens_body(
@@ -365,23 +368,22 @@
     arrived = lax.ppermute(tiles[:TC], BAND, [(i, i - 1) for i in range(1, bands)])
     tiles_mine = [along_ring(tiles, 1), None, along_ring(tiles, 3)]
     gain = norm_gain.reshape(1, D)
-    tokens, hidden, key, kv_own, ring_own = call(
+    tokens, hidden, key, kv_own = call(
         stem_body,
         [
             ((TOK, D), B16),
             ((TOK, D), B16),
             ((256, TOK), F32),
             ((KV, TOK), B16),
-            ((D, 2 * TOK), B16),
         ],
         pieces={1: 8, 3: 2},
         columns={3: (D, D + KV)},
-    )(tiles, stem_weight.reshape(-1, D), arrived, w_qkv, gain, grad_out)
+    )(tiles, stem_weight.reshape(-1, D), arrived, w_qkv, gain)
     moved = [passed_along(kv_own, offset) for offset in range(1, 4)]
     moved[0], hidden = lax.optimization_barrier((moved[0], hidden))
-    query, query_n, do = call(
+    query, query_n, do, ring_own = call(
         query_body,
-        [((D, TOK), F32), ((D, TOK), B16), ((D, TOK), B16)],
+        [((D, TOK), F32), ((D, TOK), B16), ((D, TOK), B16), ((D, 2 * TOK), B16)],
         pieces={2: 2, 3: 2},
         columns={2: (0, D)},
     )(hidden, grad_out, w_qkv, w_out)
@@ -393,12 +395,14 @@
     own_block = lax.axis_index(BLK).astype(jnp.int32).reshape(1)
     attn, d_q, own, back1, back2, back3 = call(
         attend_body,
-        [((D, TOK), B16), ((D, TOK), B16), ((KV, TOK), F32)] + [((KV, TOK), B16)] * 3,
+        [((D, TOK), B16), ((D, TOK), F32), ((KV, TOK), F32)] + [((KV, TOK), B16)] * 3,
         smem=(0, 1),
-    )(own_block, per_head_scale, positions.reshape(64, TOK), kv_own, *moved, query_n, do, query)
+    )(own_block, per_head_scale, positions.reshape(64, TOK), kv_own, *moved, query_n, do)
     returned = [passed_along(piece, -(j + 1)) for j, piece in enumerate((back1, back2, back3))]
     returned[0], d_q = lax.optimization_barrier((returned[0], d_q))
-    part = call(part_body, [((TOK, D), F32)], pieces={0: 2}, columns={0: (0, D)})(w_qkv, d_q)[0]
+    d_q, part = call(
+        part_body, [((D, TOK), B16), ((TOK, D), F32)], pieces={2: 2}, columns={2: (0, D)}
+    )(d_q, query, w_qkv)
     ring_mine = [along_ring(ring_own, by) for by in (1, 2, 3)]
     ring_mine[0], ring_mine[2], tiles_mine[1], part = lax.optimization_barrier(
         (ring_mine[0], ring_mine[2], tiles_mine[1], part)

time: 140 us -> 140 us (level)
  starting transfers between devices: 54.6 us -> 56.6 us
  waiting for transfers between devices: 50.3 us -> 48.3 us
    all_to_all x3, starting transfers between devices: 25.7 us -> 27.6 us  [exchange(): return lax.all_to_all(x, axes, split_axis=0, concat_axis=0, tiled=True)]
    ppermute x6, waiting for transfers between devices: 17.6 us -> 15.9 us  [passed_along(): return lax.ppermute(x, BLK, [(i, (i + by) % peers) for i in range(peers)])]
  transfers between devices with their start and end apart: 24 -> 24, of which waited for: 11 -> 10; matrix products, arithmetic and copies ran while one was open for 2% -> 2% of each run, Pallas kernels for 15% -> 15%
where the time goes in v9:
time: 140 us; the launch traced here: 139 us
  starting transfers between devices  56.6 us (40%)
  waiting for transfers between devices  48.3 us (34%)
  Pallas kernels  30.2 us (22%)
  local copies, waits for them, and re-layouts  2.61 us (2%)
    pallas_call x8, Pallas kernels, run(): pl.pallas_call(kernel, out_shape=shapes, in_specs=[pl.BlockSpec(memory_sp...  30.2 us
    all_to_all x3, waiting for transfers between devices, exchange(): return lax.all_to_all(x, axes, split_axis=0, concat_axis=0, tiled=True)  29.6 us
    all_to_all x3, starting transfers between devices, exchange(): return lax.all_to_all(x, axes, split_axis=0, concat_axis=0, tiled=True)  27.6 us
    ppermute x6, starting transfers between devices, passed_along(): return lax.ppermute(x, BLK, [(i, (i + by) % peers) for i in range(peers)])  17 us
    ppermute x6, waiting for transfers between devices, passed_along(): return lax.ppermute(x, BLK, [(i, (i + by) % peers) for i in range(peers)])  15.9 us
    ppermute x1, starting transfers between devices, shards(): lax.ppermute(tiles[:TC], BAND, [(i, i - 1) for i in range(1, bands)])  5.14 us
    ppermute x6, starting transfers between devices, along_ring(): lax.ppermute(x, CHIPS, [(order[i], order[(i + by) % 4]) for i in range(4)])  4.82 us
    ppermute x8, waiting for transfers between devices, other_core(): return lax.ppermute(x, 'c', [(0, 1), (1, 0)])  2.83 us
  transfers between devices with their start and end apart: 24, of which 10 were waited for; matrix products, arithmetic and copies ran while one was open for 2% of the time, Pallas kernels for 15%

profile of v9, /device:TPU:1, one launch (start us, length us, event | category | flops | bytes accessed | tf_op | source)
XLA Modules:
  0.0 139.2 jit_solution(6995334230623514505)
XLA Ops:
  0.6 0.8 slice_bitcast_fusion
  1.4 5.1 %collective-permute-start = (bf16[16,1024]{1,0:T(8,128)(2,1)S(1)}, bf16[16,1024]{1,0:T(8,128)(2,1)}, u32[]{:S(2)}, u32[]{:S(2)}) collective-permute-start(bf16[16,1024]{1,0:T(8,128)(2,1)S(1)} %slice_bitcast_fusion), channel_id=1, source_target_pairs={{1,0},{2,1},{3,2},{5,4},{6,5},{7,6},{9,8},{10,9},{11,10},{13,12},{... | collective-permute-start | bytes 98312 | tf_op jit(solution)/shard_map/ppermute | solution.py:368
  6.5 1.6 %collective-permute-start.5 = (bf16[128,1024]{1,0:T(8,128)(2,1)}, bf16[128,1024]{1,0:T(8,128)(2,1)}, u32[]{:S(2)}, u32[]{:S(2)}) collective-permute-start(bf16[128,1024]{1,0:T(8,128)(2,1)} %bitcast.16), channel_id=1, source_target_pairs={{0,130},{128,0},{2,128},{130,2},{1,131},{129,1},{3,129},{131,3},{4... | collective-permute-start | bytes 786440 | tf_op jit(solution)/shard_map/ppermute | solution.py:38
  8.1 0.0 collective-permute-start.4
  8.1 1.3 reshape.28.refs_4_.refs_7_
  9.4 4.1 %shard_map.111 = (bf16[128,768]{1,0:T(8,128)(2,1)}, bf16[128,768]{1,0:T(8,128)(2,1)}, f32[256,128]{1,0:T(8,128)}, bf16[512,128]{1,0:T(8,128)(2,1)}) custom-call(bf16[128,1024]{1,0:T(8,128)(2,1)} %bitcast.18, bf16[2048,768]{1,0:T(8,128)(2,1)} %bitcast.15, bf16[16,1024]{1,0:T(8,128)(2,1)} %collective-permute-done.refs_2_, bf16[768,1280]{1,0:T(8,128)(2,1)} %refs_5_.1, ...), custom_call_target="tpu_custom_call" | custom-call | flops 1000000000 | bytes 4194304 | tf_op jit(solution)/shard_map/pallas_call | solution.py:129
  13.6 1.7 %collective-permute-start.1 = (bf16[512,128]{1,0:T(8,128)(2,1)}, bf16[512,128]{1,0:T(8,128)(2,1)}, u32[]{:S(2)}, u32[]{:S(2)}) collective-permute-start(bf16[512,128]{1,0:T(8,128)(2,1)} %get-tuple-element.38.refs_3_), channel_id=1, source_target_pairs={{0,4},{4,8},{8,12},{12,16},{16,20},{20,24},{24,28},{28,32},{32,36}... | collective-permute-start | bytes 393224 | tf_op jit(solution)/shard_map/ppermute | solution.py:33
  15.3 5.6 %collective-permute-start.3 = (bf16[512,128]{1,0:T(8,128)(2,1)}, bf16[512,128]{1,0:T(8,128)(2,1)}, u32[]{:S(2)}, u32[]{:S(2)}) collective-permute-start(bf16[512,128]{1,0:T(8,128)(2,1)} %get-tuple-element.38.refs_3_), channel_id=1, source_target_pairs={{0,12},{4,16},{8,20},{12,24},{16,28},{20,32},{24,36},{28,40},{32,4... | collective-permute-start | bytes 393224 | tf_op jit(solution)/shard_map/ppermute | solution.py:33
  20.8 1.2 collective-permute-start.2
  22.0 3.1 %collective-permute-done.1.refs_4_ = bf16[512,128]{1,0:T(8,128)(2,1)} collective-permute-done((bf16[512,128]{1,0:T(8,128)(2,1)}, bf16[512,128]{1,0:T(8,128)(2,1)}, u32[]{:S(2)}, u32[]{:S(2)}) %collective-permute-start.1) | collective-permute-done | bytes 131104 | tf_op jit(solution)/shard_map/ppermute | solution.py:33
  25.1 3.3 %shard_map.112 = (f32[768,128]{1,0:T(8,128)}, bf16[768,128]{1,0:T(8,128)(2,1)}, bf16[768,128]{1,0:T(8,128)(2,1)}, bf16[768,256]{1,0:T(8,128)(2,1)}) custom-call(bf16[128,768]{1,0:T(8,128)(2,1)} %get-tuple-element.41.refs_0_, bf16[128,768]{1,0:T(8,128)(2,1)} %bitcast.21, bf16[768,1280]{1,0:T(8,128)(2,1)} %refs_5_.1, bf16[768,768]{1,0:T(8,128)(2,1)} %refs_3_.3), custom_call_target="tpu_custom_call" | custom-call | flops 1000000000 | bytes 4194304 | tf_op jit(solution)/shard_map/pallas_call | solution.py:129
  28.4 2.2 %collective-permute-start.10 = (bf16[768,256]{1,0:T(8,128)(2,1)}, bf16[768,256]{1,0:T(8,128)(2,1)}, u32[]{:S(2)}, u32[]{:S(2)}) collective-permute-start(bf16[768,256]{1,0:T(8,128)(2,1)} %get-tuple-element.54.refs_2_), channel_id=1, source_target_pairs={{0,130},{128,0},{2,128},{130,2},{1,131},{129,1},{3,129},{131,3},{4... | collective-permute-start | bytes 1179656 | tf_op jit(solution)/shard_map/ppermute | solution.py:38
  30.6 1.1 collective-permute-start.11
  31.6 6.5 %collective-permute-done.3.refs_6_ = bf16[512,128]{1,0:T(8,128)(2,1)} collective-permute-done((bf16[512,128]{1,0:T(8,128)(2,1)}, bf16[512,128]{1,0:T(8,128)(2,1)}, u32[]{:S(2)}, u32[]{:S(2)}) %collective-permute-start.3) | collective-permute-done | bytes 131104 | tf_op jit(solution)/shard_map/ppermute | solution.py:33
  38.1 1.3 collective-permute-done.2.refs_5_
  39.4 7.0 %shard_map.113 = (bf16[768,128]{1,0:T(8,128)(2,1)}, f32[768,128]{1,0:T(8,128)}, f32[512,128]{1,0:T(8,128)}, bf16[512,128]{1,0:T(8,128)(2,1)}, bf16[512,128]{1,0:T(8,128)(2,1)}, /*index=5*/bf16[512,128]{1,0:T(8,128)(2,1)}) custom-call(s32[1]{0:T(128)} %bitcast.2.refs_0_, f32[12]{0:T(128)} %refs_1_.1, s32[64,128]{1,0:T(8,128)} %bitcast.23, ...), custom_call_target="tpu_custom_call" | custom-call | flops 1000000000 | bytes 4194304 | tf_op jit(solution)/shard_map/pallas_call | solution.py:129
  46.4 2.2 %collective-permute-start.6 = (bf16[512,128]{1,0:T(8,128)(2,1)}, bf16[512,128]{1,0:T(8,128)(2,1)}, u32[]{:S(2)}, u32[]{:S(2)}) collective-permute-start(bf16[512,128]{1,0:T(8,128)(2,1)} %get-tuple-element.47), channel_id=1, source_target_pairs={{0,252},{4,0},{8,4},{12,8},{16,12},{20,16},{24,20},{28,24},{32,28}... | collective-permute-start | bytes 393224 | tf_op jit(solution)/shard_map/ppermute | solution.py:33
  48.6 2.4 %collective-permute-start.7 = (bf16[512,128]{1,0:T(8,128)(2,1)}, bf16[512,128]{1,0:T(8,128)(2,1)}, u32[]{:S(2)}, u32[]{:S(2)}) collective-permute-start(bf16[512,128]{1,0:T(8,128)(2,1)} %get-tuple-element.50), channel_id=1, source_target_pairs={{0,248},{4,252},{8,0},{12,4},{16,8},{20,12},{24,16},{28,20},{32,24... | collective-permute-start | bytes 393224 | tf_op jit(solution)/shard_map/ppermute | solution.py:33
  51.0 4.0 %collective-permute-done.6.refs_1_ = bf16[512,128]{1,0:T(8,128)(2,1)} collective-permute-done((bf16[512,128]{1,0:T(8,128)(2,1)}, bf16[512,128]{1,0:T(8,128)(2,1)}, u32[]{:S(2)}, u32[]{:S(2)}) %collective-permute-start.6) | collective-permute-done | bytes 131104 | tf_op jit(solution)/shard_map/ppermute | solution.py:33
  55.0 3.9 %collective-permute-start.8 = (bf16[512,128]{1,0:T(8,128)(2,1)}, bf16[512,128]{1,0:T(8,128)(2,1)}, u32[]{:S(2)}, u32[]{:S(2)}) collective-permute-start(bf16[512,128]{1,0:T(8,128)(2,1)} %get-tuple-element.51), channel_id=1, source_target_pairs={{0,244},{4,248},{8,252},{12,0},{16,4},{20,8},{24,12},{28,16},{32,2... | collective-permute-start | bytes 393224 | tf_op jit(solution)/shard_map/ppermute | solution.py:33
  58.9 0.0 collective-permute-start.12
  58.9 2.8 %shard_map.114 = (bf16[768,128]{1,0:T(8,128)(2,1)}, f32[128,768]{1,0:T(8,128)}) custom-call(f32[768,128]{1,0:T(8,128)} %get-tuple-element.56.refs_0_, f32[768,128]{1,0:T(8,128)} %get-tuple-element.57.refs_1_, bf16[768,1280]{1,0:T(8,128)(2,1)} %refs_5_.1), custom_call_target="tpu_custom_call" | custom-call | flops 1000000000 | bytes 4194304 | tf_op jit(solution)/shard_map/pallas_call | solution.py:129
  61.8 0.0 collective-permute-done.10.refs_5_
  61.8 0.0 collective-permute-done.9.refs_3_
  61.8 1.0 collective-permute-done.8.refs_3_
  62.8 3.6 %shard_map.115 = bf16[8,368,128]{2,1,0:T(8,128)(2,1)} custom-call(f32[512,128]{1,0:T(8,128)} %get-tuple-element.46.refs_0_, bf16[512,128]{1,0:T(8,128)(2,1)} %collective-permute-done.6.refs_1_, bf16[512,128]{1,0:T(8,128)(2,1)} %collective-permute-done.7.refs_2_, bf16[512,128]{1,0:T(8,128)(2,1)} %collective-permute-done.8.refs_3_, ...), custom_call_target="tpu_custom_call" | custom-call | flops 1000000000 | bytes 4194304 | tf_op jit(solution)/shard_map/pallas_call | solution.py:129
  66.4 8.6 %all-to-all-start = ((bf16[8,368,128]{2,1,0:T(8,128)(2,1)}), bf16[8,368,128]{2,1,0:T(8,128)(2,1)}, u32[]{:S(2)}, u32[]{:S(2)}) async-start(bf16[8,368,128]{2,1,0:T(8,128)(2,1)} %shard_map.115), calls=%async_computation | async-start | bytes 1507328 | tf_op jit(solution)/shard_map/all_to_all | solution.py:46
  75.0 0.2 collective-permute-start.17
  75.2 0.3 collective-permute-start.18
  75.5 0.2 collective-permute-start.20
  75.8 0.3 collective-permute-start.13
  76.0 0.9 collective-permute-done.17.refs_14_
  76.9 0.2 collective-permute-start.14
  77.1 0.3 collective-permute-start.15
  77.4 0.2 collective-permute-start.16
  77.6 0.0 collective-permute-done.20.refs_17_
  77.7 0.3 collective-permute-start.19
  77.9 0.6 pad_add_fusion.refs_0_
  78.5 1.9 %collective-permute-done.19.refs_16_ = bf16[128,1024]{1,0:T(8,128)(2,1)} collective-permute-done((bf16[128,1024]{1,0:T(8,128)(2,1)}, bf16[128,1024]{1,0:T(8,128)(2,1)}, u32[]{:S(2)}, u32[]{:S(2)}) %collective-permute-start.19) | collective-permute-done | bytes 262176 | tf_op jit(solution)/shard_map/ppermute | solution.py:42
  80.5 5.3 %all-to-all-done.refs_1_ = bf16[8,368,128]{2,1,0:T(8,128)(2,1)} async-done(((bf16[8,368,128]{2,1,0:T(8,128)(2,1)}), bf16[8,368,128]{2,1,0:T(8,128)(2,1)}, u32[]{:S(2)}, u32[]{:S(2)}) %all-to-all-start) | async-done | bytes 753696 | tf_op jit(solution)/shard_map/all_to_all | solution.py:46
  85.7 6.7 %shard_map.116 = bf16[3328,128]{1,0:T(8,128)(2,1)} custom-call(s32[2]{0:T(128)} %pad_add_fusion.refs_0_, bf16[8,368,128]{2,1,0:T(8,128)(2,1)} %all-to-all-done.refs_1_, bf16[768,256]{1,0:T(8,128)(2,1)} %get-tuple-element.54.refs_2_, bf16[768,256]{1,0:T(8,128)(2,1)} %collective-permute-done.9.refs_3_, bf16[768,256]{1,0:T(8,128)(2,1)} %collective-permute-done.12.refs_4_, ...), custom_call_target="tpu_custom_call" | custom-call | flops 1000000000 | bytes 4194304 | tf_op jit(solution)/shard_map/pallas_call | solution.py:129
  92.4 9.7 %all-to-all-start.1 = ((bf16[32,104,128]{2,1,0:T(8,128)(2,1)}), bf16[32,104,128]{2,1,0:T(8,128)(2,1)S(1)}, u32[]{:S(2)}, u32[]{:S(2)}) async-start(bf16[32,104,128]{2,1,0:T(8,128)(2,1)} %bitcast.14), calls=%async_computation.1 | async-start | bytes 1703936 | tf_op jit(solution)/shard_map/all_to_all | solution.py:46
  102.1 20.2 %all-to-all-done.1.refs_0_ = bf16[32,104,128]{2,1,0:T(8,128)(2,1)S(1)} async-done(((bf16[32,104,128]{2,1,0:T(8,128)(2,1)}), bf16[32,104,128]{2,1,0:T(8,128)(2,1)S(1)}, u32[]{:S(2)}, u32[]{:S(2)}) %all-to-all-start.1) | async-done | bytes 852000 | tf_op jit(solution)/shard_map/all_to_all | solution.py:46
  122.3 1.9 %shard_map.117 = (f32[3,2,1024]{2,1,0:T(2,128)}, f32[1,768]{1,0:T(1,128)S(1)}, f32[8,8,256]{2,1,0:T(8,128)}) custom-call(bf16[32,104,128]{2,1,0:T(8,128)(2,1)S(1)} %all-to-all-done.1.refs_0_), custom_call_target="tpu_custom_call" | custom-call | flops 1000000000 | bytes 4194304 | tf_op jit(solution)/shard_map/pallas_call | solution.py:129
  124.2 9.3 %all-to-all-start.2 = ((f32[8,8,256]{2,1,0:T(8,128)}), f32[8,8,256]{2,1,0:T(8,128)S(1)}, u32[]{:S(2)}, u32[]{:S(2)}) async-start(f32[8,8,256]{2,1,0:T(8,128)} %get-tuple-element.69), calls=%async_computation.2 | async-start | bytes 131072 | tf_op jit(solution)/shard_map/all_to_all | solution.py:46
  133.6 0.6 dynamic-slice_bitcast_fusion
  134.1 4.1 %all-to-all-done.2.refs_0_ = f32[8,8,256]{2,1,0:T(8,128)S(1)} async-done(((f32[8,8,256]{2,1,0:T(8,128)}), f32[8,8,256]{2,1,0:T(8,128)S(1)}, u32[]{:S(2)}, u32[]{:S(2)}) %all-to-all-start.2) | async-done | bytes 65568 | tf_op jit(solution)/shard_map/all_to_all | solution.py:46
  138.3 0.8 shard_map.118
  (12 shorter events, 0.0 us)
Async XLA Ops:
  1.4 8.0 %collective-permute-start = (bf16[16,1024]{1,0:T(8,128)(2,1)S(1)}, bf16[16,1024]{1,0:T(8,128)(2,1)}, u32[]{:S(2)}, u32[]{:S(2)}) collective-permute-start(bf16[16,1024]{1,0:T(8,128)(2,1)S(1)} %slice_bitcast_fusion), channel_id=1, source_target_pairs={{1,0},{2,1},{3,2},{5,4},{6,5},{7,6},{9,8},{10,9},{11,10},{13,12},{... | collective-permute-start | bytes 98312 | tf_op jit(solution)/shard_map/ppermute | solution.py:368
  6.5 24.0 %collective-permute-start.5 = (bf16[128,1024]{1,0:T(8,128)(2,1)}, bf16[128,1024]{1,0:T(8,128)(2,1)}, u32[]{:S(2)}, u32[]{:S(2)}) collective-permute-start(bf16[128,1024]{1,0:T(8,128)(2,1)} %bitcast.16), channel_id=1, source_target_pairs={{0,130},{128,0},{2,128},{130,2},{1,131},{129,1},{3,129},{131,3},{4... | collective-permute-start | bytes 786440 | tf_op jit(solution)/shard_map/ppermute | solution.py:38
  8.1 22.4 %collective-permute-start.4 = (bf16[128,1024]{1,0:T(8,128)(2,1)}, bf16[128,1024]{1,0:T(8,128)(2,1)}, u32[]{:S(2)}, u32[]{:S(2)}) collective-permute-start(bf16[128,1024]{1,0:T(8,128)(2,1)} %bitcast.17), channel_id=1, source_target_pairs={{0,128},{128,2},{2,130},{130,0},{1,129},{129,3},{3,131},{131,1},{4... | collective-permute-start | bytes 786440 | tf_op jit(solution)/shard_map/ppermute | solution.py:38
  13.6 11.5 %collective-permute-start.1 = (bf16[512,128]{1,0:T(8,128)(2,1)}, bf16[512,128]{1,0:T(8,128)(2,1)}, u32[]{:S(2)}, u32[]{:S(2)}) collective-permute-start(bf16[512,128]{1,0:T(8,128)(2,1)} %get-tuple-element.38.refs_3_), channel_id=1, source_target_pairs={{0,4},{4,8},{8,12},{12,16},{16,20},{20,24},{24,28},{28,32},{32,36}... | collective-permute-start | bytes 393224 | tf_op jit(solution)/shard_map/ppermute | solution.py:33
  15.3 22.8 %collective-permute-start.3 = (bf16[512,128]{1,0:T(8,128)(2,1)}, bf16[512,128]{1,0:T(8,128)(2,1)}, u32[]{:S(2)}, u32[]{:S(2)}) collective-permute-start(bf16[512,128]{1,0:T(8,128)(2,1)} %get-tuple-element.38.refs_3_), channel_id=1, source_target_pairs={{0,12},{4,16},{8,20},{12,24},{16,28},{20,32},{24,36},{28,40},{32,4... | collective-permute-start | bytes 393224 | tf_op jit(solution)/shard_map/ppermute | solution.py:33
  20.8 18.5 %collective-permute-start.2 = (bf16[512,128]{1,0:T(8,128)(2,1)}, bf16[512,128]{1,0:T(8,128)(2,1)}, u32[]{:S(2)}, u32[]{:S(2)}) collective-permute-start(bf16[512,128]{1,0:T(8,128)(2,1)} %get-tuple-element.38.refs_3_), channel_id=1, source_target_pairs={{0,8},{4,12},{8,16},{12,20},{16,24},{20,28},{24,32},{28,36},{32,40... | collective-permute-start | bytes 393224 | tf_op jit(solution)/shard_map/ppermute | solution.py:33
  28.4 33.4 %collective-permute-start.10 = (bf16[768,256]{1,0:T(8,128)(2,1)}, bf16[768,256]{1,0:T(8,128)(2,1)}, u32[]{:S(2)}, u32[]{:S(2)}) collective-permute-start(bf16[768,256]{1,0:T(8,128)(2,1)} %get-tuple-element.54.refs_2_), channel_id=1, source_target_pairs={{0,130},{128,0},{2,128},{130,2},{1,131},{129,1},{3,129},{131,3},{4... | collective-permute-start | bytes 1179656 | tf_op jit(solution)/shard_map/ppermute | solution.py:38
  30.5 31.2 %collective-permute-start.9 = (bf16[768,256]{1,0:T(8,128)(2,1)}, bf16[768,256]{1,0:T(8,128)(2,1)}, u32[]{:S(2)}, u32[]{:S(2)}) collective-permute-start(bf16[768,256]{1,0:T(8,128)(2,1)} %get-tuple-element.54.refs_2_), channel_id=1, source_target_pairs={{0,128},{128,2},{2,130},{130,0},{1,129},{129,3},{3,131},{131,1},{4... | collective-permute-start | bytes 1179656 | tf_op jit(solution)/shard_map/ppermute | solution.py:38
  30.6 28.4 %collective-permute-start.11 = (bf16[128,1024]{1,0:T(8,128)(2,1)}, bf16[128,1024]{1,0:T(8,128)(2,1)}, u32[]{:S(2)}, u32[]{:S(2)}) collective-permute-start(bf16[128,1024]{1,0:T(8,128)(2,1)} %collective-permute-done.4.refs_11_), channel_id=1, source_target_pairs={{0,128},{128,2},{2,130},{130,0},{1,129},{129,3},{3,131},{131,1},{4... | collective-permute-start | bytes 786440 | tf_op jit(solution)/shard_map/ppermute | solution.py:38
  46.4 8.6 %collective-permute-start.6 = (bf16[512,128]{1,0:T(8,128)(2,1)}, bf16[512,128]{1,0:T(8,128)(2,1)}, u32[]{:S(2)}, u32[]{:S(2)}) collective-permute-start(bf16[512,128]{1,0:T(8,128)(2,1)} %get-tuple-element.47), channel_id=1, source_target_pairs={{0,252},{4,0},{8,4},{12,8},{16,12},{20,16},{24,20},{28,24},{32,28}... | collective-permute-start | bytes 393224 | tf_op jit(solution)/shard_map/ppermute | solution.py:33
  48.6 13.2 %collective-permute-start.7 = (bf16[512,128]{1,0:T(8,128)(2,1)}, bf16[512,128]{1,0:T(8,128)(2,1)}, u32[]{:S(2)}, u32[]{:S(2)}) collective-permute-start(bf16[512,128]{1,0:T(8,128)(2,1)} %get-tuple-element.50), channel_id=1, source_target_pairs={{0,248},{4,252},{8,0},{12,4},{16,8},{20,12},{24,16},{28,20},{32,24... | collective-permute-start | bytes 393224 | tf_op jit(solution)/shard_map/ppermute | solution.py:33
  55.0 7.8 %collective-permute-start.8 = (bf16[512,128]{1,0:T(8,128)(2,1)}, bf16[512,128]{1,0:T(8,128)(2,1)}, u32[]{:S(2)}, u32[]{:S(2)}) collective-permute-start(bf16[512,128]{1,0:T(8,128)(2,1)} %get-tuple-element.51), channel_id=1, source_target_pairs={{0,244},{4,248},{8,252},{12,0},{16,4},{20,8},{24,12},{28,16},{32,2... | collective-permute-start | bytes 393224 | tf_op jit(solution)/shard_map/ppermute | solution.py:33
  58.9 18.2 %collective-permute-start.12 = (bf16[768,256]{1,0:T(8,128)(2,1)}, bf16[768,256]{1,0:T(8,128)(2,1)}, u32[]{:S(2)}, u32[]{:S(2)}) collective-permute-start(bf16[768,256]{1,0:T(8,128)(2,1)} %get-tuple-element.54.refs_2_), channel_id=1, source_target_pairs={{0,2},{128,130},{2,0},{130,128},{1,3},{129,131},{3,1},{131,129},{4... | collective-permute-start | bytes 1179656 | tf_op jit(solution)/shard_map/ppermute | solution.py:38
  66.4 19.3 %all-to-all-start = ((bf16[8,368,128]{2,1,0:T(8,128)(2,1)}), bf16[8,368,128]{2,1,0:T(8,128)(2,1)}, u32[]{:S(2)}, u32[]{:S(2)}) async-start(bf16[8,368,128]{2,1,0:T(8,128)(2,1)} %shard_map.115), calls=%async_computation | async-start | bytes 1507328 | tf_op jit(solution)/shard_map/all_to_all | solution.py:46
  75.0 1.9 %collective-permute-start.17 = (bf16[128,1024]{1,0:T(8,128)(2,1)}, bf16[128,1024]{1,0:T(8,128)(2,1)}, u32[]{:S(2)}, u32[]{:S(2)}) collective-permute-start(bf16[128,1024]{1,0:T(8,128)(2,1)} %bitcast.19), channel_id=1, source_target_pairs={{0,1},{1,0},{2,3},{3,2},{4,5},{5,4},{6,7},{7,6},{8,9},{9,8},{10,11... | collective-permute-start | bytes 786440 | tf_op jit(solution)/shard_map/ppermute | solution.py:42
  75.2 2.2 %collective-permute-start.18 = (bf16[128,1024]{1,0:T(8,128)(2,1)}, bf16[128,1024]{1,0:T(8,128)(2,1)}, u32[]{:S(2)}, u32[]{:S(2)}) collective-permute-start(bf16[128,1024]{1,0:T(8,128)(2,1)} %collective-permute-done.4.refs_11_), channel_id=1, source_target_pairs={{0,1},{1,0},{2,3},{3,2},{4,5},{5,4},{6,7},{7,6},{8,9},{9,8},{10,11... | collective-permute-start | bytes 786440 | tf_op jit(solution)/shard_map/ppermute | solution.py:42
  75.5 2.1 %collective-permute-start.20 = (bf16[128,1024]{1,0:T(8,128)(2,1)}, bf16[128,1024]{1,0:T(8,128)(2,1)}, u32[]{:S(2)}, u32[]{:S(2)}) collective-permute-start(bf16[128,1024]{1,0:T(8,128)(2,1)} %collective-permute-done.5.refs_13_), channel_id=1, source_target_pairs={{0,1},{1,0},{2,3},{3,2},{4,5},{5,4},{6,7},{7,6},{8,9},{9,8},{10,11... | collective-permute-start | bytes 786440 | tf_op jit(solution)/shard_map/ppermute | solution.py:42
  75.8 2.8 %collective-permute-start.13 = (bf16[768,256]{1,0:T(8,128)(2,1)}, bf16[768,256]{1,0:T(8,128)(2,1)}, u32[]{:S(2)}, u32[]{:S(2)}) collective-permute-start(bf16[768,256]{1,0:T(8,128)(2,1)} %get-tuple-element.54.refs_2_), channel_id=1, source_target_pairs={{0,1},{1,0},{2,3},{3,2},{4,5},{5,4},{6,7},{7,6},{8,9},{9,8},{10,11... | collective-permute-start | bytes 1179656 | tf_op jit(solution)/shard_map/ppermute | solution.py:42
  76.9 3.6 %collective-permute-start.14 = (bf16[768,256]{1,0:T(8,128)(2,1)}, bf16[768,256]{1,0:T(8,128)(2,1)}, u32[]{:S(2)}, u32[]{:S(2)}) collective-permute-start(bf16[768,256]{1,0:T(8,128)(2,1)} %collective-permute-done.9.refs_3_), channel_id=1, source_target_pairs={{0,1},{1,0},{2,3},{3,2},{4,5},{5,4},{6,7},{7,6},{8,9},{9,8},{10,11... | collective-permute-start | bytes 1179656 | tf_op jit(solution)/shard_map/ppermute | solution.py:42
  77.1 3.3 %collective-permute-start.15 = (bf16[768,256]{1,0:T(8,128)(2,1)}, bf16[768,256]{1,0:T(8,128)(2,1)}, u32[]{:S(2)}, u32[]{:S(2)}) collective-permute-start(bf16[768,256]{1,0:T(8,128)(2,1)} %collective-permute-done.12.refs_4_), channel_id=1, source_target_pairs={{0,1},{1,0},{2,3},{3,2},{4,5},{5,4},{6,7},{7,6},{8,9},{9,8},{10,11... | collective-permute-start | bytes 1179656 | tf_op jit(solution)/shard_map/ppermute | solution.py:42
  77.4 3.1 %collective-permute-start.16 = (bf16[768,256]{1,0:T(8,128)(2,1)}, bf16[768,256]{1,0:T(8,128)(2,1)}, u32[]{:S(2)}, u32[]{:S(2)}) collective-permute-start(bf16[768,256]{1,0:T(8,128)(2,1)} %collective-permute-done.10.refs_5_), channel_id=1, source_target_pairs={{0,1},{1,0},{2,3},{3,2},{4,5},{5,4},{6,7},{7,6},{8,9},{9,8},{10,11... | collective-permute-start | bytes 1179656 | tf_op jit(solution)/shard_map/ppermute | solution.py:42
  77.7 2.8 %collective-permute-start.19 = (bf16[128,1024]{1,0:T(8,128)(2,1)}, bf16[128,1024]{1,0:T(8,128)(2,1)}, u32[]{:S(2)}, u32[]{:S(2)}) collective-permute-start(bf16[128,1024]{1,0:T(8,128)(2,1)} %collective-permute-done.11.refs_12_), channel_id=1, source_target_pairs={{0,1},{1,0},{2,3},{3,2},{4,5},{5,4},{6,7},{7,6},{8,9},{9,8},{10,11... | collective-permute-start | bytes 786440 | tf_op jit(solution)/shard_map/ppermute | solution.py:42
  92.4 29.9 %all-to-all-start.1 = ((bf16[32,104,128]{2,1,0:T(8,128)(2,1)}), bf16[32,104,128]{2,1,0:T(8,128)(2,1)S(1)}, u32[]{:S(2)}, u32[]{:S(2)}) async-start(bf16[32,104,128]{2,1,0:T(8,128)(2,1)} %bitcast.14), calls=%async_computation.1 | async-start | bytes 1703936 | tf_op jit(solution)/shard_map/all_to_all | solution.py:46
  124.2 14.0 %all-to-all-start.2 = ((f32[8,8,256]{2,1,0:T(8,128)}), f32[8,8,256]{2,1,0:T(8,128)S(1)}, u32[]{:S(2)}, u32[]{:S(2)}) async-start(f32[8,8,256]{2,1,0:T(8,128)} %get-tuple-element.69), calls=%async_computation.2 | async-start | bytes 131072 | tf_op jit(solution)/shard_map/all_to_all | solution.py:46

commit v10 on v9

--- a/solution.py
+++ b/solution.py
@@ -433,6 +433,7 @@
         ],
         smem=(0,),
         joined=10,
+        pieces={1: 4},
     )(place, late_ring, *rings, *blocks)[0]
     stem_total, gain_total, row_total = call(
         total_body,

time: 140 us -> 140 us (level)
  no operation moved by 1% of the time
where the time goes in v10:
time: 140 us; the launch traced here: 139 us
  starting transfers between devices  56.6 us (40%)
  waiting for transfers between devices  48.3 us (34%)
  Pallas kernels  30.3 us (22%)
  local copies, waits for them, and re-layouts  2.61 us (2%)
    pallas_call x8, Pallas kernels, run(): pl.pallas_call(kernel, out_shape=shapes, in_specs=[pl.BlockSpec(memory_sp...  30.3 us
    all_to_all x3, waiting for transfers between devices, exchange(): return lax.all_to_all(x, axes, split_axis=0, concat_axis=0, tiled=True)  29.5 us
    all_to_all x3, starting transfers between devices, exchange(): return lax.all_to_all(x, axes, split_axis=0, concat_axis=0, tiled=True)  27.6 us
    ppermute x6, starting transfers between devices, passed_along(): return lax.ppermute(x, BLK, [(i, (i + by) % peers) for i in range(peers)])  17 us
    ppermute x6, waiting for transfers between devices, passed_along(): return lax.ppermute(x, BLK, [(i, (i + by) % peers) for i in range(peers)])  15.9 us
    ppermute x1, starting transfers between devices, shards(): lax.ppermute(tiles[:TC], BAND, [(i, i - 1) for i in range(1, bands)])  5.14 us
    ppermute x6, starting transfers between devices, along_ring(): lax.ppermute(x, CHIPS, [(order[i], order[(i + by) % 4]) for i in range(4)])  4.82 us
    ppermute x8, waiting for transfers between devices, other_core(): return lax.ppermute(x, 'c', [(0, 1), (1, 0)])  2.83 us
  transfers between devices with their start and end apart: 24, of which 10 were waited for; matrix products, arithmetic and copies ran while one was open for 2% of the time, Pallas kernels for 15%

profile of v10, /device:TPU:1, one launch (start us, length us, event | category | flops | bytes accessed | tf_op | source)
XLA Modules:
  0.0 139.3 jit_solution(12292780061633038180)
XLA Ops:
  0.6 0.8 slice_bitcast_fusion
  1.4 5.1 %collective-permute-start = (bf16[16,1024]{1,0:T(8,128)(2,1)S(1)}, bf16[16,1024]{1,0:T(8,128)(2,1)}, u32[]{:S(2)}, u32[]{:S(2)}) collective-permute-start(bf16[16,1024]{1,0:T(8,128)(2,1)S(1)} %slice_bitcast_fusion), channel_id=1, source_target_pairs={{1,0},{2,1},{3,2},{5,4},{6,5},{7,6},{9,8},{10,9},{11,10},{13,12},{... | collective-permute-start | bytes 98312 | tf_op jit(solution)/shard_map/ppermute | solution.py:368
  6.5 1.6 %collective-permute-start.5 = (bf16[128,1024]{1,0:T(8,128)(2,1)}, bf16[128,1024]{1,0:T(8,128)(2,1)}, u32[]{:S(2)}, u32[]{:S(2)}) collective-permute-start(bf16[128,1024]{1,0:T(8,128)(2,1)} %bitcast.16), channel_id=1, source_target_pairs={{0,130},{128,0},{2,128},{130,2},{1,131},{129,1},{3,129},{131,3},{4... | collective-permute-start | bytes 786440 | tf_op jit(solution)/shard_map/ppermute | solution.py:38
  8.1 0.0 collective-permute-start.4
  8.1 1.3 reshape.28.refs_4_.refs_7_
  9.4 4.1 %shard_map.111 = (bf16[128,768]{1,0:T(8,128)(2,1)}, bf16[128,768]{1,0:T(8,128)(2,1)}, f32[256,128]{1,0:T(8,128)}, bf16[512,128]{1,0:T(8,128)(2,1)}) custom-call(bf16[128,1024]{1,0:T(8,128)(2,1)} %bitcast.18, bf16[2048,768]{1,0:T(8,128)(2,1)} %bitcast.15, bf16[16,1024]{1,0:T(8,128)(2,1)} %collective-permute-done.refs_2_, bf16[768,1280]{1,0:T(8,128)(2,1)} %refs_5_.1, ...), custom_call_target="tpu_custom_call" | custom-call | flops 1000000000 | bytes 4194304 | tf_op jit(solution)/shard_map/pallas_call | solution.py:129
  13.6 1.7 %collective-permute-start.1 = (bf16[512,128]{1,0:T(8,128)(2,1)}, bf16[512,128]{1,0:T(8,128)(2,1)}, u32[]{:S(2)}, u32[]{:S(2)}) collective-permute-start(bf16[512,128]{1,0:T(8,128)(2,1)} %get-tuple-element.38.refs_3_), channel_id=1, source_target_pairs={{0,4},{4,8},{8,12},{12,16},{16,20},{20,24},{24,28},{28,32},{32,36}... | collective-permute-start | bytes 393224 | tf_op jit(solution)/shard_map/ppermute | solution.py:33
  15.3 5.6 %collective-permute-start.3 = (bf16[512,128]{1,0:T(8,128)(2,1)}, bf16[512,128]{1,0:T(8,128)(2,1)}, u32[]{:S(2)}, u32[]{:S(2)}) collective-permute-start(bf16[512,128]{1,0:T(8,128)(2,1)} %get-tuple-element.38.refs_3_), channel_id=1, source_target_pairs={{0,12},{4,16},{8,20},{12,24},{16,28},{20,32},{24,36},{28,40},{32,4... | collective-permute-start | bytes 393224 | tf_op jit(solution)/shard_map/ppermute | solution.py:33
  20.8 1.2 collective-permute-start.2
  22.0 3.1 %collective-permute-done.1.refs_4_ = bf16[512,128]{1,0:T(8,128)(2,1)} collective-permute-done((bf16[512,128]{1,0:T(8,128)(2,1)}, bf16[512,128]{1,0:T(8,128)(2,1)}, u32[]{:S(2)}, u32[]{:S(2)}) %collective-permute-start.1) | collective-permute-done | bytes 131104 | tf_op jit(solution)/shard_map/ppermute | solution.py:33
  25.1 3.3 %shard_map.112 = (f32[768,128]{1,0:T(8,128)}, bf16[768,128]{1,0:T(8,128)(2,1)}, bf16[768,128]{1,0:T(8,128)(2,1)}, bf16[768,256]{1,0:T(8,128)(2,1)}) custom-call(bf16[128,768]{1,0:T(8,128)(2,1)} %get-tuple-element.41.refs_0_, bf16[128,768]{1,0:T(8,128)(2,1)} %bitcast.21, bf16[768,1280]{1,0:T(8,128)(2,1)} %refs_5_.1, bf16[768,768]{1,0:T(8,128)(2,1)} %refs_3_.3), custom_call_target="tpu_custom_call" | custom-call | flops 1000000000 | bytes 4194304 | tf_op jit(solution)/shard_map/pallas_call | solution.py:129
  28.4 2.2 %collective-permute-start.10 = (bf16[768,256]{1,0:T(8,128)(2,1)}, bf16[768,256]{1,0:T(8,128)(2,1)}, u32[]{:S(2)}, u32[]{:S(2)}) collective-permute-start(bf16[768,256]{1,0:T(8,128)(2,1)} %get-tuple-element.54.refs_2_), channel_id=1, source_target_pairs={{0,130},{128,0},{2,128},{130,2},{1,131},{129,1},{3,129},{131,3},{4... | collective-permute-start | bytes 1179656 | tf_op jit(solution)/shard_map/ppermute | solution.py:38
  30.6 1.1 collective-permute-start.11
  31.6 6.5 %collective-permute-done.3.refs_6_ = bf16[512,128]{1,0:T(8,128)(2,1)} collective-permute-done((bf16[512,128]{1,0:T(8,128)(2,1)}, bf16[512,128]{1,0:T(8,128)(2,1)}, u32[]{:S(2)}, u32[]{:S(2)}) %collective-permute-start.3) | collective-permute-done | bytes 131104 | tf_op jit(solution)/shard_map/ppermute | solution.py:33
  38.1 1.3 collective-permute-done.2.refs_5_
  39.4 7.0 %shard_map.113 = (bf16[768,128]{1,0:T(8,128)(2,1)}, f32[768,128]{1,0:T(8,128)}, f32[512,128]{1,0:T(8,128)}, bf16[512,128]{1,0:T(8,128)(2,1)}, bf16[512,128]{1,0:T(8,128)(2,1)}, /*index=5*/bf16[512,128]{1,0:T(8,128)(2,1)}) custom-call(s32[1]{0:T(128)} %bitcast.2.refs_0_, f32[12]{0:T(128)} %refs_1_.1, s32[64,128]{1,0:T(8,128)} %bitcast.23, ...), custom_call_target="tpu_custom_call" | custom-call | flops 1000000000 | bytes 4194304 | tf_op jit(solution)/shard_map/pallas_call | solution.py:129
  46.4 2.2 %collective-permute-start.6 = (bf16[512,128]{1,0:T(8,128)(2,1)}, bf16[512,128]{1,0:T(8,128)(2,1)}, u32[]{:S(2)}, u32[]{:S(2)}) collective-permute-start(bf16[512,128]{1,0:T(8,128)(2,1)} %get-tuple-element.47), channel_id=1, source_target_pairs={{0,252},{4,0},{8,4},{12,8},{16,12},{20,16},{24,20},{28,24},{32,28}... | collective-permute-start | bytes 393224 | tf_op jit(solution)/shard_map/ppermute | solution.py:33
  48.6 2.4 %collective-permute-start.7 = (bf16[512,128]{1,0:T(8,128)(2,1)}, bf16[512,128]{1,0:T(8,128)(2,1)}, u32[]{:S(2)}, u32[]{:S(2)}) collective-permute-start(bf16[512,128]{1,0:T(8,128)(2,1)} %get-tuple-element.50), channel_id=1, source_target_pairs={{0,248},{4,252},{8,0},{12,4},{16,8},{20,12},{24,16},{28,20},{32,24... | collective-permute-start | bytes 393224 | tf_op jit(solution)/shard_map/ppermute | solution.py:33
  51.0 4.0 %collective-permute-done.6.refs_1_ = bf16[512,128]{1,0:T(8,128)(2,1)} collective-permute-done((bf16[512,128]{1,0:T(8,128)(2,1)}, bf16[512,128]{1,0:T(8,128)(2,1)}, u32[]{:S(2)}, u32[]{:S(2)}) %collective-permute-start.6) | collective-permute-done | bytes 131104 | tf_op jit(solution)/shard_map/ppermute | solution.py:33
  55.0 3.9 %collective-permute-start.8 = (bf16[512,128]{1,0:T(8,128)(2,1)}, bf16[512,128]{1,0:T(8,128)(2,1)}, u32[]{:S(2)}, u32[]{:S(2)}) collective-permute-start(bf16[512,128]{1,0:T(8,128)(2,1)} %get-tuple-element.51), channel_id=1, source_target_pairs={{0,244},{4,248},{8,252},{12,0},{16,4},{20,8},{24,12},{28,16},{32,2... | collective-permute-start | bytes 393224 | tf_op jit(solution)/shard_map/ppermute | solution.py:33
  58.9 0.0 collective-permute-start.12
  58.9 2.8 %shard_map.114 = (bf16[768,128]{1,0:T(8,128)(2,1)}, f32[128,768]{1,0:T(8,128)}) custom-call(f32[768,128]{1,0:T(8,128)} %get-tuple-element.56.refs_0_, f32[768,128]{1,0:T(8,128)} %get-tuple-element.57.refs_1_, bf16[768,1280]{1,0:T(8,128)(2,1)} %refs_5_.1), custom_call_target="tpu_custom_call" | custom-call | flops 1000000000 | bytes 4194304 | tf_op jit(solution)/shard_map/pallas_call | solution.py:129
  61.8 0.0 collective-permute-done.10.refs_5_
  61.8 0.0 collective-permute-done.9.refs_3_
  61.8 1.0 collective-permute-done.8.refs_3_
  62.8 3.6 %shard_map.115 = bf16[8,368,128]{2,1,0:T(8,128)(2,1)} custom-call(f32[512,128]{1,0:T(8,128)} %get-tuple-element.46.refs_0_, bf16[512,128]{1,0:T(8,128)(2,1)} %collective-permute-done.6.refs_1_, bf16[512,128]{1,0:T(8,128)(2,1)} %collective-permute-done.7.refs_2_, bf16[512,128]{1,0:T(8,128)(2,1)} %collective-permute-done.8.refs_3_, ...), custom_call_target="tpu_custom_call" | custom-call | flops 1000000000 | bytes 4194304 | tf_op jit(solution)/shard_map/pallas_call | solution.py:129
  66.4 8.6 %all-to-all-start = ((bf16[8,368,128]{2,1,0:T(8,128)(2,1)}), bf16[8,368,128]{2,1,0:T(8,128)(2,1)}, u32[]{:S(2)}, u32[]{:S(2)}) async-start(bf16[8,368,128]{2,1,0:T(8,128)(2,1)} %shard_map.115), calls=%async_computation | async-start | bytes 1507328 | tf_op jit(solution)/shard_map/all_to_all | solution.py:46
  75.0 0.2 collective-permute-start.17
  75.2 0.3 collective-permute-start.18
  75.5 0.2 collective-permute-start.20
  75.8 0.3 collective-permute-start.13
  76.0 0.9 collective-permute-done.17.refs_14_
  76.9 0.2 collective-permute-start.14
  77.1 0.3 collective-permute-start.15
  77.4 0.2 collective-permute-start.16
  77.6 0.0 collective-permute-done.20.refs_17_
  77.7 0.3 collective-permute-start.19
  77.9 0.6 pad_add_fusion.refs_0_
  78.5 1.9 %collective-permute-done.19.refs_16_ = bf16[128,1024]{1,0:T(8,128)(2,1)} collective-permute-done((bf16[128,1024]{1,0:T(8,128)(2,1)}, bf16[128,1024]{1,0:T(8,128)(2,1)}, u32[]{:S(2)}, u32[]{:S(2)}) %collective-permute-start.19) | collective-permute-done | bytes 262176 | tf_op jit(solution)/shard_map/ppermute | solution.py:42
  80.5 5.3 %all-to-all-done.refs_1_ = bf16[8,368,128]{2,1,0:T(8,128)(2,1)} async-done(((bf16[8,368,128]{2,1,0:T(8,128)(2,1)}), bf16[8,368,128]{2,1,0:T(8,128)(2,1)}, u32[]{:S(2)}, u32[]{:S(2)}) %all-to-all-start) | async-done | bytes 753696 | tf_op jit(solution)/shard_map/all_to_all | solution.py:46
  85.7 6.8 %shard_map.116 = bf16[3328,128]{1,0:T(8,128)(2,1)} custom-call(s32[2]{0:T(128)} %pad_add_fusion.refs_0_, bf16[8,368,128]{2,1,0:T(8,128)(2,1)} %all-to-all-done.refs_1_, bf16[768,256]{1,0:T(8,128)(2,1)} %get-tuple-element.54.refs_2_, bf16[768,256]{1,0:T(8,128)(2,1)} %collective-permute-done.9.refs_3_, bf16[768,256]{1,0:T(8,128)(2,1)} %collective-permute-done.12.refs_4_, ...), custom_call_target="tpu_custom_call" | custom-call | flops 1000000000 | bytes 4194304 | tf_op jit(solution)/shard_map/pallas_call | solution.py:129
  92.5 9.7 %all-to-all-start.1 = ((bf16[32,104,128]{2,1,0:T(8,128)(2,1)}), bf16[32,104,128]{2,1,0:T(8,128)(2,1)S(1)}, u32[]{:S(2)}, u32[]{:S(2)}) async-start(bf16[32,104,128]{2,1,0:T(8,128)(2,1)} %bitcast.14), calls=%async_computation.1 | async-start | bytes 1703936 | tf_op jit(solution)/shard_map/all_to_all | solution.py:46
  102.2 20.2 %all-to-all-done.1.refs_0_ = bf16[32,104,128]{2,1,0:T(8,128)(2,1)S(1)} async-done(((bf16[32,104,128]{2,1,0:T(8,128)(2,1)}), bf16[32,104,128]{2,1,0:T(8,128)(2,1)S(1)}, u32[]{:S(2)}, u32[]{:S(2)}) %all-to-all-start.1) | async-done | bytes 852000 | tf_op jit(solution)/shard_map/all_to_all | solution.py:46
  122.4 1.9 %shard_map.117 = (f32[3,2,1024]{2,1,0:T(2,128)}, f32[1,768]{1,0:T(1,128)S(1)}, f32[8,8,256]{2,1,0:T(8,128)}) custom-call(bf16[32,104,128]{2,1,0:T(8,128)(2,1)S(1)} %all-to-all-done.1.refs_0_), custom_call_target="tpu_custom_call" | custom-call | flops 1000000000 | bytes 4194304 | tf_op jit(solution)/shard_map/pallas_call | solution.py:129
  124.3 9.3 %all-to-all-start.2 = ((f32[8,8,256]{2,1,0:T(8,128)}), f32[8,8,256]{2,1,0:T(8,128)S(1)}, u32[]{:S(2)}, u32[]{:S(2)}) async-start(f32[8,8,256]{2,1,0:T(8,128)} %get-tuple-element.69), calls=%async_computation.2 | async-start | bytes 131072 | tf_op jit(solution)/shard_map/all_to_all | solution.py:46
  133.7 0.6 dynamic-slice_bitcast_fusion
  134.2 4.1 %all-to-all-done.2.refs_0_ = f32[8,8,256]{2,1,0:T(8,128)S(1)} async-done(((f32[8,8,256]{2,1,0:T(8,128)}), f32[8,8,256]{2,1,0:T(8,128)S(1)}, u32[]{:S(2)}, u32[]{:S(2)}) %all-to-all-start.2) | async-done | bytes 65568 | tf_op jit(solution)/shard_map/all_to_all | solution.py:46
  138.4 0.8 shard_map.118
  (12 shorter events, 0.0 us)
Async XLA Ops:
  1.4 8.0 %collective-permute-start = (bf16[16,1024]{1,0:T(8,128)(2,1)S(1)}, bf16[16,1024]{1,0:T(8,128)(2,1)}, u32[]{:S(2)}, u32[]{:S(2)}) collective-permute-start(bf16[16,1024]{1,0:T(8,128)(2,1)S(1)} %slice_bitcast_fusion), channel_id=1, source_target_pairs={{1,0},{2,1},{3,2},{5,4},{6,5},{7,6},{9,8},{10,9},{11,10},{13,12},{... | collective-permute-start | bytes 98312 | tf_op jit(solution)/shard_map/ppermute | solution.py:368
  6.5 24.0 %collective-permute-start.5 = (bf16[128,1024]{1,0:T(8,128)(2,1)}, bf16[128,1024]{1,0:T(8,128)(2,1)}, u32[]{:S(2)}, u32[]{:S(2)}) collective-permute-start(bf16[128,1024]{1,0:T(8,128)(2,1)} %bitcast.16), channel_id=1, source_target_pairs={{0,130},{128,0},{2,128},{130,2},{1,131},{129,1},{3,129},{131,3},{4... | collective-permute-start | bytes 786440 | tf_op jit(solution)/shard_map/ppermute | solution.py:38
  8.1 22.4 %collective-permute-start.4 = (bf16[128,1024]{1,0:T(8,128)(2,1)}, bf16[128,1024]{1,0:T(8,128)(2,1)}, u32[]{:S(2)}, u32[]{:S(2)}) collective-permute-start(bf16[128,1024]{1,0:T(8,128)(2,1)} %bitcast.17), channel_id=1, source_target_pairs={{0,128},{128,2},{2,130},{130,0},{1,129},{129,3},{3,131},{131,1},{4... | collective-permute-start | bytes 786440 | tf_op jit(solution)/shard_map/ppermute | solution.py:38
  13.6 11.5 %collective-permute-start.1 = (bf16[512,128]{1,0:T(8,128)(2,1)}, bf16[512,128]{1,0:T(8,128)(2,1)}, u32[]{:S(2)}, u32[]{:S(2)}) collective-permute-start(bf16[512,128]{1,0:T(8,128)(2,1)} %get-tuple-element.38.refs_3_), channel_id=1, source_target_pairs={{0,4},{4,8},{8,12},{12,16},{16,20},{20,24},{24,28},{28,32},{32,36}... | collective-permute-start | bytes 393224 | tf_op jit(solution)/shard_map/ppermute | solution.py:33
  15.3 22.8 %collective-permute-start.3 = (bf16[512,128]{1,0:T(8,128)(2,1)}, bf16[512,128]{1,0:T(8,128)(2,1)}, u32[]{:S(2)}, u32[]{:S(2)}) collective-permute-start(bf16[512,128]{1,0:T(8,128)(2,1)} %get-tuple-element.38.refs_3_), channel_id=1, source_target_pairs={{0,12},{4,16},{8,20},{12,24},{16,28},{20,32},{24,36},{28,40},{32,4... | collective-permute-start | bytes 393224 | tf_op jit(solution)/shard_map/ppermute | solution.py:33
  20.8 18.5 %collective-permute-start.2 = (bf16[512,128]{1,0:T(8,128)(2,1)}, bf16[512,128]{1,0:T(8,128)(2,1)}, u32[]{:S(2)}, u32[]{:S(2)}) collective-permute-start(bf16[512,128]{1,0:T(8,128)(2,1)} %get-tuple-element.38.refs_3_), channel_id=1, source_target_pairs={{0,8},{4,12},{8,16},{12,20},{16,24},{20,28},{24,32},{28,36},{32,40... | collective-permute-start | bytes 393224 | tf_op jit(solution)/shard_map/ppermute | solution.py:33
  28.4 33.4 %collective-permute-start.10 = (bf16[768,256]{1,0:T(8,128)(2,1)}, bf16[768,256]{1,0:T(8,128)(2,1)}, u32[]{:S(2)}, u32[]{:S(2)}) collective-permute-start(bf16[768,256]{1,0:T(8,128)(2,1)} %get-tuple-element.54.refs_2_), channel_id=1, source_target_pairs={{0,130},{128,0},{2,128},{130,2},{1,131},{129,1},{3,129},{131,3},{4... | collective-permute-start | bytes 1179656 | tf_op jit(solution)/shard_map/ppermute | solution.py:38
  30.5 31.2 %collective-permute-start.9 = (bf16[768,256]{1,0:T(8,128)(2,1)}, bf16[768,256]{1,0:T(8,128)(2,1)}, u32[]{:S(2)}, u32[]{:S(2)}) collective-permute-start(bf16[768,256]{1,0:T(8,128)(2,1)} %get-tuple-element.54.refs_2_), channel_id=1, source_target_pairs={{0,128},{128,2},{2,130},{130,0},{1,129},{129,3},{3,131},{131,1},{4... | collective-permute-start | bytes 1179656 | tf_op jit(solution)/shard_map/ppermute | solution.py:38
  30.6 28.4 %collective-permute-start.11 = (bf16[128,1024]{1,0:T(8,128)(2,1)}, bf16[128,1024]{1,0:T(8,128)(2,1)}, u32[]{:S(2)}, u32[]{:S(2)}) collective-permute-start(bf16[128,1024]{1,0:T(8,128)(2,1)} %collective-permute-done.4.refs_11_), channel_id=1, source_target_pairs={{0,128},{128,2},{2,130},{130,0},{1,129},{129,3},{3,131},{131,1},{4... | collective-permute-start | bytes 786440 | tf_op jit(solution)/shard_map/ppermute | solution.py:38
  46.4 8.6 %collective-permute-start.6 = (bf16[512,128]{1,0:T(8,128)(2,1)}, bf16[512,128]{1,0:T(8,128)(2,1)}, u32[]{:S(2)}, u32[]{:S(2)}) collective-permute-start(bf16[512,128]{1,0:T(8,128)(2,1)} %get-tuple-element.47), channel_id=1, source_target_pairs={{0,252},{4,0},{8,4},{12,8},{16,12},{20,16},{24,20},{28,24},{32,28}... | collective-permute-start | bytes 393224 | tf_op jit(solution)/shard_map/ppermute | solution.py:33
  48.6 13.2 %collective-permute-start.7 = (bf16[512,128]{1,0:T(8,128)(2,1)}, bf16[512,128]{1,0:T(8,128)(2,1)}, u32[]{:S(2)}, u32[]{:S(2)}) collective-permute-start(bf16[512,128]{1,0:T(8,128)(2,1)} %get-tuple-element.50), channel_id=1, source_target_pairs={{0,248},{4,252},{8,0},{12,4},{16,8},{20,12},{24,16},{28,20},{32,24... | collective-permute-start | bytes 393224 | tf_op jit(solution)/shard_map/ppermute | solution.py:33
  55.0 7.8 %collective-permute-start.8 = (bf16[512,128]{1,0:T(8,128)(2,1)}, bf16[512,128]{1,0:T(8,128)(2,1)}, u32[]{:S(2)}, u32[]{:S(2)}) collective-permute-start(bf16[512,128]{1,0:T(8,128)(2,1)} %get-tuple-element.51), channel_id=1, source_target_pairs={{0,244},{4,248},{8,252},{12,0},{16,4},{20,8},{24,12},{28,16},{32,2... | collective-permute-start | bytes 393224 | tf_op jit(solution)/shard_map/ppermute | solution.py:33
  58.9 18.2 %collective-permute-start.12 = (bf16[768,256]{1,0:T(8,128)(2,1)}, bf16[768,256]{1,0:T(8,128)(2,1)}, u32[]{:S(2)}, u32[]{:S(2)}) collective-permute-start(bf16[768,256]{1,0:T(8,128)(2,1)} %get-tuple-element.54.refs_2_), channel_id=1, source_target_pairs={{0,2},{128,130},{2,0},{130,128},{1,3},{129,131},{3,1},{131,129},{4... | collective-permute-start | bytes 1179656 | tf_op jit(solution)/shard_map/ppermute | solution.py:38
  66.4 19.3 %all-to-all-start = ((bf16[8,368,128]{2,1,0:T(8,128)(2,1)}), bf16[8,368,128]{2,1,0:T(8,128)(2,1)}, u32[]{:S(2)}, u32[]{:S(2)}) async-start(bf16[8,368,128]{2,1,0:T(8,128)(2,1)} %shard_map.115), calls=%async_computation | async-start | bytes 1507328 | tf_op jit(solution)/shard_map/all_to_all | solution.py:46
  75.0 1.9 %collective-permute-start.17 = (bf16[128,1024]{1,0:T(8,128)(2,1)}, bf16[128,1024]{1,0:T(8,128)(2,1)}, u32[]{:S(2)}, u32[]{:S(2)}) collective-permute-start(bf16[128,1024]{1,0:T(8,128)(2,1)} %bitcast.19), channel_id=1, source_target_pairs={{0,1},{1,0},{2,3},{3,2},{4,5},{5,4},{6,7},{7,6},{8,9},{9,8},{10,11... | collective-permute-start | bytes 786440 | tf_op jit(solution)/shard_map/ppermute | solution.py:42
  75.2 2.2 %collective-permute-start.18 = (bf16[128,1024]{1,0:T(8,128)(2,1)}, bf16[128,1024]{1,0:T(8,128)(2,1)}, u32[]{:S(2)}, u32[]{:S(2)}) collective-permute-start(bf16[128,1024]{1,0:T(8,128)(2,1)} %collective-permute-done.4.refs_11_), channel_id=1, source_target_pairs={{0,1},{1,0},{2,3},{3,2},{4,5},{5,4},{6,7},{7,6},{8,9},{9,8},{10,11... | collective-permute-start | bytes 786440 | tf_op jit(solution)/shard_map/ppermute | solution.py:42
  75.5 2.1 %collective-permute-start.20 = (bf16[128,1024]{1,0:T(8,128)(2,1)}, bf16[128,1024]{1,0:T(8,128)(2,1)}, u32[]{:S(2)}, u32[]{:S(2)}) collective-permute-start(bf16[128,1024]{1,0:T(8,128)(2,1)} %collective-permute-done.5.refs_13_), channel_id=1, source_target_pairs={{0,1},{1,0},{2,3},{3,2},{4,5},{5,4},{6,7},{7,6},{8,9},{9,8},{10,11... | collective-permute-start | bytes 786440 | tf_op jit(solution)/shard_map/ppermute | solution.py:42
  75.8 2.8 %collective-permute-start.13 = (bf16[768,256]{1,0:T(8,128)(2,1)}, bf16[768,256]{1,0:T(8,128)(2,1)}, u32[]{:S(2)}, u32[]{:S(2)}) collective-permute-start(bf16[768,256]{1,0:T(8,128)(2,1)} %get-tuple-element.54.refs_2_), channel_id=1, source_target_pairs={{0,1},{1,0},{2,3},{3,2},{4,5},{5,4},{6,7},{7,6},{8,9},{9,8},{10,11... | collective-permute-start | bytes 1179656 | tf_op jit(solution)/shard_map/ppermute | solution.py:42
  76.9 3.6 %collective-permute-start.14 = (bf16[768,256]{1,0:T(8,128)(2,1)}, bf16[768,256]{1,0:T(8,128)(2,1)}, u32[]{:S(2)}, u32[]{:S(2)}) collective-permute-start(bf16[768,256]{1,0:T(8,128)(2,1)} %collective-permute-done.9.refs_3_), channel_id=1, source_target_pairs={{0,1},{1,0},{2,3},{3,2},{4,5},{5,4},{6,7},{7,6},{8,9},{9,8},{10,11... | collective-permute-start | bytes 1179656 | tf_op jit(solution)/shard_map/ppermute | solution.py:42
  77.1 3.3 %collective-permute-start.15 = (bf16[768,256]{1,0:T(8,128)(2,1)}, bf16[768,256]{1,0:T(8,128)(2,1)}, u32[]{:S(2)}, u32[]{:S(2)}) collective-permute-start(bf16[768,256]{1,0:T(8,128)(2,1)} %collective-permute-done.12.refs_4_), channel_id=1, source_target_pairs={{0,1},{1,0},{2,3},{3,2},{4,5},{5,4},{6,7},{7,6},{8,9},{9,8},{10,11... | collective-permute-start | bytes 1179656 | tf_op jit(solution)/shard_map/ppermute | solution.py:42
  77.4 3.1 %collective-permute-start.16 = (bf16[768,256]{1,0:T(8,128)(2,1)}, bf16[768,256]{1,0:T(8,128)(2,1)}, u32[]{:S(2)}, u32[]{:S(2)}) collective-permute-start(bf16[768,256]{1,0:T(8,128)(2,1)} %collective-permute-done.10.refs_5_), channel_id=1, source_target_pairs={{0,1},{1,0},{2,3},{3,2},{4,5},{5,4},{6,7},{7,6},{8,9},{9,8},{10,11... | collective-permute-start | bytes 1179656 | tf_op jit(solution)/shard_map/ppermute | solution.py:42
  77.7 2.8 %collective-permute-start.19 = (bf16[128,1024]{1,0:T(8,128)(2,1)}, bf16[128,1024]{1,0:T(8,128)(2,1)}, u32[]{:S(2)}, u32[]{:S(2)}) collective-permute-start(bf16[128,1024]{1,0:T(8,128)(2,1)} %collective-permute-done.11.refs_12_), channel_id=1, source_target_pairs={{0,1},{1,0},{2,3},{3,2},{4,5},{5,4},{6,7},{7,6},{8,9},{9,8},{10,11... | collective-permute-start | bytes 786440 | tf_op jit(solution)/shard_map/ppermute | solution.py:42
  92.5 29.9 %all-to-all-start.1 = ((bf16[32,104,128]{2,1,0:T(8,128)(2,1)}), bf16[32,104,128]{2,1,0:T(8,128)(2,1)S(1)}, u32[]{:S(2)}, u32[]{:S(2)}) async-start(bf16[32,104,128]{2,1,0:T(8,128)(2,1)} %bitcast.14), calls=%async_computation.1 | async-start | bytes 1703936 | tf_op jit(solution)/shard_map/all_to_all | solution.py:46
  124.3 14.0 %all-to-all-start.2 = ((f32[8,8,256]{2,1,0:T(8,128)}), f32[8,8,256]{2,1,0:T(8,128)S(1)}, u32[]{:S(2)}, u32[]{:S(2)}) async-start(f32[8,8,256]{2,1,0:T(8,128)} %get-tuple-element.69), calls=%async_computation.2 | async-start | bytes 131072 | tf_op jit(solution)/shard_map/all_to_all | solution.py:46
